TPU v7x, 32 devices: a whole 2x2x4 slice. The times are simulated.
32 devices in a mesh: dp: 16 (over z, y, core), seq: 2 (over x).
Axes of the slice: x: 2, y: 2, z: 4, core: 2. Of those that a mesh axis runs over, the one named last changes fastest.
Arguments:
- src_ids: int32 [32, 1024], P('dp', 'seq'), may hold values from 4 to 31999
- tgt_ids: int32 [32, 1024], P('dp', 'seq'), may hold values from 4 to 31999
- src_lengths: int32 [32, 32], P('dp'), may hold values from 1 to 512, as said below
- tgt_lengths: int32 [32, 32], P('dp'), may hold values from 1 to 512, as said below
- tgt_mask: int32 [32, 1024], P('dp', 'seq'), may hold values from 0 to 1
- attn_in: float32 [3, 512, 1536], P(None, 'dp'), may hold values from -0.25 to 0.25
- attn_in_m1: float32 [3, 512, 1536], P(None, 'dp'), may hold values from -7.1525574e-07 to 7.1525574e-07
- attn_in_m2: float32 [3, 512, 1536], P(None, 'dp'), may hold values from 3.3525727e-15 to 1.3829362e-14
- attn_out: float32 [3, 512, 512], P(None, 'dp'), may hold values from -1.5 to 1.5
- attn_out_m1: float32 [3, 512, 512], P(None, 'dp'), may hold values from -7.1525574e-07 to 7.1525574e-07
- attn_out_m2: float32 [3, 512, 512], P(None, 'dp'), may hold values from 3.3525727e-15 to 1.3829362e-14
- ffn_in: float32 [2, 512, 2048], P(None, 'dp'), may hold values from -0.25 to 0.25
- ffn_in_m1: float32 [2, 512, 2048], P(None, 'dp'), may hold values from -7.1525574e-07 to 7.1525574e-07
- ffn_in_m2: float32 [2, 512, 2048], P(None, 'dp'), may hold values from 3.3525727e-15 to 1.3829362e-14
- ffn_out: float32 [2, 2048, 512], P(None, 'dp'), may hold values from -0.125 to 0.125
- ffn_out_m1: float32 [2, 2048, 512], P(None, 'dp'), may hold values from -7.1525574e-07 to 7.1525574e-07
- ffn_out_m2: float32 [2, 2048, 512], P(None, 'dp'), may hold values from 3.3525727e-15 to 1.3829362e-14
- len_head: float32 [512, 256], P('dp'), may hold values from -0.25 to 0.25
- len_head_m1: float32 [512, 256], P('dp'), may hold values from -7.1525574e-07 to 7.1525574e-07
- len_head_m2: float32 [512, 256], P('dp'), may hold values from 3.3525727e-15 to 1.3829362e-14
- norms: float32 [2, 7, 512], P(None, None, 'dp')
- norms_m1: float32 [2, 7, 512], P(None, None, 'dp'), may hold values from -2.861023e-06 to 2.861023e-06
- norms_m2: float32 [2, 7, 512], P(None, None, 'dp'), may hold values from 5.4479306e-14 to 2.1791722e-13
- table: float32 [32000, 512], P(('seq', 'dp'))
- table_m1: float32 [32000, 512], P(('seq', 'dp')), may hold values from -7.1525574e-07 to 7.1525574e-07
- table_m2: float32 [32000, 512], P(('seq', 'dp'))
Outputs:
- token_loss_sum: float32 [], replicated
- mask_count: float32 [], replicated
- len_loss_sum: float32 [], replicated
- grad_norm: float32 [], replicated
- attn_in_new: float32 [3, 512, 1536], P(None, 'dp')
- attn_in_m1_new: float32 [3, 512, 1536], P(None, 'dp')
- attn_in_m2_new: float32 [3, 512, 1536], P(None, 'dp')
- attn_out_new: float32 [3, 512, 512], P(None, 'dp')
- attn_out_m1_new: float32 [3, 512, 512], P(None, 'dp')
- attn_out_m2_new: float32 [3, 512, 512], P(None, 'dp')
- ffn_in_new: float32 [2, 512, 2048], P(None, 'dp')
- ffn_in_m1_new: float32 [2, 512, 2048], P(None, 'dp')
- ffn_in_m2_new: float32 [2, 512, 2048], P(None, 'dp')
- ffn_out_new: float32 [2, 2048, 512], P(None, 'dp')
- ffn_out_m1_new: float32 [2, 2048, 512], P(None, 'dp')
- ffn_out_m2_new: float32 [2, 2048, 512], P(None, 'dp')
- len_head_new: float32 [512, 256], P('dp')
- len_head_m1_new: float32 [512, 256], P('dp')
- len_head_m2_new: float32 [512, 256], P('dp')
- norms_new: float32 [2, 7, 512], P(None, None, 'dp')
- norms_m1_new: float32 [2, 7, 512], P(None, None, 'dp')
- norms_m2_new: float32 [2, 7, 512], P(None, None, 'dp')
- table_new: float32 [32000, 512], P(('seq', 'dp'))
- table_m1_new: float32 [32000, 512], P(('seq', 'dp'))
- table_m2_new: float32 [32000, 512], P(('seq', 'dp'))
Inputs may be any that keep to these rules, and one draw needn't show every extreme that they name: `src_lengths`: the 32 lengths of each row sum to 1024. `tgt_lengths`: the 32 lengths of each row sum to 1024.
All inputs are finite; a program needn't handle non-finite values.
Results may differ from a plain program's by a relative error of at most 0.0045.
The roundings to bfloat16 on the way count: a program that leaves them out, or rounds other values in their place, can miss the bound.
Values may be sent and summed in bfloat16 or wider, within the bound.
No kernel may reach another device: no remote copies, remote signals or barrier semaphores. Data moves between devices by JAX's collectives and lax.ppermute only.
A program may use at most 448 MiB of HBM per device.

v0:
```python
import math

import jax
import jax.numpy as jnp
from jax import lax
from jax.sharding import PartitionSpec as P

HEADS = 8
STEP = 10


length_token = 1
mask_token = 2
clip_limit = 0.002
beta_one = 0.9
beta_two = 0.98
adam_eps = 1e-08
weight_decay = 0.01
step_rates = (0.05, 0.25, 0.05, 0.025, 0.05, 0.5, 0.1)


def joined(part, axis, combine):
    gathered = jax.tree.map(lambda a: lax.all_gather(a, axis), part)

    def take(source):
        return jax.tree.map(lambda a: lax.dynamic_index_in_dim(a, source, 0, False), gathered)

    return lax.fori_loop(
        1, lax.axis_size(axis), lambda source, state: combine(state, take(source)), take(0)
    )


def layout(lengths, places):
    starts = jnp.cumsum(lengths, -1) - lengths
    covered = places[..., :, None] >= starts[..., None, :]
    segment = jnp.sum(covered.astype(jnp.int32), -1) - 1
    opening = jnp.max(jnp.where(covered, starts[..., None, :], 0), -1)
    return (segment, places - opening, starts)


def sinusoid(positions, width):
    half_width = width // 2
    frequency = jnp.exp(
        jnp.arange(half_width).astype(jnp.float32) * (-math.log(10000.0) / half_width)
    )
    angles = positions.astype(jnp.float32)[..., None] * frequency
    return jnp.concatenate([jnp.sin(angles), jnp.cos(angles)], -1)


def layer_norm(stream, norm_gain, norm_bias):
    average = jnp.mean(stream, -1, keepdims=True)
    centred = stream - average
    variance = jnp.mean(centred * centred, -1, keepdims=True)
    return centred * lax.rsqrt(variance + 1e-05) * norm_gain + norm_bias


def norm_backward(stream, norm_gain, norm_bias, grad):
    return jax.vjp(layer_norm, stream, norm_gain, norm_bias)[1](grad)


def product(left, right):
    return jnp.einsum("...d,de->...e", left, right, preferred_element_type=jnp.float32)


def weight_grad(left, right):
    return jnp.einsum("...d,...e->de", left, right, preferred_element_type=jnp.float32)


def back_product(grad, right):
    return jnp.einsum("...e,de->...d", grad, right, preferred_element_type=jnp.float32)


def split_heads(values):
    return values.reshape(values.shape[:2] + (HEADS, -1))


def scores(query_heads, key_heads, allowed):
    scaled = jnp.einsum(
        "rthd,rlhd->rhtl", query_heads, key_heads, preferred_element_type=jnp.float32
    ) * query_heads.shape[-1] ** (-0.5)
    return jnp.where(allowed[:, None], scaled, -1e30)


def attend_forward(query_in, memory_in, weight_in, weight_out, allowed):
    width = query_in.shape[-1]
    queries = product(query_in, weight_in[:, :width]).astype(jnp.bfloat16)
    key_values = product(memory_in, weight_in[:, width:]).astype(jnp.bfloat16)
    gathered = lax.all_gather(key_values, "seq", axis=1, tiled=True)
    raw = scores(split_heads(queries), split_heads(gathered[..., :width]), allowed)
    top_score = jnp.max(raw, -1, keepdims=True)
    powers = jnp.exp(raw - top_score)
    totals = jnp.sum(powers, -1, keepdims=True)
    probs = (powers / totals).astype(jnp.bfloat16)
    mixed = jnp.einsum(
        "rhtl,rlhd->rthd",
        probs,
        split_heads(gathered[..., width:]),
        preferred_element_type=jnp.float32,
    )
    mixed = mixed.reshape(queries.shape).astype(jnp.bfloat16)
    return (product(mixed, weight_out), (queries, gathered, mixed, top_score + jnp.log(totals)))


def attend_backward(query_in, memory_in, weight_in, weight_out, allowed, kept, grad):
    queries, gathered, mixed, log_total = kept
    width = queries.shape[-1]
    grad_low = grad.astype(jnp.bfloat16)
    d_out = weight_grad(mixed, grad_low)
    d_mixed = split_heads(back_product(grad_low, weight_out).astype(jnp.bfloat16))
    query_heads = split_heads(queries)
    key_heads = split_heads(gathered[..., :width])
    value_heads = split_heads(gathered[..., width:])
    probs = jnp.exp(scores(query_heads, key_heads, allowed) - log_total)
    d_values = jnp.einsum(
        "rhtl,rthd->rlhd", probs.astype(jnp.bfloat16), d_mixed, preferred_element_type=jnp.float32
    )
    d_probs = jnp.einsum(
        "rthd,rlhd->rhtl", d_mixed, value_heads, preferred_element_type=jnp.float32
    )
    d_scores = (probs * (d_probs - jnp.sum(d_probs * probs, -1, keepdims=True))).astype(
        jnp.bfloat16
    )
    scale = query_heads.shape[-1] ** (-0.5)
    d_queries = (
        jnp.einsum("rhtl,rlhd->rthd", d_scores, key_heads, preferred_element_type=jnp.float32)
        * scale
    )
    d_keys = (
        jnp.einsum("rhtl,rthd->rlhd", d_scores, query_heads, preferred_element_type=jnp.float32)
        * scale
    )
    pair_shape = gathered.shape[:2] + (width,)
    d_pairs = jnp.concatenate([d_keys.reshape(pair_shape), d_values.reshape(pair_shape)], -1)
    d_pairs = lax.psum_scatter(d_pairs.astype(jnp.bfloat16), "seq", scatter_dimension=1, tiled=True)
    d_queries = d_queries.reshape(queries.shape).astype(jnp.bfloat16)
    d_in = jnp.concatenate([weight_grad(query_in, d_queries), weight_grad(memory_in, d_pairs)], 1)
    return (
        back_product(d_queries, weight_in[:, :width]),
        back_product(d_pairs, weight_in[:, width:]),
        d_in,
        d_out,
    )


def ffn_forward(stream_in, weight_one, weight_two):
    hidden = product(stream_in, weight_one)
    active = jax.nn.gelu(hidden).astype(jnp.bfloat16)
    return (product(active, weight_two), (hidden, active))


def ffn_backward(stream_in, weight_one, weight_two, kept, grad):
    hidden, active = kept
    grad_low = grad.astype(jnp.bfloat16)
    d_two = weight_grad(active, grad_low)
    d_active = back_product(grad_low, weight_two)
    d_hidden = jax.vjp(jax.nn.gelu, hidden)[1](d_active)[0].astype(jnp.bfloat16)
    return (back_product(d_hidden, weight_one), weight_grad(stream_in, d_hidden), d_two)


def adam_update(weight, first, second, grad, rate):
    first = beta_one * first + (1 - beta_one) * grad
    second = beta_two * second + (1 - beta_two) * grad * grad
    first_hat = first / (1 - beta_one**STEP)
    second_hat = second / (1 - beta_two**STEP)
    weight = weight - rate * (first_hat / (jnp.sqrt(second_hat) + adam_eps) + weight_decay * weight)
    return (weight, first, second)


def to_owners(layer_grads, table_grad):
    return (
        lax.psum_scatter(layer_grads[0], "dp", scatter_dimension=1, tiled=True),
        lax.psum_scatter(layer_grads[1], "dp", scatter_dimension=1, tiled=True),
        lax.psum_scatter(layer_grads[2], "dp", scatter_dimension=1, tiled=True),
        lax.psum_scatter(layer_grads[3], "dp", scatter_dimension=1, tiled=True),
        lax.psum_scatter(layer_grads[4], "dp", scatter_dimension=0, tiled=True),
        lax.psum_scatter(layer_grads[5], "dp", scatter_dimension=2, tiled=True),
        lax.psum_scatter(table_grad, "dp", scatter_dimension=0, tiled=True),
    )


def on_device(
    src_ids,
    tgt_ids,
    src_lengths,
    tgt_lengths,
    tgt_mask,
    attn_in,
    attn_in_m1,
    attn_in_m2,
    attn_out,
    attn_out_m1,
    attn_out_m2,
    ffn_in,
    ffn_in_m1,
    ffn_in_m2,
    ffn_out,
    ffn_out_m1,
    ffn_out_m2,
    len_head,
    len_head_m1,
    len_head_m2,
    norms,
    norms_m1,
    norms_m2,
    table,
    table_m1,
    table_m2,
):
    rows_here, seq_rows = src_ids.shape
    row_len = seq_rows * lax.axis_size("seq")
    seq_index = lax.axis_index("seq")
    offset = seq_index * seq_rows
    low_type = jnp.bfloat16
    w_in, w_out, f_in, f_out, w_len, norm_low, table_part = (
        lax.all_gather(attn_in.astype(low_type), "dp", axis=1, tiled=True),
        lax.all_gather(attn_out.astype(low_type), "dp", axis=1, tiled=True),
        lax.all_gather(ffn_in.astype(low_type), "dp", axis=1, tiled=True),
        lax.all_gather(ffn_out.astype(low_type), "dp", axis=1, tiled=True),
        lax.all_gather(len_head.astype(low_type), "dp", axis=0, tiled=True),
        lax.all_gather(norms.astype(low_type), "dp", axis=2, tiled=True),
        lax.all_gather(table.astype(low_type), "dp", axis=0, tiled=True),
    )
    width = w_len.shape[0]
    vocab_width = table_part.shape[0]
    vocab_base = seq_index * vocab_width
    gains = norm_low[0].astype(jnp.float32)
    biases = norm_low[1].astype(jnp.float32)
    own_places = offset + jnp.arange(seq_rows)
    row_places = jnp.arange(row_len)
    src_seg, src_pos, src_start = layout(src_lengths, own_places)
    tgt_seg, tgt_pos, tgt_start = layout(tgt_lengths, own_places)
    src_every = layout(src_lengths, row_places)[0]
    tgt_every = layout(tgt_lengths, row_places)[0]
    src_in = jnp.where(src_pos == 0, length_token, src_ids)
    dec_in = jnp.where(tgt_mask == 1, mask_token, tgt_ids)
    labels = jnp.where(tgt_mask == 1, tgt_ids, -1)
    src_group, dec_group, label_group = (
        lax.all_gather(src_in, "seq", axis=1, tiled=True),
        lax.all_gather(dec_in, "seq", axis=1, tiled=True),
        lax.all_gather(labels, "seq", axis=1, tiled=True),
    )

    def lookup(token_ids):
        local = token_ids - vocab_base
        inside = (local >= 0) & (local < vocab_width)
        found = jnp.take(table_part, jnp.clip(local, 0, vocab_width - 1), axis=0).astype(
            jnp.float32
        )
        return jnp.where(inside[..., None], found, 0.0)

    def spread(token_ids, grads):
        local = token_ids - vocab_base
        inside = (local >= 0) & (local < vocab_width)
        terms = jnp.where(inside[..., None], grads, 0.0).reshape(-1, width)
        return (
            jnp.zeros((vocab_width, width), jnp.float32)
            .at[jnp.clip(local, 0, vocab_width - 1).reshape(-1)]
            .add(terms)
        )

    emb_src, emb_dec = (
        lax.psum_scatter(
            lookup(src_group).astype(jnp.bfloat16), "seq", scatter_dimension=1, tiled=True
        ).astype(jnp.float32),
        lax.psum_scatter(
            lookup(dec_group).astype(jnp.bfloat16), "seq", scatter_dimension=1, tiled=True
        ).astype(jnp.float32),
    )
    root = math.sqrt(width)
    stream0 = emb_src * root + sinusoid(src_pos, width)
    target0 = emb_dec * root + sinusoid(tgt_pos, width)
    enc_mask = src_seg[:, :, None] == src_every[:, None, :]
    self_mask = tgt_seg[:, :, None] == tgt_every[:, None, :]
    cross_mask = tgt_seg[:, :, None] == src_every[:, None, :]

    def norm(stream, index):
        return layer_norm(stream, gains[index], biases[index])

    inner0 = norm(stream0, 0).astype(low_type)
    branch0, keep_one = attend_forward(inner0, inner0, w_in[0], w_out[0], enc_mask)
    stream1 = stream0 + branch0
    inner1 = norm(stream1, 1).astype(low_type)
    branch1, keep_two = ffn_forward(inner1, f_in[0], f_out[0])
    stream2 = stream1 + branch1
    memory = norm(stream2, 2).astype(low_type)
    inner3 = norm(target0, 3).astype(low_type)
    branch3, keep_three = attend_forward(inner3, inner3, w_in[1], w_out[1], self_mask)
    target1 = target0 + branch3
    inner4 = norm(target1, 4).astype(low_type)
    branch4, keep_four = attend_forward(inner4, memory, w_in[2], w_out[2], cross_mask)
    target2 = target1 + branch4
    inner5 = norm(target2, 5).astype(low_type)
    branch5, keep_five = ffn_forward(inner5, f_in[1], f_out[1])
    target3 = target2 + branch5
    final = norm(target3, 6).astype(low_type)
    gathered = lax.all_gather(final, "seq", axis=1, tiled=True)
    block = min(512, rows_here * row_len)
    pieces = gathered.reshape(-1, block, width)
    targets = (label_group - vocab_base).reshape(-1, block)
    columns = jnp.arange(vocab_width)

    def head_stats(item):
        piece, target = item
        logits = jnp.einsum("bd,vd->bv", piece, table_part, preferred_element_type=jnp.float32)
        top_logit = jnp.max(logits, -1)
        totals = jnp.sum(jnp.exp(logits - top_logit[:, None]), -1)
        target_logit = jnp.sum(jnp.where(columns[None, :] == target[:, None], logits, 0.0), -1)
        return (top_logit, totals, target_logit)

    stats = lax.map(head_stats, (pieces, targets))

    def combine(first, second):
        top_logit = jnp.maximum(first[0], second[0])
        totals = first[1] * jnp.exp(first[0] - top_logit) + second[1] * jnp.exp(
            second[0] - top_logit
        )
        return (top_logit, totals, first[2] + second[2])

    top_logit, totals, target_logit = joined((stats[0], stats[1], stats[2]), "seq", combine)
    log_total = top_logit + jnp.log(totals)
    counted = label_group.reshape(log_total.shape) >= 0
    loss_rows = jnp.where(counted, log_total - target_logit, 0.0).reshape(rows_here, row_len)
    token_local = jnp.sum(lax.dynamic_slice_in_dim(loss_rows, offset, seq_rows, 1))
    count_local = jnp.sum(tgt_mask).astype(jnp.float32)
    pick = own_places[None, None, :] == src_start[:, :, None]
    first_rows = jnp.einsum(
        "rst,rtd->rsd", pick.astype(low_type), memory, preferred_element_type=jnp.float32
    ).astype(low_type)
    mine = jnp.any(pick, -1)
    len_logits = product(first_rows, w_len)
    classes = len_logits.shape[-1]
    len_label = jnp.minimum(tgt_lengths, classes - 1)
    len_hot = jnp.arange(classes)[None, None, :] == len_label[..., None]
    len_loss = jax.nn.logsumexp(len_logits, -1) - jnp.sum(jnp.where(len_hot, len_logits, 0.0), -1)
    len_local = jnp.sum(jnp.where(mine, len_loss, 0.0))
    token_sum, count, len_sum = lax.psum((token_local, count_local, len_local), ("dp", "seq"))
    sentences = rows_here * src_lengths.shape[1] * lax.axis_size("dp")
    row_weight = counted.astype(jnp.float32) / count

    def head_back(carry, item):
        piece, target, log_part, weight_part = item
        logits = jnp.einsum("bd,vd->bv", piece, table_part, preferred_element_type=jnp.float32)
        probs = jnp.exp(logits - log_part[:, None])
        hot = (columns[None, :] == target[:, None]).astype(jnp.float32)
        d_logits = ((probs - hot) * weight_part[:, None]).astype(low_type)
        carry = carry + jnp.einsum("bv,bd->vd", d_logits, piece, preferred_element_type=jnp.float32)
        return (carry, jnp.dot(d_logits, table_part, preferred_element_type=jnp.float32))

    d_table, d_rows = lax.scan(
        head_back,
        jnp.zeros((vocab_width, width), jnp.float32),
        (pieces, targets, log_total, row_weight),
    )
    d_final = lax.psum_scatter(
        d_rows.reshape(rows_here, row_len, width), "seq", scatter_dimension=1, tiled=True
    )
    len_prob = jax.nn.softmax(len_logits, -1)
    d_len_logits = (
        jnp.where(mine[..., None], len_prob - len_hot.astype(jnp.float32), 0.0) * (0.1 / sentences)
    ).astype(low_type)
    d_w_len = weight_grad(first_rows, d_len_logits)
    d_first = back_product(d_len_logits, w_len)
    d_memory = jnp.einsum("rst,rsd->rtd", pick.astype(jnp.float32), d_first)
    d_target3, gain6, bias6 = norm_backward(target3, gains[6], biases[6], d_final)
    d_inner5, d_fin1, d_fout1 = ffn_backward(inner5, f_in[1], f_out[1], keep_five, d_target3)
    d_target2, gain5, bias5 = norm_backward(target2, gains[5], biases[5], d_inner5)
    d_target2 = d_target2 + d_target3
    d_inner4, d_cross, d_win2, d_wout2 = attend_backward(
        inner4, memory, w_in[2], w_out[2], cross_mask, keep_four, d_target2
    )
    d_target1, gain4, bias4 = norm_backward(target1, gains[4], biases[4], d_inner4)
    d_target1 = d_target1 + d_target2
    d_query3, d_key3, d_win1, d_wout1 = attend_backward(
        inner3, inner3, w_in[1], w_out[1], self_mask, keep_three, d_target1
    )
    d_target0, gain3, bias3 = norm_backward(target0, gains[3], biases[3], d_query3 + d_key3)
    d_target0 = d_target0 + d_target1
    d_stream2, gain2, bias2 = norm_backward(stream2, gains[2], biases[2], d_memory + d_cross)
    d_inner1, d_fin0, d_fout0 = ffn_backward(inner1, f_in[0], f_out[0], keep_two, d_stream2)
    d_stream1, gain1, bias1 = norm_backward(stream1, gains[1], biases[1], d_inner1)
    d_stream1 = d_stream1 + d_stream2
    d_query0, d_key0, d_win0, d_wout0 = attend_backward(
        inner0, inner0, w_in[0], w_out[0], enc_mask, keep_one, d_stream1
    )
    d_stream0, gain0, bias0 = norm_backward(stream0, gains[0], biases[0], d_query0 + d_key0)
    d_stream0 = d_stream0 + d_stream1
    d_src_all, d_dec_all = (
        lax.all_gather((d_stream0 * root).astype(jnp.bfloat16), "seq", axis=1, tiled=True).astype(
            jnp.float32
        ),
        lax.all_gather((d_target0 * root).astype(jnp.bfloat16), "seq", axis=1, tiled=True).astype(
            jnp.float32
        ),
    )
    d_table = d_table + spread(src_group, d_src_all) + spread(dec_group, d_dec_all)
    d_norms = jnp.stack(
        [
            jnp.stack([gain0, gain1, gain2, gain3, gain4, gain5, gain6]),
            jnp.stack([bias0, bias1, bias2, bias3, bias4, bias5, bias6]),
        ]
    )
    layer_grads = (
        jnp.stack([d_win0, d_win1, d_win2]),
        jnp.stack([d_wout0, d_wout1, d_wout2]),
        jnp.stack([d_fin0, d_fin1]),
        jnp.stack([d_fout0, d_fout1]),
        d_w_len,
        d_norms,
    )
    layer_grads = tuple(
        (
            lax.psum(layer_grads[0].astype(jnp.bfloat16), "seq").astype(jnp.float32),
            lax.psum(layer_grads[1].astype(jnp.bfloat16), "seq").astype(jnp.float32),
            lax.psum(layer_grads[2].astype(jnp.bfloat16), "seq").astype(jnp.float32),
            lax.psum(layer_grads[3].astype(jnp.bfloat16), "seq").astype(jnp.float32),
            lax.psum(layer_grads[4].astype(jnp.bfloat16), "seq").astype(jnp.float32),
            lax.psum(layer_grads[5].astype(jnp.bfloat16), "seq").astype(jnp.float32),
        )
    )
    reduced = tuple(to_owners(layer_grads, d_table))
    layer_square = sum((jnp.sum(grad * grad) for grad in reduced[:6]))
    table_square = jnp.sum(reduced[6] * reduced[6])
    local_square = jnp.where(seq_index == 0, layer_square, 0.0) + table_square
    total_square = lax.psum(local_square, ("dp", "seq"))
    grad_norm = jnp.sqrt(total_square)
    factor = jnp.minimum(1.0, clip_limit / (grad_norm + 1e-06))
    masters = (attn_in, attn_out, ffn_in, ffn_out, len_head, norms, table)
    firsts = (attn_in_m1, attn_out_m1, ffn_in_m1, ffn_out_m1, len_head_m1, norms_m1, table_m1)
    seconds = (attn_in_m2, attn_out_m2, ffn_in_m2, ffn_out_m2, len_head_m2, norms_m2, table_m2)
    updates = []
    for weight, first, second, grad, rate in zip(masters, firsts, seconds, reduced, step_rates):
        updates.extend(adam_update(weight, first, second, grad * factor, rate))
    return (token_sum, count, len_sum, grad_norm, *updates)


def solution(mesh):
    in_specs = (
        P("dp", "seq"),
        P("dp", "seq"),
        P("dp", None),
        P("dp", None),
        P("dp", "seq"),
        P(None, "dp", None),
        P(None, "dp", None),
        P(None, "dp", None),
        P(None, "dp", None),
        P(None, "dp", None),
        P(None, "dp", None),
        P(None, "dp", None),
        P(None, "dp", None),
        P(None, "dp", None),
        P(None, "dp", None),
        P(None, "dp", None),
        P(None, "dp", None),
        P("dp", None),
        P("dp", None),
        P("dp", None),
        P(None, None, "dp"),
        P(None, None, "dp"),
        P(None, None, "dp"),
        P(("seq", "dp"), None),
        P(("seq", "dp"), None),
        P(("seq", "dp"), None),
    )
    out_specs = (
        P(),
        P(),
        P(),
        P(),
        P(None, "dp", None),
        P(None, "dp", None),
        P(None, "dp", None),
        P(None, "dp", None),
        P(None, "dp", None),
        P(None, "dp", None),
        P(None, "dp", None),
        P(None, "dp", None),
        P(None, "dp", None),
        P(None, "dp", None),
        P(None, "dp", None),
        P(None, "dp", None),
        P("dp", None),
        P("dp", None),
        P("dp", None),
        P(None, None, "dp"),
        P(None, None, "dp"),
        P(None, None, "dp"),
        P(("seq", "dp"), None),
        P(("seq", "dp"), None),
        P(("seq", "dp"), None),
    )
    return jax.shard_map(
        on_device, mesh=mesh, in_specs=in_specs, out_specs=out_specs, check_vma=False
    )
```

profile of v0, /device:TPU:0, one launch (start us, length us, event | category | flops | bytes accessed | tf_op | source)
XLA Modules:
  0.0 2977.1 jit_solution(2872527971154629480)
XLA Ops:
  18.0 120.0 %all-gather.18.cloned.1.call-done = bf16[16000,512]{1,0:T(8,128)(2,1)} async-done(((bf16[1000,512]{1,0:T(8,128)(2,1)}), bf16[16000,512]{1,0:T(8,128)(2,1)}) %all-gather.18.cloned.1.call-update) | async-done | bytes 16384016 | tf_op jit(solution)/shard_map/all_gather | solution.py:221
  284.7 40.4 %all-gather.22.cloned.1.call-done = bf16[2,1024,1024]{2,1,0:T(8,128)(2,1)} async-done(((bf16[2,512,1024]{2,1,0:T(8,128)(2,1)}), bf16[2,1024,1024]{2,1,0:T(8,128)(2,1)}) %all-gather.22.cloned.1.call-update) | async-done | bytes 4194320 | tf_op jit(solution)/shard_map/all_gather | solution.py:88
  337.7 45.6 %all-gather.26.cloned.1.call-done = bf16[2,1024,1024]{2,1,0:T(8,128)(2,1)} async-done(((bf16[2,512,1024]{2,1,0:T(8,128)(2,1)}), bf16[2,1024,1024]{2,1,0:T(8,128)(2,1)}) %all-gather.26.cloned.1.call-update) | async-done | bytes 4194320 | tf_op jit(solution)/shard_map/all_gather | solution.py:88
  444.6 33.5 %all-gather.28.cloned.1.call-done = bf16[2,512,2048]{2,1,0:T(8,128)(2,1)} async-done(((bf16[2,32,2048]{2,1,0:T(8,128)(2,1)}), bf16[2,512,2048]{2,1,0:T(8,128)(2,1)}) %all-gather.28.cloned.1.call-update) | async-done | bytes 4194320 | tf_op jit(solution)/shard_map/all_gather | solution.py:217
  486.3 46.3 %all-gather.30.cloned.1.call-done = bf16[2,2048,512]{1,2,0:T(8,128)(2,1)} async-done(((bf16[2,128,512]{1,2,0:T(8,128)(2,1)}), bf16[2,2048,512]{1,2,0:T(8,128)(2,1)}) %all-gather.30.cloned.1.call-update) | async-done | bytes 4194320 | tf_op jit(solution)/shard_map/all_gather | solution.py:218
  667.9 39.5 %psum.71 = f32[]{:T(128)} all-reduce(f32[]{:T(128)S(6)} %convert_element_type.355), channel_id=1, replica_groups=mesh['dp'=16,'seq'=2] {'dp','seq'}, use_global_device_ids=true, to_apply=%region_38.40 | all-reduce | flops 1 | bytes 8 | tf_op jit(solution)/shard_map/psum | solution.py:336
  716.3 161.6 %while.10 = (s32[]{:T(128)}, f32[4,512]{1,0:T(4,128)S(1)}, f32[4,512]{1,0:T(4,128)S(1)}, f32[4,512]{1,0:T(4,128)}, bf16[4,512,512]{2,1,0:T(8,128)(2,1)S(1)}, /*i...) while((s32[]{:T(128)}, f32[4,512]{1,0:T(4,128)S(1)}, ...), condition=%wide.region_34.36_spmd.clone, body=%wide.region_30.35_spmd.clone.sunk | while | flops 8437758464 | bytes 82471024 | solution.py:310
  716.3 22.8 fusion.291
  756.7 22.8 fusion.291
  797.1 22.8 fusion.291
  837.5 22.8 fusion.291
  887.2 258.2 %while.36 = (s32[]{:T(128)}, f32[16000,512]{1,0:T(8,128)}, f32[4,512,512]{2,1,0:T(8,128)}, bf16[4,512,512]{2,1,0:T(8,128)(2,1)S(1)}, bf16[16000,512]{1,0:T(8,128...) while((s32[]{:T(128)}, f32[16000,512]{1,0:T(8,128)}, ...), condition=%wide.region_47.49_spmd.clone, body=%wide.region_46.48_spmd.clone.sunk | while | flops 25231360000 | bytes 149572224 | solution.py:349
  963.1 30.2 %select_add_fusion.2 = f32[16000,512]{1,0:T(8,128)} fusion(f32[16000,512]{1,0:T(8,128)} %get-tuple-element.663, bf16[512,16000]{1,0:T(8,128)(2,1)} %multiply_convert_fusion.19, pred[]{:T(512)S(6)} %compare.3, bf16[4,512,512]{2,1,0:T(8,128)(2,1)S(1)} %get-tuple-element.675, s32[]{:T(128)} %get-tuple-element.662), kind=kOutput, calls=%fused_computation.14.clone.1 | convolution fusion | flops 8404992000 | bytes 82444296 | tf_op jit(solution)/shard_map/while/body/eval_jaxpr/bv,bd->vd/dot_general | solution.py:346
  1030.3 30.2 %select_add_fusion.2 = f32[16000,512]{1,0:T(8,128)} fusion(f32[16000,512]{1,0:T(8,128)} %get-tuple-element.663, bf16[512,16000]{1,0:T(8,128)(2,1)} %multiply_convert_fusion.19, pred[]{:T(512)S(6)} %compare.3, bf16[4,512,512]{2,1,0:T(8,128)(2,1)S(1)} %get-tuple-element.675, s32[]{:T(128)} %get-tuple-element.662), kind=kOutput, calls=%fused_computation.14.clone.1 | convolution fusion | flops 8404992000 | bytes 82444296 | tf_op jit(solution)/shard_map/while/body/eval_jaxpr/bv,bd->vd/dot_general | solution.py:346
  1097.5 30.2 %select_add_fusion.2 = f32[16000,512]{1,0:T(8,128)} fusion(f32[16000,512]{1,0:T(8,128)} %get-tuple-element.663, bf16[512,16000]{1,0:T(8,128)(2,1)} %multiply_convert_fusion.19, pred[]{:T(512)S(6)} %compare.3, bf16[4,512,512]{2,1,0:T(8,128)(2,1)S(1)} %get-tuple-element.675, s32[]{:T(128)} %get-tuple-element.662), kind=kOutput, calls=%fused_computation.14.clone.1 | convolution fusion | flops 8404992000 | bytes 82444296 | tf_op jit(solution)/shard_map/while/body/eval_jaxpr/bv,bd->vd/dot_general | solution.py:346
  1176.3 29.7 reduce-scatter.20.cloned.1.call-done
  1236.7 22.3 multiply_reduce_fusion.2
  1273.8 28.0 multiply_convert_fusion.3
  1349.3 22.7 multiply_reduce_fusion
  1372.0 27.9 multiply_convert_fusion.1
  1472.0 22.4 multiply_reduce_fusion.1
  1494.4 27.7 multiply_convert_fusion.2
  1675.2 312.6 %all-reduce.4.cloned.1.call-done = (bf16[3,512,1536]{2,1,0:T(8,128)(2,1)}, bf16[3,512,512]{2,1,0:T(8,128)(2,1)}, bf16[2,512,2048]{2,1,0:T(8,128)(2,1)}, bf16[2,2048,512]{2,1,0:T(8,128)(2,1)}, bf16[512,256]{1,0:T(8,128)(2,1)}) async-done(((bf16[3,512,1536]{2,1,0:T(8,128)(2,1)}, bf16[3,512,512]{2,1,0:T(8,128)(2,1)}, bf16[2,512,2048]{2,1,0:T(8,128)(2,1)}, bf16[2,2048,512]{2,1,0:T(8,128)(2,1)}, ...) | async-done | bytes 14942224 | tf_op jit(solution)/shard_map/psum | solution.py:412
  2032.6 25.5 all-gather.36.cloned.1.call-done
  2067.6 47.8 %scatter_custom_fusion = f32[16000,512]{1,0:T(8,128)} fusion(f32[16000,512]{1,0:T(8,128)} %get-tuple-element.146, s32[4096]{0:T(1024)S(1)} %bitcast.491, f32[2048,512]{1,0:T(8,128)} %bitcast.437, f32[]{:T(128)} %constant.112.clone.1, f32[2048,512]{1,0:T(8,128)} %bitcast.438), kind=kCustom, calls=%fused_computation.79 | custom fusion | flops 4194304 | bytes 41157120 | tf_op jit(solution)/shard_map/add | solution.py:395
  2123.9 52.4 %reduce-scatter.36.cloned.1.call-done = f32[32,256]{1,0:T(8,128)} async-done(((f32[512,256]{1,0:T(8,128)}), f32[32,256]{1,0:T(8,128)}) %reduce-scatter.36.cloned.1.call-update) | async-done | bytes 32784 | tf_op jit(solution)/shard_map/reduce_scatter | solution.py:175
  2177.7 68.1 %reduce-scatter.30.cloned.1.call-done = f32[3,32,512]{2,1,0:T(8,128)} async-done(((f32[3,512,512]{2,1,0:T(8,128)}), f32[3,32,512]{2,1,0:T(8,128)}) %reduce-scatter.30.cloned.1.call-update) | async-done | bytes 196624 | tf_op jit(solution)/shard_map/reduce_scatter | solution.py:172
  2247.4 106.6 %reduce-scatter.32.cloned.1.call-done = f32[2,32,2048]{2,1,0:T(8,128)} async-done(((f32[2,512,2048]{2,1,0:T(8,128)}), f32[2,32,2048]{2,1,0:T(8,128)}) %reduce-scatter.32.cloned.1.call-update) | async-done | bytes 524304 | tf_op jit(solution)/shard_map/reduce_scatter | solution.py:173
  2355.8 107.2 %reduce-scatter.34.cloned.1.call-done = f32[2,128,512]{2,1,0:T(8,128)} async-done(((f32[2,2048,512]{2,1,0:T(8,128)}), f32[2,128,512]{2,1,0:T(8,128)}) %reduce-scatter.34.cloned.1.call-update) | async-done | bytes 524304 | tf_op jit(solution)/shard_map/reduce_scatter | solution.py:174
  2464.8 113.8 %reduce-scatter.28.cloned.1.call-done = f32[3,32,1536]{2,1,0:T(8,128)} async-done(((f32[3,512,1536]{2,1,0:T(8,128)}), f32[3,32,1536]{2,1,0:T(8,128)}) %reduce-scatter.28.cloned.1.call-update) | async-done | bytes 589840 | tf_op jit(solution)/shard_map/reduce_scatter | solution.py:171
  2584.3 326.2 %reduce-scatter.38.cloned.1.call-done = f32[1000,512]{1,0:T(8,128)} async-done(((f32[16000,512]{1,0:T(8,128)}), f32[1000,512]{1,0:T(8,128)}) %reduce-scatter.38.cloned.1.call-update) | async-done | bytes 2048016 | tf_op jit(solution)/shard_map/reduce_scatter | solution.py:177
  2913.9 39.7 %all-reduce = (f32[]{:T(128)}, f32[]{:T(128)}, f32[]{:T(128)}) all-reduce(f32[]{:T(128)} %fusion.152, f32[]{:T(128)} %select_reduce_fusion.2, f32[]{:T(128)S(6)} %add.597), channel_id=1, replica_groups=mesh['dp'=16,'seq'=2] {'dp','seq'}, use_global_device_ids=true, to_apply=%region_36.38 | all-reduce | flops 3 | bytes 24 | tf_op jit(solution)/shard_map/psum | solution.py:336
  (890 shorter events, 1062.9 us)
Async XLA Ops:
  7.2 130.8 %all-gather.18.cloned.1.call-start = ((), (), s32[]{:S(2)}) async-start(), calls=%async_computation.13 | async-start | bytes 17408000 | tf_op jit(solution)/shard_map/all_gather | solution.py:221
  10.0 235.5 %all-gather.20.cloned.1.call-start = ((), (), s32[]{:S(2)}) async-start(), calls=%async_computation.15 | async-start | bytes 5013504 | tf_op jit(solution)/shard_map/all_gather | solution.py:215
  10.9 239.3 %reduce-scatter.18.cloned.1.call-start = ((), (), s32[]{:S(2)}) async-start(), calls=%async_computation.18 | async-start | bytes 3145728 | tf_op jit(solution)/shard_map/reduce_scatter | solution.py:262
  11.1 265.5 %copy-start.160 = (s32[2,32]{1,0:T(2,128)}, s32[2,32]{1,0:T(2,128)S(1)}, u32[]{:S(2)}) copy-start(s32[2,32]{1,0:T(2,128)S(1)} %sub.315) | copy-start | bytes 772
  159.4 99.8 %reduce-scatter.16.cloned.1.call-start = ((), (), s32[]{:S(2)}) async-start(), calls=%async_computation.14 | async-start | bytes 3145728 | tf_op jit(solution)/shard_map/reduce_scatter | solution.py:265
  187.9 137.3 %all-gather.22.cloned.1.call-start = ((), (), s32[]{:S(2)}) async-start(), calls=%async_computation.16 | async-start | bytes 6291456 | tf_op jit(solution)/shard_map/all_gather | solution.py:88
  222.6 255.5 %copy-start.202 = (f32[512]{0:T(512)}, f32[512]{0:T(512)S(1)}, u32[]{:S(2)}) copy-start(f32[512]{0:T(512)S(1)} %get-tuple-element.341) | copy-start | bytes 6148
  222.6 317.7 %copy-start.189 = (f32[512]{0:T(512)}, f32[512]{0:T(512)S(1)}, u32[]{:S(2)}) copy-start(f32[512]{0:T(512)S(1)} %get-tuple-element.340) | copy-start | bytes 6148
  268.3 115.1 %all-gather.26.cloned.1.call-start = ((), (), s32[]{:S(2)}) async-start(), calls=%async_computation.19 | async-start | bytes 6291456 | tf_op jit(solution)/shard_map/all_gather | solution.py:88
  273.2 167.0 %all-gather.24.cloned.1.call-start = ((), (), s32[]{:S(2)}) async-start(), calls=%async_computation.17 | async-start | bytes 1671168 | tf_op jit(solution)/shard_map/all_gather | solution.py:216
  274.8 203.3 %all-gather.28.cloned.1.call-start = ((), (), s32[]{:S(2)}) async-start(), calls=%async_computation.20 | async-start | bytes 4456448 | tf_op jit(solution)/shard_map/all_gather | solution.py:217
  275.7 257.0 %all-gather.30.cloned.1.call-start = ((), (), s32[]{:S(2)}) async-start(), calls=%async_computation.21 | async-start | bytes 4456448 | tf_op jit(solution)/shard_map/all_gather | solution.py:218
  276.6 322.8 %all-gather.32.cloned.1.call-start = ((), (), s32[]{:S(2)}) async-start(), calls=%async_computation.22 | async-start | bytes 6291456 | tf_op jit(solution)/shard_map/all_gather | solution.py:88
  544.3 169.0 %all-gather.34.cloned.1.call-start = ((), (), s32[]{:S(2)}) async-start(), calls=%async_computation.23 | async-start | bytes 3145728 | tf_op jit(solution)/shard_map/all_gather | solution.py:296
  667.2 538.8 %reduce-scatter.20.cloned.1.call-start = ((), (), s32[]{:S(2)}) async-start(), calls=%async_computation.24 | async-start | bytes 6291456 | tf_op jit(solution)/shard_map/reduce_scatter | solution.py:354
  1151.0 284.0 %reduce-scatter.22.cloned.1.call-start = ((), (), s32[]{:S(2)}) async-start(), calls=%async_computation.25 | async-start | bytes 6291456 | tf_op jit(solution)/shard_map/reduce_scatter | solution.py:134
  1334.5 278.8 %reduce-scatter.26.cloned.1.call-start = ((), (), s32[]{:S(2)}) async-start(), calls=%async_computation.27 | async-start | bytes 6291456 | tf_op jit(solution)/shard_map/reduce_scatter | solution.py:134
  1435.0 203.7 %reduce-scatter.24.cloned.1.call-start = ((), (), s32[]{:S(2)}) async-start(), calls=%async_computation.26 | async-start | bytes 6291456 | tf_op jit(solution)/shard_map/reduce_scatter | solution.py:134
  1560.6 427.2 %all-reduce.4.cloned.1.call-start = ((), (), s32[]{:S(2)}) async-start(), calls=%async_computation.37 | async-start | bytes 29884416 | tf_op jit(solution)/shard_map/psum | solution.py:412
  1646.3 376.7 %all-gather.38.cloned.1.call-start = ((), (), s32[]{:S(2)}) async-start(), calls=%async_computation.34 | async-start | bytes 3145728 | tf_op jit(solution)/shard_map/all_gather | solution.py:391
  1656.6 401.5 %all-gather.36.cloned.1.call-start = ((), (), s32[]{:S(2)}) async-start(), calls=%async_computation.33 | async-start | bytes 3145728 | tf_op jit(solution)/shard_map/all_gather | solution.py:388
  1666.5 455.9 %reduce-scatter.40.cloned.1.call-start = ((), (), s32[]{:S(2)}) async-start(), calls=%async_computation.36 | async-start | bytes 278528
  1675.2 501.2 %reduce-scatter.36.cloned.1.call-start = ((), (), s32[]{:S(2)}) async-start(), calls=%async_computation.32 | async-start | bytes 557056 | tf_op jit(solution)/shard_map/reduce_scatter | solution.py:175
  1989.6 256.2 %reduce-scatter.30.cloned.1.call-start = ((), (), s32[]{:S(2)}) async-start(), calls=%async_computation.29 | async-start | bytes 3342336 | tf_op jit(solution)/shard_map/reduce_scatter | solution.py:172
  1993.6 360.4 %reduce-scatter.32.cloned.1.call-start = ((), (), s32[]{:S(2)}) async-start(), calls=%async_computation.30 | async-start | bytes 8912896 | tf_op jit(solution)/shard_map/reduce_scatter | solution.py:173
  2000.4 462.6 %reduce-scatter.34.cloned.1.call-start = ((), (), s32[]{:S(2)}) async-start(), calls=%async_computation.31 | async-start | bytes 8912896 | tf_op jit(solution)/shard_map/reduce_scatter | solution.py:174
  2007.2 571.5 %reduce-scatter.28.cloned.1.call-start = ((), (), s32[]{:S(2)}) async-start(), calls=%async_computation.28 | async-start | bytes 10027008 | tf_op jit(solution)/shard_map/reduce_scatter | solution.py:171
  2014.6 896.0 %reduce-scatter.38.cloned.1.call-start = ((), (), s32[]{:S(2)}) async-start(), calls=%async_computation.35 | async-start | bytes 34816000 | tf_op jit(solution)/shard_map/reduce_scatter | solution.py:177
  2117.1 837.2 %copy-start.201 = (f32[2,7,32]{2,0,1:T(2,128)S(1)}, f32[2,7,32]{2,0,1:T(2,128)}, u32[]{:S(2)}) copy-start(f32[2,7,32]{2,0,1:T(2,128)} %param.52) | copy-start | bytes 5380
  2117.1 837.2 %copy-start.219 = (f32[2,7,32]{2,0,1:T(2,128)S(1)}, f32[2,7,32]{2,0,1:T(2,128)}, u32[]{:S(2)}) copy-start(f32[2,7,32]{2,0,1:T(2,128)} %param.53) | copy-start | bytes 5380
  2117.2 837.2 %copy-start.220 = (f32[2,7,32]{2,0,1:T(2,128)S(1)}, f32[2,7,32]{2,0,1:T(2,128)}, u32[]{:S(2)}) copy-start(f32[2,7,32]{2,0,1:T(2,128)} %param.54) | copy-start | bytes 5380
  2121.7 834.4 %copy-start.46 = (f32[1000,512]{1,0:T(8,128)S(1)}, f32[1000,512]{1,0:T(8,128)}, u32[]{:S(2)}) copy-start(f32[1000,512]{1,0:T(8,128)} %param.55) | copy-start | bytes 6144004
  (251 other events, 2380.5 us)
Sparse Core Ops, SparseCore 0:
  10.9 127.0 all-gather.17
  140.9 51.6 all-gather.19
  194.8 30.3 reduce-scatter.17
  227.4 31.8 reduce-scatter.15
  268.4 56.7 all-gather.21
  326.6 56.7 all-gather.25
  386.1 39.7 all-gather.23
  428.6 49.4 all-gather.27
  480.9 51.6 all-gather.29
  544.5 54.8 all-gather.31
  667.3 33.3 all-gather.33
  1151.1 54.8 reduce-scatter.19
  1334.6 54.2 reduce-scatter.21
  1435.0 54.4 reduce-scatter.25
  1560.7 54.1 reduce-scatter.23
  1646.4 341.3 all-reduce.3
  1989.8 33.1 all-gather.37
  2024.9 33.1 all-gather.35
  2062.2 55.2 reduce-scatter.39
  2121.5 54.8 reduce-scatter.35
  2180.6 65.1 reduce-scatter.29
  2250.4 103.5 reduce-scatter.31
  2358.6 104.3 reduce-scatter.33
  2467.5 111.0 reduce-scatter.27
  2583.0 327.5 reduce-scatter.37
where the time goes:
time: 2990 us; the launch traced here: 2980 us
  waiting for transfers between devices  1450 us (48%)
  matrix products  757 us (25%)
  other arithmetic  386 us (13%)
  local copies, waits for them, and re-layouts  202 us (7%)
  blocking collectives  155 us (5%)
    reduce_scatter x1, waiting for transfers between devices, to_owners(): lax.psum_scatter(table_grad, 'dp', scatter_dimension=0, tiled=True)  326 us
    psum x1, waiting for transfers between devices, on_device(): lax.psum(layer_grads[0].astype(jnp.bfloat16), 'seq').astype(jnp.float32)  313 us
    all_gather x1, waiting for transfers between devices, on_device(): lax.all_gather(table.astype(low_type), 'dp', axis=0, tiled=True)  120 us
    reduce_scatter x1, waiting for transfers between devices, to_owners(): lax.psum_scatter(layer_grads[0], 'dp', scatter_dimension=1, tiled=True)  114 us
    dot_general x4, matrix products, head_back(): jnp.einsum('bv,bd->vd', d_logits, piece, preferred_element_type=jnp.float32)  110 us
    reduce_scatter x1, waiting for transfers between devices, to_owners(): lax.psum_scatter(layer_grads[3], 'dp', scatter_dimension=1, tiled=True)  107 us
    reduce_scatter x1, waiting for transfers between devices, to_owners(): lax.psum_scatter(layer_grads[2], 'dp', scatter_dimension=1, tiled=True)  107 us
    dot_general x4, matrix products, head_stats(): jnp.einsum('bd,vd->bv', piece, table_part, preferred_element_type=jnp.flo...  91.4 us
  transfers between devices with their start and end apart: 25, of which 17 were waited for; matrix products, arithmetic and copies ran while one was open for 22% of the time, Pallas kernels for 0%

commit v1 on v0

v1 whole, which is shorter than its diff:
```python
import functools
import math

import jax
import jax.numpy as jnp
from jax import lax
from jax.experimental import pallas as pl
from jax.experimental.pallas import tpu as pltpu
from jax.sharding import PartitionSpec as P

HEADS = 8
STEP = 10


length_token = 1
mask_token = 2
clip_limit = 0.002
beta_one = 0.9
beta_two = 0.98
adam_eps = 1e-08
weight_decay = 0.01
step_rates = (0.05, 0.25, 0.05, 0.025, 0.05, 0.5, 0.1)

low_type = jnp.bfloat16
f32 = jnp.float32
query_block = 128
key_block = 128
place_block = 128
exact_rows = 16
vmem_bytes = 56 * 1024 * 1024


def sinusoid(positions, width):
    half_width = width // 2
    frequency = jnp.exp(jnp.arange(half_width).astype(f32) * (-math.log(10000.0) / half_width))
    angles = positions.astype(f32)[..., None] * frequency
    return jnp.concatenate([jnp.sin(angles), jnp.cos(angles)], -1)


def layer_norm(stream, norm_gain, norm_bias):
    average = jnp.mean(stream, -1, keepdims=True)
    centred = stream - average
    variance = jnp.mean(centred * centred, -1, keepdims=True)
    return centred * lax.rsqrt(variance + 1e-05) * norm_gain + norm_bias


def norm_backward(stream, norm_gain, norm_bias, grad):
    return jax.vjp(layer_norm, stream, norm_gain, norm_bias)[1](grad)


def contract(left, right, left_dim, right_dim):
    return lax.dot_general(
        left, right, (((left_dim,), (right_dim,)), ((), ())), preferred_element_type=f32
    )


def attend_forward_kernel(bounds, q_ref, k_ref, v_ref, span_ref, out_ref, lse_ref, hold, *, head):
    step = pl.program_id(0)
    first, last = bounds[0, step], bounds[1, step]
    width, queries = q_ref.shape
    heads = width // head
    scale = head**-0.5
    low, high = span_ref[0:1, :], span_ref[1:2, :]
    inner = lax.broadcasted_iota(jnp.int32, (key_block, queries), 0)

    def fold(values, op):
        return op(values.reshape(key_block // 8, 8, queries), axis=0)

    def score(block, tops):
        start = pl.multiple_of(block * key_block, key_block)
        place = inner + start
        allowed = (place >= low) & (place < high)
        result = []
        for h in range(heads):
            rows = slice(h * head, (h + 1) * head)
            s = contract(k_ref[rows, pl.ds(start, key_block)], q_ref[rows, :], 0, 0) * scale
            s = jnp.where(allowed, s, -1e30)
            hold[h, pl.ds(start, key_block), :] = s
            result.append(jnp.maximum(tops[h], fold(s, jnp.max)))
        return tuple(result)

    tops = lax.fori_loop(
        first, last, score, tuple(jnp.full((8, queries), -1e30, f32) for _ in range(heads))
    )
    tops = [jnp.max(t, axis=0, keepdims=True) for t in tops]

    def power(block, sums):
        start = pl.multiple_of(block * key_block, key_block)
        result = []
        for h in range(heads):
            e = jnp.exp(hold[h, pl.ds(start, key_block), :] - tops[h])
            hold[h, pl.ds(start, key_block), :] = e
            result.append(sums[h] + fold(e, jnp.sum))
        return tuple(result)

    sums = lax.fori_loop(
        first, last, power, tuple(jnp.zeros((8, queries), f32) for _ in range(heads))
    )
    sums = [jnp.maximum(jnp.sum(t, axis=0, keepdims=True), 1e-30) for t in sums]
    inverse = [1.0 / t for t in sums]

    def mix(block, outs):
        start = pl.multiple_of(block * key_block, key_block)
        result = []
        for h in range(heads):
            rows = slice(h * head, (h + 1) * head)
            p = (hold[h, pl.ds(start, key_block), :] * inverse[h]).astype(low_type)
            result.append(outs[h] + contract(v_ref[rows, pl.ds(start, key_block)], p, 1, 0))
        return tuple(result)

    outs = lax.fori_loop(
        first, last, mix, tuple(jnp.zeros((head, queries), f32) for _ in range(heads))
    )
    for h in range(heads):
        out_ref[h * head : (h + 1) * head, :] = outs[h].astype(low_type)
        lse_ref[h : h + 1, :] = tops[h] + jnp.log(sums[h])


def attend_backward_kernel(
    bounds, q_ref, k_ref, v_ref, span_ref, lse_ref, do_ref, dq_ref, dkv_ref, p_hold, d_hold, acc,
    *, head
):
    step = pl.program_id(0)
    first, last = bounds[0, step], bounds[1, step]
    width, queries = q_ref.shape
    heads = width // head
    scale = head**-0.5
    low, high = span_ref[0:1, :], span_ref[1:2, :]
    inner = lax.broadcasted_iota(jnp.int32, (key_block, queries), 0)

    @pl.when(step == 0)
    def _():
        acc[...] = jnp.zeros_like(acc)

    def one(block, deltas):
        start = pl.multiple_of(block * key_block, key_block)
        keys = pl.ds(start, key_block)
        place = inner + start
        allowed = (place >= low) & (place < high)
        result = []
        for h in range(heads):
            rows = slice(h * head, (h + 1) * head)
            s = contract(k_ref[rows, keys], q_ref[rows, :], 0, 0) * scale
            p = jnp.exp(jnp.where(allowed, s, -1e30) - lse_ref[h : h + 1, :])
            dp = contract(v_ref[rows, keys], do_ref[rows, :], 0, 0)
            p_hold[h, keys, :] = p
            d_hold[h, keys, :] = dp
            result.append(
                deltas[h] + jnp.sum((p * dp).reshape(key_block // 8, 8, queries), axis=0)
            )
            below = slice(width + h * head, width + (h + 1) * head)
            acc[below, keys] += contract(do_ref[rows, :], p.astype(low_type), 1, 1)
        return tuple(result)

    deltas = lax.fori_loop(
        first, last, one, tuple(jnp.zeros((8, queries), f32) for _ in range(heads))
    )
    deltas = [jnp.sum(t, axis=0, keepdims=True) for t in deltas]

    def two(block, outs):
        start = pl.multiple_of(block * key_block, key_block)
        keys = pl.ds(start, key_block)
        result = []
        for h in range(heads):
            rows = slice(h * head, (h + 1) * head)
            ds = (p_hold[h, keys, :] * (d_hold[h, keys, :] - deltas[h])).astype(low_type)
            result.append(outs[h] + contract(k_ref[rows, keys], ds, 1, 0))
            acc[rows, keys] += contract(q_ref[rows, :], ds, 1, 1) * scale
        return tuple(result)

    outs = lax.fori_loop(
        first, last, two, tuple(jnp.zeros((head, queries), f32) for _ in range(heads))
    )
    for h in range(heads):
        dq_ref[h * head : (h + 1) * head, :] = (outs[h] * scale).astype(low_type)

    @pl.when(step == pl.num_programs(0) - 1)
    def _():
        dkv_ref[...] = acc[...].astype(low_type)


def attend_specs(width, length, block, shared):
    key_row = 1 if shared else 0
    return [
        pl.BlockSpec((width, block), lambda i, *_: (0, i)),
        pl.BlockSpec((width, length), lambda i, *_: (key_row, 0)),
        pl.BlockSpec((width, length), lambda i, *_: (key_row + 1, 0)),
        pl.BlockSpec((2, block), lambda i, *_: (0, i)),
    ]


def attend_forward(queries, keys, shared, spans, bounds):
    width = keys.shape[0] // (3 if shared else 2)
    places, length = queries.shape[1], keys.shape[1]
    block = min(query_block, places)
    return pl.pallas_call(
        functools.partial(attend_forward_kernel, head=width // HEADS),
        grid_spec=pltpu.PrefetchScalarGridSpec(
            num_scalar_prefetch=1,
            grid=(places // block,),
            in_specs=attend_specs(width, length, block, shared),
            out_specs=[
                pl.BlockSpec((width, block), lambda i, *_: (0, i)),
                pl.BlockSpec((HEADS, block), lambda i, *_: (0, i)),
            ],
            scratch_shapes=[pltpu.VMEM((HEADS, length, block), f32)],
        ),
        out_shape=[
            jax.ShapeDtypeStruct((width, places), low_type),
            jax.ShapeDtypeStruct((HEADS, places), f32),
        ],
        compiler_params=pltpu.CompilerParams(vmem_limit_bytes=vmem_bytes),
        name="attend_forward",
    )(bounds, queries, keys, keys, spans)


def attend_backward(queries, keys, shared, spans, bounds, lse, d_mixed):
    width = keys.shape[0] // (3 if shared else 2)
    places, length = queries.shape[1], keys.shape[1]
    block = min(query_block, places)
    return pl.pallas_call(
        functools.partial(attend_backward_kernel, head=width // HEADS),
        grid_spec=pltpu.PrefetchScalarGridSpec(
            num_scalar_prefetch=1,
            grid=(places // block,),
            in_specs=attend_specs(width, length, block, shared)
            + [
                pl.BlockSpec((HEADS, block), lambda i, *_: (0, i)),
                pl.BlockSpec((width, block), lambda i, *_: (0, i)),
            ],
            out_specs=[
                pl.BlockSpec((width, block), lambda i, *_: (0, i)),
                pl.BlockSpec((2 * width, length), lambda i, *_: (0, 0)),
            ],
            scratch_shapes=[
                pltpu.VMEM((HEADS, length, block), f32),
                pltpu.VMEM((HEADS, length, block), f32),
                pltpu.VMEM((2 * width, length), f32),
            ],
        ),
        out_shape=[
            jax.ShapeDtypeStruct((width, places), low_type),
            jax.ShapeDtypeStruct((2 * width, length), low_type),
        ],
        compiler_params=pltpu.CompilerParams(vmem_limit_bytes=vmem_bytes),
        name="attend_backward",
    )(bounds, queries, keys, keys, spans, lse, d_mixed)


def head_stats_kernel(chunks, table_ref, rows_ref, target_ref, stats_ref, tops, sums, picks, *, group):
    step = pl.program_id(0)
    words = table_ref.shape[0]

    @pl.when(step == 0)
    def _():
        tops[...] = jnp.full_like(tops, -1e30)
        sums[...] = jnp.zeros_like(sums)
        picks[...] = jnp.zeros_like(picks)

    inner = lax.broadcasted_iota(jnp.int32, (words, place_block), 0) + step * words

    def fold(values, op):
        return op(values.reshape(words // 8, 8, place_block), axis=0)

    for source in range(rows_ref.shape[0] // group):

        def visit(chunk, carry):
            start = pl.multiple_of(source * group + chunk * place_block, place_block)
            here = pl.ds(start, place_block)
            logits = contract(table_ref[...], rows_ref[here, :], 1, 1)
            old = tops[:, here]
            top = jnp.maximum(old, fold(logits, jnp.max))
            spread = jnp.exp(logits.reshape(words // 8, 8, place_block) - top[None])
            sums[:, here] = sums[:, here] * jnp.exp(old - top) + jnp.sum(spread, axis=0)
            tops[:, here] = top
            hit = inner == target_ref[:, here]
            picks[:, here] += fold(jnp.where(hit, logits, 0.0), jnp.sum)
            return carry

        lax.fori_loop(0, chunks[source], visit, 0)

    @pl.when(step == pl.num_programs(0) - 1)
    def _():
        top = jnp.max(tops[...], axis=0, keepdims=True)
        stats_ref[0:1, :] = top
        stats_ref[1:2, :] = jnp.sum(sums[...] * jnp.exp(tops[...] - top), axis=0, keepdims=True)
        stats_ref[2:3, :] = jnp.sum(picks[...], axis=0, keepdims=True)


def head_back_kernel(chunks, table_ref, rows_ref, target_ref, log_ref, weight_ref, dt_ref, dr_ref, turned, *, group):
    step = pl.program_id(0)
    words = table_ref.shape[0]

    @pl.when(step == 0)
    def _():
        dr_ref[...] = jnp.zeros_like(dr_ref)

    dt_ref[...] = jnp.zeros_like(dt_ref)
    turned[...] = table_ref[...].T
    inner = lax.broadcasted_iota(jnp.int32, (words, place_block), 0) + step * words

    for source in range(rows_ref.shape[0] // group):

        def visit(chunk, carry):
            start = pl.multiple_of(source * group + chunk * place_block, place_block)
            here = pl.ds(start, place_block)
            rows = rows_ref[here, :]
            logits = contract(table_ref[...], rows, 1, 1)
            probs = jnp.exp(logits - log_ref[:, here])
            hot = jnp.where(inner == target_ref[:, here], 1.0, 0.0)
            d_logits = ((probs - hot) * weight_ref[:, here]).astype(low_type)
            dt_ref[...] += contract(d_logits, rows, 1, 0)
            dr_ref[:, here] += contract(turned[...], d_logits, 1, 0)
            return carry

        lax.fori_loop(0, chunks[source], visit, 0)


def word_block(words):
    return max(n for n in range(16, 641, 16) if words % n == 0)


def head_specs(words, width, places):
    return [
        pl.BlockSpec((words, width), lambda i, *_: (i, 0)),
        pl.BlockSpec((places, width), lambda i, *_: (0, 0)),
        pl.BlockSpec((1, places), lambda i, *_: (0, 0)),
    ]


def head_stats(chunks, table_part, rows, targets, group):
    words = word_block(table_part.shape[0])
    places, width = rows.shape
    return pl.pallas_call(
        functools.partial(head_stats_kernel, group=group),
        grid_spec=pltpu.PrefetchScalarGridSpec(
            num_scalar_prefetch=1,
            grid=(table_part.shape[0] // words,),
            in_specs=head_specs(words, width, places),
            out_specs=pl.BlockSpec((3, places), lambda i, *_: (0, 0)),
            scratch_shapes=[pltpu.VMEM((8, places), f32) for _ in range(3)],
        ),
        out_shape=jax.ShapeDtypeStruct((3, places), f32),
        compiler_params=pltpu.CompilerParams(vmem_limit_bytes=vmem_bytes),
        name="head_stats",
    )(chunks, table_part, rows, targets)


def head_back(chunks, table_part, rows, targets, logs, weights, group):
    words = word_block(table_part.shape[0])
    places, width = rows.shape
    return pl.pallas_call(
        functools.partial(head_back_kernel, group=group),
        grid_spec=pltpu.PrefetchScalarGridSpec(
            num_scalar_prefetch=1,
            grid=(table_part.shape[0] // words,),
            in_specs=head_specs(words, width, places)
            + [pl.BlockSpec((1, places), lambda i, *_: (0, 0)) for _ in range(2)],
            out_specs=[
                pl.BlockSpec((words, width), lambda i, *_: (i, 0)),
                pl.BlockSpec((width, places), lambda i, *_: (0, 0)),
            ],
            scratch_shapes=[pltpu.VMEM((width, words), low_type)],
        ),
        out_shape=[
            jax.ShapeDtypeStruct(table_part.shape, f32),
            jax.ShapeDtypeStruct((width, places), f32),
        ],
        compiler_params=pltpu.CompilerParams(vmem_limit_bytes=vmem_bytes),
        name="head_back",
    )(chunks, table_part, rows, targets, logs, weights)


def swap(values, axis, bit):
    size = lax.axis_size(axis)
    return lax.ppermute(values, axis, [(i, i ^ bit) for i in range(size)])


def power_of_two(size):
    return size & (size - 1) == 0


def sum_everywhere(values):
    for axis in ("dp", "seq"):
        size = lax.axis_size(axis)
        if power_of_two(size):
            bit = 1
            while bit < size:
                values = values + swap(values, axis, bit)
                bit *= 2
        else:
            values = lax.psum(values, axis)
    return values


def pick(values, dim, index):
    return lax.dynamic_index_in_dim(values, index, dim, False)


def gather_seq(values, dim):
    if lax.axis_size("seq") == 2:
        other = swap(values, "seq", 1)
        first = lax.axis_index("seq") == 0
        return jnp.stack([jnp.where(first, values, other), jnp.where(first, other, values)], dim)
    return lax.all_gather(values, "seq", axis=dim)


def scatter_seq(values):
    if lax.axis_size("seq") == 2:
        index = lax.axis_index("seq")
        return pick(values, 0, index), swap(pick(values, 0, 1 - index), "seq", 1)
    return lax.psum_scatter(values, "seq", scatter_dimension=0, tiled=False), None


def dp_bits():
    bits, bit = [], 1
    while bit < lax.axis_size("dp"):
        bits.append(bit)
        bit *= 2
    return bits


def layer_to_owner(grad):
    owners, seqs = lax.axis_size("dp"), lax.axis_size("seq")
    rows, columns = grad.shape[0] // owners, grad.shape[1]
    if not power_of_two(owners) or seqs != 2 or rows % 16:
        part = lax.psum_scatter(grad, "dp", scatter_dimension=0, tiled=True)
        part = lax.psum(part, "seq")
        return part, jnp.where(lax.axis_index("seq") == 0, jnp.sum(part * part), 0.0)
    bits = dp_bits()
    index, side = lax.axis_index("dp"), lax.axis_index("seq")
    part = grad.reshape((owners // 2, 2, rows, columns))
    mine = index & 1
    part = pick(part, 1, mine) + swap(pick(part, 1, 1 - mine), "dp", 1)
    part = part.reshape((owners // 2, 2, rows // 2, columns))
    part = pick(part, 1, side) + swap(pick(part, 1, 1 - side).astype(low_type), "seq", 1).astype(
        f32
    )
    for bit in bits[1:]:
        part = part.reshape((-1, 2, rows // 2, columns))
        mine = (index // bit) & 1
        part = pick(part, 1, mine) + swap(pick(part, 1, 1 - mine), "dp", bit)
    part = part.reshape((rows // 2, columns))
    other = swap(part, "seq", 1)
    first = side == 0
    whole = jnp.concatenate([jnp.where(first, part, other), jnp.where(first, other, part)], 0)
    return whole, jnp.sum(part * part)


def table_to_owner(grad, pieces):
    owners = lax.axis_size("dp")
    rows, width = grad.shape[0] // owners, grad.shape[1]
    if not power_of_two(owners) or rows < exact_rows or rows % 8 or width % (128 * pieces):
        return lax.psum_scatter(grad, "dp", scatter_dimension=0, tiled=True)
    bits = dp_bits()
    index = lax.axis_index("dp")
    out = []
    for piece in range(pieces):
        columns = width // pieces
        part = grad[:, piece * columns : (piece + 1) * columns]
        part = part.reshape((owners // 2, 2, rows, columns))
        mine = index & 1
        part = pick(part, 1, mine) + swap(pick(part, 1, 1 - mine), "dp", 1)
        for bit in bits[1:]:
            part = part.reshape((-1, 2, rows, columns))
            mine = (index // bit) & 1
            away = pick(part, 1, 1 - mine)
            high = lax.reduce_precision(away, 8, 7)
            rest = (away - high)[:, :exact_rows]
            got = swap(jnp.concatenate([high, rest], 1).astype(low_type), "dp", bit).astype(f32)
            added = got[:, :rows]
            added = added.at[:, :exact_rows].add(got[:, rows:])
            part = pick(part, 1, mine) + added
        out.append(part.reshape((rows, columns)))
    return jnp.concatenate(out, 1)


def adam_update(weight, first, second, grad, rate):
    first = beta_one * first + (1 - beta_one) * grad
    second = beta_two * second + (1 - beta_two) * grad * grad
    first_hat = first / (1 - beta_one**STEP)
    second_hat = second / (1 - beta_two**STEP)
    weight = weight - rate * (first_hat / (jnp.sqrt(second_hat) + adam_eps) + weight_decay * weight)
    return (weight, first, second)


def place_spans(starts, lengths, places):
    covered = places[:, None] >= starts[None, :]
    number = jnp.sum(covered.astype(jnp.int32), -1) - 1
    return number, jnp.max(jnp.where(covered, starts[None, :], 0), -1)


def key_spans(number, starts, lengths, block):
    hot = number[:, None] == jnp.arange(starts.shape[0])[None, :]
    first = jnp.sum(jnp.where(hot, starts[None, :], 0), -1)
    last = jnp.sum(jnp.where(hot, (starts + lengths)[None, :], 0), -1)
    first_block = jnp.min(first.reshape(-1, block), -1) // key_block
    last_block = (jnp.max(last.reshape(-1, block), -1) + key_block - 1) // key_block
    return (
        jnp.stack([first, last]).astype(jnp.int32),
        jnp.stack([first_block, last_block]).astype(jnp.int32),
    )


def on_device(
    src_ids,
    tgt_ids,
    src_lengths,
    tgt_lengths,
    tgt_mask,
    attn_in,
    attn_in_m1,
    attn_in_m2,
    attn_out,
    attn_out_m1,
    attn_out_m2,
    ffn_in,
    ffn_in_m1,
    ffn_in_m2,
    ffn_out,
    ffn_out_m1,
    ffn_out_m2,
    len_head,
    len_head_m1,
    len_head_m2,
    norms,
    norms_m1,
    norms_m2,
    table,
    table_m1,
    table_m2,
):
    rows_here, seq_rows = src_ids.shape
    seqs, owners = lax.axis_size("seq"), lax.axis_size("dp")
    row_len = seq_rows * seqs
    side = lax.axis_index("seq")
    group = seqs // rows_here
    span = row_len // group
    row, offset = side // group, (side % group) * span
    sharers = [[r * group + i for i in range(group)] for r in range(rows_here)]
    width = table.shape[1]
    classes = len_head.shape[1]
    vocab_width = table.shape[0] * owners
    vocab_base = side * vocab_width
    norm_count = norms.shape[1]

    table_part = lax.all_gather(table.astype(low_type), "dp", axis=0, tiled=True)

    def gather_columns(parts):
        joined = jnp.concatenate([part.astype(low_type) for part in parts], 1)
        whole = lax.all_gather(joined, "dp", axis=0, tiled=True)
        result, at = [], 0
        for part in parts:
            result.append(whole[:, at : at + part.shape[1]])
            at += part.shape[1]
        return result

    norm_columns = jnp.pad(norms.reshape(-1, norms.shape[2]).T, ((0, 0), (0, 128 - 2 * norm_count)))
    w_in0, w_out0, f_in0, w_len, norm_low = gather_columns(
        [attn_in[0], attn_out[0], ffn_in[0], len_head, norm_columns]
    )
    f_out0 = lax.all_gather(ffn_out[0].astype(low_type), "dp", axis=0, tiled=True)
    w_in1, w_out1, w_in2, w_out2, f_in1 = gather_columns(
        [attn_in[1], attn_out[1], attn_in[2], attn_out[2], ffn_in[1]]
    )
    f_out1 = lax.all_gather(ffn_out[1].astype(low_type), "dp", axis=0, tiled=True)
    norm_low = norm_low[:, : 2 * norm_count].T.astype(f32)
    gains, biases = norm_low[:norm_count], norm_low[norm_count:]

    count = sum_everywhere(jnp.sum(tgt_mask).astype(f32).reshape(1, 1))[0, 0]
    ids = gather_seq(jnp.stack([src_ids, tgt_ids, tgt_mask]), 2).reshape(3, rows_here, row_len)
    src_starts = jnp.cumsum(src_lengths, -1) - src_lengths
    tgt_starts = jnp.cumsum(tgt_lengths, -1) - tgt_lengths
    places = jnp.arange(row_len)
    opens = jnp.any(places[None, :, None] == src_starts[:, None, :], -1)
    src_in = jnp.where(opens, length_token, ids[0]).reshape(seqs, span)
    masked = (ids[2] == 1).reshape(seqs, span)
    labels = ids[1].reshape(seqs, span)
    dec_in = jnp.where(masked, mask_token, labels)
    own_places = offset + jnp.arange(span)
    src_start, src_length = pick(src_starts, 0, row), pick(src_lengths, 0, row)
    tgt_start, tgt_length = pick(tgt_starts, 0, row), pick(tgt_lengths, 0, row)
    src_number, src_open = place_spans(src_start, src_length, own_places)
    tgt_number, tgt_open = place_spans(tgt_start, tgt_length, own_places)
    block = min(query_block, span)
    enc_spans = key_spans(src_number, src_start, src_length, block)
    self_spans = key_spans(tgt_number, tgt_start, tgt_length, block)
    cross_spans = key_spans(tgt_number, src_start, src_length, block)
    src_wave, tgt_wave = lax.optimization_barrier(
        (sinusoid(own_places - src_open, width), sinusoid(own_places - tgt_open, width))
    )

    rank = jnp.cumsum(masked.astype(jnp.int32), -1) - 1
    counts = rank[:, -1] + 1
    chosen = (rank[:, None, :] == jnp.arange(span)[None, :, None]) & masked[:, None, :]
    packed_labels = jnp.sum(jnp.where(chosen, labels[:, None, :], 0), -1)
    valid = jnp.arange(span)[None, :] < counts[:, None]
    targets = jnp.where(valid, packed_labels - vocab_base, -1).reshape(1, -1)
    chunks = (counts + place_block - 1) // place_block
    own_chosen = pick(chosen, 0, side).astype(low_type)

    def lookup(token_ids):
        local = token_ids - vocab_base
        inside = (local >= 0) & (local < vocab_width)
        found = jnp.take(table_part, jnp.clip(local, 0, vocab_width - 1), axis=0)
        return jnp.where(inside[..., None], found, 0.0).astype(low_type)

    def embed(token_ids):
        if seqs == 2:
            away = swap(lookup(pick(token_ids, 0, 1 - side)), "seq", 1)
            return lookup(pick(token_ids, 0, side)).astype(f32) + away.astype(f32)
        return lax.psum_scatter(lookup(token_ids), "seq", scatter_dimension=0).astype(f32)

    root = math.sqrt(width)
    stream0 = embed(src_in) * root + src_wave
    target0 = embed(dec_in) * root + tgt_wave

    def norm(stream, index):
        return layer_norm(stream, gains[index], biases[index])

    def keys_of_row(part):
        if group == 1:
            return part
        return lax.all_gather(part, "seq", axis=1, tiled=True, axis_index_groups=sharers)

    def keys_to_place(part):
        if group == 1:
            return part
        return lax.psum_scatter(
            part, "seq", scatter_dimension=1, tiled=True, axis_index_groups=sharers
        )

    def self_attention(inner, weight_in, weight_out, spans):
        triple = contract(weight_in, inner, 0, 1).astype(low_type)
        keys = triple if group == 1 else keys_of_row(triple[width:])
        mixed, lse = attend_forward(triple, keys, group == 1, *spans)
        return contract(mixed, weight_out, 0, 0), (triple, keys, mixed, lse)

    def self_attention_back(inner, weight_in, weight_out, spans, kept, grad):
        triple, keys, mixed, lse = kept
        grad_low = grad.astype(low_type)
        d_out = contract(mixed, grad_low, 1, 0)
        d_mixed = contract(weight_out, grad_low, 1, 1).astype(low_type)
        d_query, d_keys = attend_backward(triple, keys, group == 1, *spans, lse, d_mixed)
        d_triple = jnp.concatenate([d_query, keys_to_place(d_keys)], 0)
        return contract(d_triple, weight_in, 0, 1), contract(inner, d_triple, 0, 1), d_out

    def cross_attention(inner, memory, weight_in, weight_out, spans):
        queries = contract(weight_in[:, :width], inner, 0, 1).astype(low_type)
        keys = keys_of_row(contract(weight_in[:, width:], memory, 0, 1).astype(low_type))
        mixed, lse = attend_forward(queries, keys, False, *spans)
        return contract(mixed, weight_out, 0, 0), (queries, keys, mixed, lse)

    def cross_attention_back(inner, memory, weight_in, weight_out, spans, kept, grad):
        queries, keys, mixed, lse = kept
        grad_low = grad.astype(low_type)
        d_out = contract(mixed, grad_low, 1, 0)
        d_mixed = contract(weight_out, grad_low, 1, 1).astype(low_type)
        d_query, d_keys = attend_backward(queries, keys, False, *spans, lse, d_mixed)
        d_keys = keys_to_place(d_keys)
        d_in = jnp.concatenate([contract(inner, d_query, 0, 1), contract(memory, d_keys, 0, 1)], 1)
        return (
            contract(d_query, weight_in[:, :width], 0, 1),
            contract(d_keys, weight_in[:, width:], 0, 1),
            d_in,
            d_out,
        )

    def ffn(inner, weight_one, weight_two):
        hidden = contract(inner, weight_one, 1, 0)
        active = jax.nn.gelu(hidden).astype(low_type)
        return contract(active, weight_two, 1, 0), (hidden, active)

    def ffn_back(inner, weight_one, weight_two, kept, grad):
        hidden, active = kept
        grad_low = grad.astype(low_type)
        d_two = contract(active, grad_low, 0, 0)
        d_active = contract(grad_low, weight_two, 1, 1)
        d_hidden = jax.vjp(jax.nn.gelu, hidden)[1](d_active)[0].astype(low_type)
        return contract(d_hidden, weight_one, 1, 1), contract(inner, d_hidden, 0, 0), d_two

    inner0 = norm(stream0, 0).astype(low_type)
    branch0, keep0 = self_attention(inner0, w_in0, w_out0, enc_spans)
    stream1 = stream0 + branch0
    inner1 = norm(stream1, 1).astype(low_type)
    branch1, keep1 = ffn(inner1, f_in0, f_out0)
    stream2 = stream1 + branch1
    memory = norm(stream2, 2).astype(low_type)
    inner3 = norm(target0, 3).astype(low_type)
    branch3, keep3 = self_attention(inner3, w_in1, w_out1, self_spans)
    target1 = target0 + branch3
    inner4 = norm(target1, 4).astype(low_type)
    branch4, keep4 = cross_attention(inner4, memory, w_in2, w_out2, cross_spans)
    target2 = target1 + branch4
    inner5 = norm(target2, 5).astype(low_type)
    branch5, keep5 = ffn(inner5, f_in1, f_out1)
    target3 = target2 + branch5
    final = norm(target3, 6).astype(low_type)

    packed = contract(own_chosen, final, 1, 0).astype(low_type)
    pieces = gather_seq(packed, 0).reshape(seqs * span, width)
    stats = head_stats(chunks, table_part, pieces, targets, span)
    every = gather_seq(stats, 0)
    top_logit = jnp.max(every[:, 0], 0)
    totals = jnp.sum(every[:, 1] * jnp.exp(every[:, 0] - top_logit[None]), 0)
    log_total = jnp.where(valid.reshape(-1), top_logit + jnp.log(totals), 0.0)
    target_logit = jnp.sum(every[:, 2], 0)
    loss_rows = jnp.where(valid.reshape(-1), log_total - target_logit, 0.0).reshape(seqs, span)
    token_local = jnp.sum(pick(loss_rows, 0, side))
    weights = valid.astype(f32).reshape(1, -1) / count
    d_table, d_pieces = head_back(
        chunks, table_part, pieces, targets, log_total[None], weights, span
    )
    if seqs == 2:
        d_packed = lax.dynamic_slice_in_dim(d_pieces, side * span, span, 1) + swap(
            lax.dynamic_slice_in_dim(d_pieces, (1 - side) * span, span, 1), "seq", 1
        )
    else:
        d_packed = lax.psum_scatter(d_pieces, "seq", scatter_dimension=1, tiled=True)
    d_high = lax.reduce_precision(d_packed, 8, 7)
    d_rest = (d_packed - d_high).astype(low_type)
    d_final = contract(own_chosen, d_high.astype(low_type), 0, 1) + contract(
        own_chosen, d_rest, 0, 1
    )

    first_place = own_places[None, :] == src_start[:, None]
    mine = jnp.any(first_place, -1)
    first_rows = contract(first_place.astype(low_type), memory, 1, 0).astype(low_type)
    len_logits = contract(first_rows, w_len, 1, 0)
    len_label = jnp.minimum(tgt_length, classes - 1)
    len_hot = jnp.arange(classes)[None, :] == len_label[:, None]
    len_loss = jax.nn.logsumexp(len_logits, -1) - jnp.sum(jnp.where(len_hot, len_logits, 0.0), -1)
    len_local = jnp.sum(jnp.where(mine, len_loss, 0.0))
    sentences = rows_here * src_lengths.shape[1] * owners
    len_prob = jax.nn.softmax(len_logits, -1)
    d_len_logits = (
        jnp.where(mine[:, None], len_prob - len_hot.astype(f32), 0.0) * (0.1 / sentences)
    ).astype(low_type)
    d_w_len = contract(first_rows, d_len_logits, 0, 0)
    d_first = contract(d_len_logits, w_len, 1, 1)
    d_memory = lax.dot_general(
        first_place.astype(f32),
        d_first,
        (((0,), (0,)), ((), ())),
        precision=lax.Precision.HIGHEST,
        preferred_element_type=f32,
    )

    d_target3, gain6, bias6 = norm_backward(target3, gains[6], biases[6], d_final)
    d_inner5, d_fin1, d_fout1 = ffn_back(inner5, f_in1, f_out1, keep5, d_target3)
    d_target2, gain5, bias5 = norm_backward(target2, gains[5], biases[5], d_inner5)
    d_target2 = d_target2 + d_target3
    d_inner4, d_cross, d_win2, d_wout2 = cross_attention_back(
        inner4, memory, w_in2, w_out2, cross_spans, keep4, d_target2
    )
    d_target1, gain4, bias4 = norm_backward(target1, gains[4], biases[4], d_inner4)
    d_target1 = d_target1 + d_target2
    d_inner3, d_win1, d_wout1 = self_attention_back(
        inner3, w_in1, w_out1, self_spans, keep3, d_target1
    )
    d_target0, gain3, bias3 = norm_backward(target0, gains[3], biases[3], d_inner3)
    d_target0 = d_target0 + d_target1
    d_stream2, gain2, bias2 = norm_backward(stream2, gains[2], biases[2], d_memory + d_cross)
    d_inner1, d_fin0, d_fout0 = ffn_back(inner1, f_in0, f_out0, keep1, d_stream2)
    d_stream1, gain1, bias1 = norm_backward(stream1, gains[1], biases[1], d_inner1)
    d_stream1 = d_stream1 + d_stream2
    d_inner0, d_win0, d_wout0 = self_attention_back(
        inner0, w_in0, w_out0, enc_spans, keep0, d_stream1
    )
    d_stream0, gain0, bias0 = norm_backward(stream0, gains[0], biases[0], d_inner0)
    d_stream0 = d_stream0 + d_stream1

    def spread(base, token_ids, grads):
        local = (token_ids - vocab_base).reshape(-1)
        inside = (local >= 0) & (local < vocab_width)
        terms = jnp.where(inside[:, None], grads.reshape(-1, width).astype(f32), 0.0)
        return base.at[jnp.clip(local, 0, vocab_width - 1)].add(terms)

    d_dec_all = gather_seq((d_target0 * root).astype(low_type), 0)
    d_src_all = gather_seq((d_stream0 * root).astype(low_type), 0)
    d_table = spread(spread(d_table, dec_in, d_dec_all), src_in, d_src_all)
    table_grad = table_to_owner(d_table, 4)
    norm_grads = [gain0, gain1, gain2, gain3, gain4, gain5, gain6]
    norm_grads += [bias0, bias1, bias2, bias3, bias4, bias5, bias6]
    small = jnp.concatenate(
        [d_w_len, jnp.pad(jnp.stack(norm_grads, 1), ((0, 0), (0, 128 - 2 * norm_count)))], 1
    )
    g_fout1, sq0 = layer_to_owner(d_fout1)
    g_fin1, sq1 = layer_to_owner(d_fin1)
    g_wout2, sq2 = layer_to_owner(d_wout2)
    g_win2, sq3 = layer_to_owner(d_win2)
    g_wout1, sq4 = layer_to_owner(d_wout1)
    g_win1, sq5 = layer_to_owner(d_win1)
    g_fout0, sq6 = layer_to_owner(d_fout0)
    g_fin0, sq7 = layer_to_owner(d_fin0)
    g_wout0, sq8 = layer_to_owner(d_wout0)
    g_win0, sq9 = layer_to_owner(d_win0)
    g_small, sq10 = layer_to_owner(small)
    square = sq0 + sq1 + sq2 + sq3 + sq4 + sq5 + sq6 + sq7 + sq8 + sq9 + sq10
    square = square + jnp.sum(table_grad * table_grad)
    sums = sum_everywhere(jnp.stack([token_local, len_local, square]).reshape(1, 3))[0]
    token_sum, len_sum, grad_norm = sums[0], sums[1], jnp.sqrt(sums[2])
    factor = jnp.minimum(1.0, clip_limit / (grad_norm + 1e-06))
    grads = (
        jnp.stack([g_win0, g_win1, g_win2]),
        jnp.stack([g_wout0, g_wout1, g_wout2]),
        jnp.stack([g_fin0, g_fin1]),
        jnp.stack([g_fout0, g_fout1]),
        g_small[:, :classes],
        g_small[:, classes : classes + 2 * norm_count].T.reshape(norms.shape),
        table_grad,
    )
    masters = (attn_in, attn_out, ffn_in, ffn_out, len_head, norms, table)
    firsts = (attn_in_m1, attn_out_m1, ffn_in_m1, ffn_out_m1, len_head_m1, norms_m1, table_m1)
    seconds = (attn_in_m2, attn_out_m2, ffn_in_m2, ffn_out_m2, len_head_m2, norms_m2, table_m2)
    updates = []
    for weight, first, second, grad, rate in zip(masters, firsts, seconds, grads, step_rates):
        updates.extend(adam_update(weight, first, second, grad * factor, rate))
    return (token_sum, count, len_sum, grad_norm, *updates)


def solution(mesh):
    layer, head, scales, words = P(None, "dp", None), P("dp", None), P(None, None, "dp"), P(("seq", "dp"), None)
    owned = (layer,) * 12 + (head,) * 3 + (scales,) * 3 + (words,) * 3
    ids, lengths = P("dp", "seq"), P("dp", None)
    in_specs = (ids, ids, lengths, lengths, ids) + owned
    out_specs = (P(), P(), P(), P()) + owned
    return jax.shard_map(
        on_device, mesh=mesh, in_specs=in_specs, out_specs=out_specs, check_vma=False
    )
```

time: 2990 us -> 1570 us (0.53)
  waiting for transfers between devices: 1450 us -> 529 us
  matrix products: 757 us -> 138 us
  Pallas kernels: 0 us -> 368 us
  other arithmetic: 386 us -> 201 us
  blocking collectives: 155 us -> 0 us
  starting transfers between devices: 1.45 us -> 140 us
  local copies, waits for them, and re-layouts: 202 us -> 146 us
    reduce_scatter x12 -> x0, waiting for transfers between devices: 813 us -> none  [the longest x1 326 us: to_owners(): lax.psum_scatter(table_grad, 'dp', scatter_dimension=0, tiled=True)]
    dot_general x77 -> x41, matrix products: 757 us -> 138 us  [the longest x40 136 us: contract(): lax.dot_general(left, right, (((left_dim,), (right_dim,)), ((), ())), pre...]
    ppermute x0 -> x100, waiting for transfers between devices: none -> 412 us  [swap(): return lax.ppermute(values, axis, [(i, i ^ bit) for i in range(size)])]
    pallas_call x0 -> x8, Pallas kernels: none -> 368 us  [the longest x1 173 us: head_back(): pl.pallas_call(functools.partial(head_back_kernel, group=group), grid_spe...]
    psum x1 -> x0, waiting for transfers between devices: 313 us -> none  [on_device(): lax.psum(layer_grads[0].astype(jnp.bfloat16), 'seq').astype(jnp.float32)]
    all_gather x10 -> x4, waiting for transfers between devices: 204 us -> 37 us  [the longest x2 36.9 us: gather_columns(): whole = lax.all_gather(joined, 'dp', axis=0, tiled=True)]
    ppermute x0 -> x100, starting transfers between devices: none -> 140 us  [swap(): return lax.ppermute(values, axis, [(i, i ^ bit) for i in range(size)])]
    convert_element_type x23 -> x19, other arithmetic: 127 us -> 2.91 us  [the longest x12 0.97 us: table_to_owner(): swap(jnp.concatenate([high, rest], 1).astype(low_type), 'dp', bit)]
  transfers between devices with their start and end apart: 25 -> 105, of which waited for: 17 -> 73; matrix products, arithmetic and copies ran while one was open for 22% -> 26% of each run, Pallas kernels for 0% -> 8%
where the time goes in v1:
time: 1570 us; the launch traced here: 1560 us
  waiting for transfers between devices  529 us (34%)
  Pallas kernels  368 us (23%)
  other arithmetic  201 us (13%)
  local copies, waits for them, and re-layouts  146 us (9%)
  starting transfers between devices  140 us (9%)
  matrix products  138 us (9%)
  between operations  32.7 us (2%)
    ppermute x100, waiting for transfers between devices, swap(): return lax.ppermute(values, axis, [(i, i ^ bit) for i in range(size)])  412 us
    pallas_call x1, Pallas kernels, head_back(): pl.pallas_call(functools.partial(head_back_kernel, group=group), grid_spe...  173 us
    ppermute x100, starting transfers between devices, swap(): return lax.ppermute(values, axis, [(i, i ^ bit) for i in range(size)])  140 us
    dot_general x40, matrix products, contract(): lax.dot_general(left, right, (((left_dim,), (right_dim,)), ((), ())), pre...  136 us
    all_gather x1, waiting for transfers between devices, on_device(): lax.all_gather(table.astype(low_type), 'dp', axis=0, tiled=True)  79.7 us
    pallas_call x3, Pallas kernels, attend_backward(): pl.pallas_call(functools.partial(attend_backward_kernel, head=width // HE...  77.2 us
    scatter-add x2, other arithmetic, spread(): return base.at[jnp.clip(local, 0, vocab_width - 1)].add(terms)  70.3 us
    pallas_call x1, Pallas kernels, head_stats(): pl.pallas_call(functools.partial(head_stats_kernel, group=group), grid_sp...  69 us
  transfers between devices with their start and end apart: 105, of which 73 were waited for; matrix products, arithmetic and copies ran while one was open for 26% of the time, Pallas kernels for 8%

profile of v1, /device:TPU:0, one launch (start us, length us, event | category | flops | bytes accessed | tf_op | source)
XLA Modules:
  0.0 1555.1 jit_solution(5073918413102314594)
XLA Ops:
  58.8 79.7 %all-gather.8.cloned.1.call-done.table_ref = bf16[16000,512]{1,0:T(8,128)(2,1)} async-done(((bf16[1000,512]{1,0:T(8,128)(2,1)}), bf16[16000,512]{1,0:T(8,128)(2,1)}) %all-gather.8.cloned.1.call-update) | async-done | bytes 16384016 | tf_op jit(solution)/shard_map/all_gather | solution.py:547
  138.5 11.8 gather_fusion.1
  155.3 36.9 %all-gather.12.cloned.1.call-done = bf16[512,4480]{1,0:T(8,128)(2,1)} async-done(((bf16[32,4480]{1,0:T(8,128)(2,1)}), bf16[512,4480]{1,0:T(8,128)(2,1)}) %all-gather.12.cloned.1.call-update) | async-done | bytes 4587536 | tf_op jit(solution)/shard_map/all_gather | solution.py:551
  193.1 11.8 gather_fusion.3
  210.1 12.9 gather_fusion
  223.1 11.8 gather_fusion.2
  247.0 16.0 %attend_forward.4 = (bf16[512,1024]{1,0:T(8,128)(2,1)}, f32[8,1024]{1,0:T(8,128)}) custom-call(s32[2,8]{1,0:T(2,128)} %pad_add_fusion.7.bounds, bf16[1536,1024]{1,0:T(8,128)(2,1)} %convolution_convert_fusion.q_ref.k_ref.v_ref, bf16[1536,1024]{1,0:T(8,128)(2,1)} %convolution_convert_fusion.q_ref.k_ref.v_ref, ...), custom_call_target="tpu_custom_call" | custom-call | tf_op jit(solution)/shard_map/attend_forward/pallas_call | solution.py:196
  272.3 18.1 %attend_forward.3 = (bf16[512,1024]{1,0:T(8,128)(2,1)}, f32[8,1024]{1,0:T(8,128)}) custom-call(s32[2,8]{1,0:T(2,128)} %pad_add_fusion.5.bounds, bf16[1536,1024]{1,0:T(8,128)(2,1)} %convolution_convert_fusion.1.q_ref.k_ref.v_ref, bf16[1536,1024]{1,0:T(8,128)(2,1)} %convolution_convert_fusion.1.q_ref.k_ref.v_ref, ...), custom_call_target="tpu_custom_call" | custom-call | tf_op jit(solution)/shard_map/attend_forward/pallas_call | solution.py:196
  316.3 14.5 attend_forward.5
  355.2 23.5 %collective-permute-done.3 = bf16[1024,512]{1,0:T(8,128)(2,1)S(1)} collective-permute-done((bf16[1024,512]{1,0:T(8,128)(2,1)S(1)}, bf16[1024,512]{1,0:T(8,128)(2,1)S(1)}, u32[]{:S(2)}, u32[]{:S(2)}) %collective-permute-start.3) | collective-permute-done | bytes 1048608 | tf_op jit(solution)/shard_map/ppermute | solution.py:376
  380.4 69.0 %head_stats.1 = f32[3,2048]{1,0:T(4,128)} custom-call(s32[2]{0:T(128)} %and_select_fusion.6.chunks, bf16[16000,512]{1,0:T(8,128)(2,1)} %all-gather.8.cloned.1.call-done.table_ref, bf16[2048,512]{1,0:T(8,128)(2,1)} %bitcast.650, s32[1,2048]{1,0:T(1,128)} %broadcast_select_fusion.24.target_ref), custom_call_target="tpu_custom_call" | custom-call | tf_op jit(solution)/shard_map/head_stats/pallas_call | solution.py:334
  455.1 172.6 %head_back.1 = (f32[16000,512]{1,0:T(8,128)}, f32[512,2048]{1,0:T(8,128)}) custom-call(s32[2]{0:T(128)} %and_select_fusion.6.chunks, bf16[16000,512]{1,0:T(8,128)(2,1)} %all-gather.8.cloned.1.call-done.table_ref, bf16[2048,512]{1,0:T(8,128)(2,1)} %bitcast.651, s32[1,2048]{1,0:T(1,128)} %broadcast_select_fusion.24.target_ref, ...), custom_call_target="tpu_custom_call" | custom-call | tf_op jit(solution)/shard_map/head_back/pallas_call | solution.py:352
  638.7 18.5 %collective-permute-done.10 = f32[512,1024]{1,0:T(8,128)} collective-permute-done((f32[512,1024]{1,0:T(8,128)}, f32[512,1024]{1,0:T(8,128)}, u32[]{:S(2)}, u32[]{:S(2)}) %collective-permute-start.10) | collective-permute-done | bytes 2097184 | tf_op jit(solution)/shard_map/ppermute | solution.py:376
  698.0 22.3 %attend_backward.3 = (bf16[512,1024]{1,0:T(8,128)(2,1)}, bf16[1024,1024]{1,0:T(8,128)(2,1)}) custom-call(s32[2,8]{1,0:T(2,128)} %pad_add_fusion.6.bounds, bf16[512,1024]{1,0:T(8,128)(2,1)} %convolution_convert_fusion.6.q_ref, bf16[1024,1024]{1,0:T(8,128)(2,1)} %convolution_convert_fusion.2.k_ref.v_ref, ...), custom_call_target="tpu_custom_call" | custom-call | tf_op jit(solution)/shard_map/attend_backward/pallas_call | solution.py:221
  735.1 29.4 %attend_backward.4 = (bf16[512,1024]{1,0:T(8,128)(2,1)}, bf16[1024,1024]{1,0:T(8,128)(2,1)}) custom-call(s32[2,8]{1,0:T(2,128)} %pad_add_fusion.5.bounds, bf16[1536,1024]{1,0:T(8,128)(2,1)} %convolution_convert_fusion.1.q_ref.k_ref.v_ref, bf16[1536,1024]{1,0:T(8,128)(2,1)} %convolution_convert_fusion.1.q_ref.k_ref.v_ref, ...), custom_call_target="tpu_custom_call" | custom-call | tf_op jit(solution)/shard_map/attend_backward/pallas_call | solution.py:221
  807.1 25.6 %attend_backward.5 = (bf16[512,1024]{1,0:T(8,128)(2,1)}, bf16[1024,1024]{1,0:T(8,128)(2,1)}) custom-call(s32[2,8]{1,0:T(2,128)} %pad_add_fusion.7.bounds, bf16[1536,1024]{1,0:T(8,128)(2,1)} %convolution_convert_fusion.q_ref.k_ref.v_ref, bf16[1536,1024]{1,0:T(8,128)(2,1)} %convolution_convert_fusion.q_ref.k_ref.v_ref, ...), custom_call_target="tpu_custom_call" | custom-call | tf_op jit(solution)/shard_map/attend_backward/pallas_call | solution.py:221
  885.2 35.6 %collective-permute-done.22 = bf16[8,16,512]{2,1,0:T(8,128)(2,1)S(1)} collective-permute-done((bf16[8,16,512]{2,1,0:T(8,128)(2,1)S(1)}, bf16[8,16,512]{2,1,0:T(8,128)(2,1)S(1)}, u32[]{:S(2)}, u32[]{:S(2)}) %collective-permute-start.22) | collective-permute-done | bytes 131104 | tf_op jit(solution)/shard_map/ppermute | solution.py:376
  955.4 16.9 %collective-permute-start.24 = (f32[2,16,512]{2,1,0:T(8,128)S(1)}, f32[2,16,512]{2,1,0:T(8,128)S(1)}, u32[]{:S(2)}, u32[]{:S(2)}) collective-permute-start(f32[2,16,512]{2,1,0:T(8,128)S(1)} %dynamic-slice_bitcast_fusion.43), channel_id=1, source_target_pairs={{0,8},{2,10},{4,12},{6,14},{8,0},{10,2},{12,4},{14,6},{16,24},{18,... | collective-permute-start | bytes 196616 | tf_op jit(solution)/shard_map/ppermute | solution.py:376
  1012.8 35.0 %scatter_custom_fusion = f32[16000,512]{1,0:T(8,128)} fusion(f32[16000,512]{1,0:T(8,128)} %get-tuple-element.201, s32[2048]{0:T(1024)} %bitcast.803, bf16[2048,512]{1,0:T(8,128)(2,1)S(1)} %bitcast.666, f32[]{:T(128)} %constant.1007.clone.1, pred[2048]{0:T(1024)(128)(4,1)S(1)} %copy-done.107), kind=kCustom, calls=%fused_computation.32 | custom fusion | flops 3145728 | bytes 34867712 | tf_op jit(solution)/shard_map/scatter-add | solution.py:777
  1047.8 35.3 %scatter_custom_fusion.1 = f32[16000,512]{1,0:T(8,128)} fusion(f32[16000,512]{1,0:T(8,128)} %scatter_custom_fusion, s32[2048]{0:T(1024)} %bitcast.802, bf16[2048,512]{1,0:T(8,128)(2,1)} %bitcast.667, f32[]{:T(128)} %constant.1007.clone.1, pred[2048]{0:T(1024)(128)(4,1)S(1)} %copy-done.108), kind=kCustom, calls=%fused_computation.30 | custom fusion | flops 3145728 | bytes 34867712 | tf_op jit(solution)/shard_map/scatter-add | solution.py:777
  1083.2 20.8 %fusion.225 = (f32[16000,128]{1,0:T(8,128)S(1)}, f32[16000,128]{1,0:T(8,128)}, f32[16000,128]{1,0:T(8,128)}, f32[16000,128]{1,0:T(8,128)}) fusion(f32[16000,512]{1,0:T(8,128)} %scatter_custom_fusion.1), kind=kLoop, calls=%fused_computation.768 | loop fusion | bytes 65536000 | tf_op jit(solution)/shard_map/slice | solution.py:460
  1130.1 8.8 collective-permute-done.27
  1139.4 9.6 collective-permute-done.37
  1212.4 12.5 collective-permute-done.17
  1225.4 10.8 collective-permute-done.47
  1267.5 12.7 collective-permute-done.18
  1387.3 9.6 collective-permute-done.81
  1401.9 17.2 %collective-permute-done.77 = bf16[4,1016,128]{2,1,0:T(8,128)(2,1)S(1)} collective-permute-done((bf16[4,1016,128]{2,1,0:T(8,128)(2,1)}, bf16[4,1016,128]{2,1,0:T(8,128)(2,1)S(1)}, u32[]{:S(2)}, u32[]{:S(2)}) %collective-permute-start.77) | collective-permute-done | bytes 1040416 | tf_op jit(solution)/shard_map/ppermute | solution.py:376
  1424.2 17.2 %collective-permute-done.73 = bf16[4,1016,128]{2,1,0:T(8,128)(2,1)S(1)} collective-permute-done((bf16[4,1016,128]{2,1,0:T(8,128)(2,1)}, bf16[4,1016,128]{2,1,0:T(8,128)(2,1)S(1)}, u32[]{:S(2)}, u32[]{:S(2)}) %collective-permute-start.73) | collective-permute-done | bytes 1040416 | tf_op jit(solution)/shard_map/ppermute | solution.py:376
  1446.1 11.7 collective-permute-done.69
  1463.7 11.9 collective-permute-done.70
  1476.8 12.4 collective-permute-done.83
  (950 shorter events, 669.9 us)
Async XLA Ops:
  7.2 131.3 %all-gather.8.cloned.1.call-start = ((), (), s32[]{:S(2)}) async-start(), calls=%async_computation | async-start | bytes 17408000 | tf_op jit(solution)/shard_map/all_gather | solution.py:547
  10.1 182.1 %all-gather.12.cloned.1.call-start = ((), (), s32[]{:S(2)}) async-start(), calls=%async_computation.2 | async-start | bytes 4874240 | tf_op jit(solution)/shard_map/all_gather | solution.py:551
  11.8 255.2 %all-gather.10.cloned.1.call-start = ((), (), s32[]{:S(2)}) async-start(), calls=%async_computation.1 | async-start | bytes 6684672 | tf_op jit(solution)/shard_map/all_gather | solution.py:551
  12.5 287.5 %all-gather.14.cloned.1.call-start = ((), (), s32[]{:S(2)}) async-start(), calls=%async_computation.3 | async-start | bytes 2228224 | tf_op jit(solution)/shard_map/all_gather | solution.py:562
  13.4 328.3 %all-gather.16.cloned.1.call-start = ((), (), s32[]{:S(2)}) async-start(), calls=%async_computation.4 | async-start | bytes 2228224 | tf_op jit(solution)/shard_map/all_gather | solution.py:566
  13.5 40.3 %collective-permute-start = (s32[3,2,512]{2,1,0:T(2,128)S(1)}, s32[3,2,512]{2,1,0:T(2,128)S(1)}, u32[]{:S(2)}, u32[]{:S(2)}) collective-permute-start(s32[3,2,512]{2,1,0:T(2,128)S(1)} %pad_add_fusion), channel_id=1, source_target_pairs={{0,1},{1,0},{2,3},{3,2},{4,5},{5,4},{6,7},{7,6},{8,9},{9,8},{10,11... | collective-permute-start | bytes 36872 | tf_op jit(solution)/shard_map/ppermute | solution.py:376
  151.9 83.1 %collective-permute-start.1 = (bf16[1024,512]{1,0:T(8,128)(2,1)}, bf16[1024,512]{1,0:T(8,128)(2,1)}, u32[]{:S(2)}, u32[]{:S(2)}) collective-permute-start(bf16[1024,512]{1,0:T(8,128)(2,1)} %select_select_fusion.2), channel_id=1, source_target_pairs={{0,1},{1,0},{2,3},{3,2},{4,5},{5,4},{6,7},{7,6},{8,9},{9,8},{10,11... | collective-permute-start | bytes 3145736 | tf_op jit(solution)/shard_map/ppermute | solution.py:376
  206.6 31.6 %collective-permute-start.2 = (bf16[1024,512]{1,0:T(8,128)(2,1)}, bf16[1024,512]{1,0:T(8,128)(2,1)}, u32[]{:S(2)}, u32[]{:S(2)}) collective-permute-start(bf16[1024,512]{1,0:T(8,128)(2,1)} %select_select_fusion), channel_id=1, source_target_pairs={{0,1},{1,0},{2,3},{3,2},{4,5},{5,4},{6,7},{7,6},{8,9},{9,8},{10,11... | collective-permute-start | bytes 3145736 | tf_op jit(solution)/shard_map/ppermute | solution.py:376
  673.1 487.8 %collective-permute-start.11 = (f32[8,128,512]{2,1,0:T(8,128)}, f32[8,128,512]{2,1,0:T(8,128)}, u32[]{:S(2)}, u32[]{:S(2)}) collective-permute-start(f32[8,128,512]{2,1,0:T(8,128)} %dynamic-slice_bitcast_fusion.7), channel_id=1, source_target_pairs={{0,2},{2,0},{4,6},{6,4},{8,10},{10,8},{12,14},{14,12},{16,18},{18,... | collective-permute-start | bytes 6291464 | tf_op jit(solution)/shard_map/ppermute | solution.py:376
  686.4 471.8 %collective-permute-start.16 = (f32[8,32,2048]{2,1,0:T(8,128)}, f32[8,32,2048]{2,1,0:T(8,128)}, u32[]{:S(2)}, u32[]{:S(2)}) collective-permute-start(f32[8,32,2048]{2,1,0:T(8,128)} %dynamic-slice_bitcast_fusion.6), channel_id=1, source_target_pairs={{0,2},{2,0},{4,6},{6,4},{8,10},{10,8},{12,14},{14,12},{16,18},{18,... | collective-permute-start | bytes 6291464 | tf_op jit(solution)/shard_map/ppermute | solution.py:376
  694.8 175.0 %collective-permute-start.21 = (f32[8,32,512]{2,1,0:T(8,128)}, f32[8,32,512]{2,1,0:T(8,128)}, u32[]{:S(2)}, u32[]{:S(2)}) collective-permute-start(f32[8,32,512]{2,1,0:T(8,128)} %dynamic-slice_bitcast_fusion.23), channel_id=1, source_target_pairs={{0,2},{2,0},{4,6},{6,4},{8,10},{10,8},{12,14},{14,12},{16,18},{18,... | collective-permute-start | bytes 1572872 | tf_op jit(solution)/shard_map/ppermute | solution.py:376
  732.1 140.7 %collective-permute-start.31 = (f32[8,32,512]{2,1,0:T(8,128)}, f32[8,32,512]{2,1,0:T(8,128)}, u32[]{:S(2)}, u32[]{:S(2)}) collective-permute-start(f32[8,32,512]{2,1,0:T(8,128)} %dynamic-slice_bitcast_fusion.22), channel_id=1, source_target_pairs={{0,2},{2,0},{4,6},{6,4},{8,10},{10,8},{12,14},{14,12},{16,18},{18,... | collective-permute-start | bytes 1572872 | tf_op jit(solution)/shard_map/ppermute | solution.py:376
  869.8 140.2 %collective-permute-start.66 = (bf16[1024,512]{1,0:T(8,128)(2,1)S(1)}, bf16[1024,512]{1,0:T(8,128)(2,1)S(1)}, u32[]{:S(2)}, u32[]{:S(2)}) collective-permute-start(bf16[1024,512]{1,0:T(8,128)(2,1)S(1)} %multiply_convert_fusion.3), channel_id=1, source_target_pairs={{0,1},{1,0},{2,3},{3,2},{4,5},{5,4},{6,7},{7,6},{8,9},{9,8},{10,11... | collective-permute-start | bytes 3145736 | tf_op jit(solution)/shard_map/ppermute | solution.py:376
  872.8 138.2 %collective-permute-start.67 = (bf16[1024,512]{1,0:T(8,128)(2,1)S(1)}, bf16[1024,512]{1,0:T(8,128)(2,1)S(1)}, u32[]{:S(2)}, u32[]{:S(2)}) collective-permute-start(bf16[1024,512]{1,0:T(8,128)(2,1)S(1)} %multiply_convert_fusion.2), channel_id=1, source_target_pairs={{0,1},{1,0},{2,3},{3,2},{4,5},{5,4},{6,7},{7,6},{8,9},{9,8},{10,11... | collective-permute-start | bytes 3145736 | tf_op jit(solution)/shard_map/ppermute | solution.py:376
  883.5 37.3 %collective-permute-start.22 = (bf16[8,16,512]{2,1,0:T(8,128)(2,1)S(1)}, bf16[8,16,512]{2,1,0:T(8,128)(2,1)S(1)}, u32[]{:S(2)}, u32[]{:S(2)}) collective-permute-start(bf16[8,16,512]{2,1,0:T(8,128)(2,1)S(1)} %fusion.106), channel_id=1, source_target_pairs={{0,1},{1,0},{2,3},{3,2},{4,5},{5,4},{6,7},{7,6},{8,9},{9,8},{10,11... | collective-permute-start | bytes 393224 | tf_op jit(solution)/shard_map/ppermute | solution.py:376
  1009.4 112.2 %collective-permute-start.26 = (f32[8,32,1536]{2,1,0:T(8,128)}, f32[8,32,1536]{2,1,0:T(8,128)}, u32[]{:S(2)}, u32[]{:S(2)}) collective-permute-start(f32[8,32,1536]{2,1,0:T(8,128)} %dynamic-slice_bitcast_fusion.14), channel_id=1, source_target_pairs={{0,2},{2,0},{4,6},{6,4},{8,10},{10,8},{12,14},{14,12},{16,18},{18,... | collective-permute-start | bytes 4718600 | tf_op jit(solution)/shard_map/ppermute | solution.py:376
  1010.0 115.4 %collective-permute-start.36 = (f32[8,32,1536]{2,1,0:T(8,128)}, f32[8,32,1536]{2,1,0:T(8,128)}, u32[]{:S(2)}, u32[]{:S(2)}) collective-permute-start(f32[8,32,1536]{2,1,0:T(8,128)} %dynamic-slice_bitcast_fusion.13), channel_id=1, source_target_pairs={{0,2},{2,0},{4,6},{6,4},{8,10},{10,8},{12,14},{14,12},{16,18},{18,... | collective-permute-start | bytes 4718600 | tf_op jit(solution)/shard_map/ppermute | solution.py:376
  1011.0 117.0 %collective-permute-start.56 = (f32[8,32,1536]{2,1,0:T(8,128)}, f32[8,32,1536]{2,1,0:T(8,128)}, u32[]{:S(2)}, u32[]{:S(2)}) collective-permute-start(f32[8,32,1536]{2,1,0:T(8,128)} %dynamic-slice_bitcast_fusion.12), channel_id=1, source_target_pairs={{0,2},{2,0},{4,6},{6,4},{8,10},{10,8},{12,14},{14,12},{16,18},{18,... | collective-permute-start | bytes 4718600 | tf_op jit(solution)/shard_map/ppermute | solution.py:376
  1121.7 42.3 %collective-permute-start.41 = (f32[8,128,512]{2,1,0:T(8,128)S(1)}, f32[8,128,512]{2,1,0:T(8,128)S(1)}, u32[]{:S(2)}, u32[]{:S(2)}) collective-permute-start(f32[8,128,512]{2,1,0:T(8,128)S(1)} %copy-done.48), channel_id=1, source_target_pairs={{0,2},{2,0},{4,6},{6,4},{8,10},{10,8},{12,14},{14,12},{16,18},{18,... | collective-permute-start | bytes 6291464 | tf_op jit(solution)/shard_map/ppermute | solution.py:376
  1125.5 41.2 %collective-permute-start.46 = (f32[8,32,2048]{2,1,0:T(8,128)S(1)}, f32[8,32,2048]{2,1,0:T(8,128)S(1)}, u32[]{:S(2)}, u32[]{:S(2)}) collective-permute-start(f32[8,32,2048]{2,1,0:T(8,128)S(1)} %copy-done.47), channel_id=1, source_target_pairs={{0,2},{2,0},{4,6},{6,4},{8,10},{10,8},{12,14},{14,12},{16,18},{18,... | collective-permute-start | bytes 6291464 | tf_op jit(solution)/shard_map/ppermute | solution.py:376
  1158.1 206.7 %collective-permute-start.80 = (f32[8,1000,128]{2,1,0:T(8,128)}, f32[8,1000,128]{2,1,0:T(8,128)}, u32[]{:S(2)}, u32[]{:S(2)}) collective-permute-start(f32[8,1000,128]{2,1,0:T(8,128)} %dynamic-slice_bitcast_fusion), channel_id=1, source_target_pairs={{0,2},{2,0},{4,6},{6,4},{8,10},{10,8},{12,14},{14,12},{16,18},{18,... | collective-permute-start | bytes 12288008 | tf_op jit(solution)/shard_map/ppermute | solution.py:376
  1158.3 212.8 %collective-permute-start.76 = (f32[8,1000,128]{2,1,0:T(8,128)}, f32[8,1000,128]{2,1,0:T(8,128)}, u32[]{:S(2)}, u32[]{:S(2)}) collective-permute-start(f32[8,1000,128]{2,1,0:T(8,128)} %dynamic-slice_bitcast_fusion.1), channel_id=1, source_target_pairs={{0,2},{2,0},{4,6},{6,4},{8,10},{10,8},{12,14},{14,12},{16,18},{18,... | collective-permute-start | bytes 12288008 | tf_op jit(solution)/shard_map/ppermute | solution.py:376
  1161.0 216.2 %collective-permute-start.72 = (f32[8,1000,128]{2,1,0:T(8,128)}, f32[8,1000,128]{2,1,0:T(8,128)}, u32[]{:S(2)}, u32[]{:S(2)}) collective-permute-start(f32[8,1000,128]{2,1,0:T(8,128)} %dynamic-slice_bitcast_fusion.2), channel_id=1, source_target_pairs={{0,2},{2,0},{4,6},{6,4},{8,10},{10,8},{12,14},{14,12},{16,18},{18,... | collective-permute-start | bytes 12288008 | tf_op jit(solution)/shard_map/ppermute | solution.py:376
  1248.2 33.2 %collective-permute-start.13 = (f32[4,64,512]{2,1,0:T(8,128)S(1)}, f32[4,64,512]{2,1,0:T(8,128)S(1)}, u32[]{:S(2)}, u32[]{:S(2)}) collective-permute-start(f32[4,64,512]{2,1,0:T(8,128)S(1)} %dynamic-slice_bitcast_fusion.25), channel_id=1, source_target_pairs={{0,4},{2,6},{4,0},{6,2},{8,12},{10,14},{12,8},{14,10},{16,20},{18,... | collective-permute-start | bytes 1572872 | tf_op jit(solution)/shard_map/ppermute | solution.py:376
  1312.5 70.5 %collective-permute-start.68 = (f32[8,1000,128]{2,1,0:T(8,128)}, f32[8,1000,128]{2,1,0:T(8,128)}, u32[]{:S(2)}, u32[]{:S(2)}) collective-permute-start(f32[8,1000,128]{2,1,0:T(8,128)} %dynamic-slice_bitcast_fusion.3), channel_id=1, source_target_pairs={{0,2},{2,0},{4,6},{6,4},{8,10},{10,8},{12,14},{14,12},{16,18},{18,... | collective-permute-start | bytes 12288008 | tf_op jit(solution)/shard_map/ppermute | solution.py:376
  1376.1 43.1 %collective-permute-start.77 = (bf16[4,1016,128]{2,1,0:T(8,128)(2,1)}, bf16[4,1016,128]{2,1,0:T(8,128)(2,1)S(1)}, u32[]{:S(2)}, u32[]{:S(2)}) collective-permute-start(bf16[4,1016,128]{2,1,0:T(8,128)(2,1)} %pad_maximum_fusion.9), channel_id=1, source_target_pairs={{0,4},{2,6},{4,0},{6,2},{8,12},{10,14},{12,8},{14,10},{16,20},{18,... | collective-permute-start | bytes 3121160 | tf_op jit(solution)/shard_map/ppermute | solution.py:376
  1381.9 59.6 %collective-permute-start.73 = (bf16[4,1016,128]{2,1,0:T(8,128)(2,1)}, bf16[4,1016,128]{2,1,0:T(8,128)(2,1)S(1)}, u32[]{:S(2)}, u32[]{:S(2)}) collective-permute-start(bf16[4,1016,128]{2,1,0:T(8,128)(2,1)} %pad_maximum_fusion.8), channel_id=1, source_target_pairs={{0,4},{2,6},{4,0},{6,2},{8,12},{10,14},{12,8},{14,10},{16,20},{18,... | collective-permute-start | bytes 3121160 | tf_op jit(solution)/shard_map/ppermute | solution.py:376
  1386.3 71.6 %collective-permute-start.69 = (bf16[4,1016,128]{2,1,0:T(8,128)(2,1)S(1)}, bf16[4,1016,128]{2,1,0:T(8,128)(2,1)S(1)}, u32[]{:S(2)}, u32[]{:S(2)}) collective-permute-start(bf16[4,1016,128]{2,1,0:T(8,128)(2,1)S(1)} %pad_maximum_fusion.7), channel_id=1, source_target_pairs={{0,4},{2,6},{4,0},{6,2},{8,12},{10,14},{12,8},{14,10},{16,20},{18,... | collective-permute-start | bytes 3121160 | tf_op jit(solution)/shard_map/ppermute | solution.py:376
  1397.7 61.1 %collective-permute-start.82 = (bf16[2,1016,128]{2,1,0:T(8,128)(2,1)S(1)}, bf16[2,1016,128]{2,1,0:T(8,128)(2,1)S(1)}, u32[]{:S(2)}, u32[]{:S(2)}) collective-permute-start(bf16[2,1016,128]{2,1,0:T(8,128)(2,1)S(1)} %pad_maximum_fusion.14), channel_id=1, source_target_pairs={{0,8},{2,10},{4,12},{6,14},{8,0},{10,2},{12,4},{14,6},{16,24},{18,... | collective-permute-start | bytes 1560584 | tf_op jit(solution)/shard_map/ppermute | solution.py:376
  1420.0 39.9 %collective-permute-start.78 = (bf16[2,1016,128]{2,1,0:T(8,128)(2,1)S(1)}, bf16[2,1016,128]{2,1,0:T(8,128)(2,1)S(1)}, u32[]{:S(2)}, u32[]{:S(2)}) collective-permute-start(bf16[2,1016,128]{2,1,0:T(8,128)(2,1)S(1)} %pad_maximum_fusion.13), channel_id=1, source_target_pairs={{0,8},{2,10},{4,12},{6,14},{8,0},{10,2},{12,4},{14,6},{16,24},{18,... | collective-permute-start | bytes 1560584 | tf_op jit(solution)/shard_map/ppermute | solution.py:376
  1460.2 34.6 %collective-permute-start.79 = (bf16[1,1016,128]{2,1,0:T(8,128)(2,1)S(1)}, bf16[1,1016,128]{2,1,0:T(8,128)(2,1)S(1)}, u32[]{:S(2)}, u32[]{:S(2)}) collective-permute-start(bf16[1,1016,128]{2,1,0:T(8,128)(2,1)S(1)} %pad_maximum_fusion.17), channel_id=1, source_target_pairs={{0,16},{2,18},{4,20},{6,22},{8,24},{10,26},{12,28},{14,30},{16,0},... | collective-permute-start | bytes 780296 | tf_op jit(solution)/shard_map/ppermute | solution.py:376
  1463.1 35.7 %collective-permute-start.75 = (bf16[1,1016,128]{2,1,0:T(8,128)(2,1)S(1)}, bf16[1,1016,128]{2,1,0:T(8,128)(2,1)S(1)}, u32[]{:S(2)}, u32[]{:S(2)}) collective-permute-start(bf16[1,1016,128]{2,1,0:T(8,128)(2,1)S(1)} %pad_maximum_fusion.16), channel_id=1, source_target_pairs={{0,16},{2,18},{4,20},{6,22},{8,24},{10,26},{12,28},{14,30},{16,0},... | collective-permute-start | bytes 780296 | tf_op jit(solution)/shard_map/ppermute | solution.py:376
  (208 other events, 1666.1 us)
Sparse Core Ops, SparseCore 0:
  10.9 127.5 all-gather.7
  141.4 50.7 all-gather.11
  195.0 60.4 all-gather.9
  258.1 40.2 all-gather.13
  301.0 40.1 all-gather.15

commit v2 on v1

--- a/solution.py
+++ b/solution.py
@@ -25,8 +25,7 @@
 f32 = jnp.float32
 query_block = 128
 key_block = 128
-place_block = 128
-exact_rows = 16
+place_block = 256
 vmem_bytes = 56 * 1024 * 1024
 
 
@@ -247,7 +246,19 @@
     )(bounds, queries, keys, keys, spans, lse, d_mixed)
 
 
-def head_stats_kernel(chunks, table_ref, rows_ref, target_ref, stats_ref, tops, sums, picks, *, group):
+def each_chunk(chunks, visit):
+    def wide(chunk, carry):
+        visit(pl.multiple_of(chunk * place_block, place_block), place_block)
+        return carry
+
+    lax.fori_loop(0, chunks[0], wide, 0)
+
+    @pl.when(chunks[1] > 0)
+    def _():
+        visit(pl.multiple_of(chunks[0] * place_block, place_block), place_block // 2)
+
+
+def head_stats_kernel(chunks, table_ref, rows_ref, stats_ref, tops, sums):
     step = pl.program_id(0)
     words = table_ref.shape[0]
 
@@ -255,116 +266,105 @@
     def _():
         tops[...] = jnp.full_like(tops, -1e30)
         sums[...] = jnp.zeros_like(sums)
-        picks[...] = jnp.zeros_like(picks)
-
-    inner = lax.broadcasted_iota(jnp.int32, (words, place_block), 0) + step * words
-
-    def fold(values, op):
-        return op(values.reshape(words // 8, 8, place_block), axis=0)
-
-    for source in range(rows_ref.shape[0] // group):
-
-        def visit(chunk, carry):
-            start = pl.multiple_of(source * group + chunk * place_block, place_block)
-            here = pl.ds(start, place_block)
-            logits = contract(table_ref[...], rows_ref[here, :], 1, 1)
-            old = tops[:, here]
-            top = jnp.maximum(old, fold(logits, jnp.max))
-            spread = jnp.exp(logits.reshape(words // 8, 8, place_block) - top[None])
-            sums[:, here] = sums[:, here] * jnp.exp(old - top) + jnp.sum(spread, axis=0)
-            tops[:, here] = top
-            hit = inner == target_ref[:, here]
-            picks[:, here] += fold(jnp.where(hit, logits, 0.0), jnp.sum)
-            return carry
-
-        lax.fori_loop(0, chunks[source], visit, 0)
+
+    def visit(start, size):
+        here = pl.ds(start, size)
+        logits = contract(table_ref[...], rows_ref[here, :], 1, 1).reshape(words // 8, 8, size)
+        old = tops[:, here]
+        top = jnp.maximum(old, jnp.max(logits, axis=0))
+        powers = jnp.sum(jnp.exp(logits - top[None]), axis=0)
+        sums[:, here] = sums[:, here] * jnp.exp(old - top) + powers
+        tops[:, here] = top
+
+    each_chunk(chunks, visit)
 
     @pl.when(step == pl.num_programs(0) - 1)
     def _():
         top = jnp.max(tops[...], axis=0, keepdims=True)
         stats_ref[0:1, :] = top
         stats_ref[1:2, :] = jnp.sum(sums[...] * jnp.exp(tops[...] - top), axis=0, keepdims=True)
-        stats_ref[2:3, :] = jnp.sum(picks[...], axis=0, keepdims=True)
-
-
-def head_back_kernel(chunks, table_ref, rows_ref, target_ref, log_ref, weight_ref, dt_ref, dr_ref, turned, *, group):
+
+
+def head_back_kernel(
+    chunks, table_ref, rows_ref, target_ref, log_ref, weight_ref, dt_ref, dr_ref, pick_ref, turned
+):
     step = pl.program_id(0)
     words = table_ref.shape[0]
 
     @pl.when(step == 0)
     def _():
         dr_ref[...] = jnp.zeros_like(dr_ref)
+        pick_ref[...] = jnp.zeros_like(pick_ref)
 
     dt_ref[...] = jnp.zeros_like(dt_ref)
     turned[...] = table_ref[...].T
-    inner = lax.broadcasted_iota(jnp.int32, (words, place_block), 0) + step * words
-
-    for source in range(rows_ref.shape[0] // group):
-
-        def visit(chunk, carry):
-            start = pl.multiple_of(source * group + chunk * place_block, place_block)
-            here = pl.ds(start, place_block)
-            rows = rows_ref[here, :]
-            logits = contract(table_ref[...], rows, 1, 1)
-            probs = jnp.exp(logits - log_ref[:, here])
-            hot = jnp.where(inner == target_ref[:, here], 1.0, 0.0)
-            d_logits = ((probs - hot) * weight_ref[:, here]).astype(low_type)
-            dt_ref[...] += contract(d_logits, rows, 1, 0)
-            dr_ref[:, here] += contract(turned[...], d_logits, 1, 0)
-            return carry
-
-        lax.fori_loop(0, chunks[source], visit, 0)
+
+    def visit(start, size):
+        here = pl.ds(start, size)
+        rows = rows_ref[here, :]
+        inner = lax.broadcasted_iota(jnp.int32, (words, size), 0)
+        logits = contract(table_ref[...], rows, 1, 1)
+        scaled = jnp.exp(logits - log_ref[:, here])
+        hit = inner == target_ref[:, here] - step * words
+        picked = jnp.where(hit, logits, 0.0).reshape(words // 8, 8, size)
+        pick_ref[:, here] += jnp.sum(picked, axis=0)
+        d_logits = jnp.where(hit, scaled - weight_ref[:, here], scaled).astype(low_type)
+        dt_ref[...] += contract(d_logits, rows, 1, 0)
+        dr_ref[:, here] += contract(turned[...], d_logits, 1, 0)
+
+    each_chunk(chunks, visit)
 
 
 def word_block(words):
-    return max(n for n in range(16, 641, 16) if words % n == 0)
+    return max(n for n in range(16, 1601, 16) if words % n == 0)
 
 
 def head_specs(words, width, places):
     return [
         pl.BlockSpec((words, width), lambda i, *_: (i, 0)),
         pl.BlockSpec((places, width), lambda i, *_: (0, 0)),
-        pl.BlockSpec((1, places), lambda i, *_: (0, 0)),
     ]
 
 
-def head_stats(chunks, table_part, rows, targets, group):
+def head_stats(chunks, table_part, rows):
     words = word_block(table_part.shape[0])
     places, width = rows.shape
     return pl.pallas_call(
-        functools.partial(head_stats_kernel, group=group),
+        head_stats_kernel,
         grid_spec=pltpu.PrefetchScalarGridSpec(
             num_scalar_prefetch=1,
             grid=(table_part.shape[0] // words,),
             in_specs=head_specs(words, width, places),
-            out_specs=pl.BlockSpec((3, places), lambda i, *_: (0, 0)),
-            scratch_shapes=[pltpu.VMEM((8, places), f32) for _ in range(3)],
+            out_specs=pl.BlockSpec((2, places), lambda i, *_: (0, 0)),
+            scratch_shapes=[pltpu.VMEM((8, places), f32) for _ in range(2)],
         ),
-        out_shape=jax.ShapeDtypeStruct((3, places), f32),
+        out_shape=jax.ShapeDtypeStruct((2, places), f32),
         compiler_params=pltpu.CompilerParams(vmem_limit_bytes=vmem_bytes),
         name="head_stats",
-    )(chunks, table_part, rows, targets)
-
-
-def head_back(chunks, table_part, rows, targets, logs, weights, group):
+    )(chunks, table_part, rows)
+
+
+def head_back(chunks, table_part, rows, targets, logs, weights):
     words = word_block(table_part.shape[0])
     places, width = rows.shape
     return pl.pallas_call(
-        functools.partial(head_back_kernel, group=group),
+        head_back_kernel,
         grid_spec=pltpu.PrefetchScalarGridSpec(
             num_scalar_prefetch=1,
             grid=(table_part.shape[0] // words,),
             in_specs=head_specs(words, width, places)
-            + [pl.BlockSpec((1, places), lambda i, *_: (0, 0)) for _ in range(2)],
+            + [pl.BlockSpec((1, places), lambda i, *_: (0, 0)) for _ in range(3)],
             out_specs=[
                 pl.BlockSpec((words, width), lambda i, *_: (i, 0)),
                 pl.BlockSpec((width, places), lambda i, *_: (0, 0)),
+                pl.BlockSpec((8, places), lambda i, *_: (0, 0)),
             ],
             scratch_shapes=[pltpu.VMEM((width, words), low_type)],
         ),
         out_shape=[
             jax.ShapeDtypeStruct(table_part.shape, f32),
             jax.ShapeDtypeStruct((width, places), f32),
+            jax.ShapeDtypeStruct((8, places), f32),
         ],
         compiler_params=pltpu.CompilerParams(vmem_limit_bytes=vmem_bytes),
         name="head_back",
@@ -380,16 +380,16 @@
     return size & (size - 1) == 0
 
 
-def sum_everywhere(values):
+def everywhere(values, combine, reduce):
     for axis in ("dp", "seq"):
         size = lax.axis_size(axis)
         if power_of_two(size):
             bit = 1
             while bit < size:
-                values = values + swap(values, axis, bit)
+                values = combine(values, swap(values, axis, bit))
                 bit *= 2
         else:
-            values = lax.psum(values, axis)
+            values = reduce(values, axis)
     return values
 
 
@@ -405,74 +405,88 @@
     return lax.all_gather(values, "seq", axis=dim)
 
 
-def scatter_seq(values):
-    if lax.axis_size("seq") == 2:
-        index = lax.axis_index("seq")
-        return pick(values, 0, index), swap(pick(values, 0, 1 - index), "seq", 1)
-    return lax.psum_scatter(values, "seq", scatter_dimension=0, tiled=False), None
-
-
-def dp_bits():
-    bits, bit = [], 1
-    while bit < lax.axis_size("dp"):
-        bits.append(bit)
-        bit *= 2
-    return bits
-
-
-def layer_to_owner(grad):
-    owners, seqs = lax.axis_size("dp"), lax.axis_size("seq")
-    rows, columns = grad.shape[0] // owners, grad.shape[1]
-    if not power_of_two(owners) or seqs != 2 or rows % 16:
-        part = lax.psum_scatter(grad, "dp", scatter_dimension=0, tiled=True)
-        part = lax.psum(part, "seq")
-        return part, jnp.where(lax.axis_index("seq") == 0, jnp.sum(part * part), 0.0)
-    bits = dp_bits()
-    index, side = lax.axis_index("dp"), lax.axis_index("seq")
-    part = grad.reshape((owners // 2, 2, rows, columns))
-    mine = index & 1
-    part = pick(part, 1, mine) + swap(pick(part, 1, 1 - mine), "dp", 1)
-    part = part.reshape((owners // 2, 2, rows // 2, columns))
-    part = pick(part, 1, side) + swap(pick(part, 1, 1 - side).astype(low_type), "seq", 1).astype(
-        f32
-    )
-    for bit in bits[1:]:
-        part = part.reshape((-1, 2, rows // 2, columns))
+def swap_rows(values, cut, more):
+    rest = lax.cond(
+        more, lambda part: swap(part, "seq", 1), lambda part: jnp.zeros_like(part), values[cut:]
+    )
+    return jnp.concatenate([swap(values[:cut], "seq", 1), rest], 0)
+
+
+def to_each(values):
+    return lax.all_to_all(values, ("seq", "dp"), 0, 0)
+
+
+class Halving:
+    def __init__(self, parts, joint):
+        self.parts, self.joint = parts, joint
+        self.rows = parts[0].shape[1]
+        bits = []
+        bit = 1
+        while bit < lax.axis_size("dp"):
+            bits.append(("dp", bit))
+            bit *= 2
+        self.steps = bits[:1] + ([("seq", 1)] if joint else []) + bits[1:]
+        self.fast = power_of_two(lax.axis_size("dp")) and (
+            not joint or (lax.axis_size("seq") == 2 and self.rows % 16 == 0)
+        )
+        self.fast = self.fast and all(part.shape[2] % 128 == 0 for part in parts)
+        self.fast = self.fast and self.rows % 8 == 0
+        self.pending, self.value, self.square = None, None, None
+        if self.fast:
+            self.launch()
+
+    def launch(self):
+        if self.value is not None:
+            return
+        if not self.steps:
+            self.pending = swap(self.parts[0], "seq", 1)
+            return
+        axis, bit = self.steps[0]
+        rows = self.rows // 2 if axis == "seq" else self.rows
+        index = lax.axis_index(axis)
         mine = (index // bit) & 1
-        part = pick(part, 1, mine) + swap(pick(part, 1, 1 - mine), "dp", bit)
-    part = part.reshape((rows // 2, columns))
-    other = swap(part, "seq", 1)
-    first = side == 0
-    whole = jnp.concatenate([jnp.where(first, part, other), jnp.where(first, other, part)], 0)
-    return whole, jnp.sum(part * part)
-
-
-def table_to_owner(grad, pieces):
-    owners = lax.axis_size("dp")
-    rows, width = grad.shape[0] // owners, grad.shape[1]
-    if not power_of_two(owners) or rows < exact_rows or rows % 8 or width % (128 * pieces):
-        return lax.psum_scatter(grad, "dp", scatter_dimension=0, tiled=True)
-    bits = dp_bits()
-    index = lax.axis_index("dp")
-    out = []
-    for piece in range(pieces):
-        columns = width // pieces
-        part = grad[:, piece * columns : (piece + 1) * columns]
-        part = part.reshape((owners // 2, 2, rows, columns))
-        mine = index & 1
-        part = pick(part, 1, mine) + swap(pick(part, 1, 1 - mine), "dp", 1)
-        for bit in bits[1:]:
-            part = part.reshape((-1, 2, rows, columns))
-            mine = (index // bit) & 1
-            away = pick(part, 1, 1 - mine)
-            high = lax.reduce_precision(away, 8, 7)
-            rest = (away - high)[:, :exact_rows]
-            got = swap(jnp.concatenate([high, rest], 1).astype(low_type), "dp", bit).astype(f32)
-            added = got[:, :rows]
-            added = added.at[:, :exact_rows].add(got[:, rows:])
-            part = pick(part, 1, mine) + added
-        out.append(part.reshape((rows, columns)))
-    return jnp.concatenate(out, 1)
+        halves = [part.reshape((-1, 2, rows, part.shape[2])) for part in self.parts]
+        away = [pick(half, 1, 1 - mine).astype(low_type) for half in halves]
+        self.parts = [pick(half, 1, mine) for half in halves]
+        self.rows = rows
+        self.pending = swap(jnp.concatenate(away, 2), axis, bit)
+
+    def absorb(self, got):
+        self.pending = None
+        if not self.steps:
+            first = lax.axis_index("seq") == 0
+            part = self.parts[0]
+            self.value = jnp.concatenate(
+                [jnp.where(first, part, got), jnp.where(first, got, part)], 0
+            )
+            return
+        self.steps.pop(0)
+        self.parts = [jnp.concatenate(self.parts, 2) + got.astype(f32)]
+        if not self.steps:
+            self.parts = [self.parts[0].reshape(self.rows, -1)]
+            self.square = jnp.sum(self.parts[0] * self.parts[0])
+            if not self.joint:
+                self.value = self.parts[0]
+
+    def finish(self):
+        if self.fast:
+            return
+        whole = jnp.concatenate(self.parts, 2)
+        part = lax.psum_scatter(whole, "dp", scatter_dimension=0)
+        if self.joint:
+            part = lax.psum(part, "seq")
+        self.value, self.square = part, jnp.sum(part * part)
+        if self.joint:
+            self.square = jnp.where(lax.axis_index("seq") == 0, self.square, 0.0)
+
+
+def advance(main, chains):
+    live = [chain for chain in chains if chain.pending is not None]
+    main, got = lax.optimization_barrier((main, [chain.pending for chain in live]))
+    for chain, arrived in zip(live, got):
+        chain.absorb(arrived)
+        chain.launch()
+    return main
 
 
 def adam_update(weight, first, second, grad, rate):
@@ -484,7 +498,7 @@
     return (weight, first, second)
 
 
-def place_spans(starts, lengths, places):
+def place_spans(starts, places):
     covered = places[:, None] >= starts[None, :]
     number = jnp.sum(covered.astype(jnp.int32), -1) - 1
     return number, jnp.max(jnp.where(covered, starts[None, :], 0), -1)
@@ -532,19 +546,22 @@
 ):
     rows_here, seq_rows = src_ids.shape
     seqs, owners = lax.axis_size("seq"), lax.axis_size("dp")
+    devices = seqs * owners
     row_len = seq_rows * seqs
     side = lax.axis_index("seq")
     group = seqs // rows_here
     span = row_len // group
     row, offset = side // group, (side % group) * span
     sharers = [[r * group + i for i in range(group)] for r in range(rows_here)]
-    width = table.shape[1]
+    own_words, width = table.shape
     classes = len_head.shape[1]
-    vocab_width = table.shape[0] * owners
+    vocab_width = own_words * owners
     vocab_base = side * vocab_width
     norm_count = norms.shape[1]
-
-    table_part = lax.all_gather(table.astype(low_type), "dp", axis=0, tiled=True)
+    norm_columns = 128
+
+    def columns_of(weight, rows):
+        return [weight[at : at + rows] for at in range(0, weight.shape[0], rows)]
 
     def gather_columns(parts):
         joined = jnp.concatenate([part.astype(low_type) for part in parts], 1)
@@ -555,33 +572,129 @@
             at += part.shape[1]
         return result
 
-    norm_columns = jnp.pad(norms.reshape(-1, norms.shape[2]).T, ((0, 0), (0, 128 - 2 * norm_count)))
-    w_in0, w_out0, f_in0, w_len, norm_low = gather_columns(
-        [attn_in[0], attn_out[0], ffn_in[0], len_head, norm_columns]
-    )
-    f_out0 = lax.all_gather(ffn_out[0].astype(low_type), "dp", axis=0, tiled=True)
-    w_in1, w_out1, w_in2, w_out2, f_in1 = gather_columns(
-        [attn_in[1], attn_out[1], attn_in[2], attn_out[2], ffn_in[1]]
-    )
-    f_out1 = lax.all_gather(ffn_out[1].astype(low_type), "dp", axis=0, tiled=True)
+    def join_rows(pieces):
+        blocks = [piece.reshape(owners, -1, piece.shape[1]) for piece in pieces]
+        return jnp.concatenate(blocks, 1).reshape(-1, pieces[0].shape[1])
+
+    share = attn_in.shape[1]
+    norm_part = jnp.pad(
+        norms.reshape(-1, norms.shape[2]).T, ((0, 0), (0, norm_columns - 2 * norm_count))
+    )
+    first_parts = [attn_in[0], attn_out[0], len_head, norm_part, ffn_in[0]]
+    first_parts += columns_of(ffn_out[0], share)
+    w_in0, w_out0, w_len, norm_low, f_in0, *f_out0 = gather_columns(first_parts)
+    next_parts = [attn_in[1], attn_out[1], attn_in[2], attn_out[2], ffn_in[1]]
+    next_parts += columns_of(ffn_out[1], share)
+    w_in1, w_out1, w_in2, w_out2, f_in1, *f_out1 = gather_columns(next_parts)
+    f_out0, f_out1 = join_rows(f_out0), join_rows(f_out1)
+    table_low = table.astype(low_type)
+    table_part = lax.all_gather(table_low, "dp", axis=0, tiled=True)
     norm_low = norm_low[:, : 2 * norm_count].T.astype(f32)
     gains, biases = norm_low[:norm_count], norm_low[norm_count:]
 
-    count = sum_everywhere(jnp.sum(tgt_mask).astype(f32).reshape(1, 1))[0, 0]
     ids = gather_seq(jnp.stack([src_ids, tgt_ids, tgt_mask]), 2).reshape(3, rows_here, row_len)
     src_starts = jnp.cumsum(src_lengths, -1) - src_lengths
     tgt_starts = jnp.cumsum(tgt_lengths, -1) - tgt_lengths
     places = jnp.arange(row_len)
     opens = jnp.any(places[None, :, None] == src_starts[:, None, :], -1)
-    src_in = jnp.where(opens, length_token, ids[0]).reshape(seqs, span)
+    src_in = pick(jnp.where(opens, length_token, ids[0]).reshape(seqs, span), 0, side)
     masked = (ids[2] == 1).reshape(seqs, span)
     labels = ids[1].reshape(seqs, span)
-    dec_in = jnp.where(masked, mask_token, labels)
+    dec_in = pick(jnp.where(masked, mask_token, labels), 0, side)
+    counts = jnp.sum(masked.astype(jnp.int32), -1)
+
+    slots = -(-(2 * span // devices) // 16) * 16
+    slots = max(slots, 16)
+
+    def ask(token_ids):
+        same = token_ids[:, None] == token_ids[None, :]
+        index = jnp.arange(span)
+        earlier = index[None, :] < index[:, None]
+        leader = jnp.logical_not(jnp.any(same & earlier, 1))
+        holder = token_ids // own_words
+        rank = jnp.sum(
+            (earlier & leader[None, :] & (holder[:, None] == holder[None, :])).astype(jnp.int32), 1
+        )
+        rank = jnp.sum(jnp.where(same & leader[None, :], rank[None, :], 0), 1)
+        return token_ids % own_words, holder, rank, jnp.max(rank) // slots + 1
+
+    def round_of(asked, turn):
+        local, holder, rank, _ = asked
+        code = jnp.where(rank // slots == turn, holder * slots + rank % slots, -1)
+        chosen = code[:, None] == jnp.arange(devices * slots)[None, :]
+        wanted = jnp.max(jnp.where(chosen, local[:, None], -1), 0)
+        wanted = to_each(wanted.reshape(devices, slots)).reshape(-1)
+        held = wanted[:, None] == jnp.arange(own_words)[None, :]
+        return chosen.astype(low_type), held.astype(low_type)
+
+    def fetch(maps):
+        chosen, held = maps
+        found = contract(held, table_low, 1, 0).astype(low_type)
+        found = to_each(found.reshape(devices, slots, width)).reshape(-1, width)
+        return contract(chosen, found, 1, 0)
+
+    def give(maps, grads):
+        chosen, held = maps
+        sums = contract(chosen, grads.astype(low_type), 0, 0).astype(low_type)
+        sums = to_each(sums.reshape(devices, slots, width)).reshape(-1, width)
+        return contract(held, sums, 0, 0)
+
+    def later_rounds(asked, rounds, value, visit):
+        def body(turn, carry):
+            return carry + visit(round_of(asked, turn))
+
+        return lax.fori_loop(1, rounds, body, value)
+
+    src_ask, dec_ask = ask(src_in), ask(dec_in)
+    local_facts = [
+        jnp.sum(tgt_mask),
+        jnp.max(counts),
+        src_ask[3],
+        dec_ask[3],
+    ]
+
+    def combine(first, second):
+        added = jnp.arange(len(local_facts))[None, :] == 0
+        return jnp.where(added, first + second, jnp.maximum(first, second))
+
+    def reduce(values, axis):
+        return jnp.concatenate([lax.psum(values[:, :1], axis), lax.pmax(values[:, 1:], axis)], 1)
+
+    facts = everywhere(jnp.stack(local_facts).astype(jnp.int32).reshape(1, -1), combine, reduce)[0]
+    count = facts[0].astype(f32)
+    cut = -(-(span * 3 // 8) // 128) * 128
+    more = facts[1] > cut
+    src_maps = round_of(src_ask, 0)
+    src_found = fetch(src_maps)
+    dec_maps = round_of(dec_ask, 0)
+    dec_found = fetch(dec_maps)
+
+    starts_at = jnp.cumsum(counts) - counts
+    total = jnp.sum(counts)
+    rank = jnp.cumsum(masked.astype(jnp.int32), -1) - 1
+    slot_of = jnp.where(masked, rank + starts_at[:, None], -1)
+    slot_index = jnp.arange(seqs * span)
+    slot_label = jnp.sum(
+        jnp.where(slot_of.reshape(1, -1) == slot_index[:, None], labels.reshape(1, -1), 0), -1
+    )
+    valid = slot_index < total
+    targets = jnp.where(valid, slot_label - vocab_base, -1).reshape(1, -1)
+    left = total % place_block
+    chunks = jnp.stack(
+        [
+            total // place_block + (left > place_block // 2).astype(jnp.int32),
+            ((left > 0) & (left <= place_block // 2)).astype(jnp.int32),
+        ]
+    )
+    own_rank = pick(jnp.where(masked, rank, -1), 0, side)
+    own_chosen = (own_rank[None, :] == jnp.arange(span)[:, None]).astype(low_type)
+    own_slots = (pick(slot_of, 0, side)[:, None] == slot_index[None, :]).astype(low_type)
+
     own_places = offset + jnp.arange(span)
     src_start, src_length = pick(src_starts, 0, row), pick(src_lengths, 0, row)
     tgt_start, tgt_length = pick(tgt_starts, 0, row), pick(tgt_lengths, 0, row)
-    src_number, src_open = place_spans(src_start, src_length, own_places)
-    tgt_number, tgt_open = place_spans(tgt_start, tgt_length, own_places)
+    src_number, src_open = place_spans(src_start, own_places)
+    tgt_number, tgt_open = place_spans(tgt_start, own_places)
     block = min(query_block, span)
     enc_spans = key_spans(src_number, src_start, src_length, block)
     self_spans = key_spans(tgt_number, tgt_start, tgt_length, block)
@@ -590,30 +703,11 @@
         (sinusoid(own_places - src_open, width), sinusoid(own_places - tgt_open, width))
     )
 
-    rank = jnp.cumsum(masked.astype(jnp.int32), -1) - 1
-    counts = rank[:, -1] + 1
-    chosen = (rank[:, None, :] == jnp.arange(span)[None, :, None]) & masked[:, None, :]
-    packed_labels = jnp.sum(jnp.where(chosen, labels[:, None, :], 0), -1)
-    valid = jnp.arange(span)[None, :] < counts[:, None]
-    targets = jnp.where(valid, packed_labels - vocab_base, -1).reshape(1, -1)
-    chunks = (counts + place_block - 1) // place_block
-    own_chosen = pick(chosen, 0, side).astype(low_type)
-
-    def lookup(token_ids):
-        local = token_ids - vocab_base
-        inside = (local >= 0) & (local < vocab_width)
-        found = jnp.take(table_part, jnp.clip(local, 0, vocab_width - 1), axis=0)
-        return jnp.where(inside[..., None], found, 0.0).astype(low_type)
-
-    def embed(token_ids):
-        if seqs == 2:
-            away = swap(lookup(pick(token_ids, 0, 1 - side)), "seq", 1)
-            return lookup(pick(token_ids, 0, side)).astype(f32) + away.astype(f32)
-        return lax.psum_scatter(lookup(token_ids), "seq", scatter_dimension=0).astype(f32)
-
     root = math.sqrt(width)
-    stream0 = embed(src_in) * root + src_wave
-    target0 = embed(dec_in) * root + tgt_wave
+    src_found = later_rounds(src_ask, facts[2], src_found, fetch)
+    dec_found = later_rounds(dec_ask, facts[3], dec_found, fetch)
+    stream0 = src_found * root + src_wave
+    target0 = dec_found * root + tgt_wave
 
     def norm(stream, index):
         return layer_norm(stream, gains[index], biases[index])
@@ -698,30 +792,44 @@
     final = norm(target3, 6).astype(low_type)
 
     packed = contract(own_chosen, final, 1, 0).astype(low_type)
-    pieces = gather_seq(packed, 0).reshape(seqs * span, width)
-    stats = head_stats(chunks, table_part, pieces, targets, span)
-    every = gather_seq(stats, 0)
+    if seqs == 2:
+        other = swap_rows(packed, cut, more)
+        packs = [jnp.where(side == 0, packed, other), jnp.where(side == 0, other, packed)]
+    else:
+        packs = lax.all_gather(packed, "seq", axis=0)
+        packs = [packs[s] for s in range(seqs)]
+    rows = jnp.zeros((seqs * span, width), low_type)
+    pieces = sum(
+        lax.dynamic_update_slice_in_dim(rows, packs[s], starts_at[s], 0) for s in range(seqs)
+    )
+    every = gather_seq(head_stats(chunks, table_part, pieces), 0)
     top_logit = jnp.max(every[:, 0], 0)
     totals = jnp.sum(every[:, 1] * jnp.exp(every[:, 0] - top_logit[None]), 0)
-    log_total = jnp.where(valid.reshape(-1), top_logit + jnp.log(totals), 0.0)
-    target_logit = jnp.sum(every[:, 2], 0)
-    loss_rows = jnp.where(valid.reshape(-1), log_total - target_logit, 0.0).reshape(seqs, span)
-    token_local = jnp.sum(pick(loss_rows, 0, side))
-    weights = valid.astype(f32).reshape(1, -1) / count
-    d_table, d_pieces = head_back(
-        chunks, table_part, pieces, targets, log_total[None], weights, span
-    )
+    log_total = top_logit + jnp.log(jnp.where(valid, totals, 1.0))
+    own_start = pick(starts_at, 0, side)
+    mine = (slot_index >= own_start) & (slot_index < own_start + pick(counts, 0, side))
+    token_local = jnp.sum(jnp.where(mine, log_total, 0.0))
+    logs = jnp.where(valid, log_total + jnp.log(count), 1e30)
+    weights = jnp.where(valid, 1.0 / count, 0.0)
+    d_table, d_pieces, picks = head_back(
+        chunks, table_part, pieces, targets, logs[None], weights[None]
+    )
+    token_local = token_local - jnp.sum(picks)
+    owned_table = d_table.reshape(owners, own_words, width)
+    half = width // 2
+    table_one = Halving([owned_table[:, :, :half]], False)
+    if seqs != 2:
+        d_pieces = lax.psum(d_pieces, "seq")
+    d_high = lax.reduce_precision(d_pieces, 8, 7)
+    d_rest = (d_pieces - d_high).astype(low_type)
+    d_high = d_high.astype(low_type)
+    d_final = contract(own_slots, d_high, 1, 1) + contract(own_slots, d_rest, 1, 1)
     if seqs == 2:
-        d_packed = lax.dynamic_slice_in_dim(d_pieces, side * span, span, 1) + swap(
-            lax.dynamic_slice_in_dim(d_pieces, (1 - side) * span, span, 1), "seq", 1
-        )
-    else:
-        d_packed = lax.psum_scatter(d_pieces, "seq", scatter_dimension=1, tiled=True)
-    d_high = lax.reduce_precision(d_packed, 8, 7)
-    d_rest = (d_packed - d_high).astype(low_type)
-    d_final = contract(own_chosen, d_high.astype(low_type), 0, 1) + contract(
-        own_chosen, d_rest, 0, 1
-    )
+        away_start, away_count = pick(starts_at, 0, 1 - side), pick(counts, 0, 1 - side)
+        index = jnp.arange(span)[:, None]
+        away = (slot_index[None, :] == index + away_start) & (index < away_count)
+        away = contract(away.astype(low_type), d_high, 1, 1).astype(low_type)
+        d_final = d_final + contract(own_chosen, swap_rows(away, cut, more), 0, 0)
 
     first_place = own_places[None, :] == src_start[:, None]
     mine = jnp.any(first_place, -1)
@@ -746,68 +854,107 @@
         preferred_element_type=f32,
     )
 
+    def owned(grad):
+        return grad.reshape(owners, -1, grad.shape[1])
+
+    def owned_columns(grad):
+        whole = owned(grad)
+        return [whole[:, at : at + share] for at in range(0, whole.shape[1], share)]
+
     d_target3, gain6, bias6 = norm_backward(target3, gains[6], biases[6], d_final)
     d_inner5, d_fin1, d_fout1 = ffn_back(inner5, f_in1, f_out1, keep5, d_target3)
+    chains = [table_one]
+    (d_inner5, d_target3, owned_table) = advance((d_inner5, d_target3, owned_table), chains)
+    table_two = Halving([owned_table[:, :, half:]], False)
+    chain_a = Halving([owned(d_fin1)] + owned_columns(d_fout1), True)
     d_target2, gain5, bias5 = norm_backward(target2, gains[5], biases[5], d_inner5)
     d_target2 = d_target2 + d_target3
     d_inner4, d_cross, d_win2, d_wout2 = cross_attention_back(
         inner4, memory, w_in2, w_out2, cross_spans, keep4, d_target2
     )
+    chains += [table_two, chain_a]
+    d_inner4, d_target2, d_cross = advance((d_inner4, d_target2, d_cross), chains)
+    chain_b = Halving([owned(d_win2), owned(d_wout2)], True)
     d_target1, gain4, bias4 = norm_backward(target1, gains[4], biases[4], d_inner4)
     d_target1 = d_target1 + d_target2
     d_inner3, d_win1, d_wout1 = self_attention_back(
         inner3, w_in1, w_out1, self_spans, keep3, d_target1
     )
+    chains += [chain_b]
+    d_inner3, d_target1 = advance((d_inner3, d_target1), chains)
+    chain_c = Halving([owned(d_win1), owned(d_wout1)], True)
     d_target0, gain3, bias3 = norm_backward(target0, gains[3], biases[3], d_inner3)
     d_target0 = d_target0 + d_target1
+    dec_grad = d_target0 * root
+    dec_given = give(dec_maps, dec_grad)
     d_stream2, gain2, bias2 = norm_backward(stream2, gains[2], biases[2], d_memory + d_cross)
     d_inner1, d_fin0, d_fout0 = ffn_back(inner1, f_in0, f_out0, keep1, d_stream2)
+    chains += [chain_c]
+    d_inner1, d_stream2 = advance((d_inner1, d_stream2), chains)
+    chain_d = Halving([owned(d_fin0)] + owned_columns(d_fout0), True)
     d_stream1, gain1, bias1 = norm_backward(stream1, gains[1], biases[1], d_inner1)
     d_stream1 = d_stream1 + d_stream2
     d_inner0, d_win0, d_wout0 = self_attention_back(
         inner0, w_in0, w_out0, enc_spans, keep0, d_stream1
     )
+    chains += [chain_d]
+    d_inner0, d_stream1 = advance((d_inner0, d_stream1), chains)
     d_stream0, gain0, bias0 = norm_backward(stream0, gains[0], biases[0], d_inner0)
     d_stream0 = d_stream0 + d_stream1
-
-    def spread(base, token_ids, grads):
-        local = (token_ids - vocab_base).reshape(-1)
-        inside = (local >= 0) & (local < vocab_width)
-        terms = jnp.where(inside[:, None], grads.reshape(-1, width).astype(f32), 0.0)
-        return base.at[jnp.clip(local, 0, vocab_width - 1)].add(terms)
-
-    d_dec_all = gather_seq((d_target0 * root).astype(low_type), 0)
-    d_src_all = gather_seq((d_stream0 * root).astype(low_type), 0)
-    d_table = spread(spread(d_table, dec_in, d_dec_all), src_in, d_src_all)
-    table_grad = table_to_owner(d_table, 4)
+    src_grad = d_stream0 * root
+    src_given = give(src_maps, src_grad)
     norm_grads = [gain0, gain1, gain2, gain3, gain4, gain5, gain6]
     norm_grads += [bias0, bias1, bias2, bias3, bias4, bias5, bias6]
-    small = jnp.concatenate(
-        [d_w_len, jnp.pad(jnp.stack(norm_grads, 1), ((0, 0), (0, 128 - 2 * norm_count)))], 1
-    )
-    g_fout1, sq0 = layer_to_owner(d_fout1)
-    g_fin1, sq1 = layer_to_owner(d_fin1)
-    g_wout2, sq2 = layer_to_owner(d_wout2)
-    g_win2, sq3 = layer_to_owner(d_win2)
-    g_wout1, sq4 = layer_to_owner(d_wout1)
-    g_win1, sq5 = layer_to_owner(d_win1)
-    g_fout0, sq6 = layer_to_owner(d_fout0)
-    g_fin0, sq7 = layer_to_owner(d_fin0)
-    g_wout0, sq8 = layer_to_owner(d_wout0)
-    g_win0, sq9 = layer_to_owner(d_win0)
-    g_small, sq10 = layer_to_owner(small)
-    square = sq0 + sq1 + sq2 + sq3 + sq4 + sq5 + sq6 + sq7 + sq8 + sq9 + sq10
-    square = square + jnp.sum(table_grad * table_grad)
-    sums = sum_everywhere(jnp.stack([token_local, len_local, square]).reshape(1, 3))[0]
+    g_norms = everywhere(jnp.stack(norm_grads), jnp.add, lax.psum)
+    norm_square = jnp.where((side == 0) & (lax.axis_index("dp") == 0), jnp.sum(g_norms * g_norms), 0.0)
+    norm_share = norms.shape[2]
+    g_norms = lax.dynamic_slice_in_dim(g_norms, lax.axis_index("dp") * norm_share, norm_share, 1)
+    chain_e = Halving([owned(d_win0), owned(d_wout0), owned(d_w_len)], True)
+    chains += [chain_e]
+    while any(chain.pending is not None for chain in chains):
+        advance((), chains)
+    for chain in chains:
+        chain.finish()
+
+    given = dec_given + src_given
+    given = later_rounds(dec_ask, facts[3], given, lambda maps: give(maps, dec_grad))
+    given = later_rounds(src_ask, facts[2], given, lambda maps: give(maps, src_grad))
+    table_grad = jnp.concatenate(
+        [table_one.value.reshape(own_words, -1), table_two.value.reshape(own_words, -1)], 1
+    )
+    table_grad = table_grad + given
+    square = sum(chain.square for chain in (chain_a, chain_b, chain_c, chain_d, chain_e))
+    square = square + jnp.sum(table_grad * table_grad) + norm_square
+    sums = everywhere(
+        jnp.stack([token_local, len_local, square]).reshape(1, 3), jnp.add, lax.psum
+    )[0]
     token_sum, len_sum, grad_norm = sums[0], sums[1], jnp.sqrt(sums[2])
     factor = jnp.minimum(1.0, clip_limit / (grad_norm + 1e-06))
+
+    def cut_columns(chain, sizes):
+        result, at = [], 0
+        value = chain.value.reshape(share, -1)
+        for size in sizes:
+            result.append(value[:, at : at + size])
+            at += size
+        return result
+
+    hidden_width = ffn_in.shape[2]
+    pieces_out = ffn_out.shape[1] // share
+    ffn_sizes = [hidden_width] + [width] * pieces_out
+    attn_sizes = [3 * width, width]
+    g_fin1, *g_fout1 = cut_columns(chain_a, ffn_sizes)
+    g_win2, g_wout2 = cut_columns(chain_b, attn_sizes)
+    g_win1, g_wout1 = cut_columns(chain_c, attn_sizes)
+    g_fin0, *g_fout0 = cut_columns(chain_d, ffn_sizes)
+    g_win0, g_wout0, g_len = cut_columns(chain_e, attn_sizes + [classes])
     grads = (
         jnp.stack([g_win0, g_win1, g_win2]),
         jnp.stack([g_wout0, g_wout1, g_wout2]),
         jnp.stack([g_fin0, g_fin1]),
-        jnp.stack([g_fout0, g_fout1]),
-        g_small[:, :classes],
-        g_small[:, classes : classes + 2 * norm_count].T.reshape(norms.shape),
+        jnp.stack([jnp.concatenate(g_fout0, 0), jnp.concatenate(g_fout1, 0)]),
+        g_len,
+        g_norms.reshape(norms.shape),
         table_grad,
     )
     masters = (attn_in, attn_out, ffn_in, ffn_out, len_head, norms, table)

time: 1570 us -> 1200 us (0.76)
  waiting for transfers between devices: 529 us -> 278 us
  Pallas kernels: 368 us -> 242 us
  starting transfers between devices: 140 us -> 78.4 us
  matrix products: 138 us -> 182 us
  local copies, waits for them, and re-layouts: 146 us -> 169 us
    ppermute x100 -> x57, waiting for transfers between devices: 412 us -> 219 us  [swap(): return lax.ppermute(values, axis, [(i, i ^ bit) for i in range(size)])]
    pallas_call x2, Pallas kernels: 242 us -> 114 us  [the longest x1 82.2 us: head_back(): pl.pallas_call(head_back_kernel, grid_spec=pltpu.PrefetchScalarGridSpec(n...]
    ppermute x100 -> x57, starting transfers between devices: 140 us -> 55.8 us  [swap(): return lax.ppermute(values, axis, [(i, i ^ bit) for i in range(size)])]
    all_gather x3 -> x1, waiting for transfers between devices: 79.7 us -> 0.02 us  [on_device(): table_part = lax.all_gather(table_low, 'dp', axis=0, tiled=True)]
    scatter-add x14 -> x0, other arithmetic: 70.4 us -> none  [the longest x2 70.3 us: spread(): return base.at[jnp.clip(local, 0, vocab_width - 1)].add(terms)]
    all_to_all x0 -> x6, waiting for transfers between devices: none -> 58.1 us  [to_each(): return lax.all_to_all(values, ('seq', 'dp'), 0, 0)]
    gather x4 -> x0, local copies, waits for them, and re-layouts: 48.3 us -> none  [lookup(): found = jnp.take(table_part, jnp.clip(local, 0, vocab_width - 1), axis=0)]
    dot_general x40 -> x50, matrix products: 136 us -> 180 us  [contract(): lax.dot_general(left, right, (((left_dim,), (right_dim,)), ((), ())), pre...]
  transfers between devices with their start and end apart: 105 -> 66, of which waited for: 73 -> 30; matrix products, arithmetic and copies ran while one was open for 26% -> 38% of each run, Pallas kernels for 8% -> 11%
where the time goes in v2:
time: 1200 us; the launch traced here: 1190 us
  waiting for transfers between devices  278 us (23%)
  Pallas kernels  242 us (20%)
  other arithmetic  191 us (16%)
  matrix products  182 us (15%)
  local copies, waits for them, and re-layouts  169 us (14%)
  starting transfers between devices  78.4 us (7%)
  between operations  41.1 us (3%)
    ppermute x57, waiting for transfers between devices, swap(): return lax.ppermute(values, axis, [(i, i ^ bit) for i in range(size)])  219 us
    dot_general x50, matrix products, contract(): lax.dot_general(left, right, (((left_dim,), (right_dim,)), ((), ())), pre...  180 us
    pallas_call x1, Pallas kernels, head_back(): pl.pallas_call(head_back_kernel, grid_spec=pltpu.PrefetchScalarGridSpec(n...  82.2 us
    pallas_call x3, Pallas kernels, attend_backward(): pl.pallas_call(functools.partial(attend_backward_kernel, head=width // HE...  79.4 us
    all_to_all x6, waiting for transfers between devices, to_each(): return lax.all_to_all(values, ('seq', 'dp'), 0, 0)  58.1 us
    unnamed x572, local copies, waits for them, and re-layouts  56.9 us
    ppermute x57, starting transfers between devices, swap(): return lax.ppermute(values, axis, [(i, i ^ bit) for i in range(size)])  55.8 us
    add x26, other arithmetic, absorb(): self.parts = [jnp.concatenate(self.parts, 2) + got.astype(f32)]  55.3 us
  transfers between devices with their start and end apart: 66, of which 30 were waited for; matrix products, arithmetic and copies ran while one was open for 38% of the time, Pallas kernels for 11%

profile of v2, /device:TPU:0, one launch (start us, length us, event | category | flops | bytes accessed | tf_op | source)
XLA Modules:
  0.0 1188.5 jit_solution(14267659575900078143)
XLA Ops:
  31.1 6.4 all-to-all-start.10
  61.2 7.3 multiply_sine_fusion
  85.9 20.5 %collective-permute-done.5 = s32[1,4]{1,0:T(1,128)S(1)} collective-permute-done((s32[1,4]{1,0:T(1,128)S(1)}, s32[1,4]{1,0:T(1,128)S(1)}, u32[]{:S(2)}, u32[]{:S(2)}) %collective-permute-start.5) | collective-permute-done | bytes 48 | tf_op jit(solution)/shard_map/ppermute | solution.py:376
  110.9 23.3 %collective-permute-done.6 = s32[1,4]{1,0:T(1,128)S(1)} collective-permute-done((s32[1,4]{1,0:T(1,128)S(1)}, s32[1,4]{1,0:T(1,128)S(1)}, u32[]{:S(2)}, u32[]{:S(2)}) %collective-permute-start.6) | collective-permute-done | bytes 48 | tf_op jit(solution)/shard_map/ppermute | solution.py:376
  175.0 49.7 %all-to-all-done.9 = bf16[32,64,512]{2,1,0:T(8,128)(2,1)S(1)} async-done(((bf16[32,64,512]{2,1,0:T(8,128)(2,1)}), bf16[32,64,512]{2,1,0:T(8,128)(2,1)S(1)}, u32[]{:S(2)}, u32[]{:S(2)}) %all-to-all-start.9) | async-done | bytes 2097184 | tf_op jit(solution)/shard_map/all_to_all | solution.py:416
  247.0 15.6 %attend_forward.4 = (bf16[512,1024]{1,0:T(8,128)(2,1)}, f32[8,1024]{1,0:T(8,128)}) custom-call(s32[2,8]{1,0:T(2,128)} %pad_add_fusion.7.bounds, bf16[1536,1024]{1,0:T(8,128)(2,1)} %convolution_convert_fusion.q_ref.k_ref.v_ref, bf16[1536,1024]{1,0:T(8,128)(2,1)} %convolution_convert_fusion.q_ref.k_ref.v_ref, ...), custom_call_target="tpu_custom_call" | custom-call | tf_op jit(solution)/shard_map/attend_forward/pallas_call | solution.py:195
  292.2 18.0 %attend_forward.3 = (bf16[512,1024]{1,0:T(8,128)(2,1)}, f32[8,1024]{1,0:T(8,128)}) custom-call(s32[2,8]{1,0:T(2,128)} %pad_add_fusion.5.bounds, bf16[1536,1024]{1,0:T(8,128)(2,1)} %convolution_convert_fusion.1.q_ref.k_ref.v_ref, bf16[1536,1024]{1,0:T(8,128)(2,1)} %convolution_convert_fusion.1.q_ref.k_ref.v_ref, ...), custom_call_target="tpu_custom_call" | custom-call | tf_op jit(solution)/shard_map/attend_forward/pallas_call | solution.py:195
  320.4 15.0 %attend_forward.5 = (bf16[512,1024]{1,0:T(8,128)(2,1)}, f32[8,1024]{1,0:T(8,128)}) custom-call(s32[2,8]{1,0:T(2,128)} %pad_add_fusion.6.bounds, bf16[512,1024]{1,0:T(8,128)(2,1)} %convolution_convert_fusion.6.q_ref, bf16[1024,1024]{1,0:T(8,128)(2,1)} %convolution_convert_fusion.2.k_ref.v_ref, bf16[1024,1024]{1,0:T(8,128)(2,1)} %convolution_convert_fusion.2.k_ref.v_ref, ...), custom_call_target="tpu_custom_call" | custom-call | tf_op jit(solution)/shard_map/attend_forward/pallas_call | solution.py:195
  359.0 6.2 collective-permute-done.8
  369.0 6.5 dynamic_update_slice.8
  378.4 6.5 add.1197.rows_ref
  384.9 31.7 %head_stats.1 = f32[2,2048]{1,0:T(2,128)} custom-call(s32[2]{0:T(128)} %pad_add_fusion.8.chunks, bf16[16000,512]{1,0:T(8,128)(2,1)} %all-gather.4.cloned.1.call-done.table_ref, bf16[2048,512]{1,0:T(8,128)(2,1)} %add.1197.rows_ref), custom_call_target="tpu_custom_call" | custom-call | tf_op jit(solution)/shard_map/head_stats/pallas_call | solution.py:332
  424.5 82.2 %head_back.1 = (f32[16000,512]{1,0:T(8,128)}, f32[512,2048]{1,0:T(8,128)}, f32[8,2048]{1,0:T(8,128)}) custom-call(s32[2]{0:T(128)} %pad_add_fusion.8.chunks, bf16[16000,512]{1,0:T(8,128)(2,1)} %all-gather.4.cloned.1.call-done.table_ref, bf16[2048,512]{1,0:T(8,128)(2,1)} %add.1197.rows_ref, s32[1,2048]{1,0:T(1,128)} %fusion.269.target_ref, ...), custom_call_target="tpu_custom_call" | custom-call | tf_op jit(solution)/shard_map/head_back/pallas_call | solution.py:350
  513.1 6.2 fusion.58
  519.3 6.6 slice.527
  547.6 7.8 fusion.57
  577.5 8.5 bitcast_add_fusion.1
  592.7 6.6 slice.440
  601.9 6.9 fusion.110
  613.3 24.3 %attend_backward.3 = (bf16[512,1024]{1,0:T(8,128)(2,1)}, bf16[1024,1024]{1,0:T(8,128)(2,1)}) custom-call(s32[2,8]{1,0:T(2,128)} %pad_add_fusion.6.bounds, bf16[512,1024]{1,0:T(8,128)(2,1)} %convolution_convert_fusion.6.q_ref, bf16[1024,1024]{1,0:T(8,128)(2,1)} %convolution_convert_fusion.2.k_ref.v_ref, ...), custom_call_target="tpu_custom_call" | custom-call | tf_op jit(solution)/shard_map/attend_backward/pallas_call | solution.py:220
  676.5 7.4 fusion.50
  692.9 8.7 bitcast_add_fusion
  717.9 29.6 %attend_backward.4 = (bf16[512,1024]{1,0:T(8,128)(2,1)}, bf16[1024,1024]{1,0:T(8,128)(2,1)}) custom-call(s32[2,8]{1,0:T(2,128)} %pad_add_fusion.5.bounds, bf16[1536,1024]{1,0:T(8,128)(2,1)} %convolution_convert_fusion.1.q_ref.k_ref.v_ref, bf16[1536,1024]{1,0:T(8,128)(2,1)} %convolution_convert_fusion.1.q_ref.k_ref.v_ref, ...), custom_call_target="tpu_custom_call" | custom-call | tf_op jit(solution)/shard_map/attend_backward/pallas_call | solution.py:220
  757.2 5.7 fusion.128
  765.9 5.8 fusion.116
  811.7 20.1 %collective-permute-done.20 = bf16[2,1000,256]{2,1,0:T(8,128)(2,1)} collective-permute-done((bf16[2,1000,256]{2,1,0:T(8,128)(2,1)}, bf16[2,1000,256]{2,1,0:T(8,128)(2,1)}, u32[]{:S(2)}, u32[]{:S(2)}) %collective-permute-start.20) | collective-permute-done | bytes 1024032 | tf_op jit(solution)/shard_map/ppermute | solution.py:376
  859.3 25.5 %attend_backward.5 = (bf16[512,1024]{1,0:T(8,128)(2,1)}, bf16[1024,1024]{1,0:T(8,128)(2,1)}) custom-call(s32[2,8]{1,0:T(2,128)} %pad_add_fusion.7.bounds, bf16[1536,1024]{1,0:T(8,128)(2,1)} %convolution_convert_fusion.q_ref.k_ref.v_ref, bf16[1536,1024]{1,0:T(8,128)(2,1)} %convolution_convert_fusion.q_ref.k_ref.v_ref, ...), custom_call_target="tpu_custom_call" | custom-call | tf_op jit(solution)/shard_map/attend_backward/pallas_call | solution.py:220
  972.0 10.8 collective-permute-done.34
  1013.6 44.4 %collective-permute-done.44 = bf16[1,16,4096]{2,1,0:T(8,128)(2,1)} collective-permute-done((bf16[1,16,4096]{2,1,0:T(8,128)(2,1)}, bf16[1,16,4096]{2,1,0:T(8,128)(2,1)}, u32[]{:S(2)}, u32[]{:S(2)}) %collective-permute-start.44) | collective-permute-done | bytes 131104 | tf_op jit(solution)/shard_map/ppermute | solution.py:376
  1069.8 44.6 %collective-permute-done.47 = bf16[1,16,2304]{2,1,0:T(8,128)(2,1)S(1)} collective-permute-done((bf16[1,16,2304]{2,1,0:T(8,128)(2,1)S(1)}, bf16[1,16,2304]{2,1,0:T(8,128)(2,1)S(1)}, u32[]{:S(2)}, u32[]{:S(2)}) %collective-permute-start.47) | collective-permute-done | bytes 73760 | tf_op jit(solution)/shard_map/ppermute | solution.py:376
  1127.7 6.3 fusion.124
  1165.8 7.5 multiply_subtract_fusion
  (1069 shorter events, 577.0 us)
Async XLA Ops:
  7.2 230.8 %all-gather.8.cloned.1.call-start = ((), (), s32[]{:S(2)}) async-start(), calls=%async_computation.16 | async-start | bytes 7102464 | tf_op jit(solution)/shard_map/all_gather | solution.py:568
  12.4 274.8 %all-gather.6.cloned.1.call-start = ((), (), s32[]{:S(2)}) async-start(), calls=%async_computation.15 | async-start | bytes 8912896 | tf_op jit(solution)/shard_map/all_gather | solution.py:568
  55.6 87.3 %all-to-all-start.11 = ((bf16[32,64,512]{2,1,0:T(8,128)(2,1)}), bf16[32,64,512]{2,1,0:T(8,128)(2,1)S(1)}, u32[]{:S(2)}, u32[]{:S(2)}) async-start(bf16[32,64,512]{2,1,0:T(8,128)(2,1)} %bitcast.73), calls=%async_computation.11 | async-start | bytes 4194304 | tf_op jit(solution)/shard_map/all_to_all | solution.py:416
  58.5 326.4 %all-gather.4.cloned.1.call-start = ((), (), s32[]{:S(2)}) async-start(), calls=%async_computation.14 | async-start | bytes 17408000 | tf_op jit(solution)/shard_map/all_gather | solution.py:591
  106.3 27.8 %collective-permute-start.6 = (s32[1,4]{1,0:T(1,128)S(1)}, s32[1,4]{1,0:T(1,128)S(1)}, u32[]{:S(2)}, u32[]{:S(2)}) collective-permute-start(s32[1,4]{1,0:T(1,128)S(1)} %maximum_select_fusion.2), channel_id=1, source_target_pairs={{0,16},{2,18},{4,20},{6,22},{8,24},{10,26},{12,28},{14,30},{16,0},... | collective-permute-start | bytes 56 | tf_op jit(solution)/shard_map/ppermute | solution.py:376
  147.8 77.0 %all-to-all-start.9 = ((bf16[32,64,512]{2,1,0:T(8,128)(2,1)}), bf16[32,64,512]{2,1,0:T(8,128)(2,1)S(1)}, u32[]{:S(2)}, u32[]{:S(2)}) async-start(bf16[32,64,512]{2,1,0:T(8,128)(2,1)} %bitcast.758), calls=%async_computation.9 | async-start | bytes 4194304 | tf_op jit(solution)/shard_map/all_to_all | solution.py:416
  512.8 28.0 %collective-permute-start.10 = (bf16[384,512]{1,0:T(8,128)(2,1)S(1)}, bf16[384,512]{1,0:T(8,128)(2,1)S(1)}, u32[]{:S(2)}, u32[]{:S(2)}) collective-permute-start(bf16[384,512]{1,0:T(8,128)(2,1)S(1)} %slice.522), channel_id=1, source_target_pairs={{0,1},{1,0},{2,3},{3,2},{4,5},{5,4},{6,7},{7,6},{8,9},{9,8},{10,11... | collective-permute-start | bytes 1179656 | tf_op jit(solution)/shard_map/ppermute | solution.py:376
  533.8 43.7 %collective-permute-start.11 = (bf16[8,1000,256]{2,1,0:T(8,128)(2,1)}, bf16[8,1000,256]{2,1,0:T(8,128)(2,1)}, u32[]{:S(2)}, u32[]{:S(2)}) collective-permute-start(bf16[8,1000,256]{2,1,0:T(8,128)(2,1)} %fusion.96), channel_id=1, source_target_pairs={{0,2},{2,0},{4,6},{6,4},{8,10},{10,8},{12,14},{14,12},{16,18},{18,... | collective-permute-start | bytes 12288008 | tf_op jit(solution)/shard_map/ppermute | solution.py:376
  566.7 89.9 %collective-permute-start.14 = (bf16[8,32,4096]{2,1,0:T(8,128)(2,1)}, bf16[8,32,4096]{2,1,0:T(8,128)(2,1)}, u32[]{:S(2)}, u32[]{:S(2)}) collective-permute-start(bf16[8,32,4096]{2,1,0:T(8,128)(2,1)} %fusion.192), channel_id=1, source_target_pairs={{0,2},{2,0},{4,6},{6,4},{8,10},{10,8},{12,14},{14,12},{16,18},{18,... | collective-permute-start | bytes 6291464 | tf_op jit(solution)/shard_map/ppermute | solution.py:376
  601.9 54.7 %collective-permute-start.13 = (bf16[8,1000,256]{2,1,0:T(8,128)(2,1)}, bf16[8,1000,256]{2,1,0:T(8,128)(2,1)}, u32[]{:S(2)}, u32[]{:S(2)}) collective-permute-start(bf16[8,1000,256]{2,1,0:T(8,128)(2,1)} %fusion.97), channel_id=1, source_target_pairs={{0,2},{2,0},{4,6},{6,4},{8,10},{10,8},{12,14},{14,12},{16,18},{18,... | collective-permute-start | bytes 12288008 | tf_op jit(solution)/shard_map/ppermute | solution.py:376
  608.8 47.8 %collective-permute-start.12 = (bf16[4,1000,256]{2,1,0:T(8,128)(2,1)}, bf16[4,1000,256]{2,1,0:T(8,128)(2,1)}, u32[]{:S(2)}, u32[]{:S(2)}) collective-permute-start(bf16[4,1000,256]{2,1,0:T(8,128)(2,1)} %fusion.110), channel_id=1, source_target_pairs={{0,4},{2,6},{4,0},{6,2},{8,12},{10,14},{12,8},{14,10},{16,20},{18,... | collective-permute-start | bytes 6144008 | tf_op jit(solution)/shard_map/ppermute | solution.py:376
  647.9 123.7 %collective-permute-start.18 = (bf16[8,32,2048]{2,1,0:T(8,128)(2,1)}, bf16[8,32,2048]{2,1,0:T(8,128)(2,1)}, u32[]{:S(2)}, u32[]{:S(2)}) collective-permute-start(bf16[8,32,2048]{2,1,0:T(8,128)(2,1)} %pad_maximum_fusion.7), channel_id=1, source_target_pairs={{0,2},{2,0},{4,6},{6,4},{8,10},{10,8},{12,14},{14,12},{16,18},{18,... | collective-permute-start | bytes 3145736 | tf_op jit(solution)/shard_map/ppermute | solution.py:376
  705.9 65.7 %collective-permute-start.15 = (bf16[2,1000,256]{2,1,0:T(8,128)(2,1)}, bf16[2,1000,256]{2,1,0:T(8,128)(2,1)}, u32[]{:S(2)}, u32[]{:S(2)}) collective-permute-start(bf16[2,1000,256]{2,1,0:T(8,128)(2,1)} %fusion.144), channel_id=1, source_target_pairs={{0,8},{2,10},{4,12},{6,14},{8,0},{10,2},{12,4},{14,6},{16,24},{18,... | collective-permute-start | bytes 3072008 | tf_op jit(solution)/shard_map/ppermute | solution.py:376
  709.5 62.2 %collective-permute-start.17 = (bf16[8,16,4096]{2,1,0:T(8,128)(2,1)S(1)}, bf16[8,16,4096]{2,1,0:T(8,128)(2,1)}, u32[]{:S(2)}, u32[]{:S(2)}) collective-permute-start(bf16[8,16,4096]{2,1,0:T(8,128)(2,1)S(1)} %fusion.131), channel_id=1, source_target_pairs={{0,1},{1,0},{2,3},{3,2},{4,5},{5,4},{6,7},{7,6},{8,9},{9,8},{10,11... | collective-permute-start | bytes 3145736 | tf_op jit(solution)/shard_map/ppermute | solution.py:376
  715.1 56.5 %collective-permute-start.16 = (bf16[4,1000,256]{2,1,0:T(8,128)(2,1)}, bf16[4,1000,256]{2,1,0:T(8,128)(2,1)}, u32[]{:S(2)}, u32[]{:S(2)}) collective-permute-start(bf16[4,1000,256]{2,1,0:T(8,128)(2,1)} %fusion.111), channel_id=1, source_target_pairs={{0,4},{2,6},{4,0},{6,2},{8,12},{10,14},{12,8},{14,10},{16,20},{18,... | collective-permute-start | bytes 6144008 | tf_op jit(solution)/shard_map/ppermute | solution.py:376
  754.1 52.9 %collective-permute-start.23 = (bf16[8,32,2048]{2,1,0:T(8,128)(2,1)}, bf16[8,32,2048]{2,1,0:T(8,128)(2,1)}, u32[]{:S(2)}, u32[]{:S(2)}) collective-permute-start(bf16[8,32,2048]{2,1,0:T(8,128)(2,1)} %pad_maximum_fusion.8), channel_id=1, source_target_pairs={{0,2},{2,0},{4,6},{6,4},{8,10},{10,8},{12,14},{14,12},{16,18},{18,... | collective-permute-start | bytes 3145736 | tf_op jit(solution)/shard_map/ppermute | solution.py:376
  785.8 25.9 %collective-permute-start.19 = (bf16[1,1000,256]{2,1,0:T(8,128)(2,1)}, bf16[1,1000,256]{2,1,0:T(8,128)(2,1)}, u32[]{:S(2)}, u32[]{:S(2)}) collective-permute-start(bf16[1,1000,256]{2,1,0:T(8,128)(2,1)} %dynamic-slice_convert_fusion.13), channel_id=1, source_target_pairs={{0,16},{2,18},{4,20},{6,22},{8,24},{10,26},{12,28},{14,30},{16,0},... | collective-permute-start | bytes 1536008 | tf_op jit(solution)/shard_map/ppermute | solution.py:376
  797.5 34.2 %collective-permute-start.20 = (bf16[2,1000,256]{2,1,0:T(8,128)(2,1)}, bf16[2,1000,256]{2,1,0:T(8,128)(2,1)}, u32[]{:S(2)}, u32[]{:S(2)}) collective-permute-start(bf16[2,1000,256]{2,1,0:T(8,128)(2,1)} %fusion.145), channel_id=1, source_target_pairs={{0,8},{2,10},{4,12},{6,14},{8,0},{10,2},{12,4},{14,6},{16,24},{18,... | collective-permute-start | bytes 3072008 | tf_op jit(solution)/shard_map/ppermute | solution.py:376
  807.1 92.3 %collective-permute-start.28 = (bf16[8,32,4096]{2,1,0:T(8,128)(2,1)}, bf16[8,32,4096]{2,1,0:T(8,128)(2,1)}, u32[]{:S(2)}, u32[]{:S(2)}) collective-permute-start(bf16[8,32,4096]{2,1,0:T(8,128)(2,1)} %fusion.202), channel_id=1, source_target_pairs={{0,2},{2,0},{4,6},{6,4},{8,10},{10,8},{12,14},{14,12},{16,18},{18,... | collective-permute-start | bytes 6291464 | tf_op jit(solution)/shard_map/ppermute | solution.py:376
  848.1 54.2 %collective-permute-start.26 = (bf16[4,16,2048]{2,1,0:T(8,128)(2,1)S(1)}, bf16[4,16,2048]{2,1,0:T(8,128)(2,1)S(1)}, u32[]{:S(2)}, u32[]{:S(2)}) collective-permute-start(bf16[4,16,2048]{2,1,0:T(8,128)(2,1)S(1)} %fusion.194), channel_id=1, source_target_pairs={{0,4},{2,6},{4,0},{6,2},{8,12},{10,14},{12,8},{14,10},{16,20},{18,... | collective-permute-start | bytes 786440 | tf_op jit(solution)/shard_map/ppermute | solution.py:376
  848.8 53.6 %collective-permute-start.25 = (bf16[2,16,4096]{2,1,0:T(8,128)(2,1)S(1)}, bf16[2,16,4096]{2,1,0:T(8,128)(2,1)S(1)}, u32[]{:S(2)}, u32[]{:S(2)}) collective-permute-start(bf16[2,16,4096]{2,1,0:T(8,128)(2,1)S(1)} %fusion.193), channel_id=1, source_target_pairs={{0,8},{2,10},{4,12},{6,14},{8,0},{10,2},{12,4},{14,6},{16,24},{18,... | collective-permute-start | bytes 786440 | tf_op jit(solution)/shard_map/ppermute | solution.py:376
  849.0 53.3 %collective-permute-start.24 = (bf16[1,1000,256]{2,1,0:T(8,128)(2,1)S(1)}, bf16[1,1000,256]{2,1,0:T(8,128)(2,1)S(1)}, u32[]{:S(2)}, u32[]{:S(2)}) collective-permute-start(bf16[1,1000,256]{2,1,0:T(8,128)(2,1)S(1)} %dynamic-slice_convert_fusion.12), channel_id=1, source_target_pairs={{0,16},{2,18},{4,20},{6,22},{8,24},{10,26},{12,28},{14,30},{16,0},... | collective-permute-start | bytes 1536008 | tf_op jit(solution)/shard_map/ppermute | solution.py:376
  853.6 50.3 %collective-permute-start.27 = (bf16[8,16,2048]{2,1,0:T(8,128)(2,1)S(1)}, bf16[8,16,2048]{2,1,0:T(8,128)(2,1)}, u32[]{:S(2)}, u32[]{:S(2)}) collective-permute-start(bf16[8,16,2048]{2,1,0:T(8,128)(2,1)S(1)} %fusion.158), channel_id=1, source_target_pairs={{0,1},{1,0},{2,3},{3,2},{4,5},{5,4},{6,7},{7,6},{8,9},{9,8},{10,11... | collective-permute-start | bytes 1572872 | tf_op jit(solution)/shard_map/ppermute | solution.py:376
  899.4 51.0 %collective-permute-start.33 = (bf16[8,32,2304]{2,1,0:T(8,128)(2,1)}, bf16[8,32,2304]{2,1,0:T(8,128)(2,1)}, u32[]{:S(2)}, u32[]{:S(2)}) collective-permute-start(bf16[8,32,2304]{2,1,0:T(8,128)(2,1)} %pad_maximum_fusion.5), channel_id=1, source_target_pairs={{0,2},{2,0},{4,6},{6,4},{8,10},{10,8},{12,14},{14,12},{16,18},{18,... | collective-permute-start | bytes 3538952 | tf_op jit(solution)/shard_map/ppermute | solution.py:376
  927.3 26.3 %collective-permute-start.32 = (bf16[8,16,4096]{2,1,0:T(8,128)(2,1)}, bf16[8,16,4096]{2,1,0:T(8,128)(2,1)}, u32[]{:S(2)}, u32[]{:S(2)}) collective-permute-start(bf16[8,16,4096]{2,1,0:T(8,128)(2,1)} %fusion.132), channel_id=1, source_target_pairs={{0,1},{1,0},{2,3},{3,2},{4,5},{5,4},{6,7},{7,6},{8,9},{9,8},{10,11... | collective-permute-start | bytes 3145736 | tf_op jit(solution)/shard_map/ppermute | solution.py:376
  999.4 58.7 %all-to-all-start.13 = ((bf16[32,64,512]{2,1,0:T(8,128)(2,1)}), bf16[32,64,512]{2,1,0:T(8,128)(2,1)}, u32[]{:S(2)}, u32[]{:S(2)}) async-start(bf16[32,64,512]{2,1,0:T(8,128)(2,1)} %bitcast.757), calls=%async_computation.13 | async-start | bytes 4194304 | tf_op jit(solution)/shard_map/all_to_all | solution.py:416
  1005.0 53.1 %collective-permute-start.44 = (bf16[1,16,4096]{2,1,0:T(8,128)(2,1)}, bf16[1,16,4096]{2,1,0:T(8,128)(2,1)}, u32[]{:S(2)}, u32[]{:S(2)}) collective-permute-start(bf16[1,16,4096]{2,1,0:T(8,128)(2,1)} %dynamic-slice_convert_fusion.26), channel_id=1, source_target_pairs={{0,16},{2,18},{4,20},{6,22},{8,24},{10,26},{12,28},{14,30},{16,0},... | collective-permute-start | bytes 393224 | tf_op jit(solution)/shard_map/ppermute | solution.py:376
  1009.1 49.0 %collective-permute-start.43 = (f32[16,2048]{1,0:T(8,128)S(1)}, f32[16,2048]{1,0:T(8,128)S(1)}, u32[]{:S(2)}, u32[]{:S(2)}) collective-permute-start(f32[16,2048]{1,0:T(8,128)S(1)} %get-tuple-element.1250), channel_id=1, source_target_pairs={{0,1},{1,0},{2,3},{3,2},{4,5},{5,4},{6,7},{7,6},{8,9},{9,8},{10,11... | collective-permute-start | bytes 393224 | tf_op jit(solution)/shard_map/ppermute | solution.py:376
  1010.6 47.4 %collective-permute-start.45 = (bf16[2,16,2304]{2,1,0:T(8,128)(2,1)S(1)}, bf16[2,16,2304]{2,1,0:T(8,128)(2,1)S(1)}, u32[]{:S(2)}, u32[]{:S(2)}) collective-permute-start(bf16[2,16,2304]{2,1,0:T(8,128)(2,1)S(1)} %fusion.228), channel_id=1, source_target_pairs={{0,8},{2,10},{4,12},{6,14},{8,0},{10,2},{12,4},{14,6},{16,24},{18,... | collective-permute-start | bytes 442376 | tf_op jit(solution)/shard_map/ppermute | solution.py:376
  1058.2 69.5 %all-to-all-start.12 = ((bf16[32,64,512]{2,1,0:T(8,128)(2,1)}), bf16[32,64,512]{2,1,0:T(8,128)(2,1)}, u32[]{:S(2)}, u32[]{:S(2)}) async-start(bf16[32,64,512]{2,1,0:T(8,128)(2,1)} %bitcast.753), calls=%async_computation.12 | async-start | bytes 4194304 | tf_op jit(solution)/shard_map/all_to_all | solution.py:416
  1063.6 50.9 %collective-permute-start.47 = (bf16[1,16,2304]{2,1,0:T(8,128)(2,1)S(1)}, bf16[1,16,2304]{2,1,0:T(8,128)(2,1)S(1)}, u32[]{:S(2)}, u32[]{:S(2)}) collective-permute-start(bf16[1,16,2304]{2,1,0:T(8,128)(2,1)S(1)} %dynamic-slice_convert_fusion.29), channel_id=1, source_target_pairs={{0,16},{2,18},{4,20},{6,22},{8,24},{10,26},{12,28},{14,30},{16,0},... | collective-permute-start | bytes 221192 | tf_op jit(solution)/shard_map/ppermute | solution.py:376
  1066.3 48.1 %collective-permute-start.46 = (f32[16,4096]{1,0:T(8,128)S(1)}, f32[16,4096]{1,0:T(8,128)S(1)}, u32[]{:S(2)}, u32[]{:S(2)}) collective-permute-start(f32[16,4096]{1,0:T(8,128)S(1)} %get-tuple-element.1248), channel_id=1, source_target_pairs={{0,1},{1,0},{2,3},{3,2},{4,5},{5,4},{6,7},{7,6},{8,9},{9,8},{10,11... | collective-permute-start | bytes 786440 | tf_op jit(solution)/shard_map/ppermute | solution.py:376
  (303 other events, 3325.2 us)
Sparse Core Ops, SparseCore 0:
  12.5 87.8 all-gather.7
  103.1 108.0 all-gather.5
  213.5 128.0 all-gather.3

commit v3 on v2

--- a/solution.py
+++ b/solution.py
@@ -23,7 +23,7 @@
 
 low_type = jnp.bfloat16
 f32 = jnp.float32
-query_block = 128
+query_block = 256
 key_block = 128
 place_block = 256
 vmem_bytes = 56 * 1024 * 1024
@@ -41,10 +41,6 @@
     centred = stream - average
     variance = jnp.mean(centred * centred, -1, keepdims=True)
     return centred * lax.rsqrt(variance + 1e-05) * norm_gain + norm_bias
-
-
-def norm_backward(stream, norm_gain, norm_bias, grad):
-    return jax.vjp(layer_norm, stream, norm_gain, norm_bias)[1](grad)
 
 
 def contract(left, right, left_dim, right_dim):
@@ -246,21 +242,88 @@
     )(bounds, queries, keys, keys, spans, lse, d_mixed)
 
 
-def each_chunk(chunks, visit):
-    def wide(chunk, carry):
-        visit(pl.multiple_of(chunk * place_block, place_block), place_block)
+def norm_back_kernel(stream_ref, gain_ref, grad_ref, rest_ref, out_ref, sums_ref):
+    @pl.when(pl.program_id(0) == 0)
+    def _():
+        sums_ref[...] = jnp.zeros_like(sums_ref)
+
+    stream, grad = stream_ref[...], grad_ref[...]
+    rows, width = stream.shape
+    average = jnp.mean(stream, -1, keepdims=True)
+    centred = stream - average
+    variance = jnp.mean(centred * centred, -1, keepdims=True)
+    inverse = lax.rsqrt(variance + 1e-05)
+    unit = centred * inverse
+    scaled = grad * gain_ref[...]
+    along = jnp.mean(scaled * unit, -1, keepdims=True)
+    level = jnp.mean(scaled, -1, keepdims=True)
+    out_ref[...] = rest_ref[...] + (scaled - level - unit * along) * inverse
+    sums_ref[0:8, :] += jnp.sum((grad * unit).reshape(rows // 8, 8, width), 0)
+    sums_ref[8:16, :] += jnp.sum(grad.reshape(rows // 8, 8, width), 0)
+
+
+def norm_backward(stream, gain, grad, rest):
+    places, width = stream.shape
+    rows = min(256, places)
+    block = pl.BlockSpec((rows, width), lambda i: (i, 0))
+    out, sums = pl.pallas_call(
+        norm_back_kernel,
+        grid=(places // rows,),
+        in_specs=[block, pl.BlockSpec((1, width), lambda i: (0, 0)), block, block],
+        out_specs=[block, pl.BlockSpec((16, width), lambda i: (0, 0))],
+        out_shape=[
+            jax.ShapeDtypeStruct((places, width), f32),
+            jax.ShapeDtypeStruct((16, width), f32),
+        ],
+        compiler_params=pltpu.CompilerParams(vmem_limit_bytes=vmem_bytes),
+        name="norm_backward",
+    )(stream, gain[None], grad, rest)
+    return out, jnp.sum(sums[:8], 0), jnp.sum(sums[8:], 0)
+
+
+def each_chunk(plan, visit):
+    wides = plan.shape[0] - 2
+
+    def wide(index, carry):
+        visit(pl.multiple_of(plan[2 + index], place_block // 2), place_block)
         return carry
 
-    lax.fori_loop(0, chunks[0], wide, 0)
-
-    @pl.when(chunks[1] > 0)
-    def _():
-        visit(pl.multiple_of(chunks[0] * place_block, place_block), place_block // 2)
-
-
-def head_stats_kernel(chunks, table_ref, rows_ref, stats_ref, tops, sums):
+    def narrow(index, carry):
+        visit(pl.multiple_of(plan[wides + 1 - index], place_block // 2), place_block // 2)
+        return carry
+
+    lax.fori_loop(0, plan[0], wide, 0)
+    lax.fori_loop(0, plan[1], narrow, 0)
+
+
+def chunk_plan(counts, span):
+    half = place_block // 2
+    left = counts % place_block
+    wides = counts // place_block + (left > half).astype(jnp.int32)
+    narrows = ((left > 0) & (left <= half)).astype(jnp.int32)
+    segments = counts.shape[0]
+    base = jnp.arange(segments) * span
+    index = jnp.arange(span // place_block)
+    used = (index[None, :] < wides[:, None]).reshape(-1)
+    begins = (base[:, None] + index[None, :] * place_block).reshape(-1)
+    total = used.shape[0] + segments
+    at = jnp.where(used, jnp.cumsum(used.astype(jnp.int32)) - 1, -1)
+    narrow_at = jnp.where(narrows > 0, total - jnp.cumsum(narrows), -1)
+    at = jnp.concatenate([at, narrow_at])
+    begins = jnp.concatenate([begins, base + wides * place_block])
+    listed = jnp.sum(jnp.where(at[None, :] == jnp.arange(total)[:, None], begins[None, :], 0), 1)
+    return jnp.concatenate([jnp.stack([jnp.sum(wides), jnp.sum(narrows)]), listed]).astype(jnp.int32)
+
+
+def parts_of(words):
+    for count in (5, 4, 2):
+        if words % (16 * count) == 0:
+            return [slice(i * (words // count), (i + 1) * (words // count)) for i in range(count)]
+    return [slice(0, words)]
+
+
+def head_stats_kernel(plan, table_ref, rows_ref, stats_ref, tops, sums):
     step = pl.program_id(0)
-    words = table_ref.shape[0]
 
     @pl.when(step == 0)
     def _():
@@ -269,14 +332,19 @@
 
     def visit(start, size):
         here = pl.ds(start, size)
-        logits = contract(table_ref[...], rows_ref[here, :], 1, 1).reshape(words // 8, 8, size)
-        old = tops[:, here]
-        top = jnp.maximum(old, jnp.max(logits, axis=0))
-        powers = jnp.sum(jnp.exp(logits - top[None]), axis=0)
-        sums[:, here] = sums[:, here] * jnp.exp(old - top) + powers
-        tops[:, here] = top
-
-    each_chunk(chunks, visit)
+        rows = rows_ref[here, :]
+        old, total = tops[:, here], sums[:, here]
+        for part in parts_of(table_ref.shape[0]):
+            logits = contract(table_ref[part, :], rows, 1, 1)
+            logits = logits.reshape(logits.shape[0] // 8, 8, size)
+            top = jnp.maximum(old, jnp.max(logits, axis=0))
+            powers = jnp.sum(jnp.exp(logits - top[None]), axis=0)
+            total = total * jnp.exp(old - top) + powers
+            old = top
+        sums[:, here] = total
+        tops[:, here] = old
+
+    each_chunk(plan, visit)
 
     @pl.when(step == pl.num_programs(0) - 1)
     def _():
@@ -286,33 +354,43 @@
 
 
 def head_back_kernel(
-    chunks, table_ref, rows_ref, target_ref, log_ref, weight_ref, dt_ref, dr_ref, pick_ref, turned
+    plan, table_ref, rows_ref, target_ref, log_ref, weight_ref, one_ref, two_ref, dr_ref, pick_ref
 ):
     step = pl.program_id(0)
-    words = table_ref.shape[0]
+    words, width = table_ref.shape
+    half = one_ref.shape[1]
 
     @pl.when(step == 0)
     def _():
         dr_ref[...] = jnp.zeros_like(dr_ref)
         pick_ref[...] = jnp.zeros_like(pick_ref)
 
-    dt_ref[...] = jnp.zeros_like(dt_ref)
-    turned[...] = table_ref[...].T
+    one_ref[...] = jnp.zeros_like(one_ref)
+    two_ref[...] = jnp.zeros_like(two_ref)
 
     def visit(start, size):
         here = pl.ds(start, size)
         rows = rows_ref[here, :]
-        inner = lax.broadcasted_iota(jnp.int32, (words, size), 0)
-        logits = contract(table_ref[...], rows, 1, 1)
-        scaled = jnp.exp(logits - log_ref[:, here])
-        hit = inner == target_ref[:, here] - step * words
-        picked = jnp.where(hit, logits, 0.0).reshape(words // 8, 8, size)
-        pick_ref[:, here] += jnp.sum(picked, axis=0)
-        d_logits = jnp.where(hit, scaled - weight_ref[:, here], scaled).astype(low_type)
-        dt_ref[...] += contract(d_logits, rows, 1, 0)
-        dr_ref[:, here] += contract(turned[...], d_logits, 1, 0)
-
-    each_chunk(chunks, visit)
+        target = target_ref[:, here] - step * words
+        log, weight = log_ref[:, here], weight_ref[:, here]
+        back = jnp.zeros((size, width), f32)
+        found = jnp.zeros((8, size), f32)
+        for part in parts_of(words):
+            block = table_ref[part, :]
+            count = block.shape[0]
+            inner = lax.broadcasted_iota(jnp.int32, (count, size), 0) + part.start
+            logits = contract(block, rows, 1, 1)
+            scaled = jnp.exp(logits - log)
+            hit = inner == target
+            found += jnp.sum(jnp.where(hit, logits, 0.0).reshape(count // 8, 8, size), axis=0)
+            d_logits = jnp.where(hit, scaled - weight, scaled).astype(low_type)
+            one_ref[part, :] += contract(d_logits, rows[:, :half], 1, 0)
+            two_ref[part, :] += contract(d_logits, rows[:, half:], 1, 0)
+            back += contract(d_logits, block, 0, 0)
+        pick_ref[:, here] += found
+        dr_ref[here, :] += back
+
+    each_chunk(plan, visit)
 
 
 def word_block(words):
@@ -326,7 +404,7 @@
     ]
 
 
-def head_stats(chunks, table_part, rows):
+def head_stats(plan, table_part, rows):
     words = word_block(table_part.shape[0])
     places, width = rows.shape
     return pl.pallas_call(
@@ -341,12 +419,13 @@
         out_shape=jax.ShapeDtypeStruct((2, places), f32),
         compiler_params=pltpu.CompilerParams(vmem_limit_bytes=vmem_bytes),
         name="head_stats",
-    )(chunks, table_part, rows)
-
-
-def head_back(chunks, table_part, rows, targets, logs, weights):
+    )(plan, table_part, rows)
+
+
+def head_back(plan, table_part, rows, targets, logs, weights):
     words = word_block(table_part.shape[0])
     places, width = rows.shape
+    half = width // 2
     return pl.pallas_call(
         head_back_kernel,
         grid_spec=pltpu.PrefetchScalarGridSpec(
@@ -355,20 +434,21 @@
             in_specs=head_specs(words, width, places)
             + [pl.BlockSpec((1, places), lambda i, *_: (0, 0)) for _ in range(3)],
             out_specs=[
-                pl.BlockSpec((words, width), lambda i, *_: (i, 0)),
-                pl.BlockSpec((width, places), lambda i, *_: (0, 0)),
+                pl.BlockSpec((words, half), lambda i, *_: (i, 0)),
+                pl.BlockSpec((words, half), lambda i, *_: (i, 0)),
+                pl.BlockSpec((places, width), lambda i, *_: (0, 0)),
                 pl.BlockSpec((8, places), lambda i, *_: (0, 0)),
             ],
-            scratch_shapes=[pltpu.VMEM((width, words), low_type)],
         ),
         out_shape=[
-            jax.ShapeDtypeStruct(table_part.shape, f32),
-            jax.ShapeDtypeStruct((width, places), f32),
+            jax.ShapeDtypeStruct((table_part.shape[0], half), f32),
+            jax.ShapeDtypeStruct((table_part.shape[0], half), f32),
+            jax.ShapeDtypeStruct((places, width), f32),
             jax.ShapeDtypeStruct((8, places), f32),
         ],
         compiler_params=pltpu.CompilerParams(vmem_limit_bytes=vmem_bytes),
         name="head_back",
-    )(chunks, table_part, rows, targets, logs, weights)
+    )(plan, table_part, rows, targets, logs, weights)
 
 
 def swap(values, axis, bit):
@@ -431,7 +511,7 @@
         )
         self.fast = self.fast and all(part.shape[2] % 128 == 0 for part in parts)
         self.fast = self.fast and self.rows % 8 == 0
-        self.pending, self.value, self.square = None, None, None
+        self.pending, self.value, self.square, self.got = None, None, None, None
         if self.fast:
             self.launch()
 
@@ -445,10 +525,20 @@
         rows = self.rows // 2 if axis == "seq" else self.rows
         index = lax.axis_index(axis)
         mine = (index // bit) & 1
-        halves = [part.reshape((-1, 2, rows, part.shape[2])) for part in self.parts]
-        away = [pick(half, 1, 1 - mine).astype(low_type) for half in halves]
-        self.parts = [pick(half, 1, mine) for half in halves]
-        self.rows = rows
+
+        def half(side):
+            halves = [
+                pick(part.reshape((-1, 2, rows, part.shape[2])), 1, side) for part in self.parts
+            ]
+            if self.got is not None:
+                halves[0] = halves[0] + pick(
+                    self.got.reshape((-1, 2, rows, self.got.shape[2])), 1, side
+                ).astype(f32)
+            return halves
+
+        away = [part.astype(low_type) for part in half(1 - mine)]
+        self.parts = [jnp.concatenate(half(mine), 2)]
+        self.rows, self.got = rows, None
         self.pending = swap(jnp.concatenate(away, 2), axis, bit)
 
     def absorb(self, got):
@@ -461,12 +551,13 @@
             )
             return
         self.steps.pop(0)
-        self.parts = [jnp.concatenate(self.parts, 2) + got.astype(f32)]
+        self.got = got
         if not self.steps:
-            self.parts = [self.parts[0].reshape(self.rows, -1)]
-            self.square = jnp.sum(self.parts[0] * self.parts[0])
+            part = (self.parts[0] + got.astype(f32)).reshape(self.rows, -1)
+            self.parts = [part]
+            self.square = jnp.sum(part * part)
             if not self.joint:
-                self.value = self.parts[0]
+                self.value = part
 
     def finish(self):
         if self.fast:
@@ -565,7 +656,12 @@
 
     def gather_columns(parts):
         joined = jnp.concatenate([part.astype(low_type) for part in parts], 1)
-        whole = lax.all_gather(joined, "dp", axis=0, tiled=True)
+        if joined.shape[0] % (16 * seqs) == 0:
+            rows = joined.shape[0] // seqs
+            joined = lax.dynamic_slice_in_dim(joined, side * rows, rows, 0)
+            whole = lax.all_gather(joined, ("dp", "seq"), axis=0, tiled=True)
+        else:
+            whole = lax.all_gather(joined, "dp", axis=0, tiled=True)
         result, at = [], 0
         for part in parts:
             result.append(whole[:, at : at + part.shape[1]])
@@ -603,10 +699,12 @@
     dec_in = pick(jnp.where(masked, mask_token, labels), 0, side)
     counts = jnp.sum(masked.astype(jnp.int32), -1)
 
-    slots = -(-(2 * span // devices) // 16) * 16
-    slots = max(slots, 16)
-
-    def ask(token_ids):
+    def slots_for(expected):
+        return max(-(-expected // 16) * 16, 16)
+
+    src_slots, dec_slots = slots_for(2 * span // devices), slots_for(3 * span // (2 * devices))
+
+    def ask(token_ids, slots):
         same = token_ids[:, None] == token_ids[None, :]
         index = jnp.arange(span)
         earlier = index[None, :] < index[:, None]
@@ -616,79 +714,72 @@
             (earlier & leader[None, :] & (holder[:, None] == holder[None, :])).astype(jnp.int32), 1
         )
         rank = jnp.sum(jnp.where(same & leader[None, :], rank[None, :], 0), 1)
-        return token_ids % own_words, holder, rank, jnp.max(rank) // slots + 1
+        return token_ids % own_words, holder, rank, slots
+
+    def chosen_of(asked, turn):
+        local, holder, rank, slots = asked
+        code = jnp.where(rank // slots == turn, holder * slots + rank % slots, -1)
+        return code[:, None] == jnp.arange(devices * slots)[None, :]
+
+    def wanted_of(asked, chosen):
+        return jnp.max(jnp.where(chosen, asked[0][:, None], -1), 0).reshape(devices, -1)
+
+    def maps_of(chosen, wanted):
+        held = wanted.reshape(-1)[:, None] == jnp.arange(own_words)[None, :]
+        return chosen.astype(low_type), held.astype(low_type)
 
     def round_of(asked, turn):
-        local, holder, rank, _ = asked
-        code = jnp.where(rank // slots == turn, holder * slots + rank % slots, -1)
-        chosen = code[:, None] == jnp.arange(devices * slots)[None, :]
-        wanted = jnp.max(jnp.where(chosen, local[:, None], -1), 0)
-        wanted = to_each(wanted.reshape(devices, slots)).reshape(-1)
-        held = wanted[:, None] == jnp.arange(own_words)[None, :]
-        return chosen.astype(low_type), held.astype(low_type)
+        chosen = chosen_of(asked, turn)
+        return maps_of(chosen, to_each(wanted_of(asked, chosen)))
 
     def fetch(maps):
         chosen, held = maps
         found = contract(held, table_low, 1, 0).astype(low_type)
-        found = to_each(found.reshape(devices, slots, width)).reshape(-1, width)
+        found = to_each(found.reshape(devices, -1, width)).reshape(-1, width)
         return contract(chosen, found, 1, 0)
 
     def give(maps, grads):
         chosen, held = maps
         sums = contract(chosen, grads.astype(low_type), 0, 0).astype(low_type)
-        sums = to_each(sums.reshape(devices, slots, width)).reshape(-1, width)
+        sums = to_each(sums.reshape(devices, -1, width)).reshape(-1, width)
         return contract(held, sums, 0, 0)
 
-    def later_rounds(asked, rounds, value, visit):
-        def body(turn, carry):
-            return carry + visit(round_of(asked, turn))
-
-        return lax.fori_loop(1, rounds, body, value)
-
-    src_ask, dec_ask = ask(src_in), ask(dec_in)
-    local_facts = [
-        jnp.sum(tgt_mask),
-        jnp.max(counts),
-        src_ask[3],
-        dec_ask[3],
-    ]
-
-    def combine(first, second):
-        added = jnp.arange(len(local_facts))[None, :] == 0
-        return jnp.where(added, first + second, jnp.maximum(first, second))
-
-    def reduce(values, axis):
-        return jnp.concatenate([lax.psum(values[:, :1], axis), lax.pmax(values[:, 1:], axis)], 1)
-
-    facts = everywhere(jnp.stack(local_facts).astype(jnp.int32).reshape(1, -1), combine, reduce)[0]
-    count = facts[0].astype(f32)
+    def later_rounds(rounds, value, visit):
+        return lax.fori_loop(1, rounds, lambda turn, carry: carry + visit(turn), value)
+
+    src_ask, dec_ask = ask(src_in, src_slots), ask(dec_in, dec_slots)
+    src_chosen, dec_chosen = chosen_of(src_ask, 0), chosen_of(dec_ask, 0)
+    facts = jnp.stack(
+        [
+            jnp.sum(tgt_mask),
+            jnp.max(counts),
+            jnp.max(src_ask[2]) // src_slots + 1,
+            jnp.max(dec_ask[2]) // dec_slots + 1,
+        ]
+    )
+    facts = jnp.broadcast_to(jnp.pad(facts, (0, 12))[None, :], (devices, 16))
+    asked = [wanted_of(src_ask, src_chosen), wanted_of(dec_ask, dec_chosen), facts]
+    asked = to_each(jnp.concatenate(asked, 1).astype(jnp.int32))
+    facts = asked[:, src_slots + dec_slots :]
+    count = jnp.sum(facts[:, 0]).astype(f32)
     cut = -(-(span * 3 // 8) // 128) * 128
-    more = facts[1] > cut
-    src_maps = round_of(src_ask, 0)
+    more = jnp.max(facts[:, 1]) > cut
+    src_rounds, dec_rounds = jnp.max(facts[:, 2]), jnp.max(facts[:, 3])
+    src_maps = maps_of(src_chosen, asked[:, :src_slots])
     src_found = fetch(src_maps)
-    dec_maps = round_of(dec_ask, 0)
+    dec_maps = maps_of(dec_chosen, asked[:, src_slots : src_slots + dec_slots])
     dec_found = fetch(dec_maps)
 
-    starts_at = jnp.cumsum(counts) - counts
-    total = jnp.sum(counts)
-    rank = jnp.cumsum(masked.astype(jnp.int32), -1) - 1
-    slot_of = jnp.where(masked, rank + starts_at[:, None], -1)
-    slot_index = jnp.arange(seqs * span)
-    slot_label = jnp.sum(
-        jnp.where(slot_of.reshape(1, -1) == slot_index[:, None], labels.reshape(1, -1), 0), -1
-    )
-    valid = slot_index < total
+    order = jnp.stack([side, 1 - side]) if seqs == 2 else jnp.arange(seqs)
+    masked, labels, counts = masked[order], labels[order], counts[order]
+    rank = jnp.where(masked, jnp.cumsum(masked.astype(jnp.int32), -1) - 1, -1)
+    chosen = rank[:, None, :] == jnp.arange(span)[None, :, None]
+    slot_label = jnp.sum(jnp.where(chosen, labels[:, None, :], 0), -1).reshape(-1)
+    valid = (jnp.arange(span)[None, :] < counts[:, None]).reshape(-1)
     targets = jnp.where(valid, slot_label - vocab_base, -1).reshape(1, -1)
-    left = total % place_block
-    chunks = jnp.stack(
-        [
-            total // place_block + (left > place_block // 2).astype(jnp.int32),
-            ((left > 0) & (left <= place_block // 2)).astype(jnp.int32),
-        ]
-    )
-    own_rank = pick(jnp.where(masked, rank, -1), 0, side)
-    own_chosen = (own_rank[None, :] == jnp.arange(span)[:, None]).astype(low_type)
-    own_slots = (pick(slot_of, 0, side)[:, None] == slot_index[None, :]).astype(low_type)
+    plan = chunk_plan(counts, span)
+    own_segment = 0 if seqs == 2 else side
+    own_chosen = pick(chosen, 0, own_segment).astype(low_type)
 
     own_places = offset + jnp.arange(span)
     src_start, src_length = pick(src_starts, 0, row), pick(src_lengths, 0, row)
@@ -704,8 +795,8 @@
     )
 
     root = math.sqrt(width)
-    src_found = later_rounds(src_ask, facts[2], src_found, fetch)
-    dec_found = later_rounds(dec_ask, facts[3], dec_found, fetch)
+    src_found = later_rounds(src_rounds, src_found, lambda turn: fetch(round_of(src_ask, turn)))
+    dec_found = later_rounds(dec_rounds, dec_found, lambda turn: fetch(round_of(dec_ask, turn)))
     stream0 = src_found * root + src_wave
     target0 = dec_found * root + tgt_wave
 
@@ -793,43 +884,45 @@
 
     packed = contract(own_chosen, final, 1, 0).astype(low_type)
     if seqs == 2:
-        other = swap_rows(packed, cut, more)
-        packs = [jnp.where(side == 0, packed, other), jnp.where(side == 0, other, packed)]
+        pieces = jnp.concatenate([packed, swap_rows(packed, cut, more)], 0)
     else:
-        packs = lax.all_gather(packed, "seq", axis=0)
-        packs = [packs[s] for s in range(seqs)]
-    rows = jnp.zeros((seqs * span, width), low_type)
-    pieces = sum(
-        lax.dynamic_update_slice_in_dim(rows, packs[s], starts_at[s], 0) for s in range(seqs)
-    )
-    every = gather_seq(head_stats(chunks, table_part, pieces), 0)
+        pieces = lax.all_gather(packed, "seq", axis=0, tiled=True)
+    stats = head_stats(plan, table_part, pieces)
+    if seqs == 2:
+        every = jnp.stack([stats, jnp.roll(swap(stats, "seq", 1), span, 1)])
+    else:
+        every = lax.all_gather(stats, "seq", axis=0)
     top_logit = jnp.max(every[:, 0], 0)
     totals = jnp.sum(every[:, 1] * jnp.exp(every[:, 0] - top_logit[None]), 0)
     log_total = top_logit + jnp.log(jnp.where(valid, totals, 1.0))
-    own_start = pick(starts_at, 0, side)
-    mine = (slot_index >= own_start) & (slot_index < own_start + pick(counts, 0, side))
-    token_local = jnp.sum(jnp.where(mine, log_total, 0.0))
+    own_logs = pick(jnp.where(valid, log_total, 0.0).reshape(seqs, span), 0, own_segment)
     logs = jnp.where(valid, log_total + jnp.log(count), 1e30)
     weights = jnp.where(valid, 1.0 / count, 0.0)
-    d_table, d_pieces, picks = head_back(
-        chunks, table_part, pieces, targets, logs[None], weights[None]
-    )
-    token_local = token_local - jnp.sum(picks)
-    owned_table = d_table.reshape(owners, own_words, width)
-    half = width // 2
-    table_one = Halving([owned_table[:, :, :half]], False)
-    if seqs != 2:
+    d_one, d_two, d_pieces, picks = head_back(
+        plan, table_part, pieces, targets, logs[None], weights[None]
+    )
+    token_local = jnp.sum(own_logs) - jnp.sum(picks)
+    table_one = Halving([d_one.reshape(owners, own_words, -1)], False)
+
+    def to_places(first, last):
+        own = lax.dynamic_slice_in_dim(d_pieces, own_segment * span + first, last - first, 0)
+        if seqs == 2:
+            away = d_pieces[span + first : span + last].astype(low_type)
+            own = own + swap(away, "seq", 1).astype(f32)
+        high = lax.reduce_precision(own, 8, 7)
+        rest = (own - high).astype(low_type)
+        chosen_here = own_chosen[first:last]
+        return contract(chosen_here, high.astype(low_type), 0, 0) + contract(chosen_here, rest, 0, 0)
+
+    if seqs == 2:
+        d_final = to_places(0, cut)
+        if cut < span:
+            d_final = lax.cond(
+                more, lambda part: part + to_places(cut, span), lambda part: part, d_final
+            )
+    else:
         d_pieces = lax.psum(d_pieces, "seq")
-    d_high = lax.reduce_precision(d_pieces, 8, 7)
-    d_rest = (d_pieces - d_high).astype(low_type)
-    d_high = d_high.astype(low_type)
-    d_final = contract(own_slots, d_high, 1, 1) + contract(own_slots, d_rest, 1, 1)
-    if seqs == 2:
-        away_start, away_count = pick(starts_at, 0, 1 - side), pick(counts, 0, 1 - side)
-        index = jnp.arange(span)[:, None]
-        away = (slot_index[None, :] == index + away_start) & (index < away_count)
-        away = contract(away.astype(low_type), d_high, 1, 1).astype(low_type)
-        d_final = d_final + contract(own_chosen, swap_rows(away, cut, more), 0, 0)
+        d_final = to_places(0, span)
 
     first_place = own_places[None, :] == src_start[:, None]
     mine = jnp.any(first_place, -1)
@@ -861,52 +954,50 @@
         whole = owned(grad)
         return [whole[:, at : at + share] for at in range(0, whole.shape[1], share)]
 
-    d_target3, gain6, bias6 = norm_backward(target3, gains[6], biases[6], d_final)
+    none = jnp.zeros_like(stream0)
+    d_target3, gain6, bias6 = norm_backward(target3, gains[6], d_final, none)
     d_inner5, d_fin1, d_fout1 = ffn_back(inner5, f_in1, f_out1, keep5, d_target3)
     chains = [table_one]
-    (d_inner5, d_target3, owned_table) = advance((d_inner5, d_target3, owned_table), chains)
-    table_two = Halving([owned_table[:, :, half:]], False)
+    (d_inner5, d_target3, d_two) = advance((d_inner5, d_target3, d_two), chains)
+    table_two = Halving([d_two.reshape(owners, own_words, -1)], False)
     chain_a = Halving([owned(d_fin1)] + owned_columns(d_fout1), True)
-    d_target2, gain5, bias5 = norm_backward(target2, gains[5], biases[5], d_inner5)
-    d_target2 = d_target2 + d_target3
+    d_target2, gain5, bias5 = norm_backward(target2, gains[5], d_inner5, d_target3)
     d_inner4, d_cross, d_win2, d_wout2 = cross_attention_back(
         inner4, memory, w_in2, w_out2, cross_spans, keep4, d_target2
     )
     chains += [table_two, chain_a]
     d_inner4, d_target2, d_cross = advance((d_inner4, d_target2, d_cross), chains)
     chain_b = Halving([owned(d_win2), owned(d_wout2)], True)
-    d_target1, gain4, bias4 = norm_backward(target1, gains[4], biases[4], d_inner4)
-    d_target1 = d_target1 + d_target2
+    d_target1, gain4, bias4 = norm_backward(target1, gains[4], d_inner4, d_target2)
     d_inner3, d_win1, d_wout1 = self_attention_back(
         inner3, w_in1, w_out1, self_spans, keep3, d_target1
     )
     chains += [chain_b]
     d_inner3, d_target1 = advance((d_inner3, d_target1), chains)
     chain_c = Halving([owned(d_win1), owned(d_wout1)], True)
-    d_target0, gain3, bias3 = norm_backward(target0, gains[3], biases[3], d_inner3)
-    d_target0 = d_target0 + d_target1
+    d_target0, gain3, bias3 = norm_backward(target0, gains[3], d_inner3, d_target1)
     dec_grad = d_target0 * root
     dec_given = give(dec_maps, dec_grad)
-    d_stream2, gain2, bias2 = norm_backward(stream2, gains[2], biases[2], d_memory + d_cross)
+    d_stream2, gain2, bias2 = norm_backward(stream2, gains[2], d_memory + d_cross, none)
     d_inner1, d_fin0, d_fout0 = ffn_back(inner1, f_in0, f_out0, keep1, d_stream2)
     chains += [chain_c]
     d_inner1, d_stream2 = advance((d_inner1, d_stream2), chains)
     chain_d = Halving([owned(d_fin0)] + owned_columns(d_fout0), True)
-    d_stream1, gain1, bias1 = norm_backward(stream1, gains[1], biases[1], d_inner1)
-    d_stream1 = d_stream1 + d_stream2
+    d_stream1, gain1, bias1 = norm_backward(stream1, gains[1], d_inner1, d_stream2)
     d_inner0, d_win0, d_wout0 = self_attention_back(
         inner0, w_in0, w_out0, enc_spans, keep0, d_stream1
     )
     chains += [chain_d]
-    d_inner0, d_stream1 = advance((d_inner0, d_stream1), chains)
-    d_stream0, gain0, bias0 = norm_backward(stream0, gains[0], biases[0], d_inner0)
-    d_stream0 = d_stream0 + d_stream1
+    d_inner0, d_stream1, dec_given = advance((d_inner0, d_stream1, dec_given), chains)
+    d_stream0, gain0, bias0 = norm_backward(stream0, gains[0], d_inner0, d_stream1)
     src_grad = d_stream0 * root
     src_given = give(src_maps, src_grad)
     norm_grads = [gain0, gain1, gain2, gain3, gain4, gain5, gain6]
     norm_grads += [bias0, bias1, bias2, bias3, bias4, bias5, bias6]
-    g_norms = everywhere(jnp.stack(norm_grads), jnp.add, lax.psum)
-    norm_square = jnp.where((side == 0) & (lax.axis_index("dp") == 0), jnp.sum(g_norms * g_norms), 0.0)
+    g_norms = jnp.sum(lax.all_gather(jnp.stack(norm_grads), ("dp", "seq"), axis=0), 0)
+    norm_square = jnp.where(
+        (side == 0) & (lax.axis_index("dp") == 0), jnp.sum(g_norms * g_norms), 0.0
+    )
     norm_share = norms.shape[2]
     g_norms = lax.dynamic_slice_in_dim(g_norms, lax.axis_index("dp") * norm_share, norm_share, 1)
     chain_e = Halving([owned(d_win0), owned(d_wout0), owned(d_w_len)], True)
@@ -917,8 +1008,12 @@
         chain.finish()
 
     given = dec_given + src_given
-    given = later_rounds(dec_ask, facts[3], given, lambda maps: give(maps, dec_grad))
-    given = later_rounds(src_ask, facts[2], given, lambda maps: give(maps, src_grad))
+    given = later_rounds(
+        jnp.maximum(src_rounds, dec_rounds),
+        given,
+        lambda turn: give(round_of(dec_ask, turn), dec_grad)
+        + give(round_of(src_ask, turn), src_grad),
+    )
     table_grad = jnp.concatenate(
         [table_one.value.reshape(own_words, -1), table_two.value.reshape(own_words, -1)], 1
     )

time: 1200 us -> 1190 us (level)
  blocking collectives: 0 us -> 85.6 us
  local copies, waits for them, and re-layouts: 169 us -> 107 us
  waiting for transfers between devices: 278 us -> 253 us
  other arithmetic: 191 us -> 169 us
  Pallas kernels: 242 us -> 259 us
    ppermute x57 -> x47, waiting for transfers between devices: 219 us -> 110 us  [swap(): return lax.ppermute(values, axis, [(i, i ^ bit) for i in range(size)])]
    all_gather x0 -> x1, blocking collectives: none -> 85.6 us  [on_device(): lax.all_gather(jnp.stack(norm_grads), ('dp', 'seq'), axis=0)]
    all_to_all x6 -> x5, waiting for transfers between devices: 58.1 us -> 131 us  [to_each(): return lax.all_to_all(values, ('seq', 'dp'), 0, 0)]
    pallas_call x0 -> x7, Pallas kernels: none -> 37.7 us  [norm_backward(): pl.pallas_call(norm_back_kernel, grid=(places // rows,), in_specs=[block,...]
    add x30 -> x20, other arithmetic: 58.5 us -> 38.1 us  [the longest x16 34.5 us: half(): halves[0]]
    convert_element_type x37 -> x10, local copies, waits for them, and re-layouts: 33.9 us -> 14.2 us  [the longest x9 14.2 us: launch(): away = [part.astype(low_type) for part in half(1 - mine)]]
    optimization_barrier x6 -> x0, local copies, waits for them, and re-layouts: 18.3 us -> none  [advance(): lax.optimization_barrier((main, [chain.pending for chain in live]))]
    convert_element_type x1 -> x16, other arithmetic: 0.01 us -> 17.3 us  [the longest x14 17.2 us: launch(): away = [part.astype(low_type) for part in half(1 - mine)]]
  transfers between devices with their start and end apart: 66 -> 55, of which waited for: 30 -> 20; matrix products, arithmetic and copies ran while one was open for 38% -> 33% of each run, Pallas kernels for 11% -> 13%
where the time goes in v3:
time: 1190 us; the launch traced here: 1170 us
  Pallas kernels  259 us (22%)
  waiting for transfers between devices  253 us (21%)
  matrix products  179 us (15%)
  other arithmetic  169 us (14%)
  local copies, waits for them, and re-layouts  107 us (9%)
  blocking collectives  85.6 us (7%)
  starting transfers between devices  84.4 us (7%)
  between operations  33.2 us (3%)
    dot_general x48, matrix products, contract(): lax.dot_general(left, right, (((left_dim,), (right_dim,)), ((), ())), pre...  176 us
    all_to_all x5, waiting for transfers between devices, to_each(): return lax.all_to_all(values, ('seq', 'dp'), 0, 0)  131 us
    ppermute x47, waiting for transfers between devices, swap(): return lax.ppermute(values, axis, [(i, i ^ bit) for i in range(size)])  110 us
    all_gather x1, blocking collectives, on_device(): lax.all_gather(jnp.stack(norm_grads), ('dp', 'seq'), axis=0)  85.6 us
    pallas_call x1, Pallas kernels, head_back(): pl.pallas_call(head_back_kernel, grid_spec=pltpu.PrefetchScalarGridSpec(n...  82.4 us
    pallas_call x3, Pallas kernels, attend_backward(): pl.pallas_call(functools.partial(attend_backward_kernel, head=width // HE...  72.4 us
    ppermute x47, starting transfers between devices, swap(): return lax.ppermute(values, axis, [(i, i ^ bit) for i in range(size)])  64.6 us
    unnamed x413, local copies, waits for them, and re-layouts  49.8 us
  transfers between devices with their start and end apart: 55, of which 20 were waited for; matrix products, arithmetic and copies ran while one was open for 33% of the time, Pallas kernels for 13%

profile of v3, /device:TPU:0, one launch (start us, length us, event | category | flops | bytes accessed | tf_op | source)
XLA Modules:
  0.0 1172.0 jit_solution(17560338977172153815)
XLA Ops:
  26.7 7.3 multiply_sine_fusion
  59.6 6.2 all-to-all-done.8
  84.1 38.7 %all-to-all-done.9 = bf16[32,48,512]{2,1,0:T(8,128)(2,1)S(1)} async-done(((bf16[32,48,512]{2,1,0:T(8,128)(2,1)}), bf16[32,48,512]{2,1,0:T(8,128)(2,1)S(1)}, u32[]{:S(2)}, u32[]{:S(2)}) %all-to-all-start.9) | async-done | bytes 1572896 | tf_op jit(solution)/shard_map/all_to_all | solution.py:496
  146.6 61.1 %all-to-all-done.10 = bf16[32,64,512]{2,1,0:T(8,128)(2,1)} async-done(((bf16[32,64,512]{2,1,0:T(8,128)(2,1)}), bf16[32,64,512]{2,1,0:T(8,128)(2,1)}, u32[]{:S(2)}, u32[]{:S(2)}) %all-to-all-start.10) | async-done | bytes 2097184 | tf_op jit(solution)/shard_map/all_to_all | solution.py:496
  223.8 13.6 %attend_forward.4 = (bf16[512,1024]{1,0:T(8,128)(2,1)}, f32[8,1024]{1,0:T(8,128)}) custom-call(s32[2,4]{1,0:T(2,128)} %pad_add_fusion.7.bounds, bf16[1536,1024]{1,0:T(8,128)(2,1)} %convolution_convert_fusion.q_ref.k_ref.v_ref, bf16[1536,1024]{1,0:T(8,128)(2,1)} %convolution_convert_fusion.q_ref.k_ref.v_ref, ...), custom_call_target="tpu_custom_call" | custom-call | tf_op jit(solution)/shard_map/attend_forward/pallas_call | solution.py:191
  263.3 13.5 %attend_forward.3 = (bf16[512,1024]{1,0:T(8,128)(2,1)}, f32[8,1024]{1,0:T(8,128)}) custom-call(s32[2,4]{1,0:T(2,128)} %pad_add_fusion.5.bounds, bf16[1536,1024]{1,0:T(8,128)(2,1)} %convolution_convert_fusion.1.q_ref.k_ref.v_ref, bf16[1536,1024]{1,0:T(8,128)(2,1)} %convolution_convert_fusion.1.q_ref.k_ref.v_ref, ...), custom_call_target="tpu_custom_call" | custom-call | tf_op jit(solution)/shard_map/attend_forward/pallas_call | solution.py:191
  286.9 13.1 %attend_forward.5 = (bf16[512,1024]{1,0:T(8,128)(2,1)}, f32[8,1024]{1,0:T(8,128)}) custom-call(s32[2,4]{1,0:T(2,128)} %pad_add_fusion.6.bounds, bf16[512,1024]{1,0:T(8,128)(2,1)} %convolution_convert_fusion.7.q_ref, bf16[1024,1024]{1,0:T(8,128)(2,1)} %convolution_convert_fusion.2.k_ref.v_ref, bf16[1024,1024]{1,0:T(8,128)(2,1)} %convolution_convert_fusion.2.k_ref.v_ref, ...), custom_call_target="tpu_custom_call" | custom-call | tf_op jit(solution)/shard_map/attend_forward/pallas_call | solution.py:191
  329.0 12.5 %all-gather.6.cloned.1.call-done.table_ref = bf16[16000,512]{1,0:T(8,128)(2,1)} async-done(((bf16[1000,512]{1,0:T(8,128)(2,1)}), bf16[16000,512]{1,0:T(8,128)(2,1)}) %all-gather.6.cloned.1.call-update) | async-done | bytes 16384016 | tf_op jit(solution)/shard_map/all_gather | solution.py:687
  341.6 26.1 %head_stats.1 = f32[2,2048]{1,0:T(2,128)} custom-call(s32[12]{0:T(128)} %pad_add_fusion.10.plan, bf16[16000,512]{1,0:T(8,128)(2,1)} %all-gather.6.cloned.1.call-done.table_ref, bf16[2048,512]{1,0:T(8,128)(2,1)} %pad_maximum_fusion.6.rows_ref), custom_call_target="tpu_custom_call" | custom-call | tf_op jit(solution)/shard_map/head_stats/pallas_call | solution.py:410
  374.3 82.4 %head_back.1 = (f32[16000,256]{1,0:T(8,128)}, f32[16000,256]{1,0:T(8,128)}, f32[2048,512]{1,0:T(8,128)S(1)}, f32[8,2048]{1,0:T(8,128)}) custom-call(s32[12]{0:T(128)} %pad_add_fusion.10.plan, bf16[16000,512]{1,0:T(8,128)(2,1)} %all-gather.6.cloned.1.call-done.table_ref, bf16[2048,512]{1,0:T(8,128)(2,1)} %pad_maximum_fusion.6.rows_ref, ...), custom_call_target="tpu_custom_call" | custom-call | tf_op jit(solution)/shard_map/head_back/pallas_call | solution.py:429
  461.1 5.8 fusion.80
  470.9 7.1 constant_dynamic-slice_fusion.16
  491.1 9.7 fusion.61
  505.5 6.1 fusion.165
  521.1 5.9 fusion.94.grad_ref
  526.9 5.7 fusion.81
  533.2 6.0 convert_add_fusion.2
  539.2 29.5 %collective-permute-start.7 = (bf16[4,1000,256]{2,1,0:T(8,128)(2,1)}, bf16[4,1000,256]{2,1,0:T(8,128)(2,1)}, u32[]{:S(2)}, u32[]{:S(2)}) collective-permute-start(bf16[4,1000,256]{2,1,0:T(8,128)(2,1)} %get-tuple-element.1066), channel_id=1, source_target_pairs={{0,4},{2,6},{4,0},{6,2},{8,12},{10,14},{12,8},{14,10},{16,20},{18,... | collective-permute-start | bytes 6144008 | tf_op jit(solution)/shard_map/ppermute | solution.py:456
  577.6 24.2 %attend_backward.3 = (bf16[512,1024]{1,0:T(8,128)(2,1)}, bf16[1024,1024]{1,0:T(8,128)(2,1)}) custom-call(s32[2,4]{1,0:T(2,128)} %pad_add_fusion.6.bounds, bf16[512,1024]{1,0:T(8,128)(2,1)} %convolution_convert_fusion.7.q_ref, bf16[1024,1024]{1,0:T(8,128)(2,1)} %convolution_convert_fusion.2.k_ref.v_ref, ...), custom_call_target="tpu_custom_call" | custom-call | tf_op jit(solution)/shard_map/attend_backward/pallas_call | solution.py:216
  638.9 10.3 fusion.54
  649.4 10.7 fusion.156
  669.1 24.3 %attend_backward.4 = (bf16[512,1024]{1,0:T(8,128)(2,1)}, bf16[1024,1024]{1,0:T(8,128)(2,1)}) custom-call(s32[2,4]{1,0:T(2,128)} %pad_add_fusion.5.bounds, bf16[1536,1024]{1,0:T(8,128)(2,1)} %convolution_convert_fusion.1.q_ref.k_ref.v_ref, bf16[1536,1024]{1,0:T(8,128)(2,1)} %convolution_convert_fusion.1.q_ref.k_ref.v_ref, ...), custom_call_target="tpu_custom_call" | custom-call | tf_op jit(solution)/shard_map/attend_backward/pallas_call | solution.py:216
  734.6 13.2 %collective-permute-done.11 = bf16[4,1000,256]{2,1,0:T(8,128)(2,1)S(1)} collective-permute-done((bf16[4,1000,256]{2,1,0:T(8,128)(2,1)S(1)}, bf16[4,1000,256]{2,1,0:T(8,128)(2,1)S(1)}, u32[]{:S(2)}, u32[]{:S(2)}) %collective-permute-start.11) | collective-permute-done | bytes 2048032 | tf_op jit(solution)/shard_map/ppermute | solution.py:456
  756.8 5.6 norm_backward.12
  770.1 19.9 %collective-permute-done.14 = bf16[1,1000,256]{2,1,0:T(8,128)(2,1)} collective-permute-done((bf16[1,1000,256]{2,1,0:T(8,128)(2,1)S(1)}, bf16[1,1000,256]{2,1,0:T(8,128)(2,1)}, u32[]{:S(2)}, u32[]{:S(2)}) %collective-permute-start.14) | collective-permute-done | bytes 512032 | tf_op jit(solution)/shard_map/ppermute | solution.py:456
  801.9 23.9 %attend_backward.5 = (bf16[512,1024]{1,0:T(8,128)(2,1)}, bf16[1024,1024]{1,0:T(8,128)(2,1)}) custom-call(s32[2,4]{1,0:T(2,128)} %pad_add_fusion.7.bounds, bf16[1536,1024]{1,0:T(8,128)(2,1)} %convolution_convert_fusion.q_ref.k_ref.v_ref, bf16[1536,1024]{1,0:T(8,128)(2,1)} %convolution_convert_fusion.q_ref.k_ref.v_ref, ...), custom_call_target="tpu_custom_call" | custom-call | tf_op jit(solution)/shard_map/attend_backward/pallas_call | solution.py:216
  861.7 24.6 %all-to-all-done.11 = bf16[32,48,512]{2,1,0:T(8,128)(2,1)} async-done(((bf16[32,48,512]{2,1,0:T(8,128)(2,1)}), bf16[32,48,512]{2,1,0:T(8,128)(2,1)}, u32[]{:S(2)}, u32[]{:S(2)}) %all-to-all-start.11) | async-done | bytes 1572896 | tf_op jit(solution)/shard_map/all_to_all | solution.py:496
  904.7 5.4 norm_backward.13
  913.0 85.6 %all-gather.1 = f32[32,14,512]{2,1,0:T(8,128)} all-gather(f32[1,14,512]{2,1,0:T(8,128)S(1)} %bitcast.867), channel_id=2, replica_groups=mesh['dp'=16,'seq'=2] {'dp','seq'}, dimensions={0}, use_global_device_ids=true | all-gather | bytes 946176 | tf_op jit(solution)/shard_map/all_gather | solution.py:997
  1024.6 5.6 collective-permute-done.33
  1064.3 43.3 %collective-permute-done.42 = bf16[1,16,2304]{2,1,0:T(8,128)(2,1)S(1)} collective-permute-done((bf16[1,16,2304]{2,1,0:T(8,128)(2,1)S(1)}, bf16[1,16,2304]{2,1,0:T(8,128)(2,1)S(1)}, u32[]{:S(2)}, u32[]{:S(2)}) %collective-permute-start.42) | collective-permute-done | bytes 73760 | tf_op jit(solution)/shard_map/ppermute | solution.py:456
  1148.7 7.2 multiply_subtract_fusion
  (853 shorter events, 485.4 us)
Async XLA Ops:
  7.2 209.9 %all-gather.10.cloned.1.call-start = ((), (), s32[]{:S(2)}) async-start(), calls=%async_computation.15 | async-start | bytes 6893568 | tf_op jit(solution)/shard_map/all_gather | solution.py:662
  18.6 239.4 %all-gather.8.cloned.1.call-start = ((), (), s32[]{:S(2)}) async-start(), calls=%async_computation.14 | async-start | bytes 8650752 | tf_op jit(solution)/shard_map/all_gather | solution.py:662
  20.4 321.2 %all-gather.6.cloned.1.call-start = ((), (), s32[]{:S(2)}) async-start(), calls=%async_computation.13 | async-start | bytes 17408000 | tf_op jit(solution)/shard_map/all_gather | solution.py:687
  68.9 53.9 %all-to-all-start.9 = ((bf16[32,48,512]{2,1,0:T(8,128)(2,1)}), bf16[32,48,512]{2,1,0:T(8,128)(2,1)S(1)}, u32[]{:S(2)}, u32[]{:S(2)}) async-start(bf16[32,48,512]{2,1,0:T(8,128)(2,1)} %bitcast.851), calls=%async_computation.9 | async-start | bytes 3145728 | tf_op jit(solution)/shard_map/all_to_all | solution.py:496
  127.7 80.1 %all-to-all-start.10 = ((bf16[32,64,512]{2,1,0:T(8,128)(2,1)}), bf16[32,64,512]{2,1,0:T(8,128)(2,1)}, u32[]{:S(2)}, u32[]{:S(2)}) async-start(bf16[32,64,512]{2,1,0:T(8,128)(2,1)} %bitcast.817), calls=%async_computation.10 | async-start | bytes 4194304 | tf_op jit(solution)/shard_map/all_to_all | solution.py:496
  466.8 60.1 %collective-permute-start.6 = (bf16[8,1000,256]{2,1,0:T(8,128)(2,1)}, bf16[8,1000,256]{2,1,0:T(8,128)(2,1)}, u32[]{:S(2)}, u32[]{:S(2)}) collective-permute-start(bf16[8,1000,256]{2,1,0:T(8,128)(2,1)} %fusion.80), channel_id=1, source_target_pairs={{0,2},{2,0},{4,6},{6,4},{8,10},{10,8},{12,14},{14,12},{16,18},{18,... | collective-permute-start | bytes 12288008 | tf_op jit(solution)/shard_map/ppermute | solution.py:456
  515.1 106.9 %collective-permute-start.9 = (bf16[8,32,4096]{2,1,0:T(8,128)(2,1)}, bf16[8,32,4096]{2,1,0:T(8,128)(2,1)}, u32[]{:S(2)}, u32[]{:S(2)}) collective-permute-start(bf16[8,32,4096]{2,1,0:T(8,128)(2,1)} %fusion.187), channel_id=1, source_target_pairs={{0,2},{2,0},{4,6},{6,4},{8,10},{10,8},{12,14},{14,12},{16,18},{18,... | collective-permute-start | bytes 6291464 | tf_op jit(solution)/shard_map/ppermute | solution.py:456
  532.6 89.4 %collective-permute-start.8 = (bf16[8,1000,256]{2,1,0:T(8,128)(2,1)}, bf16[8,1000,256]{2,1,0:T(8,128)(2,1)}, u32[]{:S(2)}, u32[]{:S(2)}) collective-permute-start(bf16[8,1000,256]{2,1,0:T(8,128)(2,1)} %fusion.81), channel_id=1, source_target_pairs={{0,2},{2,0},{4,6},{6,4},{8,10},{10,8},{12,14},{14,12},{16,18},{18,... | collective-permute-start | bytes 12288008 | tf_op jit(solution)/shard_map/ppermute | solution.py:456
  539.2 82.8 %collective-permute-start.7 = (bf16[4,1000,256]{2,1,0:T(8,128)(2,1)}, bf16[4,1000,256]{2,1,0:T(8,128)(2,1)}, u32[]{:S(2)}, u32[]{:S(2)}) collective-permute-start(bf16[4,1000,256]{2,1,0:T(8,128)(2,1)} %get-tuple-element.1066), channel_id=1, source_target_pairs={{0,4},{2,6},{4,0},{6,2},{8,12},{10,14},{12,8},{14,10},{16,20},{18,... | collective-permute-start | bytes 6144008 | tf_op jit(solution)/shard_map/ppermute | solution.py:456
  608.5 126.1 %collective-permute-start.13 = (bf16[8,32,2048]{2,1,0:T(8,128)(2,1)}, bf16[8,32,2048]{2,1,0:T(8,128)(2,1)}, u32[]{:S(2)}, u32[]{:S(2)}) collective-permute-start(bf16[8,32,2048]{2,1,0:T(8,128)(2,1)} %pad_maximum_fusion.8), channel_id=1, source_target_pairs={{0,2},{2,0},{4,6},{6,4},{8,10},{10,8},{12,14},{14,12},{16,18},{18,... | collective-permute-start | bytes 3145736 | tf_op jit(solution)/shard_map/ppermute | solution.py:456
  700.5 34.0 %collective-permute-start.10 = (bf16[2,1000,256]{2,1,0:T(8,128)(2,1)}, bf16[2,1000,256]{2,1,0:T(8,128)(2,1)}, u32[]{:S(2)}, u32[]{:S(2)}) collective-permute-start(bf16[2,1000,256]{2,1,0:T(8,128)(2,1)} %get-tuple-element.1080), channel_id=1, source_target_pairs={{0,8},{2,10},{4,12},{6,14},{8,0},{10,2},{12,4},{14,6},{16,24},{18,... | collective-permute-start | bytes 3072008 | tf_op jit(solution)/shard_map/ppermute | solution.py:456
  703.9 43.9 %collective-permute-start.11 = (bf16[4,1000,256]{2,1,0:T(8,128)(2,1)S(1)}, bf16[4,1000,256]{2,1,0:T(8,128)(2,1)S(1)}, u32[]{:S(2)}, u32[]{:S(2)}) collective-permute-start(bf16[4,1000,256]{2,1,0:T(8,128)(2,1)S(1)} %get-tuple-element.1064), channel_id=1, source_target_pairs={{0,4},{2,6},{4,0},{6,2},{8,12},{10,14},{12,8},{14,10},{16,20},{18,... | collective-permute-start | bytes 6144008 | tf_op jit(solution)/shard_map/ppermute | solution.py:456
  707.5 27.1 %collective-permute-start.12 = (bf16[8,16,4096]{2,1,0:T(8,128)(2,1)S(1)}, bf16[8,16,4096]{2,1,0:T(8,128)(2,1)S(1)}, u32[]{:S(2)}, u32[]{:S(2)}) collective-permute-start(bf16[8,16,4096]{2,1,0:T(8,128)(2,1)S(1)} %get-tuple-element.1077), channel_id=1, source_target_pairs={{0,1},{1,0},{2,3},{3,2},{4,5},{5,4},{6,7},{7,6},{8,9},{9,8},{10,11... | collective-permute-start | bytes 3145736 | tf_op jit(solution)/shard_map/ppermute | solution.py:456
  714.1 56.0 %collective-permute-start.18 = (bf16[8,32,2048]{2,1,0:T(8,128)(2,1)}, bf16[8,32,2048]{2,1,0:T(8,128)(2,1)S(1)}, u32[]{:S(2)}, u32[]{:S(2)}) collective-permute-start(bf16[8,32,2048]{2,1,0:T(8,128)(2,1)} %pad_maximum_fusion.9), channel_id=1, source_target_pairs={{0,2},{2,0},{4,6},{6,4},{8,10},{10,8},{12,14},{14,12},{16,18},{18,... | collective-permute-start | bytes 3145736 | tf_op jit(solution)/shard_map/ppermute | solution.py:456
  749.2 40.8 %collective-permute-start.15 = (bf16[2,1000,256]{2,1,0:T(8,128)(2,1)}, bf16[2,1000,256]{2,1,0:T(8,128)(2,1)}, u32[]{:S(2)}, u32[]{:S(2)}) collective-permute-start(bf16[2,1000,256]{2,1,0:T(8,128)(2,1)} %fusion.130), channel_id=1, source_target_pairs={{0,8},{2,10},{4,12},{6,14},{8,0},{10,2},{12,4},{14,6},{16,24},{18,... | collective-permute-start | bytes 3072008 | tf_op jit(solution)/shard_map/ppermute | solution.py:456
  752.0 38.0 %collective-permute-start.16 = (bf16[4,16,4096]{2,1,0:T(8,128)(2,1)}, bf16[4,16,4096]{2,1,0:T(8,128)(2,1)}, u32[]{:S(2)}, u32[]{:S(2)}) collective-permute-start(bf16[4,16,4096]{2,1,0:T(8,128)(2,1)} %get-tuple-element.1097), channel_id=1, source_target_pairs={{0,4},{2,6},{4,0},{6,2},{8,12},{10,14},{12,8},{14,10},{16,20},{18,... | collective-permute-start | bytes 1572872 | tf_op jit(solution)/shard_map/ppermute | solution.py:456
  755.9 34.1 %collective-permute-start.17 = (bf16[8,16,2048]{2,1,0:T(8,128)(2,1)}, bf16[8,16,2048]{2,1,0:T(8,128)(2,1)}, u32[]{:S(2)}, u32[]{:S(2)}) collective-permute-start(bf16[8,16,2048]{2,1,0:T(8,128)(2,1)} %get-tuple-element.1096), channel_id=1, source_target_pairs={{0,1},{1,0},{2,3},{3,2},{4,5},{5,4},{6,7},{7,6},{8,9},{9,8},{10,11... | collective-permute-start | bytes 1572872 | tf_op jit(solution)/shard_map/ppermute | solution.py:456
  766.0 24.0 %collective-permute-start.14 = (bf16[1,1000,256]{2,1,0:T(8,128)(2,1)S(1)}, bf16[1,1000,256]{2,1,0:T(8,128)(2,1)}, u32[]{:S(2)}, u32[]{:S(2)}) collective-permute-start(bf16[1,1000,256]{2,1,0:T(8,128)(2,1)S(1)} %fusion.136), channel_id=1, source_target_pairs={{0,16},{2,18},{4,20},{6,22},{8,24},{10,26},{12,28},{14,30},{16,0},... | collective-permute-start | bytes 1536008 | tf_op jit(solution)/shard_map/ppermute | solution.py:456
  770.1 121.2 %collective-permute-start.23 = (bf16[8,32,4096]{2,1,0:T(8,128)(2,1)}, bf16[8,32,4096]{2,1,0:T(8,128)(2,1)}, u32[]{:S(2)}, u32[]{:S(2)}) collective-permute-start(bf16[8,32,4096]{2,1,0:T(8,128)(2,1)} %fusion.197), channel_id=1, source_target_pairs={{0,2},{2,0},{4,6},{6,4},{8,10},{10,8},{12,14},{14,12},{16,18},{18,... | collective-permute-start | bytes 6291464 | tf_op jit(solution)/shard_map/ppermute | solution.py:456
  830.1 61.2 %collective-permute-start.19 = (bf16[1,1000,256]{2,1,0:T(8,128)(2,1)}, bf16[1,1000,256]{2,1,0:T(8,128)(2,1)}, u32[]{:S(2)}, u32[]{:S(2)}) collective-permute-start(bf16[1,1000,256]{2,1,0:T(8,128)(2,1)} %fusion.135), channel_id=1, source_target_pairs={{0,16},{2,18},{4,20},{6,22},{8,24},{10,26},{12,28},{14,30},{16,0},... | collective-permute-start | bytes 1536008 | tf_op jit(solution)/shard_map/ppermute | solution.py:456
  832.2 59.1 %collective-permute-start.20 = (bf16[2,16,4096]{2,1,0:T(8,128)(2,1)}, bf16[2,16,4096]{2,1,0:T(8,128)(2,1)}, u32[]{:S(2)}, u32[]{:S(2)}) collective-permute-start(bf16[2,16,4096]{2,1,0:T(8,128)(2,1)} %get-tuple-element.1105), channel_id=1, source_target_pairs={{0,8},{2,10},{4,12},{6,14},{8,0},{10,2},{12,4},{14,6},{16,24},{18,... | collective-permute-start | bytes 786440 | tf_op jit(solution)/shard_map/ppermute | solution.py:456
  835.9 55.4 %collective-permute-start.21 = (bf16[4,16,2048]{2,1,0:T(8,128)(2,1)}, bf16[4,16,2048]{2,1,0:T(8,128)(2,1)}, u32[]{:S(2)}, u32[]{:S(2)}) collective-permute-start(bf16[4,16,2048]{2,1,0:T(8,128)(2,1)} %get-tuple-element.1104), channel_id=1, source_target_pairs={{0,4},{2,6},{4,0},{6,2},{8,12},{10,14},{12,8},{14,10},{16,20},{18,... | collective-permute-start | bytes 786440 | tf_op jit(solution)/shard_map/ppermute | solution.py:456
  839.8 51.5 %collective-permute-start.22 = (bf16[8,16,2048]{2,1,0:T(8,128)(2,1)}, bf16[8,16,2048]{2,1,0:T(8,128)(2,1)}, u32[]{:S(2)}, u32[]{:S(2)}) collective-permute-start(bf16[8,16,2048]{2,1,0:T(8,128)(2,1)} %get-tuple-element.1094), channel_id=1, source_target_pairs={{0,1},{1,0},{2,3},{3,2},{4,5},{5,4},{6,7},{7,6},{8,9},{9,8},{10,11... | collective-permute-start | bytes 1572872 | tf_op jit(solution)/shard_map/ppermute | solution.py:456
  839.8 46.5 %all-to-all-start.11 = ((bf16[32,48,512]{2,1,0:T(8,128)(2,1)}), bf16[32,48,512]{2,1,0:T(8,128)(2,1)}, u32[]{:S(2)}, u32[]{:S(2)}) async-start(bf16[32,48,512]{2,1,0:T(8,128)(2,1)} %bitcast.849), calls=%async_computation.11 | async-start | bytes 3145728 | tf_op jit(solution)/shard_map/all_to_all | solution.py:496
  891.3 118.2 %collective-permute-start.28 = (bf16[8,32,2304]{2,1,0:T(8,128)(2,1)}, bf16[8,32,2304]{2,1,0:T(8,128)(2,1)}, u32[]{:S(2)}, u32[]{:S(2)}) collective-permute-start(bf16[8,32,2304]{2,1,0:T(8,128)(2,1)} %pad_maximum_fusion.7), channel_id=1, source_target_pairs={{0,2},{2,0},{4,6},{6,4},{8,10},{10,8},{12,14},{14,12},{16,18},{18,... | collective-permute-start | bytes 3538952 | tf_op jit(solution)/shard_map/ppermute | solution.py:456
  892.4 117.2 %collective-permute-start.24 = (bf16[1,16,4096]{2,1,0:T(8,128)(2,1)S(1)}, bf16[1,16,4096]{2,1,0:T(8,128)(2,1)}, u32[]{:S(2)}, u32[]{:S(2)}) collective-permute-start(bf16[1,16,4096]{2,1,0:T(8,128)(2,1)S(1)} %fusion.215), channel_id=1, source_target_pairs={{0,16},{2,18},{4,20},{6,22},{8,24},{10,26},{12,28},{14,30},{16,0},... | collective-permute-start | bytes 393224 | tf_op jit(solution)/shard_map/ppermute | solution.py:456
  895.6 113.9 %collective-permute-start.25 = (bf16[2,16,2048]{2,1,0:T(8,128)(2,1)}, bf16[2,16,2048]{2,1,0:T(8,128)(2,1)}, u32[]{:S(2)}, u32[]{:S(2)}) collective-permute-start(bf16[2,16,2048]{2,1,0:T(8,128)(2,1)} %get-tuple-element.1108), channel_id=1, source_target_pairs={{0,8},{2,10},{4,12},{6,14},{8,0},{10,2},{12,4},{14,6},{16,24},{18,... | collective-permute-start | bytes 393224 | tf_op jit(solution)/shard_map/ppermute | solution.py:456
  897.8 111.7 %collective-permute-start.26 = (bf16[4,16,2048]{2,1,0:T(8,128)(2,1)}, bf16[4,16,2048]{2,1,0:T(8,128)(2,1)}, u32[]{:S(2)}, u32[]{:S(2)}) collective-permute-start(bf16[4,16,2048]{2,1,0:T(8,128)(2,1)} %get-tuple-element.1102), channel_id=1, source_target_pairs={{0,4},{2,6},{4,0},{6,2},{8,12},{10,14},{12,8},{14,10},{16,20},{18,... | collective-permute-start | bytes 786440 | tf_op jit(solution)/shard_map/ppermute | solution.py:456
  903.3 106.2 %collective-permute-start.27 = (bf16[8,16,4096]{2,1,0:T(8,128)(2,1)}, bf16[8,16,4096]{2,1,0:T(8,128)(2,1)}, u32[]{:S(2)}, u32[]{:S(2)}) collective-permute-start(bf16[8,16,4096]{2,1,0:T(8,128)(2,1)} %get-tuple-element.1076), channel_id=1, source_target_pairs={{0,1},{1,0},{2,3},{3,2},{4,5},{5,4},{6,7},{7,6},{8,9},{9,8},{10,11... | collective-permute-start | bytes 3145736 | tf_op jit(solution)/shard_map/ppermute | solution.py:456
  1050.7 64.3 %all-to-all-start.12 = ((bf16[32,64,512]{2,1,0:T(8,128)(2,1)}), bf16[32,64,512]{2,1,0:T(8,128)(2,1)}, u32[]{:S(2)}, u32[]{:S(2)}) async-start(bf16[32,64,512]{2,1,0:T(8,128)(2,1)} %bitcast.814), calls=%async_computation.12 | async-start | bytes 4194304 | tf_op jit(solution)/shard_map/all_to_all | solution.py:496
  1058.1 49.4 %collective-permute-start.41 = (f32[16,4096]{1,0:T(8,128)S(1)}, f32[16,4096]{1,0:T(8,128)S(1)}, u32[]{:S(2)}, u32[]{:S(2)}) collective-permute-start(f32[16,4096]{1,0:T(8,128)S(1)} %get-tuple-element.1041), channel_id=1, source_target_pairs={{0,1},{1,0},{2,3},{3,2},{4,5},{5,4},{6,7},{7,6},{8,9},{9,8},{10,11... | collective-permute-start | bytes 786440 | tf_op jit(solution)/shard_map/ppermute | solution.py:456
  1059.8 47.7 %collective-permute-start.42 = (bf16[1,16,2304]{2,1,0:T(8,128)(2,1)S(1)}, bf16[1,16,2304]{2,1,0:T(8,128)(2,1)S(1)}, u32[]{:S(2)}, u32[]{:S(2)}) collective-permute-start(bf16[1,16,2304]{2,1,0:T(8,128)(2,1)S(1)} %fusion.231), channel_id=1, source_target_pairs={{0,16},{2,18},{4,20},{6,22},{8,24},{10,26},{12,28},{14,30},{16,0},... | collective-permute-start | bytes 221192 | tf_op jit(solution)/shard_map/ppermute | solution.py:456
  (212 other events, 2713.6 us)
Sparse Core Ops, SparseCore 0:
  18.7 89.3 all-gather.9
  111.6 104.4 all-gather.7
  218.4 123.1 all-gather.5

commit v4 on v3

--- a/solution.py
+++ b/solution.py
@@ -25,22 +25,22 @@
 f32 = jnp.float32
 query_block = 256
 key_block = 128
-place_block = 256
+place_block = 512
 vmem_bytes = 56 * 1024 * 1024
 
 
 def sinusoid(positions, width):
     half_width = width // 2
     frequency = jnp.exp(jnp.arange(half_width).astype(f32) * (-math.log(10000.0) / half_width))
-    angles = positions.astype(f32)[..., None] * frequency
-    return jnp.concatenate([jnp.sin(angles), jnp.cos(angles)], -1)
+    angles = frequency[:, None] * positions.astype(f32)[None, :]
+    return jnp.concatenate([jnp.sin(angles), jnp.cos(angles)], 0)
 
 
 def layer_norm(stream, norm_gain, norm_bias):
-    average = jnp.mean(stream, -1, keepdims=True)
+    average = jnp.mean(stream, 0, keepdims=True)
     centred = stream - average
-    variance = jnp.mean(centred * centred, -1, keepdims=True)
-    return centred * lax.rsqrt(variance + 1e-05) * norm_gain + norm_bias
+    variance = jnp.mean(centred * centred, 0, keepdims=True)
+    return centred * lax.rsqrt(variance + 1e-05) * norm_gain[:, None] + norm_bias[:, None]
 
 
 def contract(left, right, left_dim, right_dim):
@@ -248,71 +248,62 @@
         sums_ref[...] = jnp.zeros_like(sums_ref)
 
     stream, grad = stream_ref[...], grad_ref[...]
-    rows, width = stream.shape
-    average = jnp.mean(stream, -1, keepdims=True)
+    width, places = stream.shape
+    average = jnp.mean(stream, 0, keepdims=True)
     centred = stream - average
-    variance = jnp.mean(centred * centred, -1, keepdims=True)
+    variance = jnp.mean(centred * centred, 0, keepdims=True)
     inverse = lax.rsqrt(variance + 1e-05)
     unit = centred * inverse
     scaled = grad * gain_ref[...]
-    along = jnp.mean(scaled * unit, -1, keepdims=True)
-    level = jnp.mean(scaled, -1, keepdims=True)
+    along = jnp.mean(scaled * unit, 0, keepdims=True)
+    level = jnp.mean(scaled, 0, keepdims=True)
     out_ref[...] = rest_ref[...] + (scaled - level - unit * along) * inverse
-    sums_ref[0:8, :] += jnp.sum((grad * unit).reshape(rows // 8, 8, width), 0)
-    sums_ref[8:16, :] += jnp.sum(grad.reshape(rows // 8, 8, width), 0)
+    weighted = grad * unit
+    for at in range(0, places, 128):
+        sums_ref[0] += weighted[:, at : at + 128]
+        sums_ref[1] += grad[:, at : at + 128]
 
 
 def norm_backward(stream, gain, grad, rest):
-    places, width = stream.shape
-    rows = min(256, places)
-    block = pl.BlockSpec((rows, width), lambda i: (i, 0))
-    out, sums = pl.pallas_call(
+    width, places = stream.shape
+    columns = min(256, places)
+    block = pl.BlockSpec((width, columns), lambda i: (0, i))
+    return pl.pallas_call(
         norm_back_kernel,
-        grid=(places // rows,),
-        in_specs=[block, pl.BlockSpec((1, width), lambda i: (0, 0)), block, block],
-        out_specs=[block, pl.BlockSpec((16, width), lambda i: (0, 0))],
+        grid=(places // columns,),
+        in_specs=[block, pl.BlockSpec((width, 1), lambda i: (0, 0)), block, block],
+        out_specs=[block, pl.BlockSpec((2, width, 128), lambda i: (0, 0, 0))],
         out_shape=[
-            jax.ShapeDtypeStruct((places, width), f32),
-            jax.ShapeDtypeStruct((16, width), f32),
+            jax.ShapeDtypeStruct((width, places), f32),
+            jax.ShapeDtypeStruct((2, width, 128), f32),
         ],
         compiler_params=pltpu.CompilerParams(vmem_limit_bytes=vmem_bytes),
         name="norm_backward",
-    )(stream, gain[None], grad, rest)
-    return out, jnp.sum(sums[:8], 0), jnp.sum(sums[8:], 0)
+    )(stream, gain[:, None], grad, rest)
+
+
+def chunk_plan(total):
+    quarter = place_block // 4
+    units = (jnp.maximum(total - place_block, 0) + quarter - 1) // quarter
+    left = units % 4
+    wides = units // 4 + (left == 3).astype(jnp.int32)
+    return jnp.stack([wides, left == 2, left == 1]).astype(jnp.int32)
 
 
 def each_chunk(plan, visit):
-    wides = plan.shape[0] - 2
+    visit(0, place_block, True)
 
     def wide(index, carry):
-        visit(pl.multiple_of(plan[2 + index], place_block // 2), place_block)
+        visit(pl.multiple_of((index + 1) * place_block, place_block), place_block, False)
         return carry
 
-    def narrow(index, carry):
-        visit(pl.multiple_of(plan[wides + 1 - index], place_block // 2), place_block // 2)
-        return carry
-
     lax.fori_loop(0, plan[0], wide, 0)
-    lax.fori_loop(0, plan[1], narrow, 0)
-
-
-def chunk_plan(counts, span):
-    half = place_block // 2
-    left = counts % place_block
-    wides = counts // place_block + (left > half).astype(jnp.int32)
-    narrows = ((left > 0) & (left <= half)).astype(jnp.int32)
-    segments = counts.shape[0]
-    base = jnp.arange(segments) * span
-    index = jnp.arange(span // place_block)
-    used = (index[None, :] < wides[:, None]).reshape(-1)
-    begins = (base[:, None] + index[None, :] * place_block).reshape(-1)
-    total = used.shape[0] + segments
-    at = jnp.where(used, jnp.cumsum(used.astype(jnp.int32)) - 1, -1)
-    narrow_at = jnp.where(narrows > 0, total - jnp.cumsum(narrows), -1)
-    at = jnp.concatenate([at, narrow_at])
-    begins = jnp.concatenate([begins, base + wides * place_block])
-    listed = jnp.sum(jnp.where(at[None, :] == jnp.arange(total)[:, None], begins[None, :], 0), 1)
-    return jnp.concatenate([jnp.stack([jnp.sum(wides), jnp.sum(narrows)]), listed]).astype(jnp.int32)
+    after = pl.multiple_of((plan[0] + 1) * place_block, place_block)
+    for index, share in ((1, 2), (2, 4)):
+
+        @pl.when(plan[index] > 0)
+        def _(share=share):
+            visit(after, place_block // share, False)
 
 
 def parts_of(words):
@@ -322,7 +313,7 @@
     return [slice(0, words)]
 
 
-def head_stats_kernel(plan, table_ref, rows_ref, stats_ref, tops, sums):
+def head_stats_kernel(plan, table_ref, turned_ref, stats_ref, tops, sums):
     step = pl.program_id(0)
 
     @pl.when(step == 0)
@@ -330,12 +321,12 @@
         tops[...] = jnp.full_like(tops, -1e30)
         sums[...] = jnp.zeros_like(sums)
 
-    def visit(start, size):
+    def visit(start, size, first):
         here = pl.ds(start, size)
-        rows = rows_ref[here, :]
+        turned = turned_ref[:, here]
         old, total = tops[:, here], sums[:, here]
         for part in parts_of(table_ref.shape[0]):
-            logits = contract(table_ref[part, :], rows, 1, 1)
+            logits = contract(table_ref[part, :], turned, 1, 0)
             logits = logits.reshape(logits.shape[0] // 8, 8, size)
             top = jnp.maximum(old, jnp.max(logits, axis=0))
             powers = jnp.sum(jnp.exp(logits - top[None]), axis=0)
@@ -354,101 +345,120 @@
 
 
 def head_back_kernel(
-    plan, table_ref, rows_ref, target_ref, log_ref, weight_ref, one_ref, two_ref, dr_ref, pick_ref
+    plan, table_ref, rows_ref, turned_ref, target_ref, log_ref, weight_ref, *refs, owned
 ):
+    (*out_refs, dr_ref, pick_ref, acc) = refs
     step = pl.program_id(0)
     words, width = table_ref.shape
-    half = one_ref.shape[1]
 
     @pl.when(step == 0)
     def _():
         dr_ref[...] = jnp.zeros_like(dr_ref)
         pick_ref[...] = jnp.zeros_like(pick_ref)
 
-    one_ref[...] = jnp.zeros_like(one_ref)
-    two_ref[...] = jnp.zeros_like(two_ref)
-
-    def visit(start, size):
+    def visit(start, size, first):
         here = pl.ds(start, size)
-        rows = rows_ref[here, :]
+        rows, turned = rows_ref[here, :], turned_ref[:, here]
         target = target_ref[:, here] - step * words
         log, weight = log_ref[:, here], weight_ref[:, here]
-        back = jnp.zeros((size, width), f32)
         found = jnp.zeros((8, size), f32)
         for part in parts_of(words):
             block = table_ref[part, :]
             count = block.shape[0]
             inner = lax.broadcasted_iota(jnp.int32, (count, size), 0) + part.start
-            logits = contract(block, rows, 1, 1)
+            logits = contract(block, turned, 1, 0)
             scaled = jnp.exp(logits - log)
             hit = inner == target
             found += jnp.sum(jnp.where(hit, logits, 0.0).reshape(count // 8, 8, size), axis=0)
             d_logits = jnp.where(hit, scaled - weight, scaled).astype(low_type)
-            one_ref[part, :] += contract(d_logits, rows[:, :half], 1, 0)
-            two_ref[part, :] += contract(d_logits, rows[:, half:], 1, 0)
-            back += contract(d_logits, block, 0, 0)
+            if first:
+                acc[part, :] = contract(d_logits, rows, 1, 0)
+            else:
+                acc[part, :] += contract(d_logits, rows, 1, 0)
+            dr_ref[here, :] += contract(d_logits, block, 0, 0)
         pick_ref[:, here] += found
-        dr_ref[here, :] += back
 
     each_chunk(plan, visit)
+    if not owned:
+        out_refs[0][...] = acc[...]
+        return
+    mine = plan[3]
+    half = width // 2
+    keep = pl.ds(pl.multiple_of(mine * owned, 8), owned)
+    away = pl.ds(pl.multiple_of((1 - mine) * owned, 8), owned)
+    out_refs[0][0] = acc[keep, :half]
+    out_refs[1][0] = acc[keep, half:]
+    out_refs[2][0] = acc[away, :half].astype(low_type)
+    out_refs[3][0] = acc[away, half:].astype(low_type)
 
 
 def word_block(words):
     return max(n for n in range(16, 1601, 16) if words % n == 0)
 
 
-def head_specs(words, width, places):
-    return [
-        pl.BlockSpec((words, width), lambda i, *_: (i, 0)),
-        pl.BlockSpec((places, width), lambda i, *_: (0, 0)),
-    ]
-
-
-def head_stats(plan, table_part, rows):
+def head_stats(plan, table_part, turned):
     words = word_block(table_part.shape[0])
-    places, width = rows.shape
+    width, places = turned.shape
     return pl.pallas_call(
         head_stats_kernel,
         grid_spec=pltpu.PrefetchScalarGridSpec(
             num_scalar_prefetch=1,
             grid=(table_part.shape[0] // words,),
-            in_specs=head_specs(words, width, places),
+            in_specs=[
+                pl.BlockSpec((words, width), lambda i, *_: (i, 0)),
+                pl.BlockSpec((width, places), lambda i, *_: (0, 0)),
+            ],
             out_specs=pl.BlockSpec((2, places), lambda i, *_: (0, 0)),
             scratch_shapes=[pltpu.VMEM((8, places), f32) for _ in range(2)],
         ),
         out_shape=jax.ShapeDtypeStruct((2, places), f32),
         compiler_params=pltpu.CompilerParams(vmem_limit_bytes=vmem_bytes),
         name="head_stats",
-    )(plan, table_part, rows)
-
-
-def head_back(plan, table_part, rows, targets, logs, weights):
-    words = word_block(table_part.shape[0])
+    )(plan, table_part, turned)
+
+
+def head_back(plan, table_part, rows, turned, targets, logs, weights, owned):
+    total = table_part.shape[0]
+    words = 2 * owned if owned else word_block(total)
     places, width = rows.shape
     half = width // 2
+    row = pl.BlockSpec((1, places), lambda i, *_: (0, 0))
+    if owned:
+        share = pl.BlockSpec((1, owned, half), lambda i, *_: (i, 0, 0))
+        out_specs = [share] * 4
+        shape = (total // words, owned, half)
+        out_shape = [jax.ShapeDtypeStruct(shape, t) for t in (f32, f32, low_type, low_type)]
+    else:
+        out_specs = [pl.BlockSpec((words, width), lambda i, *_: (i, 0))]
+        out_shape = [jax.ShapeDtypeStruct((total, width), f32)]
     return pl.pallas_call(
-        head_back_kernel,
+        functools.partial(head_back_kernel, owned=owned),
         grid_spec=pltpu.PrefetchScalarGridSpec(
             num_scalar_prefetch=1,
-            grid=(table_part.shape[0] // words,),
-            in_specs=head_specs(words, width, places)
-            + [pl.BlockSpec((1, places), lambda i, *_: (0, 0)) for _ in range(3)],
-            out_specs=[
-                pl.BlockSpec((words, half), lambda i, *_: (i, 0)),
-                pl.BlockSpec((words, half), lambda i, *_: (i, 0)),
+            grid=(total // words,),
+            in_specs=[
+                pl.BlockSpec((words, width), lambda i, *_: (i, 0)),
+                pl.BlockSpec((places, width), lambda i, *_: (0, 0)),
+                pl.BlockSpec((width, places), lambda i, *_: (0, 0)),
+                row,
+                row,
+                row,
+            ],
+            out_specs=out_specs
+            + [
                 pl.BlockSpec((places, width), lambda i, *_: (0, 0)),
                 pl.BlockSpec((8, places), lambda i, *_: (0, 0)),
             ],
+            scratch_shapes=[pltpu.VMEM((words, width), f32)],
         ),
-        out_shape=[
-            jax.ShapeDtypeStruct((table_part.shape[0], half), f32),
-            jax.ShapeDtypeStruct((table_part.shape[0], half), f32),
+        out_shape=out_shape
+        + [
             jax.ShapeDtypeStruct((places, width), f32),
             jax.ShapeDtypeStruct((8, places), f32),
         ],
         compiler_params=pltpu.CompilerParams(vmem_limit_bytes=vmem_bytes),
         name="head_back",
-    )(plan, table_part, rows, targets, logs, weights)
+    )(plan, table_part, rows, turned, targets, logs, weights)
 
 
 def swap(values, axis, bit):
@@ -485,90 +495,104 @@
     return lax.all_gather(values, "seq", axis=dim)
 
 
-def swap_rows(values, cut, more):
-    rest = lax.cond(
-        more, lambda part: swap(part, "seq", 1), lambda part: jnp.zeros_like(part), values[cut:]
-    )
-    return jnp.concatenate([swap(values[:cut], "seq", 1), rest], 0)
-
-
 def to_each(values):
     return lax.all_to_all(values, ("seq", "dp"), 0, 0)
 
 
-class Halving:
-    def __init__(self, parts, joint):
-        self.parts, self.joint = parts, joint
+def halving_fits(rows, columns, joint):
+    owners, seqs = lax.axis_size("dp"), lax.axis_size("seq")
+    fits = power_of_two(owners) and owners > 2 and columns % 128 == 0
+    return fits and (rows % 16 == 0 and seqs == 2 if joint else rows % 8 == 0)
+
+
+class Chain:
+    pending = value = square = None
+
+class LayerChain(Chain):
+    def __init__(self, parts):
+        self.parts, self.step = parts, 0
         self.rows = parts[0].shape[1]
-        bits = []
-        bit = 1
-        while bit < lax.axis_size("dp"):
-            bits.append(("dp", bit))
-            bit *= 2
-        self.steps = bits[:1] + ([("seq", 1)] if joint else []) + bits[1:]
-        self.fast = power_of_two(lax.axis_size("dp")) and (
-            not joint or (lax.axis_size("seq") == 2 and self.rows % 16 == 0)
-        )
-        self.fast = self.fast and all(part.shape[2] % 128 == 0 for part in parts)
-        self.fast = self.fast and self.rows % 8 == 0
-        self.pending, self.value, self.square, self.got = None, None, None, None
+        self.fast = halving_fits(self.rows, parts[0].shape[2], True)
         if self.fast:
             self.launch()
 
     def launch(self):
-        if self.value is not None:
+        owners = lax.axis_size("dp")
+        if self.step == 4:
             return
-        if not self.steps:
-            self.pending = swap(self.parts[0], "seq", 1)
-            return
-        axis, bit = self.steps[0]
-        rows = self.rows // 2 if axis == "seq" else self.rows
-        index = lax.axis_index(axis)
-        mine = (index // bit) & 1
-
-        def half(side):
-            halves = [
-                pick(part.reshape((-1, 2, rows, part.shape[2])), 1, side) for part in self.parts
-            ]
-            if self.got is not None:
-                halves[0] = halves[0] + pick(
-                    self.got.reshape((-1, 2, rows, self.got.shape[2])), 1, side
-                ).astype(f32)
-            return halves
-
-        away = [part.astype(low_type) for part in half(1 - mine)]
-        self.parts = [jnp.concatenate(half(mine), 2)]
-        self.rows, self.got = rows, None
-        self.pending = swap(jnp.concatenate(away, 2), axis, bit)
+        if self.step == 3:
+            self.pending = swap(self.part, "seq", 1)
+        elif self.step == 2:
+            groups = [list(range(core, owners, 2)) for core in range(2)]
+            whole = (self.part + self.got.astype(f32)).astype(low_type)
+            self.pending = lax.all_to_all(whole, "dp", 0, 0, axis_index_groups=groups)
+        else:
+            axis = ("dp", "seq")[self.step]
+            mine = lax.axis_index(axis) & 1
+            if self.step == 1:
+                self.rows //= 2
+
+            def half(side):
+                if self.step == 0:
+                    shape = (owners // 2, 2, self.rows)
+                    parts = [part.reshape(shape + part.shape[2:]) for part in self.parts]
+                    return jnp.concatenate([pick(part, 1, side) for part in parts], 2)
+                shape = (owners // 2, 2, self.rows, -1)
+                first, second = self.part.reshape(shape), self.got.reshape(shape)
+                return pick(first, 1, side) + pick(second, 1, side).astype(f32)
+
+            away = half(1 - mine).astype(low_type)
+            self.part = half(mine)
+            self.pending = swap(away, axis, 1)
 
     def absorb(self, got):
         self.pending = None
-        if not self.steps:
+        self.step += 1
+        if self.step < 3:
+            self.got = got
+        elif self.step == 3:
+            self.part = jnp.sum(got.astype(f32), 0)
+            self.square = jnp.sum(self.part * self.part)
+        else:
             first = lax.axis_index("seq") == 0
-            part = self.parts[0]
+            part = self.part
             self.value = jnp.concatenate(
                 [jnp.where(first, part, got), jnp.where(first, got, part)], 0
             )
+
+    def finish(self):
+        if not self.fast:
+            whole = jnp.concatenate(self.parts, 2)
+            part = lax.psum(lax.psum_scatter(whole, "dp", scatter_dimension=0), "seq")
+            self.value = part
+            self.square = jnp.where(lax.axis_index("seq") == 0, jnp.sum(part * part), 0.0)
+
+
+class TableChain(Chain):
+    def __init__(self, keep, away):
+        self.part, self.got = keep, None
+        self.rows, self.bit = keep.shape[1], 2
+        self.pending = swap(away, "dp", 1)
+
+    def launch(self):
+        if self.bit == lax.axis_size("dp"):
             return
-        self.steps.pop(0)
-        self.got = got
-        if not self.steps:
-            part = (self.parts[0] + got.astype(f32)).reshape(self.rows, -1)
-            self.parts = [part]
-            self.square = jnp.sum(part * part)
-            if not self.joint:
-                self.value = part
-
-    def finish(self):
-        if self.fast:
-            return
-        whole = jnp.concatenate(self.parts, 2)
-        part = lax.psum_scatter(whole, "dp", scatter_dimension=0)
-        if self.joint:
-            part = lax.psum(part, "seq")
-        self.value, self.square = part, jnp.sum(part * part)
-        if self.joint:
-            self.square = jnp.where(lax.axis_index("seq") == 0, self.square, 0.0)
+        mine = (lax.axis_index("dp") // self.bit) & 1
+        shape = (-1, 2, self.rows, self.part.shape[2])
+        first, second = self.part.reshape(shape), self.got.reshape(shape)
+
+        def half(side):
+            return pick(first, 1, side) + pick(second, 1, side).astype(f32)
+
+        away = half(1 - mine).astype(low_type)
+        self.part = half(mine)
+        self.pending = swap(away, "dp", self.bit)
+        self.bit *= 2
+
+    def absorb(self, got):
+        self.pending, self.got = None, got
+        if self.bit == lax.axis_size("dp"):
+            self.value = (self.part + got.astype(f32)).reshape(self.rows, -1)
 
 
 def advance(main, chains):
@@ -732,15 +756,17 @@
         chosen = chosen_of(asked, turn)
         return maps_of(chosen, to_each(wanted_of(asked, chosen)))
 
+    def send_rows(held):
+        found = contract(held, table_low, 1, 0).astype(low_type)
+        return to_each(found.reshape(devices, -1, width)).reshape(-1, width)
+
     def fetch(maps):
         chosen, held = maps
-        found = contract(held, table_low, 1, 0).astype(low_type)
-        found = to_each(found.reshape(devices, -1, width)).reshape(-1, width)
-        return contract(chosen, found, 1, 0)
+        return contract(send_rows(held), chosen, 0, 1)
 
     def give(maps, grads):
         chosen, held = maps
-        sums = contract(chosen, grads.astype(low_type), 0, 0).astype(low_type)
+        sums = contract(chosen, grads.astype(low_type), 0, 1).astype(low_type)
         sums = to_each(sums.reshape(devices, -1, width)).reshape(-1, width)
         return contract(held, sums, 0, 0)
 
@@ -768,18 +794,30 @@
     src_maps = maps_of(src_chosen, asked[:, :src_slots])
     src_found = fetch(src_maps)
     dec_maps = maps_of(dec_chosen, asked[:, src_slots : src_slots + dec_slots])
-    dec_found = fetch(dec_maps)
-
-    order = jnp.stack([side, 1 - side]) if seqs == 2 else jnp.arange(seqs)
-    masked, labels, counts = masked[order], labels[order], counts[order]
+    dec_rows = send_rows(dec_maps[1])
+
+    starts_at = jnp.cumsum(counts) - counts
+    total = jnp.sum(counts)
     rank = jnp.where(masked, jnp.cumsum(masked.astype(jnp.int32), -1) - 1, -1)
-    chosen = rank[:, None, :] == jnp.arange(span)[None, :, None]
-    slot_label = jnp.sum(jnp.where(chosen, labels[:, None, :], 0), -1).reshape(-1)
-    valid = (jnp.arange(span)[None, :] < counts[:, None]).reshape(-1)
+    slot_of = jnp.where(masked, rank + starts_at[:, None], -1)
+    slot_index = jnp.arange(seqs * span)
+    slot_label = jnp.sum(
+        jnp.where(slot_of.reshape(1, -1) == slot_index[:, None], labels.reshape(1, -1), 0), -1
+    )
+    valid = slot_index < total
     targets = jnp.where(valid, slot_label - vocab_base, -1).reshape(1, -1)
-    plan = chunk_plan(counts, span)
-    own_segment = 0 if seqs == 2 else side
-    own_chosen = pick(chosen, 0, own_segment).astype(low_type)
+    plan = jnp.concatenate([chunk_plan(total), lax.axis_index("dp")[None] & 1]).astype(jnp.int32)
+    own_rank, own_slot = pick(rank, 0, side), pick(slot_of, 0, side)
+
+    def packing(slots, rows):
+        slot, index = jnp.arange(slots), jnp.arange(rows)
+        far_start, far_count = pick(starts_at, 0, 1 - side), pick(counts, 0, 1 - side)
+        far = jnp.where(index < far_count, index + far_start, -1)
+        return (
+            (own_rank[None, :] == index[:, None]).astype(low_type),
+            (own_slot[None, :] == slot[:, None]).astype(low_type),
+            (far[None, :] == slot[:, None]).astype(low_type),
+        )
 
     own_places = offset + jnp.arange(span)
     src_start, src_length = pick(src_starts, 0, row), pick(src_lengths, 0, row)
@@ -796,9 +834,7 @@
 
     root = math.sqrt(width)
     src_found = later_rounds(src_rounds, src_found, lambda turn: fetch(round_of(src_ask, turn)))
-    dec_found = later_rounds(dec_rounds, dec_found, lambda turn: fetch(round_of(dec_ask, turn)))
     stream0 = src_found * root + src_wave
-    target0 = dec_found * root + tgt_wave
 
     def norm(stream, index):
         return layer_norm(stream, gains[index], biases[index])
@@ -816,53 +852,53 @@
         )
 
     def self_attention(inner, weight_in, weight_out, spans):
-        triple = contract(weight_in, inner, 0, 1).astype(low_type)
+        triple = contract(weight_in, inner, 0, 0).astype(low_type)
         keys = triple if group == 1 else keys_of_row(triple[width:])
         mixed, lse = attend_forward(triple, keys, group == 1, *spans)
-        return contract(mixed, weight_out, 0, 0), (triple, keys, mixed, lse)
+        return contract(weight_out, mixed, 0, 0), (triple, keys, mixed, lse)
 
     def self_attention_back(inner, weight_in, weight_out, spans, kept, grad):
         triple, keys, mixed, lse = kept
         grad_low = grad.astype(low_type)
-        d_out = contract(mixed, grad_low, 1, 0)
-        d_mixed = contract(weight_out, grad_low, 1, 1).astype(low_type)
+        d_out = contract(mixed, grad_low, 1, 1)
+        d_mixed = contract(weight_out, grad_low, 1, 0).astype(low_type)
         d_query, d_keys = attend_backward(triple, keys, group == 1, *spans, lse, d_mixed)
         d_triple = jnp.concatenate([d_query, keys_to_place(d_keys)], 0)
-        return contract(d_triple, weight_in, 0, 1), contract(inner, d_triple, 0, 1), d_out
+        return contract(weight_in, d_triple, 1, 0), contract(inner, d_triple, 1, 1), d_out
 
     def cross_attention(inner, memory, weight_in, weight_out, spans):
-        queries = contract(weight_in[:, :width], inner, 0, 1).astype(low_type)
-        keys = keys_of_row(contract(weight_in[:, width:], memory, 0, 1).astype(low_type))
+        queries = contract(weight_in[:, :width], inner, 0, 0).astype(low_type)
+        keys = keys_of_row(contract(weight_in[:, width:], memory, 0, 0).astype(low_type))
         mixed, lse = attend_forward(queries, keys, False, *spans)
-        return contract(mixed, weight_out, 0, 0), (queries, keys, mixed, lse)
+        return contract(weight_out, mixed, 0, 0), (queries, keys, mixed, lse)
 
     def cross_attention_back(inner, memory, weight_in, weight_out, spans, kept, grad):
         queries, keys, mixed, lse = kept
         grad_low = grad.astype(low_type)
-        d_out = contract(mixed, grad_low, 1, 0)
-        d_mixed = contract(weight_out, grad_low, 1, 1).astype(low_type)
+        d_out = contract(mixed, grad_low, 1, 1)
+        d_mixed = contract(weight_out, grad_low, 1, 0).astype(low_type)
         d_query, d_keys = attend_backward(queries, keys, False, *spans, lse, d_mixed)
         d_keys = keys_to_place(d_keys)
-        d_in = jnp.concatenate([contract(inner, d_query, 0, 1), contract(memory, d_keys, 0, 1)], 1)
+        d_in = jnp.concatenate([contract(inner, d_query, 1, 1), contract(memory, d_keys, 1, 1)], 1)
         return (
-            contract(d_query, weight_in[:, :width], 0, 1),
-            contract(d_keys, weight_in[:, width:], 0, 1),
+            contract(weight_in[:, :width], d_query, 1, 0),
+            contract(weight_in[:, width:], d_keys, 1, 0),
             d_in,
             d_out,
         )
 
     def ffn(inner, weight_one, weight_two):
-        hidden = contract(inner, weight_one, 1, 0)
+        hidden = contract(weight_one, inner, 0, 0)
         active = jax.nn.gelu(hidden).astype(low_type)
-        return contract(active, weight_two, 1, 0), (hidden, active)
+        return contract(weight_two, active, 0, 0), (hidden, active)
 
     def ffn_back(inner, weight_one, weight_two, kept, grad):
         hidden, active = kept
         grad_low = grad.astype(low_type)
-        d_two = contract(active, grad_low, 0, 0)
-        d_active = contract(grad_low, weight_two, 1, 1)
+        d_two = contract(active, grad_low, 1, 1)
+        d_active = contract(weight_two, grad_low, 1, 0)
         d_hidden = jax.vjp(jax.nn.gelu, hidden)[1](d_active)[0].astype(low_type)
-        return contract(d_hidden, weight_one, 1, 1), contract(inner, d_hidden, 0, 0), d_two
+        return contract(weight_one, d_hidden, 1, 0), contract(inner, d_hidden, 1, 1), d_two
 
     inner0 = norm(stream0, 0).astype(low_type)
     branch0, keep0 = self_attention(inner0, w_in0, w_out0, enc_spans)
@@ -871,6 +907,10 @@
     branch1, keep1 = ffn(inner1, f_in0, f_out0)
     stream2 = stream1 + branch1
     memory = norm(stream2, 2).astype(low_type)
+    memory, dec_chosen = lax.optimization_barrier((memory, dec_maps[0]))
+    dec_found = contract(dec_rows, dec_chosen, 0, 1)
+    dec_found = later_rounds(dec_rounds, dec_found, lambda turn: fetch(round_of(dec_ask, turn)))
+    target0 = dec_found * root + tgt_wave
     inner3 = norm(target0, 3).astype(low_type)
     branch3, keep3 = self_attention(inner3, w_in1, w_out1, self_spans)
     target1 = target0 + branch3
@@ -882,51 +922,61 @@
     target3 = target2 + branch5
     final = norm(target3, 6).astype(low_type)
 
-    packed = contract(own_chosen, final, 1, 0).astype(low_type)
+    def pack(slots, rows):
+        own_chosen, own_slots, far_slots = packing(slots, rows)
+        far = swap(contract(own_chosen, final, 1, 1).astype(low_type), "seq", 1)
+        packed = contract(own_slots, final, 1, 1) + contract(far_slots, far, 1, 0)
+        return jnp.pad(packed.astype(low_type), ((0, seqs * span - slots), (0, 0)))
+
+    def unpack(slots, rows):
+        own_chosen, own_slots, far_slots = packing(slots, rows)
+        high = lax.reduce_precision(d_pieces[:slots], 8, 7)
+        rest = (d_pieces[:slots] - high).astype(low_type)
+        high = high.astype(low_type)
+        far = swap(contract(far_slots, high, 0, 0).astype(low_type), "seq", 1)
+        return (
+            contract(high, own_slots, 0, 0)
+            + contract(rest, own_slots, 0, 0)
+            + contract(far, own_chosen, 0, 0)
+        )
+
     if seqs == 2:
-        pieces = jnp.concatenate([packed, swap_rows(packed, cut, more)], 0)
+        pieces = lax.cond(
+            more, lambda: pack(2 * span, span), lambda: pack(min(2 * cut, 2 * span), cut)
+        )
     else:
-        pieces = lax.all_gather(packed, "seq", axis=0, tiled=True)
-    stats = head_stats(plan, table_part, pieces)
-    if seqs == 2:
-        every = jnp.stack([stats, jnp.roll(swap(stats, "seq", 1), span, 1)])
-    else:
-        every = lax.all_gather(stats, "seq", axis=0)
+        own_slots = packing(seqs * span, span)[1]
+        pieces = lax.psum(contract(own_slots, final, 1, 1), "seq").astype(low_type)
+    turned = pieces.T
+    every = gather_seq(head_stats(plan, table_part, turned), 0)
     top_logit = jnp.max(every[:, 0], 0)
     totals = jnp.sum(every[:, 1] * jnp.exp(every[:, 0] - top_logit[None]), 0)
     log_total = top_logit + jnp.log(jnp.where(valid, totals, 1.0))
-    own_logs = pick(jnp.where(valid, log_total, 0.0).reshape(seqs, span), 0, own_segment)
+    own_start = pick(starts_at, 0, side)
+    mine = (slot_index >= own_start) & (slot_index < own_start + pick(counts, 0, side))
+    token_local = jnp.sum(jnp.where(mine, log_total, 0.0))
     logs = jnp.where(valid, log_total + jnp.log(count), 1e30)
     weights = jnp.where(valid, 1.0 / count, 0.0)
-    d_one, d_two, d_pieces, picks = head_back(
-        plan, table_part, pieces, targets, logs[None], weights[None]
-    )
-    token_local = jnp.sum(own_logs) - jnp.sum(picks)
-    table_one = Halving([d_one.reshape(owners, own_words, -1)], False)
-
-    def to_places(first, last):
-        own = lax.dynamic_slice_in_dim(d_pieces, own_segment * span + first, last - first, 0)
-        if seqs == 2:
-            away = d_pieces[span + first : span + last].astype(low_type)
-            own = own + swap(away, "seq", 1).astype(f32)
-        high = lax.reduce_precision(own, 8, 7)
-        rest = (own - high).astype(low_type)
-        chosen_here = own_chosen[first:last]
-        return contract(chosen_here, high.astype(low_type), 0, 0) + contract(chosen_here, rest, 0, 0)
-
+    split = halving_fits(own_words, width // 2, False) and own_words % 8 == 0
+    *d_table, d_pieces, picks = head_back(
+        plan, table_part, pieces, turned, targets, logs[None], weights[None], split and own_words
+    )
+    token_local = token_local - jnp.sum(picks)
+    if split:
+        table_chains = [TableChain(d_table[0], d_table[2])]
     if seqs == 2:
-        d_final = to_places(0, cut)
-        if cut < span:
-            d_final = lax.cond(
-                more, lambda part: part + to_places(cut, span), lambda part: part, d_final
-            )
+        d_final = lax.cond(
+            more, lambda: unpack(2 * span, span), lambda: unpack(min(2 * cut, 2 * span), cut)
+        )
     else:
         d_pieces = lax.psum(d_pieces, "seq")
-        d_final = to_places(0, span)
+        high = lax.reduce_precision(d_pieces, 8, 7)
+        rest = (d_pieces - high).astype(low_type)
+        d_final = contract(high.astype(low_type), own_slots, 0, 0) + contract(rest, own_slots, 0, 0)
 
     first_place = own_places[None, :] == src_start[:, None]
     mine = jnp.any(first_place, -1)
-    first_rows = contract(first_place.astype(low_type), memory, 1, 0).astype(low_type)
+    first_rows = contract(first_place.astype(low_type), memory, 1, 1).astype(low_type)
     len_logits = contract(first_rows, w_len, 1, 0)
     len_label = jnp.minimum(tgt_length, classes - 1)
     len_hot = jnp.arange(classes)[None, :] == len_label[:, None]
@@ -940,8 +990,8 @@
     d_w_len = contract(first_rows, d_len_logits, 0, 0)
     d_first = contract(d_len_logits, w_len, 1, 1)
     d_memory = lax.dot_general(
+        d_first,
         first_place.astype(f32),
-        d_first,
         (((0,), (0,)), ((), ())),
         precision=lax.Precision.HIGHEST,
         preferred_element_type=f32,
@@ -955,56 +1005,56 @@
         return [whole[:, at : at + share] for at in range(0, whole.shape[1], share)]
 
     none = jnp.zeros_like(stream0)
-    d_target3, gain6, bias6 = norm_backward(target3, gains[6], d_final, none)
+    d_target3, scale6 = norm_backward(target3, gains[6], d_final, none)
     d_inner5, d_fin1, d_fout1 = ffn_back(inner5, f_in1, f_out1, keep5, d_target3)
-    chains = [table_one]
-    (d_inner5, d_target3, d_two) = advance((d_inner5, d_target3, d_two), chains)
-    table_two = Halving([d_two.reshape(owners, own_words, -1)], False)
-    chain_a = Halving([owned(d_fin1)] + owned_columns(d_fout1), True)
-    d_target2, gain5, bias5 = norm_backward(target2, gains[5], d_inner5, d_target3)
+    chains = list(table_chains) if split else []
+    d_inner5, d_target3, d_table = advance((d_inner5, d_target3, d_table), chains)
+    if split:
+        table_chains.append(TableChain(d_table[1], d_table[3]))
+    chain_a = LayerChain([owned(d_fin1)] + owned_columns(d_fout1))
+    d_target2, scale5 = norm_backward(target2, gains[5], d_inner5, d_target3)
     d_inner4, d_cross, d_win2, d_wout2 = cross_attention_back(
         inner4, memory, w_in2, w_out2, cross_spans, keep4, d_target2
     )
-    chains += [table_two, chain_a]
+    chains = (table_chains if split else []) + [chain_a]
     d_inner4, d_target2, d_cross = advance((d_inner4, d_target2, d_cross), chains)
-    chain_b = Halving([owned(d_win2), owned(d_wout2)], True)
-    d_target1, gain4, bias4 = norm_backward(target1, gains[4], d_inner4, d_target2)
+    chain_b = LayerChain([owned(d_win2), owned(d_wout2)])
+    d_target1, scale4 = norm_backward(target1, gains[4], d_inner4, d_target2)
     d_inner3, d_win1, d_wout1 = self_attention_back(
         inner3, w_in1, w_out1, self_spans, keep3, d_target1
     )
     chains += [chain_b]
     d_inner3, d_target1 = advance((d_inner3, d_target1), chains)
-    chain_c = Halving([owned(d_win1), owned(d_wout1)], True)
-    d_target0, gain3, bias3 = norm_backward(target0, gains[3], d_inner3, d_target1)
+    chain_c = LayerChain([owned(d_win1), owned(d_wout1)])
+    d_target0, scale3 = norm_backward(target0, gains[3], d_inner3, d_target1)
     dec_grad = d_target0 * root
     dec_given = give(dec_maps, dec_grad)
-    d_stream2, gain2, bias2 = norm_backward(stream2, gains[2], d_memory + d_cross, none)
+    d_stream2, scale2 = norm_backward(stream2, gains[2], d_memory + d_cross, none)
     d_inner1, d_fin0, d_fout0 = ffn_back(inner1, f_in0, f_out0, keep1, d_stream2)
     chains += [chain_c]
     d_inner1, d_stream2 = advance((d_inner1, d_stream2), chains)
-    chain_d = Halving([owned(d_fin0)] + owned_columns(d_fout0), True)
-    d_stream1, gain1, bias1 = norm_backward(stream1, gains[1], d_inner1, d_stream2)
+    chain_d = LayerChain([owned(d_fin0)] + owned_columns(d_fout0))
+    d_stream1, scale1 = norm_backward(stream1, gains[1], d_inner1, d_stream2)
     d_inner0, d_win0, d_wout0 = self_attention_back(
         inner0, w_in0, w_out0, enc_spans, keep0, d_stream1
     )
     chains += [chain_d]
     d_inner0, d_stream1, dec_given = advance((d_inner0, d_stream1, dec_given), chains)
-    d_stream0, gain0, bias0 = norm_backward(stream0, gains[0], d_inner0, d_stream1)
+    d_stream0, scale0 = norm_backward(stream0, gains[0], d_inner0, d_stream1)
     src_grad = d_stream0 * root
     src_given = give(src_maps, src_grad)
-    norm_grads = [gain0, gain1, gain2, gain3, gain4, gain5, gain6]
-    norm_grads += [bias0, bias1, bias2, bias3, bias4, bias5, bias6]
-    g_norms = jnp.sum(lax.all_gather(jnp.stack(norm_grads), ("dp", "seq"), axis=0), 0)
-    norm_square = jnp.where(
-        (side == 0) & (lax.axis_index("dp") == 0), jnp.sum(g_norms * g_norms), 0.0
-    )
+    chain_e = LayerChain([owned(d_win0), owned(d_wout0), owned(d_w_len)])
     norm_share = norms.shape[2]
-    g_norms = lax.dynamic_slice_in_dim(g_norms, lax.axis_index("dp") * norm_share, norm_share, 1)
-    chain_e = Halving([owned(d_win0), owned(d_wout0), owned(d_w_len)], True)
+    scales = jnp.sum(jnp.stack([scale0, scale1, scale2, scale3, scale4, scale5, scale6], 1), 3)
+    scales = scales.reshape(2 * norm_count, owners, norm_share).transpose(1, 0, 2)
+    scales = jnp.broadcast_to(scales[None], (seqs,) + scales.shape)
+    g_norms = jnp.sum(to_each(scales.reshape((devices,) + scales.shape[2:])), 0)
+    norm_square = jnp.where(side == 0, jnp.sum(g_norms * g_norms), 0.0)
     chains += [chain_e]
     while any(chain.pending is not None for chain in chains):
         advance((), chains)
-    for chain in chains:
+    layer_chains = [chain_a, chain_b, chain_c, chain_d, chain_e]
+    for chain in layer_chains:
         chain.finish()
 
     given = dec_given + src_given
@@ -1014,11 +1064,12 @@
         lambda turn: give(round_of(dec_ask, turn), dec_grad)
         + give(round_of(src_ask, turn), src_grad),
     )
-    table_grad = jnp.concatenate(
-        [table_one.value.reshape(own_words, -1), table_two.value.reshape(own_words, -1)], 1
-    )
+    if split:
+        table_grad = jnp.concatenate([chain.value for chain in table_chains], 1)
+    else:
+        table_grad = lax.psum_scatter(d_table[0], "dp", scatter_dimension=0, tiled=True)
     table_grad = table_grad + given
-    square = sum(chain.square for chain in (chain_a, chain_b, chain_c, chain_d, chain_e))
+    square = sum(chain.square for chain in layer_chains)
     square = square + jnp.sum(table_grad * table_grad) + norm_square
     sums = everywhere(
         jnp.stack([token_local, len_local, square]).reshape(1, 3), jnp.add, lax.psum

time: 1190 us -> 1050 us (0.88)
  blocking collectives: 85.6 us -> 0 us
  waiting for transfers between devices: 253 us -> 228 us
  Pallas kernels: 259 us -> 237 us
    all_gather x1 -> x0, blocking collectives: 85.6 us -> none  [on_device(): lax.all_gather(jnp.stack(norm_grads), ('dp', 'seq'), axis=0)]
    ppermute x47 -> x32, starting transfers between devices: 64.6 us -> 32 us  [swap(): return lax.ppermute(values, axis, [(i, i ^ bit) for i in range(size)])]
    ppermute x47 -> x32, waiting for transfers between devices: 110 us -> 86.7 us  [swap(): return lax.ppermute(values, axis, [(i, i ^ bit) for i in range(size)])]
    add x18 -> x3, other arithmetic: 34.5 us -> 11.7 us  [half(): return pick(first, 1, side) + pick(second, 1, side).astype(f32)]
    all_to_all x0 -> x5, starting transfers between devices: none -> 21.2 us  [launch(): self.pending = lax.all_to_all(whole, 'dp', 0, 0, axis_index_groups=groups)]
    convert_element_type x20, other arithmetic: 21.2 us -> 39.7 us  [the longest x9 19.3 us: launch(): away = half(1 - mine).astype(low_type)]
    all_to_all x0 -> x5, waiting for transfers between devices: none -> 14.6 us  [launch(): self.pending = lax.all_to_all(whole, 'dp', 0, 0, axis_index_groups=groups)]
    convert_element_type x10 -> x2, local copies, waits for them, and re-layouts: 14.2 us -> 0.02 us  [on_device(): counts = jnp.sum(masked.astype(jnp.int32), -1)]
  transfers between devices with their start and end apart: 55 -> 46, of which waited for: 20 -> 25; matrix products, arithmetic and copies ran while one was open for 33% -> 36% of each run, Pallas kernels for 13% -> 13%
where the time goes in v4:
time: 1050 us; the launch traced here: 1030 us
  Pallas kernels  237 us (23%)
  waiting for transfers between devices  228 us (22%)
  matrix products  190 us (18%)
  other arithmetic  164 us (16%)
  local copies, waits for them, and re-layouts  97.8 us (9%)
  starting transfers between devices  79.3 us (8%)
  between operations  35 us (3%)
    dot_general x52, matrix products, contract(): lax.dot_general(left, right, (((left_dim,), (right_dim,)), ((), ())), pre...  188 us
    all_to_all x6, waiting for transfers between devices, to_each(): return lax.all_to_all(values, ('seq', 'dp'), 0, 0)  126 us
    ppermute x32, waiting for transfers between devices, swap(): return lax.ppermute(values, axis, [(i, i ^ bit) for i in range(size)])  86.7 us
    pallas_call x3, Pallas kernels, attend_backward(): pl.pallas_call(functools.partial(attend_backward_kernel, head=width // HE...  66.2 us
    pallas_call x1, Pallas kernels, head_back(): pl.pallas_call(functools.partial(head_back_kernel, owned=owned), grid_spe...  64.2 us
    unnamed x417, local copies, waits for them, and re-layouts  52.6 us
    pallas_call x7, Pallas kernels, norm_backward(): pl.pallas_call(norm_back_kernel, grid=(places // columns,), in_specs=[blo...  46.4 us
    pallas_call x3, Pallas kernels, attend_forward(): pl.pallas_call(functools.partial(attend_forward_kernel, head=width // HEA...  36.6 us
  transfers between devices with their start and end apart: 46, of which 25 were waited for; matrix products, arithmetic and copies ran while one was open for 36% of the time, Pallas kernels for 13%

profile of v4, /device:TPU:0, one launch (start us, length us, event | category | flops | bytes accessed | tf_op | source)
XLA Modules:
  0.0 1033.9 jit_solution(12899488742513565240)
XLA Ops:
  25.6 7.3 multiply_sine_fusion
  94.0 46.0 %all-to-all-done.10 = bf16[32,64,512]{2,1,0:T(8,128)(2,1)S(1)} async-done(((bf16[32,64,512]{2,1,0:T(8,128)(2,1)}), bf16[32,64,512]{2,1,0:T(8,128)(2,1)S(1)}, u32[]{:S(2)}, u32[]{:S(2)}) %all-to-all-start.10) | async-done | bytes 2097184 | tf_op jit(solution)/shard_map/all_to_all | solution.py:499
  158.6 11.6 %attend_forward.3 = (bf16[512,1024]{1,0:T(8,128)(2,1)}, f32[8,1024]{1,0:T(8,128)}) custom-call(s32[2,4]{1,0:T(2,128)} %pad_add_fusion.5.bounds, bf16[1536,1024]{1,0:T(8,128)(2,1)} %convolution_convert_fusion.2.q_ref.k_ref.v_ref, bf16[1536,1024]{1,0:T(8,128)(2,1)} %convolution_convert_fusion.2.q_ref.k_ref.v_ref, ...), custom_call_target="tpu_custom_call" | custom-call | tf_op jit(solution)/shard_map/attend_forward/pallas_call | solution.py:191
  175.5 7.7 fusion.138
  187.1 6.7 fusion.339
  198.6 52.4 %all-to-all-done.9 = bf16[32,48,512]{2,1,0:T(8,128)(2,1)} async-done(((bf16[32,48,512]{2,1,0:T(8,128)(2,1)}), bf16[32,48,512]{2,1,0:T(8,128)(2,1)}, u32[]{:S(2)}, u32[]{:S(2)}) %all-to-all-start.9) | async-done | bytes 1572896 | tf_op jit(solution)/shard_map/all_to_all | solution.py:499
  270.6 13.2 %attend_forward.4 = (bf16[512,1024]{1,0:T(8,128)(2,1)}, f32[8,1024]{1,0:T(8,128)}) custom-call(s32[2,4]{1,0:T(2,128)} %pad_add_fusion.6.bounds, bf16[1536,1024]{1,0:T(8,128)(2,1)} %convolution_convert_fusion.1.q_ref.k_ref.v_ref, bf16[1536,1024]{1,0:T(8,128)(2,1)} %convolution_convert_fusion.1.q_ref.k_ref.v_ref, ...), custom_call_target="tpu_custom_call" | custom-call | tf_op jit(solution)/shard_map/attend_forward/pallas_call | solution.py:191
  293.6 11.8 %attend_forward.5 = (bf16[512,1024]{1,0:T(8,128)(2,1)}, f32[8,1024]{1,0:T(8,128)}) custom-call(s32[2,4]{1,0:T(2,128)} %pad_add_fusion.7.bounds, bf16[512,1024]{1,0:T(8,128)(2,1)} %convolution_convert_fusion.8.q_ref, bf16[1024,1024]{1,0:T(8,128)(2,1)} %convolution_convert_fusion.4.k_ref.v_ref, bf16[1024,1024]{1,0:T(8,128)(2,1)} %convolution_convert_fusion.4.k_ref.v_ref, ...), custom_call_target="tpu_custom_call" | custom-call | tf_op jit(solution)/shard_map/attend_forward/pallas_call | solution.py:191
  320.7 15.5 %conditional.2 = (bf16[2048,512]{1,0:T(8,128)(2,1)}) conditional(s32[]{:T(128)} %convert_element_type.550, (s32[1024]{0:T(1024)S(1)}, bf16[512,1024]{1,0:T(8,128)(2,1)}, s32[]{:T(128)}, s32[2]{0:T(128)S(1)}, s32[2]{0:T(128)S(1)}, /*index=5*/s32[1024]{0:T(1024)S(1)}) %tuple.316, (s32[1024]{0:T(1024)S(1)}, bf16[512,1024]{1,0:T(8,128)(2,1)}, ...), branch_computations={%region_59.60_spmd, %region_60.61_spmd} | conditional | flops 5376576512 | bytes 18890878 | solution.py:944
  340.2 23.6 %head_stats.1 = f32[2,2048]{1,0:T(2,128)} custom-call(s32[4]{0:T(128)} %pad_add_fusion.8.plan, bf16[16000,512]{1,0:T(8,128)(2,1)} %all-gather.4.cloned.1.call-done.table_ref, bf16[512,2048]{1,0:T(8,128)(2,1)} %bitcast.713), custom_call_target="tpu_custom_call" | custom-call | tf_op jit(solution)/shard_map/head_stats/pallas_call | solution.py:402
  369.8 64.2 %head_back.1 = (f32[8,1000,256]{2,1,0:T(8,128)}, f32[8,1000,256]{2,1,0:T(8,128)}, bf16[8,1000,256]{2,1,0:T(8,128)(2,1)}, bf16[8,1000,256]{2,1,0:T(8,128)(2,1)}, f32[2048,512]{1,0:T(8,128)}, /*index=5*/f32[8,2048]{1,0:T(8,128)}) custom-call(s32[4]{0:T(128)} %pad_add_fusion.8.plan, bf16[16000,512]{1,0:T(8,128)(2,1)} %all-gather.4.cloned.1.call-done.table_ref, ...), custom_call_target="tpu_custom_call" | custom-call | tf_op jit(solution)/shard_map/head_back/pallas_call | solution.py:434
  434.1 18.8 %conditional.3 = (f32[512,1024]{1,0:T(8,128)}) conditional(s32[]{:T(128)} %convert_element_type.550, (s32[1024]{0:T(1024)S(1)}, f32[2048,512]{1,0:T(8,128)}, s32[]{:T(128)}, s32[2]{0:T(128)S(1)}, s32[2]{0:T(128)S(1)}, /*index=5*/s32[1024]{0:T(1024)S(1)}) %tuple.318, (s32[1024]{0:T(1024)S(1)}, f32[2048,512]{1,0:T(8,128)}, s32[]{:T(128)}, ...), branch_computations={%region_73.74_spmd, %region_74.75_spmd} | conditional | flops 7532448768 | bytes 50352280 | solution.py:968
  455.2 11.4 %norm_backward.7 = (f32[512,1024]{1,0:T(8,128)}, f32[2,512,128]{2,1,0:T(8,128)}) custom-call(f32[512,1024]{1,0:T(8,128)} %copy-done.10, f32[512,1]{1,0:T(8,128)} %get-tuple-element.1127.gain_ref, f32[512,1024]{1,0:T(8,128)S(1)} %copy-done.21, f32[512,1024]{1,0:T(8,128)} %broadcast_in_dim.407.rest_ref), custom_call_target="tpu_custom_call" | custom-call | tf_op jit(solution)/shard_map/norm_backward/pallas_call | solution.py:271
  466.6 9.6 fusion.95
  502.9 5.8 norm_backward.8
  512.2 21.3 %attend_backward.3 = (bf16[512,1024]{1,0:T(8,128)(2,1)}, bf16[1024,1024]{1,0:T(8,128)(2,1)}) custom-call(s32[2,4]{1,0:T(2,128)} %pad_add_fusion.7.bounds, bf16[512,1024]{1,0:T(8,128)(2,1)} %convolution_convert_fusion.8.q_ref, bf16[1024,1024]{1,0:T(8,128)(2,1)} %convolution_convert_fusion.4.k_ref.v_ref, ...), custom_call_target="tpu_custom_call" | custom-call | tf_op jit(solution)/shard_map/attend_backward/pallas_call | solution.py:216
  551.9 6.0 norm_backward.9
  557.9 9.6 fusion.88
  567.5 7.0 fusion.199
  585.5 5.8 norm_backward.10
  597.9 24.2 %attend_backward.4 = (bf16[512,1024]{1,0:T(8,128)(2,1)}, bf16[1024,1024]{1,0:T(8,128)(2,1)}) custom-call(s32[2,4]{1,0:T(2,128)} %pad_add_fusion.6.bounds, bf16[1536,1024]{1,0:T(8,128)(2,1)} %convolution_convert_fusion.1.q_ref.k_ref.v_ref, bf16[1536,1024]{1,0:T(8,128)(2,1)} %convolution_convert_fusion.1.q_ref.k_ref.v_ref, ...), custom_call_target="tpu_custom_call" | custom-call | tf_op jit(solution)/shard_map/attend_backward/pallas_call | solution.py:216
  625.5 7.4 bitcast_add_fusion.4
  663.1 17.3 %collective-permute-done.11 = bf16[4,1000,256]{2,1,0:T(8,128)(2,1)S(1)} collective-permute-done((bf16[4,1000,256]{2,1,0:T(8,128)(2,1)S(1)}, bf16[4,1000,256]{2,1,0:T(8,128)(2,1)S(1)}, u32[]{:S(2)}, u32[]{:S(2)}) %collective-permute-start.11) | collective-permute-done | bytes 2048032 | tf_op jit(solution)/shard_map/ppermute | solution.py:466
  690.1 6.6 fusion.136.grad_ref
  706.0 5.8 norm_backward.12
  718.9 20.6 %collective-permute-done.14 = bf16[1,1000,256]{2,1,0:T(8,128)(2,1)} collective-permute-done((bf16[1,1000,256]{2,1,0:T(8,128)(2,1)}, bf16[1,1000,256]{2,1,0:T(8,128)(2,1)}, u32[]{:S(2)}, u32[]{:S(2)}) %collective-permute-start.14) | collective-permute-done | bytes 512032 | tf_op jit(solution)/shard_map/ppermute | solution.py:466
  748.2 6.1 all-to-all-start.12
  767.5 20.8 %attend_backward.5 = (bf16[512,1024]{1,0:T(8,128)(2,1)}, bf16[1024,1024]{1,0:T(8,128)(2,1)}) custom-call(s32[2,4]{1,0:T(2,128)} %pad_add_fusion.5.bounds, bf16[1536,1024]{1,0:T(8,128)(2,1)} %convolution_convert_fusion.2.q_ref.k_ref.v_ref, bf16[1536,1024]{1,0:T(8,128)(2,1)} %convolution_convert_fusion.2.q_ref.k_ref.v_ref, ...), custom_call_target="tpu_custom_call" | custom-call | tf_op jit(solution)/shard_map/attend_backward/pallas_call | solution.py:216
  846.0 9.7 collective-permute-done.22
  911.9 9.5 all-to-all-done.16
  961.0 15.0 %all-to-all-done.17 = bf16[32,64,512]{2,1,0:T(8,128)(2,1)} async-done(((bf16[32,64,512]{2,1,0:T(8,128)(2,1)}), bf16[32,64,512]{2,1,0:T(8,128)(2,1)}, u32[]{:S(2)}, u32[]{:S(2)}) %all-to-all-start.17) | async-done | bytes 2097184 | tf_op jit(solution)/shard_map/all_to_all | solution.py:499
  1011.2 7.2 multiply_subtract_fusion
  (816 shorter events, 527.4 us)
Async XLA Ops:
  7.2 143.0 %all-gather.6.cloned.1.call-start = ((), (), s32[]{:S(2)}) async-start(), calls=%async_computation.20 | async-start | bytes 6893568 | tf_op jit(solution)/shard_map/all_gather | solution.py:686
  18.6 247.1 %all-gather.8.cloned.1.call-start = ((), (), s32[]{:S(2)}) async-start(), calls=%async_computation.21 | async-start | bytes 8650752 | tf_op jit(solution)/shard_map/all_gather | solution.py:686
  20.4 319.8 %all-gather.4.cloned.1.call-start = ((), (), s32[]{:S(2)}) async-start(), calls=%async_computation.19 | async-start | bytes 17408000 | tf_op jit(solution)/shard_map/all_gather | solution.py:711
  72.5 67.5 %all-to-all-start.10 = ((bf16[32,64,512]{2,1,0:T(8,128)(2,1)}), bf16[32,64,512]{2,1,0:T(8,128)(2,1)S(1)}, u32[]{:S(2)}, u32[]{:S(2)}) async-start(bf16[32,64,512]{2,1,0:T(8,128)(2,1)} %bitcast.768), calls=%async_computation.10 | async-start | bytes 4194304 | tf_op jit(solution)/shard_map/all_to_all | solution.py:499
  183.3 67.8 %all-to-all-start.9 = ((bf16[32,48,512]{2,1,0:T(8,128)(2,1)}), bf16[32,48,512]{2,1,0:T(8,128)(2,1)}, u32[]{:S(2)}, u32[]{:S(2)}) async-start(bf16[32,48,512]{2,1,0:T(8,128)(2,1)} %bitcast.800), calls=%async_computation.9 | async-start | bytes 3145728 | tf_op jit(solution)/shard_map/all_to_all | solution.py:499
  476.2 21.7 %collective-permute-start.6 = (bf16[8,1000,256]{2,1,0:T(8,128)(2,1)S(1)}, bf16[8,1000,256]{2,1,0:T(8,128)(2,1)S(1)}, u32[]{:S(2)}, u32[]{:S(2)}) collective-permute-start(bf16[8,1000,256]{2,1,0:T(8,128)(2,1)S(1)} %copy-done.182), channel_id=1, source_target_pairs={{0,2},{2,0},{4,6},{6,4},{8,10},{10,8},{12,14},{14,12},{16,18},{18,... | collective-permute-start | bytes 12288008 | tf_op jit(solution)/shard_map/ppermute | solution.py:466
  489.7 57.8 %collective-permute-start.9 = (bf16[8,32,4096]{2,1,0:T(8,128)(2,1)}, bf16[8,32,4096]{2,1,0:T(8,128)(2,1)}, u32[]{:S(2)}, u32[]{:S(2)}) collective-permute-start(bf16[8,32,4096]{2,1,0:T(8,128)(2,1)} %fusion.224), channel_id=1, source_target_pairs={{0,2},{2,0},{4,6},{6,4},{8,10},{10,8},{12,14},{14,12},{16,18},{18,... | collective-permute-start | bytes 6291464 | tf_op jit(solution)/shard_map/ppermute | solution.py:466
  498.0 52.2 %collective-permute-start.8 = (bf16[8,1000,256]{2,1,0:T(8,128)(2,1)}, bf16[8,1000,256]{2,1,0:T(8,128)(2,1)}, u32[]{:S(2)}, u32[]{:S(2)}) collective-permute-start(bf16[8,1000,256]{2,1,0:T(8,128)(2,1)} %get-tuple-element.766), channel_id=1, source_target_pairs={{0,2},{2,0},{4,6},{6,4},{8,10},{10,8},{12,14},{14,12},{16,18},{18,... | collective-permute-start | bytes 12288008 | tf_op jit(solution)/shard_map/ppermute | solution.py:466
  502.9 47.3 %collective-permute-start.7 = (bf16[4,1000,256]{2,1,0:T(8,128)(2,1)}, bf16[4,1000,256]{2,1,0:T(8,128)(2,1)}, u32[]{:S(2)}, u32[]{:S(2)}) collective-permute-start(bf16[4,1000,256]{2,1,0:T(8,128)(2,1)} %get-tuple-element.1086), channel_id=1, source_target_pairs={{0,4},{2,6},{4,0},{6,2},{8,12},{10,14},{12,8},{14,10},{16,20},{18,... | collective-permute-start | bytes 6144008 | tf_op jit(solution)/shard_map/ppermute | solution.py:466
  539.5 119.5 %collective-permute-start.13 = (bf16[8,32,2048]{2,1,0:T(8,128)(2,1)}, bf16[8,32,2048]{2,1,0:T(8,128)(2,1)}, u32[]{:S(2)}, u32[]{:S(2)}) collective-permute-start(bf16[8,32,2048]{2,1,0:T(8,128)(2,1)} %pad_maximum_fusion.7), channel_id=1, source_target_pairs={{0,2},{2,0},{4,6},{6,4},{8,10},{10,8},{12,14},{14,12},{16,18},{18,... | collective-permute-start | bytes 3145736 | tf_op jit(solution)/shard_map/ppermute | solution.py:466
  585.5 235.1 %collective-permute-start.21 = (bf16[8,32,4096]{2,1,0:T(8,128)(2,1)}, bf16[8,32,4096]{2,1,0:T(8,128)(2,1)}, u32[]{:S(2)}, u32[]{:S(2)}) collective-permute-start(bf16[8,32,4096]{2,1,0:T(8,128)(2,1)} %fusion.232), channel_id=1, source_target_pairs={{0,2},{2,0},{4,6},{6,4},{8,10},{10,8},{12,14},{14,12},{16,18},{18,... | collective-permute-start | bytes 6291464 | tf_op jit(solution)/shard_map/ppermute | solution.py:466
  625.5 37.7 %collective-permute-start.12 = (bf16[8,16,4096]{2,1,0:T(8,128)(2,1)S(1)}, bf16[8,16,4096]{2,1,0:T(8,128)(2,1)S(1)}, u32[]{:S(2)}, u32[]{:S(2)}) collective-permute-start(bf16[8,16,4096]{2,1,0:T(8,128)(2,1)S(1)} %fusion.150), channel_id=1, source_target_pairs={{0,1},{1,0},{2,3},{3,2},{4,5},{5,4},{6,7},{7,6},{8,9},{9,8},{10,11... | collective-permute-start | bytes 3145736 | tf_op jit(solution)/shard_map/ppermute | solution.py:466
  633.0 47.4 %collective-permute-start.11 = (bf16[4,1000,256]{2,1,0:T(8,128)(2,1)S(1)}, bf16[4,1000,256]{2,1,0:T(8,128)(2,1)S(1)}, u32[]{:S(2)}, u32[]{:S(2)}) collective-permute-start(bf16[4,1000,256]{2,1,0:T(8,128)(2,1)S(1)} %get-tuple-element.1084), channel_id=1, source_target_pairs={{0,4},{2,6},{4,0},{6,2},{8,12},{10,14},{12,8},{14,10},{16,20},{18,... | collective-permute-start | bytes 6144008 | tf_op jit(solution)/shard_map/ppermute | solution.py:466
  638.9 24.3 %collective-permute-start.10 = (bf16[2,1000,256]{2,1,0:T(8,128)(2,1)S(1)}, bf16[2,1000,256]{2,1,0:T(8,128)(2,1)S(1)}, u32[]{:S(2)}, u32[]{:S(2)}) collective-permute-start(bf16[2,1000,256]{2,1,0:T(8,128)(2,1)S(1)} %get-tuple-element.1095), channel_id=1, source_target_pairs={{0,8},{2,10},{4,12},{6,14},{8,0},{10,2},{12,4},{14,6},{16,24},{18,... | collective-permute-start | bytes 3072008 | tf_op jit(solution)/shard_map/ppermute | solution.py:466
  659.0 59.9 %collective-permute-start.17 = (bf16[8,32,2048]{2,1,0:T(8,128)(2,1)}, bf16[8,32,2048]{2,1,0:T(8,128)(2,1)}, u32[]{:S(2)}, u32[]{:S(2)}) collective-permute-start(bf16[8,32,2048]{2,1,0:T(8,128)(2,1)} %pad_maximum_fusion.8), channel_id=1, source_target_pairs={{0,2},{2,0},{4,6},{6,4},{8,10},{10,8},{12,14},{14,12},{16,18},{18,... | collective-permute-start | bytes 3145736 | tf_op jit(solution)/shard_map/ppermute | solution.py:466
  684.3 57.7 %all-to-all-start.11 = ((bf16[8,16,4096]{2,1,0:T(8,128)(2,1)}), bf16[8,16,4096]{2,1,0:T(8,128)(2,1)}, u32[]{:S(2)}, u32[]{:S(2)}) async-start(bf16[8,16,4096]{2,1,0:T(8,128)(2,1)} %fusion.127), calls=%async_computation.11 | async-start | bytes 2097152 | tf_op jit(solution)/shard_map/all_to_all | solution.py:528
  698.0 44.0 %collective-permute-start.15 = (bf16[2,1000,256]{2,1,0:T(8,128)(2,1)}, bf16[2,1000,256]{2,1,0:T(8,128)(2,1)}, u32[]{:S(2)}, u32[]{:S(2)}) collective-permute-start(bf16[2,1000,256]{2,1,0:T(8,128)(2,1)} %fusion.173), channel_id=1, source_target_pairs={{0,8},{2,10},{4,12},{6,14},{8,0},{10,2},{12,4},{14,6},{16,24},{18,... | collective-permute-start | bytes 3072008 | tf_op jit(solution)/shard_map/ppermute | solution.py:466
  701.9 37.7 %collective-permute-start.16 = (bf16[8,16,2048]{2,1,0:T(8,128)(2,1)}, bf16[8,16,2048]{2,1,0:T(8,128)(2,1)}, u32[]{:S(2)}, u32[]{:S(2)}) collective-permute-start(bf16[8,16,2048]{2,1,0:T(8,128)(2,1)} %fusion.191), channel_id=1, source_target_pairs={{0,1},{1,0},{2,3},{3,2},{4,5},{5,4},{6,7},{7,6},{8,9},{9,8},{10,11... | collective-permute-start | bytes 1572872 | tf_op jit(solution)/shard_map/ppermute | solution.py:466
  703.7 35.8 %collective-permute-start.14 = (bf16[1,1000,256]{2,1,0:T(8,128)(2,1)}, bf16[1,1000,256]{2,1,0:T(8,128)(2,1)}, u32[]{:S(2)}, u32[]{:S(2)}) collective-permute-start(bf16[1,1000,256]{2,1,0:T(8,128)(2,1)} %fusion.179), channel_id=1, source_target_pairs={{0,16},{2,18},{4,20},{6,22},{8,24},{10,26},{12,28},{14,30},{16,0},... | collective-permute-start | bytes 1536008 | tf_op jit(solution)/shard_map/ppermute | solution.py:466
  744.3 76.3 %collective-permute-start.20 = (bf16[8,16,2048]{2,1,0:T(8,128)(2,1)}, bf16[8,16,2048]{2,1,0:T(8,128)(2,1)}, u32[]{:S(2)}, u32[]{:S(2)}) collective-permute-start(bf16[8,16,2048]{2,1,0:T(8,128)(2,1)} %fusion.192), channel_id=1, source_target_pairs={{0,1},{1,0},{2,3},{3,2},{4,5},{5,4},{6,7},{7,6},{8,9},{9,8},{10,11... | collective-permute-start | bytes 1572872 | tf_op jit(solution)/shard_map/ppermute | solution.py:466
  747.2 73.4 %collective-permute-start.18 = (bf16[1,1000,256]{2,1,0:T(8,128)(2,1)}, bf16[1,1000,256]{2,1,0:T(8,128)(2,1)}, u32[]{:S(2)}, u32[]{:S(2)}) collective-permute-start(bf16[1,1000,256]{2,1,0:T(8,128)(2,1)} %fusion.178), channel_id=1, source_target_pairs={{0,16},{2,18},{4,20},{6,22},{8,24},{10,26},{12,28},{14,30},{16,0},... | collective-permute-start | bytes 1536008 | tf_op jit(solution)/shard_map/ppermute | solution.py:466
  748.2 58.5 %all-to-all-start.12 = ((bf16[32,48,512]{2,1,0:T(8,128)(2,1)}), bf16[32,48,512]{2,1,0:T(8,128)(2,1)}, u32[]{:S(2)}, u32[]{:S(2)}) async-start(bf16[32,48,512]{2,1,0:T(8,128)(2,1)} %bitcast.801), calls=%async_computation.12 | async-start | bytes 3145728 | tf_op jit(solution)/shard_map/all_to_all | solution.py:499
  756.3 64.3 %collective-permute-start.19 = (f32[16,4096]{1,0:T(8,128)}, f32[16,4096]{1,0:T(8,128)}, u32[]{:S(2)}, u32[]{:S(2)}) collective-permute-start(f32[16,4096]{1,0:T(8,128)} %convert_reduce_fusion.3), channel_id=1, source_target_pairs={{0,1},{1,0},{2,3},{3,2},{4,5},{5,4},{6,7},{7,6},{8,9},{9,8},{10,11... | collective-permute-start | bytes 786440 | tf_op jit(solution)/shard_map/ppermute | solution.py:466
  798.0 48.0 %collective-permute-start.24 = (bf16[8,32,2304]{2,1,0:T(8,128)(2,1)}, bf16[8,32,2304]{2,1,0:T(8,128)(2,1)}, u32[]{:S(2)}, u32[]{:S(2)}) collective-permute-start(bf16[8,32,2304]{2,1,0:T(8,128)(2,1)} %pad_maximum_fusion.6), channel_id=1, source_target_pairs={{0,2},{2,0},{4,6},{6,4},{8,10},{10,8},{12,14},{14,12},{16,18},{18,... | collective-permute-start | bytes 3538952 | tf_op jit(solution)/shard_map/ppermute | solution.py:466
  806.7 18.7 %all-to-all-start.13 = ((bf16[8,16,2048]{2,1,0:T(8,128)(2,1)}), bf16[8,16,2048]{2,1,0:T(8,128)(2,1)S(1)}, u32[]{:S(2)}, u32[]{:S(2)}) async-start(bf16[8,16,2048]{2,1,0:T(8,128)(2,1)} %fusion.167), calls=%async_computation.13 | async-start | bytes 1048576 | tf_op jit(solution)/shard_map/all_to_all | solution.py:528
  828.5 27.2 %collective-permute-start.23 = (bf16[8,16,4096]{2,1,0:T(8,128)(2,1)}, bf16[8,16,4096]{2,1,0:T(8,128)(2,1)}, u32[]{:S(2)}, u32[]{:S(2)}) collective-permute-start(bf16[8,16,4096]{2,1,0:T(8,128)(2,1)} %fusion.153), channel_id=1, source_target_pairs={{0,1},{1,0},{2,3},{3,2},{4,5},{5,4},{6,7},{7,6},{8,9},{9,8},{10,11... | collective-permute-start | bytes 3145736 | tf_op jit(solution)/shard_map/ppermute | solution.py:466
  831.3 24.4 %all-to-all-start.14 = ((bf16[8,16,2048]{2,1,0:T(8,128)(2,1)}), bf16[8,16,2048]{2,1,0:T(8,128)(2,1)S(1)}, u32[]{:S(2)}, u32[]{:S(2)}) async-start(bf16[8,16,2048]{2,1,0:T(8,128)(2,1)} %fusion.158), calls=%async_computation.14 | async-start | bytes 1048576 | tf_op jit(solution)/shard_map/all_to_all | solution.py:528
  836.8 18.9 %collective-permute-start.22 = (f32[16,2048]{1,0:T(8,128)S(1)}, f32[16,2048]{1,0:T(8,128)S(1)}, u32[]{:S(2)}, u32[]{:S(2)}) collective-permute-start(f32[16,2048]{1,0:T(8,128)S(1)} %convert_reduce_fusion.6), channel_id=1, source_target_pairs={{0,1},{1,0},{2,3},{3,2},{4,5},{5,4},{6,7},{7,6},{8,9},{9,8},{10,11... | collective-permute-start | bytes 393224 | tf_op jit(solution)/shard_map/ppermute | solution.py:466
  859.5 30.1 %all-to-all-start.15 = ((bf16[8,16,4096]{2,1,0:T(8,128)(2,1)}), bf16[8,16,4096]{2,1,0:T(8,128)(2,1)S(1)}, u32[]{:S(2)}, u32[]{:S(2)}) async-start(bf16[8,16,4096]{2,1,0:T(8,128)(2,1)} %fusion.126), calls=%async_computation.15 | async-start | bytes 2097152 | tf_op jit(solution)/shard_map/all_to_all | solution.py:528
  901.5 19.9 %all-to-all-start.16 = ((bf16[8,16,2304]{2,1,0:T(8,128)(2,1)}), bf16[8,16,2304]{2,1,0:T(8,128)(2,1)S(1)}, u32[]{:S(2)}, u32[]{:S(2)}) async-start(bf16[8,16,2304]{2,1,0:T(8,128)(2,1)} %fusion.147), calls=%async_computation.16 | async-start | bytes 1179648 | tf_op jit(solution)/shard_map/all_to_all | solution.py:528
  922.3 53.8 %all-to-all-start.17 = ((bf16[32,64,512]{2,1,0:T(8,128)(2,1)}), bf16[32,64,512]{2,1,0:T(8,128)(2,1)}, u32[]{:S(2)}, u32[]{:S(2)}) async-start(bf16[32,64,512]{2,1,0:T(8,128)(2,1)} %bitcast.771), calls=%async_computation.17 | async-start | bytes 4194304 | tf_op jit(solution)/shard_map/all_to_all | solution.py:499
  956.7 29.2 %collective-permute-start.33 = (f32[16,2304]{1,0:T(8,128)S(1)}, f32[16,2304]{1,0:T(8,128)}, u32[]{:S(2)}, u32[]{:S(2)}) collective-permute-start(f32[16,2304]{1,0:T(8,128)S(1)} %convert_reduce_fusion.4), channel_id=1, source_target_pairs={{0,1},{1,0},{2,3},{3,2},{4,5},{5,4},{6,7},{7,6},{8,9},{9,8},{10,11... | collective-permute-start | bytes 442376 | tf_op jit(solution)/shard_map/ppermute | solution.py:466
  (202 other events, 2196.1 us)
Sparse Core Ops, SparseCore 0:
  18.7 88.2 all-gather.5
  110.5 83.6 all-gather.7
  196.5 139.6 all-gather.3

commit v5 on v4

--- a/solution.py
+++ b/solution.py
@@ -383,13 +383,10 @@
         out_refs[0][...] = acc[...]
         return
     mine = plan[3]
-    half = width // 2
     keep = pl.ds(pl.multiple_of(mine * owned, 8), owned)
     away = pl.ds(pl.multiple_of((1 - mine) * owned, 8), owned)
-    out_refs[0][0] = acc[keep, :half]
-    out_refs[1][0] = acc[keep, half:]
-    out_refs[2][0] = acc[away, :half].astype(low_type)
-    out_refs[3][0] = acc[away, half:].astype(low_type)
+    out_refs[0][0] = acc[keep, :]
+    out_refs[1][0] = acc[away, :].astype(low_type)
 
 
 def word_block(words):
@@ -421,13 +418,11 @@
     total = table_part.shape[0]
     words = 2 * owned if owned else word_block(total)
     places, width = rows.shape
-    half = width // 2
     row = pl.BlockSpec((1, places), lambda i, *_: (0, 0))
     if owned:
-        share = pl.BlockSpec((1, owned, half), lambda i, *_: (i, 0, 0))
-        out_specs = [share] * 4
-        shape = (total // words, owned, half)
-        out_shape = [jax.ShapeDtypeStruct(shape, t) for t in (f32, f32, low_type, low_type)]
+        out_specs = [pl.BlockSpec((1, owned, width), lambda i, *_: (i, 0, 0))] * 2
+        shape = (total // words, owned, width)
+        out_shape = [jax.ShapeDtypeStruct(shape, f32), jax.ShapeDtypeStruct(shape, low_type)]
     else:
         out_specs = [pl.BlockSpec((words, width), lambda i, *_: (i, 0))]
         out_shape = [jax.ShapeDtypeStruct((total, width), f32)]
@@ -468,19 +463,6 @@
 
 def power_of_two(size):
     return size & (size - 1) == 0
-
-
-def everywhere(values, combine, reduce):
-    for axis in ("dp", "seq"):
-        size = lax.axis_size(axis)
-        if power_of_two(size):
-            bit = 1
-            while bit < size:
-                values = combine(values, swap(values, axis, bit))
-                bit *= 2
-        else:
-            values = reduce(values, axis)
-    return values
 
 
 def pick(values, dim, index):
@@ -678,6 +660,13 @@
     def columns_of(weight, rows):
         return [weight[at : at + rows] for at in range(0, weight.shape[0], rows)]
 
+    def cut_parts(whole, parts):
+        result, at = [], 0
+        for part in parts:
+            result.append(whole[:, at : at + part.shape[1]])
+            at += part.shape[1]
+        return result
+
     def gather_columns(parts):
         joined = jnp.concatenate([part.astype(low_type) for part in parts], 1)
         if joined.shape[0] % (16 * seqs) == 0:
@@ -686,11 +675,28 @@
             whole = lax.all_gather(joined, ("dp", "seq"), axis=0, tiled=True)
         else:
             whole = lax.all_gather(joined, "dp", axis=0, tiled=True)
-        result, at = [], 0
-        for part in parts:
-            result.append(whole[:, at : at + part.shape[1]])
-            at += part.shape[1]
-        return result
+        return cut_parts(whole, parts)
+
+    def gather_by_swaps(parts, after):
+        if seqs != 2 or share % 32 or not power_of_two(owners):
+            return gather_columns(parts)
+        joined = jnp.concatenate([part.astype(low_type) for part in parts], 1)
+        rows = share // 2
+        part = lax.dynamic_slice_in_dim(joined, side * rows, rows, 0)
+        part = lax.optimization_barrier((part, after))[0]
+        bits = []
+        bit = owners // 2
+        while bit > 1:
+            bits.append(bit)
+            bit //= 2
+        index = lax.axis_index("dp")
+        steps = [("dp", bit, at) for at, bit in enumerate(bits)]
+        steps += [("seq", 1, len(bits)), ("dp", 1, len(bits))]
+        for axis, bit, at in steps:
+            other = swap(part, axis, bit)
+            first = (lax.axis_index(axis) // bit) & 1 == 0
+            part = jnp.stack([jnp.where(first, part, other), jnp.where(first, other, part)], at)
+        return cut_parts(part.reshape(-1, part.shape[-1]), parts)
 
     def join_rows(pieces):
         blocks = [piece.reshape(owners, -1, piece.shape[1]) for piece in pieces]
@@ -705,8 +711,7 @@
     w_in0, w_out0, w_len, norm_low, f_in0, *f_out0 = gather_columns(first_parts)
     next_parts = [attn_in[1], attn_out[1], attn_in[2], attn_out[2], ffn_in[1]]
     next_parts += columns_of(ffn_out[1], share)
-    w_in1, w_out1, w_in2, w_out2, f_in1, *f_out1 = gather_columns(next_parts)
-    f_out0, f_out1 = join_rows(f_out0), join_rows(f_out1)
+    f_out0 = join_rows(f_out0)
     table_low = table.astype(low_type)
     table_part = lax.all_gather(table_low, "dp", axis=0, tiled=True)
     norm_low = norm_low[:, : 2 * norm_count].T.astype(f32)
@@ -764,11 +769,12 @@
         chosen, held = maps
         return contract(send_rows(held), chosen, 0, 1)
 
+    def give_rows(chosen, grads):
+        sums = contract(chosen, grads.astype(low_type), 0, 1).astype(low_type)
+        return to_each(sums.reshape(devices, -1, width)).reshape(-1, width)
+
     def give(maps, grads):
-        chosen, held = maps
-        sums = contract(chosen, grads.astype(low_type), 0, 1).astype(low_type)
-        sums = to_each(sums.reshape(devices, -1, width)).reshape(-1, width)
-        return contract(held, sums, 0, 0)
+        return contract(maps[1], give_rows(maps[0], grads), 0, 0)
 
     def later_rounds(rounds, value, visit):
         return lax.fori_loop(1, rounds, lambda turn, carry: carry + visit(turn), value)
@@ -787,6 +793,8 @@
     asked = [wanted_of(src_ask, src_chosen), wanted_of(dec_ask, dec_chosen), facts]
     asked = to_each(jnp.concatenate(asked, 1).astype(jnp.int32))
     facts = asked[:, src_slots + dec_slots :]
+    w_in1, w_out1, w_in2, w_out2, f_in1, *f_out1 = gather_by_swaps(next_parts, asked)
+    f_out1 = join_rows(f_out1)
     count = jnp.sum(facts[:, 0]).astype(f32)
     cut = -(-(span * 3 // 8) // 128) * 128
     more = jnp.max(facts[:, 1]) > cut
@@ -957,13 +965,12 @@
     token_local = jnp.sum(jnp.where(mine, log_total, 0.0))
     logs = jnp.where(valid, log_total + jnp.log(count), 1e30)
     weights = jnp.where(valid, 1.0 / count, 0.0)
-    split = halving_fits(own_words, width // 2, False) and own_words % 8 == 0
+    split = halving_fits(own_words, width, False)
     *d_table, d_pieces, picks = head_back(
         plan, table_part, pieces, turned, targets, logs[None], weights[None], split and own_words
     )
     token_local = token_local - jnp.sum(picks)
-    if split:
-        table_chains = [TableChain(d_table[0], d_table[2])]
+    table_chain = [TableChain(*d_table)] if split else []
     if seqs == 2:
         d_final = lax.cond(
             more, lambda: unpack(2 * span, span), lambda: unpack(min(2 * cut, 2 * span), cut)
@@ -1007,57 +1014,52 @@
     none = jnp.zeros_like(stream0)
     d_target3, scale6 = norm_backward(target3, gains[6], d_final, none)
     d_inner5, d_fin1, d_fout1 = ffn_back(inner5, f_in1, f_out1, keep5, d_target3)
-    chains = list(table_chains) if split else []
-    d_inner5, d_target3, d_table = advance((d_inner5, d_target3, d_table), chains)
-    if split:
-        table_chains.append(TableChain(d_table[1], d_table[3]))
-    chain_a = LayerChain([owned(d_fin1)] + owned_columns(d_fout1))
+    d_inner5, d_target3 = advance((d_inner5, d_target3), table_chain)
     d_target2, scale5 = norm_backward(target2, gains[5], d_inner5, d_target3)
     d_inner4, d_cross, d_win2, d_wout2 = cross_attention_back(
         inner4, memory, w_in2, w_out2, cross_spans, keep4, d_target2
     )
-    chains = (table_chains if split else []) + [chain_a]
-    d_inner4, d_target2, d_cross = advance((d_inner4, d_target2, d_cross), chains)
-    chain_b = LayerChain([owned(d_win2), owned(d_wout2)])
+    chain_one = LayerChain([owned(d_fin1)] + owned_columns(d_fout1) + [owned(d_win2), owned(d_wout2)])
     d_target1, scale4 = norm_backward(target1, gains[4], d_inner4, d_target2)
     d_inner3, d_win1, d_wout1 = self_attention_back(
         inner3, w_in1, w_out1, self_spans, keep3, d_target1
     )
-    chains += [chain_b]
-    d_inner3, d_target1 = advance((d_inner3, d_target1), chains)
-    chain_c = LayerChain([owned(d_win1), owned(d_wout1)])
+    chains = table_chain + [chain_one]
+    d_inner3, d_target1, d_cross = advance((d_inner3, d_target1, d_cross), chains)
     d_target0, scale3 = norm_backward(target0, gains[3], d_inner3, d_target1)
     dec_grad = d_target0 * root
-    dec_given = give(dec_maps, dec_grad)
+    dec_sums = give_rows(dec_maps[0], dec_grad)
     d_stream2, scale2 = norm_backward(stream2, gains[2], d_memory + d_cross, none)
     d_inner1, d_fin0, d_fout0 = ffn_back(inner1, f_in0, f_out0, keep1, d_stream2)
-    chains += [chain_c]
     d_inner1, d_stream2 = advance((d_inner1, d_stream2), chains)
-    chain_d = LayerChain([owned(d_fin0)] + owned_columns(d_fout0))
+    chain_two = LayerChain([owned(d_win1), owned(d_wout1), owned(d_fin0)] + owned_columns(d_fout0))
     d_stream1, scale1 = norm_backward(stream1, gains[1], d_inner1, d_stream2)
     d_inner0, d_win0, d_wout0 = self_attention_back(
         inner0, w_in0, w_out0, enc_spans, keep0, d_stream1
     )
-    chains += [chain_d]
-    d_inner0, d_stream1, dec_given = advance((d_inner0, d_stream1, dec_given), chains)
+    chains += [chain_two]
+    d_inner0, d_stream1, dec_sums = advance((d_inner0, d_stream1, dec_sums), chains)
     d_stream0, scale0 = norm_backward(stream0, gains[0], d_inner0, d_stream1)
     src_grad = d_stream0 * root
-    src_given = give(src_maps, src_grad)
-    chain_e = LayerChain([owned(d_win0), owned(d_wout0), owned(d_w_len)])
+    src_sums = give_rows(src_maps[0], src_grad)
+    chain_three = LayerChain([owned(d_win0), owned(d_wout0), owned(d_w_len)])
     norm_share = norms.shape[2]
     scales = jnp.sum(jnp.stack([scale0, scale1, scale2, scale3, scale4, scale5, scale6], 1), 3)
     scales = scales.reshape(2 * norm_count, owners, norm_share).transpose(1, 0, 2)
     scales = jnp.broadcast_to(scales[None], (seqs,) + scales.shape)
-    g_norms = jnp.sum(to_each(scales.reshape((devices,) + scales.shape[2:])), 0)
-    norm_square = jnp.where(side == 0, jnp.sum(g_norms * g_norms), 0.0)
-    chains += [chain_e]
+    scales = to_each(scales.reshape((devices,) + scales.shape[2:]))
+    chains += [chain_three]
+    advance((), chains)
+    src_sums, scales = advance((src_sums, scales), chains)
     while any(chain.pending is not None for chain in chains):
         advance((), chains)
-    layer_chains = [chain_a, chain_b, chain_c, chain_d, chain_e]
+    layer_chains = [chain_one, chain_two, chain_three]
     for chain in layer_chains:
         chain.finish()
 
-    given = dec_given + src_given
+    g_norms = jnp.sum(scales, 0)
+    norm_square = jnp.where(side == 0, jnp.sum(g_norms * g_norms), 0.0)
+    given = contract(dec_maps[1], dec_sums, 0, 0) + contract(src_maps[1], src_sums, 0, 0)
     given = later_rounds(
         jnp.maximum(src_rounds, dec_rounds),
         given,
@@ -1065,15 +1067,14 @@
         + give(round_of(src_ask, turn), src_grad),
     )
     if split:
-        table_grad = jnp.concatenate([chain.value for chain in table_chains], 1)
+        table_grad = table_chain[0].value
     else:
         table_grad = lax.psum_scatter(d_table[0], "dp", scatter_dimension=0, tiled=True)
     table_grad = table_grad + given
     square = sum(chain.square for chain in layer_chains)
     square = square + jnp.sum(table_grad * table_grad) + norm_square
-    sums = everywhere(
-        jnp.stack([token_local, len_local, square]).reshape(1, 3), jnp.add, lax.psum
-    )[0]
+    sums = jnp.pad(jnp.stack([token_local, len_local, square]), (0, 5))
+    sums = jnp.sum(to_each(jnp.broadcast_to(sums[None], (devices, 8))), 0)
     token_sum, len_sum, grad_norm = sums[0], sums[1], jnp.sqrt(sums[2])
     factor = jnp.minimum(1.0, clip_limit / (grad_norm + 1e-06))
 
@@ -1089,11 +1090,9 @@
     pieces_out = ffn_out.shape[1] // share
     ffn_sizes = [hidden_width] + [width] * pieces_out
     attn_sizes = [3 * width, width]
-    g_fin1, *g_fout1 = cut_columns(chain_a, ffn_sizes)
-    g_win2, g_wout2 = cut_columns(chain_b, attn_sizes)
-    g_win1, g_wout1 = cut_columns(chain_c, attn_sizes)
-    g_fin0, *g_fout0 = cut_columns(chain_d, ffn_sizes)
-    g_win0, g_wout0, g_len = cut_columns(chain_e, attn_sizes + [classes])
+    g_fin1, *g_fout1, g_win2, g_wout2 = cut_columns(chain_one, ffn_sizes + attn_sizes)
+    g_win1, g_wout1, g_fin0, *g_fout0 = cut_columns(chain_two, attn_sizes + ffn_sizes)
+    g_win0, g_wout0, g_len = cut_columns(chain_three, attn_sizes + [classes])
     grads = (
         jnp.stack([g_win0, g_win1, g_win2]),
         jnp.stack([g_wout0, g_wout1, g_wout2]),

time: 1050 us -> 1190 us (1.13)
  waiting for transfers between devices: 228 us -> 391 us
  Pallas kernels: 237 us -> 213 us
    ppermute x32 -> x22, waiting for transfers between devices: 86.7 us -> 274 us  [swap(): return lax.ppermute(values, axis, [(i, i ^ bit) for i in range(size)])]
    all_to_all x6 -> x7, waiting for transfers between devices: 126 us -> 102 us  [to_each(): return lax.all_to_all(values, ('seq', 'dp'), 0, 0)]
    another operation x8 -> x19, other arithmetic: 4.03 us -> 25.1 us  [the longest x10 19.2 us: gather_by_swaps(): jnp.stack([jnp.where(first, part, other), jnp.where(first, other, part)],...]
    pallas_call x1, Pallas kernels: 64.2 us -> 44.2 us  [head_back(): pl.pallas_call(functools.partial(head_back_kernel, owned=owned), grid_spe...]
    ppermute x32 -> x22, starting transfers between devices: 32 us -> 44.3 us  [swap(): return lax.ppermute(values, axis, [(i, i ^ bit) for i in range(size)])]
    unnamed x417 -> x408, local copies, waits for them, and re-layouts: 52.6 us -> 60.9 us
    all_to_all x6 -> x7, starting transfers between devices: 26.1 us -> 26.4 us  [to_each(): return lax.all_to_all(values, ('seq', 'dp'), 0, 0)]
  transfers between devices with their start and end apart: 46 -> 34, of which waited for: 25 -> 23; matrix products, arithmetic and copies ran while one was open for 36% -> 29% of each run, Pallas kernels for 13% -> 9%
where the time goes in v5:
time: 1190 us; the launch traced here: 1180 us
  waiting for transfers between devices  391 us (33%)
  Pallas kernels  213 us (18%)
  matrix products  193 us (16%)
  other arithmetic  161 us (14%)
  local copies, waits for them, and re-layouts  104 us (9%)
  starting transfers between devices  85.1 us (7%)
  between operations  33.9 us (3%)
    ppermute x22, waiting for transfers between devices, swap(): return lax.ppermute(values, axis, [(i, i ^ bit) for i in range(size)])  274 us
    dot_general x52, matrix products, contract(): lax.dot_general(left, right, (((left_dim,), (right_dim,)), ((), ())), pre...  191 us
    all_to_all x7, waiting for transfers between devices, to_each(): return lax.all_to_all(values, ('seq', 'dp'), 0, 0)  102 us
    pallas_call x3, Pallas kernels, attend_backward(): pl.pallas_call(functools.partial(attend_backward_kernel, head=width // HE...  71.4 us
    unnamed x408, local copies, waits for them, and re-layouts  60.9 us
    ppermute x22, starting transfers between devices, swap(): return lax.ppermute(values, axis, [(i, i ^ bit) for i in range(size)])  44.3 us
    pallas_call x1, Pallas kernels, head_back(): pl.pallas_call(functools.partial(head_back_kernel, owned=owned), grid_spe...  44.2 us
    pallas_call x7, Pallas kernels, norm_backward(): pl.pallas_call(norm_back_kernel, grid=(places // columns,), in_specs=[blo...  40.9 us
  transfers between devices with their start and end apart: 34, of which 23 were waited for; matrix products, arithmetic and copies ran while one was open for 29% of the time, Pallas kernels for 9%

profile of v5, /device:TPU:0, one launch (start us, length us, event | category | flops | bytes accessed | tf_op | source)
XLA Modules:
  0.0 1182.5 jit_solution(6563438667429159462)
XLA Ops:
  25.5 7.3 multiply_sine_fusion
  70.7 27.2 %collective-permute-done.5 = bf16[16,8192]{1,0:T(8,128)(2,1)S(1)} collective-permute-done((bf16[16,8192]{1,0:T(8,128)(2,1)S(1)}, bf16[16,8192]{1,0:T(8,128)(2,1)S(1)}, u32[]{:S(2)}, u32[]{:S(2)}) %collective-permute-start.5) | collective-permute-done | bytes 262176 | tf_op jit(solution)/shard_map/ppermute | solution.py:461
  100.8 10.3 collective-permute-done.6
  115.3 31.7 %collective-permute-done.7 = bf16[2,2,16,8192]{3,2,1,0:T(8,128)(2,1)S(1)} collective-permute-done((bf16[2,2,16,8192]{3,2,1,0:T(8,128)(2,1)S(1)}, bf16[2,2,16,8192]{3,2,1,0:T(8,128)(2,1)S(1)}, u32[]{:S(2)}, u32[]{:S(2)}) %collective-permute-start.7) | collective-permute-done | bytes 1048608 | tf_op jit(solution)/shard_map/ppermute | solution.py:461
  170.4 38.2 %collective-permute-done.8 = bf16[2,2,2,16,8192]{4,3,2,1,0:T(8,128)(2,1)} collective-permute-done((bf16[2,2,2,16,8192]{4,3,2,1,0:T(8,128)(2,1)}, bf16[2,2,2,16,8192]{4,3,2,1,0:T(8,128)(2,1)}, u32[]{:S(2)}, u32[]{:S(2)}) %collective-permute-start.8) | collective-permute-done | bytes 2097184 | tf_op jit(solution)/shard_map/ppermute | solution.py:461
  213.8 50.1 %all-to-all-done.10 = bf16[32,64,512]{2,1,0:T(8,128)(2,1)} async-done(((bf16[32,64,512]{2,1,0:T(8,128)(2,1)}), bf16[32,64,512]{2,1,0:T(8,128)(2,1)}, u32[]{:S(2)}, u32[]{:S(2)}) %all-to-all-start.10) | async-done | bytes 2097184 | tf_op jit(solution)/shard_map/all_to_all | solution.py:481
  282.2 7.4 pad_maximum_fusion
  301.0 13.1 %attend_forward.3 = (bf16[512,1024]{1,0:T(8,128)(2,1)}, f32[8,1024]{1,0:T(8,128)}) custom-call(s32[2,4]{1,0:T(2,128)} %pad_add_fusion.5.bounds, bf16[1536,1024]{1,0:T(8,128)(2,1)} %convolution_convert_fusion.2.q_ref.k_ref.v_ref, bf16[1536,1024]{1,0:T(8,128)(2,1)} %convolution_convert_fusion.2.q_ref.k_ref.v_ref, ...), custom_call_target="tpu_custom_call" | custom-call | tf_op jit(solution)/shard_map/attend_forward/pallas_call | solution.py:191
  316.6 7.7 fusion.139
  339.2 26.9 %all-to-all-done.9 = bf16[32,48,512]{2,1,0:T(8,128)(2,1)S(1)} async-done(((bf16[32,48,512]{2,1,0:T(8,128)(2,1)}), bf16[32,48,512]{2,1,0:T(8,128)(2,1)S(1)}, u32[]{:S(2)}, u32[]{:S(2)}) %all-to-all-start.9) | async-done | bytes 1572896 | tf_op jit(solution)/shard_map/all_to_all | solution.py:481
  380.6 13.3 %attend_forward.4 = (bf16[512,1024]{1,0:T(8,128)(2,1)}, f32[8,1024]{1,0:T(8,128)}) custom-call(s32[2,4]{1,0:T(2,128)} %pad_add_fusion.6.bounds, bf16[1536,1024]{1,0:T(8,128)(2,1)} %convolution_convert_fusion.1.q_ref.k_ref.v_ref, bf16[1536,1024]{1,0:T(8,128)(2,1)} %convolution_convert_fusion.1.q_ref.k_ref.v_ref, ...), custom_call_target="tpu_custom_call" | custom-call | tf_op jit(solution)/shard_map/attend_forward/pallas_call | solution.py:191
  403.7 12.4 %attend_forward.5 = (bf16[512,1024]{1,0:T(8,128)(2,1)}, f32[8,1024]{1,0:T(8,128)}) custom-call(s32[2,4]{1,0:T(2,128)} %pad_add_fusion.7.bounds, bf16[512,1024]{1,0:T(8,128)(2,1)} %convolution_convert_fusion.8.q_ref, bf16[1024,1024]{1,0:T(8,128)(2,1)} %convolution_convert_fusion.4.k_ref.v_ref, bf16[1024,1024]{1,0:T(8,128)(2,1)} %convolution_convert_fusion.4.k_ref.v_ref, ...), custom_call_target="tpu_custom_call" | custom-call | tf_op jit(solution)/shard_map/attend_forward/pallas_call | solution.py:191
  428.3 17.7 %conditional.2 = (bf16[2048,512]{1,0:T(8,128)(2,1)}) conditional(s32[]{:T(128)} %convert_element_type.457, (s32[1024]{0:T(1024)S(1)}, bf16[512,1024]{1,0:T(8,128)(2,1)}, s32[]{:T(128)}, s32[2]{0:T(128)S(1)}, s32[2]{0:T(128)S(1)}, /*index=5*/s32[1024]{0:T(1024)S(1)}) %tuple.319, (s32[1024]{0:T(1024)S(1)}, bf16[512,1024]{1,0:T(8,128)(2,1)}, ...), branch_computations={%region_59.60_spmd, %region_60.61_spmd} | conditional | flops 5376576512 | bytes 18890878 | solution.py:952
  450.5 17.4 %head_stats.1 = f32[2,2048]{1,0:T(2,128)} custom-call(s32[4]{0:T(128)} %pad_add_fusion.8.plan, bf16[16000,512]{1,0:T(8,128)(2,1)} %all-gather.3.cloned.1.call-done.table_ref, bf16[512,2048]{1,0:T(8,128)(2,1)} %bitcast.696), custom_call_target="tpu_custom_call" | custom-call | tf_op jit(solution)/shard_map/head_stats/pallas_call | solution.py:399
  473.9 44.2 %head_back.1 = (f32[8,1000,512]{2,1,0:T(8,128)}, bf16[8,1000,512]{2,1,0:T(8,128)(2,1)}, f32[2048,512]{1,0:T(8,128)}, f32[8,2048]{1,0:T(8,128)}) custom-call(s32[4]{0:T(128)} %pad_add_fusion.8.plan, bf16[16000,512]{1,0:T(8,128)(2,1)} %all-gather.3.cloned.1.call-done.table_ref, bf16[2048,512]{1,0:T(8,128)(2,1)S(1)} %copy-done.14, bf16[512,2048]{1,0:T(8,128)(2,1)} %bitcast.697, ...), custom_call_target="tpu_custom_call" | custom-call | tf_op jit(solution)/shard_map/head_back/pallas_call | solution.py:429
  525.3 21.1 %conditional.3 = (f32[512,1024]{1,0:T(8,128)}) conditional(s32[]{:T(128)} %convert_element_type.457, (s32[1024]{0:T(1024)S(1)}, f32[2048,512]{1,0:T(8,128)}, s32[]{:T(128)}, s32[2]{0:T(128)S(1)}, s32[2]{0:T(128)S(1)}, /*index=5*/s32[1024]{0:T(1024)S(1)}) %tuple.321, (s32[1024]{0:T(1024)S(1)}, f32[2048,512]{1,0:T(8,128)}, s32[]{:T(128)}, ...), branch_computations={%region_73.74_spmd, %region_74.75_spmd} | conditional | flops 7532448768 | bytes 50352280 | solution.py:975
  554.2 9.4 fusion.95
  597.0 23.2 %attend_backward.3 = (bf16[512,1024]{1,0:T(8,128)(2,1)}, bf16[1024,1024]{1,0:T(8,128)(2,1)}) custom-call(s32[2,4]{1,0:T(2,128)} %pad_add_fusion.7.bounds, bf16[512,1024]{1,0:T(8,128)(2,1)} %convolution_convert_fusion.8.q_ref, bf16[1024,1024]{1,0:T(8,128)(2,1)} %convolution_convert_fusion.4.k_ref.v_ref, ...), custom_call_target="tpu_custom_call" | custom-call | tf_op jit(solution)/shard_map/attend_backward/pallas_call | solution.py:216
  633.8 8.0 bitcast_add_fusion.2
  641.8 26.1 %collective-permute-start.12 = (bf16[4,1000,512]{2,1,0:T(8,128)(2,1)}, bf16[4,1000,512]{2,1,0:T(8,128)(2,1)S(1)}, u32[]{:S(2)}, u32[]{:S(2)}) collective-permute-start(bf16[4,1000,512]{2,1,0:T(8,128)(2,1)} %get-tuple-element.1058), channel_id=1, source_target_pairs={{0,4},{2,6},{4,0},{6,2},{8,12},{10,14},{12,8},{14,10},{16,20},{18,... | collective-permute-start | bytes 12288008 | tf_op jit(solution)/shard_map/ppermute | solution.py:461
  677.3 24.3 %attend_backward.4 = (bf16[512,1024]{1,0:T(8,128)(2,1)}, bf16[1024,1024]{1,0:T(8,128)(2,1)}) custom-call(s32[2,4]{1,0:T(2,128)} %pad_add_fusion.6.bounds, bf16[1536,1024]{1,0:T(8,128)(2,1)} %convolution_convert_fusion.1.q_ref.k_ref.v_ref, bf16[1536,1024]{1,0:T(8,128)(2,1)} %convolution_convert_fusion.1.q_ref.k_ref.v_ref, ...), custom_call_target="tpu_custom_call" | custom-call | tf_op jit(solution)/shard_map/attend_backward/pallas_call | solution.py:216
  722.0 35.3 %collective-permute-done.12 = bf16[4,1000,512]{2,1,0:T(8,128)(2,1)S(1)} collective-permute-done((bf16[4,1000,512]{2,1,0:T(8,128)(2,1)}, bf16[4,1000,512]{2,1,0:T(8,128)(2,1)S(1)}, u32[]{:S(2)}, u32[]{:S(2)}) %collective-permute-start.12) | collective-permute-done | bytes 4096032 | tf_op jit(solution)/shard_map/ppermute | solution.py:461
  765.9 11.8 fusion.88
  794.9 6.7 fusion.292
  835.4 17.9 %collective-permute-done.14 = bf16[2,1000,512]{2,1,0:T(8,128)(2,1)} collective-permute-done((bf16[2,1000,512]{2,1,0:T(8,128)(2,1)}, bf16[2,1000,512]{2,1,0:T(8,128)(2,1)}, u32[]{:S(2)}, u32[]{:S(2)}) %collective-permute-start.14) | collective-permute-done | bytes 2048032 | tf_op jit(solution)/shard_map/ppermute | solution.py:461
  857.9 7.7 all-to-all-done.11
  890.4 23.9 %attend_backward.5 = (bf16[512,1024]{1,0:T(8,128)(2,1)}, bf16[1024,1024]{1,0:T(8,128)(2,1)}) custom-call(s32[2,4]{1,0:T(2,128)} %pad_add_fusion.5.bounds, bf16[1536,1024]{1,0:T(8,128)(2,1)} %convolution_convert_fusion.2.q_ref.k_ref.v_ref, bf16[1536,1024]{1,0:T(8,128)(2,1)} %convolution_convert_fusion.2.q_ref.k_ref.v_ref, ...), custom_call_target="tpu_custom_call" | custom-call | tf_op jit(solution)/shard_map/attend_backward/pallas_call | solution.py:216
  924.7 28.2 %collective-permute-done.16 = bf16[1,1000,512]{2,1,0:T(8,128)(2,1)} collective-permute-done((bf16[1,1000,512]{2,1,0:T(8,128)(2,1)S(1)}, bf16[1,1000,512]{2,1,0:T(8,128)(2,1)}, u32[]{:S(2)}, u32[]{:S(2)}) %collective-permute-start.16) | collective-permute-done | bytes 1024032 | tf_op jit(solution)/shard_map/ppermute | solution.py:461
  995.4 57.2 %collective-permute-done.18 = f32[16,6144]{1,0:T(8,128)S(1)} collective-permute-done((f32[16,6144]{1,0:T(8,128)S(1)}, f32[16,6144]{1,0:T(8,128)S(1)}, u32[]{:S(2)}, u32[]{:S(2)}) %collective-permute-start.18) | collective-permute-done | bytes 393248 | tf_op jit(solution)/shard_map/ppermute | solution.py:461
  1082.4 6.8 collective-permute-done.21
  1089.2 11.0 all-to-all-done.15
  1148.5 7.0 all-to-all-done.17
  (768 shorter events, 536.0 us)
Async XLA Ops:
  7.2 285.6 %all-gather.5.cloned.1.call-start = ((), (), s32[]{:S(2)}) async-start(), calls=%async_computation.19 | async-start | bytes 6893568 | tf_op jit(solution)/shard_map/all_gather | solution.py:675
  19.1 431.4 %all-gather.3.cloned.1.call-start = ((), (), s32[]{:S(2)}) async-start(), calls=%async_computation.18 | async-start | bytes 17408000 | tf_op jit(solution)/shard_map/all_gather | solution.py:716
  19.2 17.9 %collective-permute-start.4 = (s32[3,2,512]{2,1,0:T(2,128)S(1)}, s32[3,2,512]{2,1,0:T(2,128)S(1)}, u32[]{:S(2)}, u32[]{:S(2)}) collective-permute-start(s32[3,2,512]{2,1,0:T(2,128)S(1)} %pad_add_fusion), channel_id=1, source_target_pairs={{0,1},{1,0},{2,3},{3,2},{4,5},{5,4},{6,7},{7,6},{8,9},{9,8},{10,11... | collective-permute-start | bytes 36872 | tf_op jit(solution)/shard_map/ppermute | solution.py:461
  57.2 12.0 %all-to-all-start.8 = ((s32[32,1,128]{2,1,0:T(1,128)}), s32[32,1,128]{2,1,0:T(1,128)S(1)}, u32[]{:S(2)}, u32[]{:S(2)}) async-start(s32[32,1,128]{2,1,0:T(1,128)} %bitcast.44), calls=%async_computation.8 | async-start | bytes 32768 | tf_op jit(solution)/shard_map/all_to_all | solution.py:481
  69.2 28.7 %collective-permute-start.5 = (bf16[16,8192]{1,0:T(8,128)(2,1)S(1)}, bf16[16,8192]{1,0:T(8,128)(2,1)S(1)}, u32[]{:S(2)}, u32[]{:S(2)}) collective-permute-start(bf16[16,8192]{1,0:T(8,128)(2,1)S(1)} %constant_dynamic-slice_fusion.20), channel_id=1, source_target_pairs={{0,16},{2,18},{4,20},{6,22},{8,24},{10,26},{12,28},{14,30},{16,0},... | collective-permute-start | bytes 786440 | tf_op jit(solution)/shard_map/ppermute | solution.py:461
  98.0 13.1 %collective-permute-start.6 = (bf16[2,16,8192]{2,1,0:T(8,128)(2,1)S(1)}, bf16[2,16,8192]{2,1,0:T(8,128)(2,1)S(1)}, u32[]{:S(2)}, u32[]{:S(2)}) collective-permute-start(bf16[2,16,8192]{2,1,0:T(8,128)(2,1)S(1)} %pad_maximum_fusion.11), channel_id=1, source_target_pairs={{0,8},{2,10},{4,12},{6,14},{8,0},{10,2},{12,4},{14,6},{16,24},{18,... | collective-permute-start | bytes 1572872 | tf_op jit(solution)/shard_map/ppermute | solution.py:461
  111.3 35.6 %collective-permute-start.7 = (bf16[2,2,16,8192]{3,2,1,0:T(8,128)(2,1)S(1)}, bf16[2,2,16,8192]{3,2,1,0:T(8,128)(2,1)S(1)}, u32[]{:S(2)}, u32[]{:S(2)}) collective-permute-start(bf16[2,2,16,8192]{3,2,1,0:T(8,128)(2,1)S(1)} %pad_maximum_fusion.10), channel_id=1, source_target_pairs={{0,4},{2,6},{4,0},{6,2},{8,12},{10,14},{12,8},{14,10},{16,20},{18,... | collective-permute-start | bytes 3145736 | tf_op jit(solution)/shard_map/ppermute | solution.py:461
  148.6 60.0 %collective-permute-start.8 = (bf16[2,2,2,16,8192]{4,3,2,1,0:T(8,128)(2,1)}, bf16[2,2,2,16,8192]{4,3,2,1,0:T(8,128)(2,1)}, u32[]{:S(2)}, u32[]{:S(2)}) collective-permute-start(bf16[2,2,2,16,8192]{4,3,2,1,0:T(8,128)(2,1)} %pad_maximum_fusion.7), channel_id=1, source_target_pairs={{0,1},{1,0},{2,3},{3,2},{4,5},{5,4},{6,7},{7,6},{8,9},{9,8},{10,11... | collective-permute-start | bytes 6291464 | tf_op jit(solution)/shard_map/ppermute | solution.py:461
  157.4 106.4 %all-to-all-start.10 = ((bf16[32,64,512]{2,1,0:T(8,128)(2,1)}), bf16[32,64,512]{2,1,0:T(8,128)(2,1)}, u32[]{:S(2)}, u32[]{:S(2)}) async-start(bf16[32,64,512]{2,1,0:T(8,128)(2,1)} %bitcast.743), calls=%async_computation.10 | async-start | bytes 4194304 | tf_op jit(solution)/shard_map/all_to_all | solution.py:481
  213.8 61.1 %collective-permute-start.9 = (bf16[2,2,2,2,16,8192]{5,4,3,2,1,0:T(8,128)(2,1)}, bf16[2,2,2,2,16,8192]{5,4,3,2,1,0:T(8,128)(2,1)}, u32[]{:S(2)}, u32[]{:S(2)}) collective-permute-start(bf16[2,2,2,2,16,8192]{5,4,3,2,1,0:T(8,128)(2,1)} %pad_maximum_fusion.1), channel_id=1, source_target_pairs={{0,2},{2,0},{4,6},{6,4},{8,10},{10,8},{12,14},{14,12},{16,18},{18,... | collective-permute-start | bytes 12582920 | tf_op jit(solution)/shard_map/ppermute | solution.py:461
  324.4 41.8 %all-to-all-start.9 = ((bf16[32,48,512]{2,1,0:T(8,128)(2,1)}), bf16[32,48,512]{2,1,0:T(8,128)(2,1)S(1)}, u32[]{:S(2)}, u32[]{:S(2)}) async-start(bf16[32,48,512]{2,1,0:T(8,128)(2,1)} %bitcast.47), calls=%async_computation.9 | async-start | bytes 3145728 | tf_op jit(solution)/shard_map/all_to_all | solution.py:481
  430.9 11.7 collective-permute-start.2
  518.2 68.6 %collective-permute-start.11 = (bf16[8,1000,512]{2,1,0:T(8,128)(2,1)}, bf16[8,1000,512]{2,1,0:T(8,128)(2,1)}, u32[]{:S(2)}, u32[]{:S(2)}) collective-permute-start(bf16[8,1000,512]{2,1,0:T(8,128)(2,1)} %get-tuple-element.744), channel_id=1, source_target_pairs={{0,2},{2,0},{4,6},{6,4},{8,10},{10,8},{12,14},{14,12},{16,18},{18,... | collective-permute-start | bytes 24576008 | tf_op jit(solution)/shard_map/ppermute | solution.py:461
  529.7 11.6 collective-permute-start
  632.5 89.5 %collective-permute-start.13 = (bf16[8,32,6144]{2,1,0:T(8,128)(2,1)}, bf16[8,32,6144]{2,1,0:T(8,128)(2,1)}, u32[]{:S(2)}, u32[]{:S(2)}) collective-permute-start(bf16[8,32,6144]{2,1,0:T(8,128)(2,1)} %fusion.210), channel_id=1, source_target_pairs={{0,2},{2,0},{4,6},{6,4},{8,10},{10,8},{12,14},{14,12},{16,18},{18,... | collective-permute-start | bytes 9437192 | tf_op jit(solution)/shard_map/ppermute | solution.py:461
  641.8 115.5 %collective-permute-start.12 = (bf16[4,1000,512]{2,1,0:T(8,128)(2,1)}, bf16[4,1000,512]{2,1,0:T(8,128)(2,1)S(1)}, u32[]{:S(2)}, u32[]{:S(2)}) collective-permute-start(bf16[4,1000,512]{2,1,0:T(8,128)(2,1)} %get-tuple-element.1058), channel_id=1, source_target_pairs={{0,4},{2,6},{4,0},{6,2},{8,12},{10,14},{12,8},{14,10},{16,20},{18,... | collective-permute-start | bytes 12288008 | tf_op jit(solution)/shard_map/ppermute | solution.py:461
  787.0 48.4 %collective-permute-start.15 = (bf16[8,16,6144]{2,1,0:T(8,128)(2,1)}, bf16[8,16,6144]{2,1,0:T(8,128)(2,1)}, u32[]{:S(2)}, u32[]{:S(2)}) collective-permute-start(bf16[8,16,6144]{2,1,0:T(8,128)(2,1)} %fusion.142), channel_id=1, source_target_pairs={{0,1},{1,0},{2,3},{3,2},{4,5},{5,4},{6,7},{7,6},{8,9},{9,8},{10,11... | collective-permute-start | bytes 4718600 | tf_op jit(solution)/shard_map/ppermute | solution.py:461
  793.5 59.9 %collective-permute-start.14 = (bf16[2,1000,512]{2,1,0:T(8,128)(2,1)}, bf16[2,1000,512]{2,1,0:T(8,128)(2,1)}, u32[]{:S(2)}, u32[]{:S(2)}) collective-permute-start(bf16[2,1000,512]{2,1,0:T(8,128)(2,1)} %get-tuple-element.1060), channel_id=1, source_target_pairs={{0,8},{2,10},{4,12},{6,14},{8,0},{10,2},{12,4},{14,6},{16,24},{18,... | collective-permute-start | bytes 6144008 | tf_op jit(solution)/shard_map/ppermute | solution.py:461
  817.6 48.1 %all-to-all-start.11 = ((bf16[32,48,512]{2,1,0:T(8,128)(2,1)}), bf16[32,48,512]{2,1,0:T(8,128)(2,1)}, u32[]{:S(2)}, u32[]{:S(2)}) async-start(bf16[32,48,512]{2,1,0:T(8,128)(2,1)} %bitcast.772), calls=%async_computation.11 | async-start | bytes 3145728 | tf_op jit(solution)/shard_map/all_to_all | solution.py:481
  825.5 127.5 %collective-permute-start.17 = (bf16[8,32,6144]{2,1,0:T(8,128)(2,1)}, bf16[8,32,6144]{2,1,0:T(8,128)(2,1)}, u32[]{:S(2)}, u32[]{:S(2)}) collective-permute-start(bf16[8,32,6144]{2,1,0:T(8,128)(2,1)} %fusion.208), channel_id=1, source_target_pairs={{0,2},{2,0},{4,6},{6,4},{8,10},{10,8},{12,14},{14,12},{16,18},{18,... | collective-permute-start | bytes 9437192 | tf_op jit(solution)/shard_map/ppermute | solution.py:461
  865.6 87.3 %all-to-all-start.12 = ((bf16[8,16,6144]{2,1,0:T(8,128)(2,1)}), bf16[8,16,6144]{2,1,0:T(8,128)(2,1)}, u32[]{:S(2)}, u32[]{:S(2)}) async-start(bf16[8,16,6144]{2,1,0:T(8,128)(2,1)} %fusion.121), calls=%async_computation.12 | async-start | bytes 3145728 | tf_op jit(solution)/shard_map/all_to_all | solution.py:510
  878.2 74.8 %collective-permute-start.16 = (bf16[1,1000,512]{2,1,0:T(8,128)(2,1)S(1)}, bf16[1,1000,512]{2,1,0:T(8,128)(2,1)}, u32[]{:S(2)}, u32[]{:S(2)}) collective-permute-start(bf16[1,1000,512]{2,1,0:T(8,128)(2,1)S(1)} %fusion.132), channel_id=1, source_target_pairs={{0,16},{2,18},{4,20},{6,22},{8,24},{10,26},{12,28},{14,30},{16,0},... | collective-permute-start | bytes 3072008 | tf_op jit(solution)/shard_map/ppermute | solution.py:461
  970.4 11.2 all-to-all-start.14
  981.6 75.8 %all-to-all-start.13 = ((bf16[32,64,512]{2,1,0:T(8,128)(2,1)}), bf16[32,64,512]{2,1,0:T(8,128)(2,1)}, u32[]{:S(2)}, u32[]{:S(2)}) async-start(bf16[32,64,512]{2,1,0:T(8,128)(2,1)} %bitcast.742), calls=%async_computation.13 | async-start | bytes 4194304 | tf_op jit(solution)/shard_map/all_to_all | solution.py:481
  990.7 62.6 %collective-permute-start.19 = (bf16[8,16,6144]{2,1,0:T(8,128)(2,1)S(1)}, bf16[8,16,6144]{2,1,0:T(8,128)(2,1)S(1)}, u32[]{:S(2)}, u32[]{:S(2)}) collective-permute-start(bf16[8,16,6144]{2,1,0:T(8,128)(2,1)S(1)} %fusion.141), channel_id=1, source_target_pairs={{0,1},{1,0},{2,3},{3,2},{4,5},{5,4},{6,7},{7,6},{8,9},{9,8},{10,11... | collective-permute-start | bytes 4718600 | tf_op jit(solution)/shard_map/ppermute | solution.py:461
  994.3 58.3 %collective-permute-start.18 = (f32[16,6144]{1,0:T(8,128)S(1)}, f32[16,6144]{1,0:T(8,128)S(1)}, u32[]{:S(2)}, u32[]{:S(2)}) collective-permute-start(f32[16,6144]{1,0:T(8,128)S(1)} %convert_reduce_fusion.3), channel_id=1, source_target_pairs={{0,1},{1,0},{2,3},{3,2},{4,5},{5,4},{6,7},{7,6},{8,9},{9,8},{10,11... | collective-permute-start | bytes 1179656 | tf_op jit(solution)/shard_map/ppermute | solution.py:461
  1057.5 42.7 %all-to-all-start.15 = ((bf16[8,16,6144]{2,1,0:T(8,128)(2,1)}), bf16[8,16,6144]{2,1,0:T(8,128)(2,1)S(1)}, u32[]{:S(2)}, u32[]{:S(2)}) async-start(bf16[8,16,6144]{2,1,0:T(8,128)(2,1)} %fusion.119), calls=%async_computation.15 | async-start | bytes 3145728 | tf_op jit(solution)/shard_map/all_to_all | solution.py:510
  1074.1 15.1 %collective-permute-start.21 = (bf16[8,16,2304]{2,1,0:T(8,128)(2,1)}, bf16[8,16,2304]{2,1,0:T(8,128)(2,1)}, u32[]{:S(2)}, u32[]{:S(2)}) collective-permute-start(bf16[8,16,2304]{2,1,0:T(8,128)(2,1)} %fusion.166), channel_id=1, source_target_pairs={{0,1},{1,0},{2,3},{3,2},{4,5},{5,4},{6,7},{7,6},{8,9},{9,8},{10,11... | collective-permute-start | bytes 1769480 | tf_op jit(solution)/shard_map/ppermute | solution.py:461
  1112.6 19.9 %all-to-all-start.16 = ((bf16[8,16,2304]{2,1,0:T(8,128)(2,1)}), bf16[8,16,2304]{2,1,0:T(8,128)(2,1)S(1)}, u32[]{:S(2)}, u32[]{:S(2)}) async-start(bf16[8,16,2304]{2,1,0:T(8,128)(2,1)} %fusion.151), calls=%async_computation.16 | async-start | bytes 1179648 | tf_op jit(solution)/shard_map/all_to_all | solution.py:510
  1118.1 10.8 collective-permute-start.22
  1135.3 5.5 collective-permute-start.23
  1145.1 10.4 all-to-all-start.17
  (182 other events, 2237.9 us)
Sparse Core Ops, SparseCore 0:
  19.2 82.5 all-gather.4
  104.1 169.5 all-gather.2

commit v6 on v5

--- a/solution.py
+++ b/solution.py
@@ -550,31 +550,12 @@
             self.square = jnp.where(lax.axis_index("seq") == 0, jnp.sum(part * part), 0.0)
 
 
-class TableChain(Chain):
-    def __init__(self, keep, away):
-        self.part, self.got = keep, None
-        self.rows, self.bit = keep.shape[1], 2
-        self.pending = swap(away, "dp", 1)
-
-    def launch(self):
-        if self.bit == lax.axis_size("dp"):
-            return
-        mine = (lax.axis_index("dp") // self.bit) & 1
-        shape = (-1, 2, self.rows, self.part.shape[2])
-        first, second = self.part.reshape(shape), self.got.reshape(shape)
-
-        def half(side):
-            return pick(first, 1, side) + pick(second, 1, side).astype(f32)
-
-        away = half(1 - mine).astype(low_type)
-        self.part = half(mine)
-        self.pending = swap(away, "dp", self.bit)
-        self.bit *= 2
-
-    def absorb(self, got):
-        self.pending, self.got = None, got
-        if self.bit == lax.axis_size("dp"):
-            self.value = (self.part + got.astype(f32)).reshape(self.rows, -1)
+def table_to_owner(keep, arrived):
+    owners = lax.axis_size("dp")
+    groups = [list(range(core, owners, 2)) for core in range(2)]
+    return lax.psum_scatter(
+        keep + arrived.astype(f32), "dp", scatter_dimension=0, axis_index_groups=groups
+    )
 
 
 def advance(main, chains):
@@ -677,27 +658,6 @@
             whole = lax.all_gather(joined, "dp", axis=0, tiled=True)
         return cut_parts(whole, parts)
 
-    def gather_by_swaps(parts, after):
-        if seqs != 2 or share % 32 or not power_of_two(owners):
-            return gather_columns(parts)
-        joined = jnp.concatenate([part.astype(low_type) for part in parts], 1)
-        rows = share // 2
-        part = lax.dynamic_slice_in_dim(joined, side * rows, rows, 0)
-        part = lax.optimization_barrier((part, after))[0]
-        bits = []
-        bit = owners // 2
-        while bit > 1:
-            bits.append(bit)
-            bit //= 2
-        index = lax.axis_index("dp")
-        steps = [("dp", bit, at) for at, bit in enumerate(bits)]
-        steps += [("seq", 1, len(bits)), ("dp", 1, len(bits))]
-        for axis, bit, at in steps:
-            other = swap(part, axis, bit)
-            first = (lax.axis_index(axis) // bit) & 1 == 0
-            part = jnp.stack([jnp.where(first, part, other), jnp.where(first, other, part)], at)
-        return cut_parts(part.reshape(-1, part.shape[-1]), parts)
-
     def join_rows(pieces):
         blocks = [piece.reshape(owners, -1, piece.shape[1]) for piece in pieces]
         return jnp.concatenate(blocks, 1).reshape(-1, pieces[0].shape[1])
@@ -706,12 +666,15 @@
     norm_part = jnp.pad(
         norms.reshape(-1, norms.shape[2]).T, ((0, 0), (0, norm_columns - 2 * norm_count))
     )
-    first_parts = [attn_in[0], attn_out[0], len_head, norm_part, ffn_in[0]]
-    first_parts += columns_of(ffn_out[0], share)
-    w_in0, w_out0, w_len, norm_low, f_in0, *f_out0 = gather_columns(first_parts)
-    next_parts = [attn_in[1], attn_out[1], attn_in[2], attn_out[2], ffn_in[1]]
-    next_parts += columns_of(ffn_out[1], share)
-    f_out0 = join_rows(f_out0)
+    out_pieces = ffn_out.shape[1] // share
+    parts = [attn_in[0], attn_out[0], len_head, norm_part, ffn_in[0]]
+    parts += columns_of(ffn_out[0], share)
+    parts += [attn_in[1], attn_out[1], attn_in[2], attn_out[2], ffn_in[1]]
+    parts += columns_of(ffn_out[1], share)
+    w_in0, w_out0, w_len, norm_low, f_in0, *others = gather_columns(parts)
+    f_out0 = join_rows(others[:out_pieces])
+    w_in1, w_out1, w_in2, w_out2, f_in1, *f_out1 = others[out_pieces:]
+    f_out1 = join_rows(f_out1)
     table_low = table.astype(low_type)
     table_part = lax.all_gather(table_low, "dp", axis=0, tiled=True)
     norm_low = norm_low[:, : 2 * norm_count].T.astype(f32)
@@ -793,8 +756,6 @@
     asked = [wanted_of(src_ask, src_chosen), wanted_of(dec_ask, dec_chosen), facts]
     asked = to_each(jnp.concatenate(asked, 1).astype(jnp.int32))
     facts = asked[:, src_slots + dec_slots :]
-    w_in1, w_out1, w_in2, w_out2, f_in1, *f_out1 = gather_by_swaps(next_parts, asked)
-    f_out1 = join_rows(f_out1)
     count = jnp.sum(facts[:, 0]).astype(f32)
     cut = -(-(span * 3 // 8) // 128) * 128
     more = jnp.max(facts[:, 1]) > cut
@@ -911,6 +872,7 @@
     inner0 = norm(stream0, 0).astype(low_type)
     branch0, keep0 = self_attention(inner0, w_in0, w_out0, enc_spans)
     stream1 = stream0 + branch0
+    stream1, dec_rows = lax.optimization_barrier((stream1, dec_rows))
     inner1 = norm(stream1, 1).astype(low_type)
     branch1, keep1 = ffn(inner1, f_in0, f_out0)
     stream2 = stream1 + branch1
@@ -970,7 +932,8 @@
         plan, table_part, pieces, turned, targets, logs[None], weights[None], split and own_words
     )
     token_local = token_local - jnp.sum(picks)
-    table_chain = [TableChain(*d_table)] if split else []
+    if split:
+        arrived = swap(d_table[1], "dp", 1)
     if seqs == 2:
         d_final = lax.cond(
             more, lambda: unpack(2 * span, span), lambda: unpack(min(2 * cut, 2 * span), cut)
@@ -1014,46 +977,55 @@
     none = jnp.zeros_like(stream0)
     d_target3, scale6 = norm_backward(target3, gains[6], d_final, none)
     d_inner5, d_fin1, d_fout1 = ffn_back(inner5, f_in1, f_out1, keep5, d_target3)
-    d_inner5, d_target3 = advance((d_inner5, d_target3), table_chain)
+    if split:
+        d_inner5, d_target3, arrived = lax.optimization_barrier((d_inner5, d_target3, arrived))
+        table_grad = table_to_owner(d_table[0], arrived)
+    else:
+        table_grad = lax.psum_scatter(d_table[0], "dp", scatter_dimension=0, tiled=True)
+    chain_a = LayerChain([owned(d_fin1)] + owned_columns(d_fout1))
     d_target2, scale5 = norm_backward(target2, gains[5], d_inner5, d_target3)
     d_inner4, d_cross, d_win2, d_wout2 = cross_attention_back(
         inner4, memory, w_in2, w_out2, cross_spans, keep4, d_target2
     )
-    chain_one = LayerChain([owned(d_fin1)] + owned_columns(d_fout1) + [owned(d_win2), owned(d_wout2)])
+    chains = [chain_a]
+    d_inner4, d_target2, d_cross = advance((d_inner4, d_target2, d_cross), chains)
+    chain_b = LayerChain([owned(d_win2), owned(d_wout2)])
     d_target1, scale4 = norm_backward(target1, gains[4], d_inner4, d_target2)
     d_inner3, d_win1, d_wout1 = self_attention_back(
         inner3, w_in1, w_out1, self_spans, keep3, d_target1
     )
-    chains = table_chain + [chain_one]
-    d_inner3, d_target1, d_cross = advance((d_inner3, d_target1, d_cross), chains)
+    chains += [chain_b]
+    d_inner3, d_target1 = advance((d_inner3, d_target1), chains)
+    chain_c = LayerChain([owned(d_win1), owned(d_wout1)])
     d_target0, scale3 = norm_backward(target0, gains[3], d_inner3, d_target1)
     dec_grad = d_target0 * root
     dec_sums = give_rows(dec_maps[0], dec_grad)
     d_stream2, scale2 = norm_backward(stream2, gains[2], d_memory + d_cross, none)
     d_inner1, d_fin0, d_fout0 = ffn_back(inner1, f_in0, f_out0, keep1, d_stream2)
+    chains += [chain_c]
     d_inner1, d_stream2 = advance((d_inner1, d_stream2), chains)
-    chain_two = LayerChain([owned(d_win1), owned(d_wout1), owned(d_fin0)] + owned_columns(d_fout0))
+    chain_d = LayerChain([owned(d_fin0)] + owned_columns(d_fout0))
     d_stream1, scale1 = norm_backward(stream1, gains[1], d_inner1, d_stream2)
     d_inner0, d_win0, d_wout0 = self_attention_back(
         inner0, w_in0, w_out0, enc_spans, keep0, d_stream1
     )
-    chains += [chain_two]
+    chains += [chain_d]
     d_inner0, d_stream1, dec_sums = advance((d_inner0, d_stream1, dec_sums), chains)
     d_stream0, scale0 = norm_backward(stream0, gains[0], d_inner0, d_stream1)
     src_grad = d_stream0 * root
     src_sums = give_rows(src_maps[0], src_grad)
-    chain_three = LayerChain([owned(d_win0), owned(d_wout0), owned(d_w_len)])
+    chain_e = LayerChain([owned(d_win0), owned(d_wout0), owned(d_w_len)])
     norm_share = norms.shape[2]
     scales = jnp.sum(jnp.stack([scale0, scale1, scale2, scale3, scale4, scale5, scale6], 1), 3)
     scales = scales.reshape(2 * norm_count, owners, norm_share).transpose(1, 0, 2)
     scales = jnp.broadcast_to(scales[None], (seqs,) + scales.shape)
     scales = to_each(scales.reshape((devices,) + scales.shape[2:]))
-    chains += [chain_three]
+    chains += [chain_e]
     advance((), chains)
     src_sums, scales = advance((src_sums, scales), chains)
     while any(chain.pending is not None for chain in chains):
         advance((), chains)
-    layer_chains = [chain_one, chain_two, chain_three]
+    layer_chains = [chain_a, chain_b, chain_c, chain_d, chain_e]
     for chain in layer_chains:
         chain.finish()
 
@@ -1066,10 +1038,6 @@
         lambda turn: give(round_of(dec_ask, turn), dec_grad)
         + give(round_of(src_ask, turn), src_grad),
     )
-    if split:
-        table_grad = table_chain[0].value
-    else:
-        table_grad = lax.psum_scatter(d_table[0], "dp", scatter_dimension=0, tiled=True)
     table_grad = table_grad + given
     square = sum(chain.square for chain in layer_chains)
     square = square + jnp.sum(table_grad * table_grad) + norm_square
@@ -1087,12 +1055,13 @@
         return result
 
     hidden_width = ffn_in.shape[2]
-    pieces_out = ffn_out.shape[1] // share
-    ffn_sizes = [hidden_width] + [width] * pieces_out
+    ffn_sizes = [hidden_width] + [width] * out_pieces
     attn_sizes = [3 * width, width]
-    g_fin1, *g_fout1, g_win2, g_wout2 = cut_columns(chain_one, ffn_sizes + attn_sizes)
-    g_win1, g_wout1, g_fin0, *g_fout0 = cut_columns(chain_two, attn_sizes + ffn_sizes)
-    g_win0, g_wout0, g_len = cut_columns(chain_three, attn_sizes + [classes])
+    g_fin1, *g_fout1 = cut_columns(chain_a, ffn_sizes)
+    g_win2, g_wout2 = cut_columns(chain_b, attn_sizes)
+    g_win1, g_wout1 = cut_columns(chain_c, attn_sizes)
+    g_fin0, *g_fout0 = cut_columns(chain_d, ffn_sizes)
+    g_win0, g_wout0, g_len = cut_columns(chain_e, attn_sizes + [classes])
     grads = (
         jnp.stack([g_win0, g_win1, g_win2]),
         jnp.stack([g_wout0, g_wout1, g_wout2]),

time: 1190 us -> 1100 us (0.924)
  waiting for transfers between devices: 391 us -> 316 us
    ppermute x22 -> x20, waiting for transfers between devices: 274 us -> 62.7 us  [swap(): return lax.ppermute(values, axis, [(i, i ^ bit) for i in range(size)])]
    all_to_all x3 -> x5, waiting for transfers between devices: 14.6 us -> 64.8 us  [launch(): self.pending = lax.all_to_all(whole, 'dp', 0, 0, axis_index_groups=groups)]
    reduce_scatter x0 -> x1, waiting for transfers between devices: none -> 49.7 us  [table_to_owner(): lax.psum_scatter(keep + arrived.astype(f32), 'dp', scatter_dimension=0, a...]
    all_to_all x7, waiting for transfers between devices: 102 us -> 139 us  [to_each(): return lax.all_to_all(values, ('seq', 'dp'), 0, 0)]
    all_to_all x3 -> x5, starting transfers between devices: 14.2 us -> 47.8 us  [launch(): self.pending = lax.all_to_all(whole, 'dp', 0, 0, axis_index_groups=groups)]
    ppermute x22 -> x20, starting transfers between devices: 44.3 us -> 14.7 us  [swap(): return lax.ppermute(values, axis, [(i, i ^ bit) for i in range(size)])]
    another operation x18 -> x8, other arithmetic: 24.3 us -> 4.29 us  [the longest x10 19.2 us: gather_by_swaps(): jnp.stack([jnp.where(first, part, other), jnp.where(first, other, part)],...]
    unnamed x408 -> x437, local copies, waits for them, and re-layouts: 60.9 us -> 64.1 us
  transfers between devices with their start and end apart: 34 -> 35, of which waited for: 23 -> 21; matrix products, arithmetic and copies ran while one was open for 29% -> 31% of each run, Pallas kernels for 9% -> 11%
where the time goes in v6:
time: 1100 us; the launch traced here: 1090 us
  waiting for transfers between devices  316 us (29%)
  Pallas kernels  212 us (19%)
  matrix products  182 us (17%)
  other arithmetic  151 us (14%)
  local copies, waits for them, and re-layouts  105 us (10%)
  starting transfers between devices  87.2 us (8%)
  between operations  34.6 us (3%)
    dot_general x52, matrix products, contract(): lax.dot_general(left, right, (((left_dim,), (right_dim,)), ((), ())), pre...  180 us
    all_to_all x7, waiting for transfers between devices, to_each(): return lax.all_to_all(values, ('seq', 'dp'), 0, 0)  139 us
    pallas_call x3, Pallas kernels, attend_backward(): pl.pallas_call(functools.partial(attend_backward_kernel, head=width // HE...  70.5 us
    all_to_all x5, waiting for transfers between devices, launch(): self.pending = lax.all_to_all(whole, 'dp', 0, 0, axis_index_groups=groups)  64.8 us
    unnamed x437, local copies, waits for them, and re-layouts  64.1 us
    ppermute x20, waiting for transfers between devices, swap(): return lax.ppermute(values, axis, [(i, i ^ bit) for i in range(size)])  62.7 us
    reduce_scatter x1, waiting for transfers between devices, table_to_owner(): lax.psum_scatter(keep + arrived.astype(f32), 'dp', scatter_dimension=0, a...  49.7 us
    all_to_all x5, starting transfers between devices, launch(): self.pending = lax.all_to_all(whole, 'dp', 0, 0, axis_index_groups=groups)  47.8 us
  transfers between devices with their start and end apart: 35, of which 21 were waited for; matrix products, arithmetic and copies ran while one was open for 31% of the time, Pallas kernels for 11%

profile of v6, /device:TPU:0, one launch (start us, length us, event | category | flops | bytes accessed | tf_op | source)
XLA Modules:
  0.0 1091.4 jit_solution(14598412677586714848)
XLA Ops:
  55.3 7.1 all-to-all-done.8
  71.0 8.3 multiply_sine_fusion
  99.0 63.0 %all-to-all-done.9 = bf16[32,64,512]{2,1,0:T(8,128)(2,1)} async-done(((bf16[32,64,512]{2,1,0:T(8,128)(2,1)}), bf16[32,64,512]{2,1,0:T(8,128)(2,1)}, u32[]{:S(2)}, u32[]{:S(2)}) %all-to-all-start.9) | async-done | bytes 2097184 | tf_op jit(solution)/shard_map/all_to_all | solution.py:481
  187.6 13.2 %attend_forward.3 = (bf16[512,1024]{1,0:T(8,128)(2,1)}, f32[8,1024]{1,0:T(8,128)}) custom-call(s32[2,4]{1,0:T(2,128)} %pad_add_fusion.5.bounds, bf16[1536,1024]{1,0:T(8,128)(2,1)} %convolution_convert_fusion.2.q_ref.k_ref.v_ref, bf16[1536,1024]{1,0:T(8,128)(2,1)} %convolution_convert_fusion.2.q_ref.k_ref.v_ref, ...), custom_call_target="tpu_custom_call" | custom-call | tf_op jit(solution)/shard_map/attend_forward/pallas_call | solution.py:191
  204.4 36.0 %all-to-all-done.10 = bf16[32,48,512]{2,1,0:T(8,128)(2,1)} async-done(((bf16[32,48,512]{2,1,0:T(8,128)(2,1)}), bf16[32,48,512]{2,1,0:T(8,128)(2,1)}, u32[]{:S(2)}, u32[]{:S(2)}) %all-to-all-start.10) | async-done | bytes 1572896 | tf_op jit(solution)/shard_map/all_to_all | solution.py:481
  273.3 13.5 %attend_forward.4 = (bf16[512,1024]{1,0:T(8,128)(2,1)}, f32[8,1024]{1,0:T(8,128)}) custom-call(s32[2,4]{1,0:T(2,128)} %pad_add_fusion.6.bounds, bf16[1536,1024]{1,0:T(8,128)(2,1)} %convolution_convert_fusion.1.q_ref.k_ref.v_ref, bf16[1536,1024]{1,0:T(8,128)(2,1)} %convolution_convert_fusion.1.q_ref.k_ref.v_ref, ...), custom_call_target="tpu_custom_call" | custom-call | tf_op jit(solution)/shard_map/attend_forward/pallas_call | solution.py:191
  296.7 12.4 %attend_forward.5 = (bf16[512,1024]{1,0:T(8,128)(2,1)}, f32[8,1024]{1,0:T(8,128)}) custom-call(s32[2,4]{1,0:T(2,128)} %pad_add_fusion.7.bounds, bf16[512,1024]{1,0:T(8,128)(2,1)} %convolution_convert_fusion.8.q_ref, bf16[1024,1024]{1,0:T(8,128)(2,1)} %convolution_convert_fusion.4.k_ref.v_ref, bf16[1024,1024]{1,0:T(8,128)(2,1)} %convolution_convert_fusion.4.k_ref.v_ref, ...), custom_call_target="tpu_custom_call" | custom-call | tf_op jit(solution)/shard_map/attend_forward/pallas_call | solution.py:191
  322.9 15.7 %conditional.2 = (bf16[2048,512]{1,0:T(8,128)(2,1)}) conditional(s32[]{:T(128)} %convert_element_type.461, (s32[1024]{0:T(1024)S(1)}, bf16[512,1024]{1,0:T(8,128)(2,1)}, s32[]{:T(128)}, s32[2]{0:T(128)S(1)}, s32[2]{0:T(128)S(1)}, /*index=5*/s32[1024]{0:T(1024)S(1)}) %tuple.308, (s32[1024]{0:T(1024)S(1)}, bf16[512,1024]{1,0:T(8,128)(2,1)}, ...), branch_computations={%region_59.60_spmd, %region_60.61_spmd} | conditional | flops 5376576512 | bytes 18890878 | solution.py:914
  343.1 17.4 %head_stats.1 = f32[2,2048]{1,0:T(2,128)} custom-call(s32[4]{0:T(128)} %pad_add_fusion.8.plan, bf16[16000,512]{1,0:T(8,128)(2,1)} %all-gather.3.cloned.1.call-done.table_ref, bf16[512,2048]{1,0:T(8,128)(2,1)} %bitcast.649), custom_call_target="tpu_custom_call" | custom-call | tf_op jit(solution)/shard_map/head_stats/pallas_call | solution.py:399
  366.6 44.2 %head_back.1 = (f32[8,1000,512]{2,1,0:T(8,128)}, bf16[8,1000,512]{2,1,0:T(8,128)(2,1)}, f32[2048,512]{1,0:T(8,128)}, f32[8,2048]{1,0:T(8,128)}) custom-call(s32[4]{0:T(128)} %pad_add_fusion.8.plan, bf16[16000,512]{1,0:T(8,128)(2,1)} %all-gather.3.cloned.1.call-done.table_ref, bf16[2048,512]{1,0:T(8,128)(2,1)S(1)} %copy-done.13, bf16[512,2048]{1,0:T(8,128)(2,1)} %bitcast.650, ...), custom_call_target="tpu_custom_call" | custom-call | tf_op jit(solution)/shard_map/head_back/pallas_call | solution.py:429
  417.9 21.4 %conditional.3 = (f32[512,1024]{1,0:T(8,128)}) conditional(s32[]{:T(128)} %convert_element_type.461, (s32[1024]{0:T(1024)S(1)}, f32[2048,512]{1,0:T(8,128)}, s32[]{:T(128)}, s32[2]{0:T(128)S(1)}, s32[2]{0:T(128)S(1)}, /*index=5*/s32[1024]{0:T(1024)S(1)}) %tuple.310, (s32[1024]{0:T(1024)S(1)}, f32[2048,512]{1,0:T(8,128)}, s32[]{:T(128)}, ...), branch_computations={%region_73.74_spmd, %region_74.75_spmd} | conditional | flops 7532448768 | bytes 50352280 | solution.py:938
  427.6 6.3 collective-permute-done
  447.1 9.4 fusion.95
  489.9 22.6 %attend_backward.3 = (bf16[512,1024]{1,0:T(8,128)(2,1)}, bf16[1024,1024]{1,0:T(8,128)(2,1)}) custom-call(s32[2,4]{1,0:T(2,128)} %pad_add_fusion.7.bounds, bf16[512,1024]{1,0:T(8,128)(2,1)} %convolution_convert_fusion.8.q_ref, bf16[1024,1024]{1,0:T(8,128)(2,1)} %convolution_convert_fusion.4.k_ref.v_ref, ...), custom_call_target="tpu_custom_call" | custom-call | tf_op jit(solution)/shard_map/attend_backward/pallas_call | solution.py:216
  532.3 11.1 %fusion.88 = bf16[2048,1024]{1,0:T(8,128)(2,1)} fusion(f32[2048,1024]{1,0:T(8,128)} %copy-done.193, bf16[2048,512]{1,0:T(8,128)(2,1)S(1)} %bitcast.694, f32[512,1024]{1,0:T(8,128)} %get-tuple-element.771.rest_ref), kind=kOutput, calls=%fused_computation.151 | convolution fusion | flops 2189950976 | bytes 16777216 | tf_op jit(solution)/shard_map/dot_general | solution.py:47
  548.6 6.1 norm_backward.10
  560.4 24.0 %attend_backward.4 = (bf16[512,1024]{1,0:T(8,128)(2,1)}, bf16[1024,1024]{1,0:T(8,128)(2,1)}) custom-call(s32[2,4]{1,0:T(2,128)} %pad_add_fusion.6.bounds, bf16[1536,1024]{1,0:T(8,128)(2,1)} %convolution_convert_fusion.1.q_ref.k_ref.v_ref, bf16[1536,1024]{1,0:T(8,128)(2,1)} %convolution_convert_fusion.1.q_ref.k_ref.v_ref, ...), custom_call_target="tpu_custom_call" | custom-call | tf_op jit(solution)/shard_map/attend_backward/pallas_call | solution.py:216
  615.6 8.4 collective-permute-done.8
  627.0 31.0 %all-to-all-start.11 = ((bf16[8,16,4096]{2,1,0:T(8,128)(2,1)}), bf16[8,16,4096]{2,1,0:T(8,128)(2,1)}, u32[]{:S(2)}, u32[]{:S(2)}) async-start(bf16[8,16,4096]{2,1,0:T(8,128)(2,1)} %fusion.125), calls=%async_computation.11 | async-start | bytes 2097152 | tf_op jit(solution)/shard_map/all_to_all | solution.py:510
  658.0 14.1 %convert_add_fusion = f32[8,1000,512]{2,1,0:T(8,128)} fusion(f32[8,1000,512]{2,1,0:T(8,128)} %get-tuple-element.799, bf16[8,1000,512]{2,1,0:T(8,128)(2,1)} %collective-permute-done.6), kind=kLoop, calls=%fused_computation.140 | loop fusion | flops 8192000 | bytes 40960000 | tf_op jit(solution)/shard_map/add | solution.py:557
  685.4 6.9 collective-permute-done.10
  719.6 8.9 all-to-all-done.13
  735.0 23.9 %attend_backward.5 = (bf16[512,1024]{1,0:T(8,128)(2,1)}, bf16[1024,1024]{1,0:T(8,128)(2,1)}) custom-call(s32[2,4]{1,0:T(2,128)} %pad_add_fusion.5.bounds, bf16[1536,1024]{1,0:T(8,128)(2,1)} %convolution_convert_fusion.2.q_ref.k_ref.v_ref, bf16[1536,1024]{1,0:T(8,128)(2,1)} %convolution_convert_fusion.2.q_ref.k_ref.v_ref, ...), custom_call_target="tpu_custom_call" | custom-call | tf_op jit(solution)/shard_map/attend_backward/pallas_call | solution.py:216
  777.9 14.9 %collective-permute-done.12 = f32[16,4096]{1,0:T(8,128)S(1)} collective-permute-done((f32[16,4096]{1,0:T(8,128)S(1)}, f32[16,4096]{1,0:T(8,128)S(1)}, u32[]{:S(2)}, u32[]{:S(2)}) %collective-permute-start.12) | collective-permute-done | bytes 262176 | tf_op jit(solution)/shard_map/ppermute | solution.py:461
  792.8 13.5 %all-to-all-done.12 = bf16[32,48,512]{2,1,0:T(8,128)(2,1)} async-done(((bf16[32,48,512]{2,1,0:T(8,128)(2,1)}), bf16[32,48,512]{2,1,0:T(8,128)(2,1)}, u32[]{:S(2)}, u32[]{:S(2)}) %all-to-all-start.12) | async-done | bytes 1572896 | tf_op jit(solution)/shard_map/all_to_all | solution.py:481
  837.0 17.2 %all-to-all-done.14 = bf16[8,16,2048]{2,1,0:T(8,128)(2,1)S(1)} async-done(((bf16[8,16,2048]{2,1,0:T(8,128)(2,1)}), bf16[8,16,2048]{2,1,0:T(8,128)(2,1)S(1)}, u32[]{:S(2)}, u32[]{:S(2)}) %all-to-all-start.14) | async-done | bytes 524320 | tf_op jit(solution)/shard_map/all_to_all | solution.py:510
  874.6 22.5 %all-to-all-done.17 = bf16[8,16,4096]{2,1,0:T(8,128)(2,1)S(1)} async-done(((bf16[8,16,4096]{2,1,0:T(8,128)(2,1)}), bf16[8,16,4096]{2,1,0:T(8,128)(2,1)S(1)}, u32[]{:S(2)}, u32[]{:S(2)}) %all-to-all-start.17) | async-done | bytes 1048608 | tf_op jit(solution)/shard_map/all_to_all | solution.py:510
  926.4 16.3 %collective-permute-done.18 = f32[16,2048]{1,0:T(8,128)} collective-permute-done((f32[16,2048]{1,0:T(8,128)}, f32[16,2048]{1,0:T(8,128)}, u32[]{:S(2)}, u32[]{:S(2)}) %collective-permute-start.18) | collective-permute-done | bytes 131104 | tf_op jit(solution)/shard_map/ppermute | solution.py:461
  942.7 8.2 all-to-all-done.15
  974.5 16.2 %all-to-all-done.18 = bf16[8,16,2304]{2,1,0:T(8,128)(2,1)S(1)} async-done(((bf16[8,16,2304]{2,1,0:T(8,128)(2,1)}), bf16[8,16,2304]{2,1,0:T(8,128)(2,1)S(1)}, u32[]{:S(2)}, u32[]{:S(2)}) %all-to-all-start.18) | async-done | bytes 589856 | tf_op jit(solution)/shard_map/all_to_all | solution.py:510
  998.3 49.7 %reduce-scatter.2.cloned.1.call-done = f32[1,1000,512]{2,1,0:T(8,128)} async-done(((f32[8,1000,512]{2,1,0:T(8,128)}), f32[1,1000,512]{2,1,0:T(8,128)}) %reduce-scatter.2.cloned.1.call-update) | async-done | bytes 2048016 | tf_op jit(solution)/shard_map/reduce_scatter | solution.py:556
  1056.8 6.4 all-to-all-done.19
  (801 shorter events, 503.3 us)
Async XLA Ops:
  7.2 172.2 %all-gather.5.cloned.1.call-start = ((), (), s32[]{:S(2)}) async-start(), calls=%async_computation.22 | async-start | bytes 15544320 | tf_op jit(solution)/shard_map/all_gather | solution.py:656
  24.0 319.2 %all-gather.3.cloned.1.call-start = ((), (), s32[]{:S(2)}) async-start(), calls=%async_computation.21 | async-start | bytes 17408000 | tf_op jit(solution)/shard_map/all_gather | solution.py:679
  50.4 12.0 %all-to-all-start.8 = ((s32[32,1,128]{2,1,0:T(1,128)}), s32[32,1,128]{2,1,0:T(1,128)S(1)}, u32[]{:S(2)}, u32[]{:S(2)}) async-start(s32[32,1,128]{2,1,0:T(1,128)} %bitcast.44), calls=%async_computation.8 | async-start | bytes 32768 | tf_op jit(solution)/shard_map/all_to_all | solution.py:481
  67.3 94.7 %all-to-all-start.9 = ((bf16[32,64,512]{2,1,0:T(8,128)(2,1)}), bf16[32,64,512]{2,1,0:T(8,128)(2,1)}, u32[]{:S(2)}, u32[]{:S(2)}) async-start(bf16[32,64,512]{2,1,0:T(8,128)(2,1)} %bitcast.47), calls=%async_computation.9 | async-start | bytes 4194304 | tf_op jit(solution)/shard_map/all_to_all | solution.py:481
  168.6 71.7 %all-to-all-start.10 = ((bf16[32,48,512]{2,1,0:T(8,128)(2,1)}), bf16[32,48,512]{2,1,0:T(8,128)(2,1)}, u32[]{:S(2)}, u32[]{:S(2)}) async-start(bf16[32,48,512]{2,1,0:T(8,128)(2,1)} %bitcast.726), calls=%async_computation.10 | async-start | bytes 3145728 | tf_op jit(solution)/shard_map/all_to_all | solution.py:481
  325.5 9.9 collective-permute-start.2
  410.8 69.8 %collective-permute-start.6 = (bf16[8,1000,512]{2,1,0:T(8,128)(2,1)}, bf16[8,1000,512]{2,1,0:T(8,128)(2,1)}, u32[]{:S(2)}, u32[]{:S(2)}) collective-permute-start(bf16[8,1000,512]{2,1,0:T(8,128)(2,1)} %get-tuple-element.751), channel_id=1, source_target_pairs={{0,2},{2,0},{4,6},{6,4},{8,10},{10,8},{12,14},{14,12},{16,18},{18,... | collective-permute-start | bytes 24576008 | tf_op jit(solution)/shard_map/ppermute | solution.py:461
  422.3 11.6 %collective-permute-start = (bf16[384,512]{1,0:T(8,128)(2,1)S(1)}, bf16[384,512]{1,0:T(8,128)(2,1)S(1)}, u32[]{:S(2)}, u32[]{:S(2)}) collective-permute-start(bf16[384,512]{1,0:T(8,128)(2,1)S(1)} %convolution_convert_fusion), channel_id=1, source_target_pairs={{0,1},{1,0},{2,3},{3,2},{4,5},{5,4},{6,7},{7,6},{8,9},{9,8},{10,11... | collective-permute-start | bytes 1179656 | tf_op jit(solution)/shard_map/cond/branch_0_fun/ppermute | solution.py:461
  469.8 54.6 %collective-permute-start.7 = (bf16[8,32,4096]{2,1,0:T(8,128)(2,1)}, bf16[8,32,4096]{2,1,0:T(8,128)(2,1)S(1)}, u32[]{:S(2)}, u32[]{:S(2)}) collective-permute-start(bf16[8,32,4096]{2,1,0:T(8,128)(2,1)} %fusion.213), channel_id=1, source_target_pairs={{0,2},{2,0},{4,6},{6,4},{8,10},{10,8},{12,14},{14,12},{16,18},{18,... | collective-permute-start | bytes 6291464 | tf_op jit(solution)/shard_map/ppermute | solution.py:461
  591.9 93.5 %collective-permute-start.11 = (bf16[8,32,2048]{2,1,0:T(8,128)(2,1)}, bf16[8,32,2048]{2,1,0:T(8,128)(2,1)}, u32[]{:S(2)}, u32[]{:S(2)}) collective-permute-start(bf16[8,32,2048]{2,1,0:T(8,128)(2,1)} %pad_maximum_fusion.8), channel_id=1, source_target_pairs={{0,2},{2,0},{4,6},{6,4},{8,10},{10,8},{12,14},{14,12},{16,18},{18,... | collective-permute-start | bytes 3145736 | tf_op jit(solution)/shard_map/ppermute | solution.py:461
  593.7 21.9 %collective-permute-start.9 = (bf16[8,32,2048]{2,1,0:T(8,128)(2,1)S(1)}, bf16[8,32,2048]{2,1,0:T(8,128)(2,1)S(1)}, u32[]{:S(2)}, u32[]{:S(2)}) collective-permute-start(bf16[8,32,2048]{2,1,0:T(8,128)(2,1)S(1)} %pad_maximum_fusion.7), channel_id=1, source_target_pairs={{0,2},{2,0},{4,6},{6,4},{8,10},{10,8},{12,14},{14,12},{16,18},{18,... | collective-permute-start | bytes 3145736 | tf_op jit(solution)/shard_map/ppermute | solution.py:461
  598.4 25.6 %collective-permute-start.8 = (bf16[8,16,4096]{2,1,0:T(8,128)(2,1)S(1)}, bf16[8,16,4096]{2,1,0:T(8,128)(2,1)S(1)}, u32[]{:S(2)}, u32[]{:S(2)}) collective-permute-start(bf16[8,16,4096]{2,1,0:T(8,128)(2,1)S(1)} %fusion.145), channel_id=1, source_target_pairs={{0,1},{1,0},{2,3},{3,2},{4,5},{5,4},{6,7},{7,6},{8,9},{9,8},{10,11... | collective-permute-start | bytes 3145736 | tf_op jit(solution)/shard_map/ppermute | solution.py:461
  608.8 169.1 %collective-permute-start.14 = (bf16[8,32,4096]{2,1,0:T(8,128)(2,1)}, bf16[8,32,4096]{2,1,0:T(8,128)(2,1)}, u32[]{:S(2)}, u32[]{:S(2)}) collective-permute-start(bf16[8,32,4096]{2,1,0:T(8,128)(2,1)} %fusion.221), channel_id=1, source_target_pairs={{0,2},{2,0},{4,6},{6,4},{8,10},{10,8},{12,14},{14,12},{16,18},{18,... | collective-permute-start | bytes 6291464 | tf_op jit(solution)/shard_map/ppermute | solution.py:461
  627.0 65.3 %all-to-all-start.11 = ((bf16[8,16,4096]{2,1,0:T(8,128)(2,1)}), bf16[8,16,4096]{2,1,0:T(8,128)(2,1)}, u32[]{:S(2)}, u32[]{:S(2)}) async-start(bf16[8,16,4096]{2,1,0:T(8,128)(2,1)} %fusion.125), calls=%async_computation.11 | async-start | bytes 2097152 | tf_op jit(solution)/shard_map/all_to_all | solution.py:510
  658.0 390.0 %reduce-scatter.2.cloned.1.call-start = ((), (), s32[]{:S(2)}) async-start(), calls=%async_computation.23 | async-start | bytes 18432000 | tf_op jit(solution)/shard_map/reduce_scatter | solution.py:556
  678.6 13.7 %collective-permute-start.10 = (bf16[8,16,2048]{2,1,0:T(8,128)(2,1)S(1)}, bf16[8,16,2048]{2,1,0:T(8,128)(2,1)S(1)}, u32[]{:S(2)}, u32[]{:S(2)}) collective-permute-start(bf16[8,16,2048]{2,1,0:T(8,128)(2,1)S(1)} %fusion.180), channel_id=1, source_target_pairs={{0,1},{1,0},{2,3},{3,2},{4,5},{5,4},{6,7},{7,6},{8,9},{9,8},{10,11... | collective-permute-start | bytes 1572872 | tf_op jit(solution)/shard_map/ppermute | solution.py:461
  694.3 34.2 %all-to-all-start.13 = ((bf16[8,16,2048]{2,1,0:T(8,128)(2,1)}), bf16[8,16,2048]{2,1,0:T(8,128)(2,1)S(1)}, u32[]{:S(2)}, u32[]{:S(2)}) async-start(bf16[8,16,2048]{2,1,0:T(8,128)(2,1)} %fusion.164), calls=%async_computation.13 | async-start | bytes 1048576 | tf_op jit(solution)/shard_map/all_to_all | solution.py:510
  728.5 77.8 %all-to-all-start.12 = ((bf16[32,48,512]{2,1,0:T(8,128)(2,1)}), bf16[32,48,512]{2,1,0:T(8,128)(2,1)}, u32[]{:S(2)}, u32[]{:S(2)}) async-start(bf16[32,48,512]{2,1,0:T(8,128)(2,1)} %bitcast.727), calls=%async_computation.12 | async-start | bytes 3145728 | tf_op jit(solution)/shard_map/all_to_all | solution.py:481
  767.2 67.4 %collective-permute-start.17 = (bf16[8,32,2304]{2,1,0:T(8,128)(2,1)}, bf16[8,32,2304]{2,1,0:T(8,128)(2,1)}, u32[]{:S(2)}, u32[]{:S(2)}) collective-permute-start(bf16[8,32,2304]{2,1,0:T(8,128)(2,1)} %pad_maximum_fusion.6), channel_id=1, source_target_pairs={{0,2},{2,0},{4,6},{6,4},{8,10},{10,8},{12,14},{14,12},{16,18},{18,... | collective-permute-start | bytes 3538952 | tf_op jit(solution)/shard_map/ppermute | solution.py:461
  769.8 23.0 %collective-permute-start.13 = (bf16[8,16,2048]{2,1,0:T(8,128)(2,1)S(1)}, bf16[8,16,2048]{2,1,0:T(8,128)(2,1)S(1)}, u32[]{:S(2)}, u32[]{:S(2)}) collective-permute-start(bf16[8,16,2048]{2,1,0:T(8,128)(2,1)S(1)} %fusion.181), channel_id=1, source_target_pairs={{0,1},{1,0},{2,3},{3,2},{4,5},{5,4},{6,7},{7,6},{8,9},{9,8},{10,11... | collective-permute-start | bytes 1572872 | tf_op jit(solution)/shard_map/ppermute | solution.py:461
  773.0 19.8 %collective-permute-start.12 = (f32[16,4096]{1,0:T(8,128)S(1)}, f32[16,4096]{1,0:T(8,128)S(1)}, u32[]{:S(2)}, u32[]{:S(2)}) collective-permute-start(f32[16,4096]{1,0:T(8,128)S(1)} %convert_reduce_fusion.3), channel_id=1, source_target_pairs={{0,1},{1,0},{2,3},{3,2},{4,5},{5,4},{6,7},{7,6},{8,9},{9,8},{10,11... | collective-permute-start | bytes 786440 | tf_op jit(solution)/shard_map/ppermute | solution.py:461
  809.4 44.9 %collective-permute-start.16 = (bf16[8,16,4096]{2,1,0:T(8,128)(2,1)}, bf16[8,16,4096]{2,1,0:T(8,128)(2,1)}, u32[]{:S(2)}, u32[]{:S(2)}) collective-permute-start(bf16[8,16,4096]{2,1,0:T(8,128)(2,1)} %fusion.150), channel_id=1, source_target_pairs={{0,1},{1,0},{2,3},{3,2},{4,5},{5,4},{6,7},{7,6},{8,9},{9,8},{10,11... | collective-permute-start | bytes 3145736 | tf_op jit(solution)/shard_map/ppermute | solution.py:461
  809.9 27.2 %collective-permute-start.15 = (f32[16,2048]{1,0:T(8,128)S(1)}, f32[16,2048]{1,0:T(8,128)S(1)}, u32[]{:S(2)}, u32[]{:S(2)}) collective-permute-start(f32[16,2048]{1,0:T(8,128)S(1)} %convert_reduce_fusion.6), channel_id=1, source_target_pairs={{0,1},{1,0},{2,3},{3,2},{4,5},{5,4},{6,7},{7,6},{8,9},{9,8},{10,11... | collective-permute-start | bytes 393224 | tf_op jit(solution)/shard_map/ppermute | solution.py:461
  823.3 31.0 %all-to-all-start.14 = ((bf16[8,16,2048]{2,1,0:T(8,128)(2,1)}), bf16[8,16,2048]{2,1,0:T(8,128)(2,1)S(1)}, u32[]{:S(2)}, u32[]{:S(2)}) async-start(bf16[8,16,2048]{2,1,0:T(8,128)(2,1)} %fusion.155), calls=%async_computation.14 | async-start | bytes 1048576 | tf_op jit(solution)/shard_map/all_to_all | solution.py:510
  854.3 11.0 %all-to-all-start.16 = ((f32[32,1,448]{2,1,0:T(1,128)}), f32[32,1,448]{2,1,0:T(1,128)S(1)}, u32[]{:S(2)}, u32[]{:S(2)}) async-start(f32[32,1,448]{2,1,0:T(1,128)} %reshape.1440), calls=%async_computation.16 | async-start | bytes 131072 | tf_op jit(solution)/shard_map/all_to_all | solution.py:481
  865.3 31.8 %all-to-all-start.17 = ((bf16[8,16,4096]{2,1,0:T(8,128)(2,1)}), bf16[8,16,4096]{2,1,0:T(8,128)(2,1)S(1)}, u32[]{:S(2)}, u32[]{:S(2)}) async-start(bf16[8,16,4096]{2,1,0:T(8,128)(2,1)} %fusion.126), calls=%async_computation.17 | async-start | bytes 2097152 | tf_op jit(solution)/shard_map/all_to_all | solution.py:510
  897.1 53.8 %all-to-all-start.15 = ((bf16[32,64,512]{2,1,0:T(8,128)(2,1)}), bf16[32,64,512]{2,1,0:T(8,128)(2,1)}, u32[]{:S(2)}, u32[]{:S(2)}) async-start(bf16[32,64,512]{2,1,0:T(8,128)(2,1)} %bitcast.699), calls=%async_computation.15 | async-start | bytes 4194304 | tf_op jit(solution)/shard_map/all_to_all | solution.py:481
  918.0 24.7 %collective-permute-start.19 = (bf16[8,16,2304]{2,1,0:T(8,128)(2,1)}, bf16[8,16,2304]{2,1,0:T(8,128)(2,1)}, u32[]{:S(2)}, u32[]{:S(2)}) collective-permute-start(bf16[8,16,2304]{2,1,0:T(8,128)(2,1)} %fusion.177), channel_id=1, source_target_pairs={{0,1},{1,0},{2,3},{3,2},{4,5},{5,4},{6,7},{7,6},{8,9},{9,8},{10,11... | collective-permute-start | bytes 1769480 | tf_op jit(solution)/shard_map/ppermute | solution.py:461
  920.3 22.4 %collective-permute-start.18 = (f32[16,2048]{1,0:T(8,128)}, f32[16,2048]{1,0:T(8,128)}, u32[]{:S(2)}, u32[]{:S(2)}) collective-permute-start(f32[16,2048]{1,0:T(8,128)} %convert_reduce_fusion.5), channel_id=1, source_target_pairs={{0,1},{1,0},{2,3},{3,2},{4,5},{5,4},{6,7},{7,6},{8,9},{9,8},{10,11... | collective-permute-start | bytes 393224 | tf_op jit(solution)/shard_map/ppermute | solution.py:461
  951.8 22.7 %collective-permute-start.20 = (f32[16,4096]{1,0:T(8,128)}, f32[16,4096]{1,0:T(8,128)S(1)}, u32[]{:S(2)}, u32[]{:S(2)}) collective-permute-start(f32[16,4096]{1,0:T(8,128)} %convert_reduce_fusion.2), channel_id=1, source_target_pairs={{0,1},{1,0},{2,3},{3,2},{4,5},{5,4},{6,7},{7,6},{8,9},{9,8},{10,11... | collective-permute-start | bytes 786440 | tf_op jit(solution)/shard_map/ppermute | solution.py:461
  960.5 30.1 %all-to-all-start.18 = ((bf16[8,16,2304]{2,1,0:T(8,128)(2,1)}), bf16[8,16,2304]{2,1,0:T(8,128)(2,1)S(1)}, u32[]{:S(2)}, u32[]{:S(2)}) async-start(bf16[8,16,2304]{2,1,0:T(8,128)(2,1)} %fusion.144), calls=%async_computation.18 | async-start | bytes 1179648 | tf_op jit(solution)/shard_map/all_to_all | solution.py:510
  1053.6 9.7 all-to-all-start.19
  (198 other events, 2298.5 us)
Sparse Core Ops, SparseCore 0:
  24.1 145.7 all-gather.4
  172.2 148.9 all-gather.2
  672.3 375.7 reduce-scatter.1

commit v7 on v6

--- a/solution.py
+++ b/solution.py
@@ -40,7 +40,9 @@
     average = jnp.mean(stream, 0, keepdims=True)
     centred = stream - average
     variance = jnp.mean(centred * centred, 0, keepdims=True)
-    return centred * lax.rsqrt(variance + 1e-05) * norm_gain[:, None] + norm_bias[:, None]
+    inverse = lax.rsqrt(variance + 1e-05)
+    normed = centred * inverse * norm_gain[:, None] + norm_bias[:, None]
+    return normed.astype(low_type), (stream, average, inverse)
 
 
 def contract(left, right, left_dim, right_dim):
@@ -242,36 +244,40 @@
     )(bounds, queries, keys, keys, spans, lse, d_mixed)
 
 
-def norm_back_kernel(stream_ref, gain_ref, grad_ref, rest_ref, out_ref, sums_ref):
+def norm_back_kernel(stream_ref, average_ref, inverse_ref, gain_ref, grad_ref, *refs):
+    (*rest_refs, out_ref, sums_ref) = refs
+
     @pl.when(pl.program_id(0) == 0)
     def _():
         sums_ref[...] = jnp.zeros_like(sums_ref)
 
-    stream, grad = stream_ref[...], grad_ref[...]
-    width, places = stream.shape
-    average = jnp.mean(stream, 0, keepdims=True)
-    centred = stream - average
-    variance = jnp.mean(centred * centred, 0, keepdims=True)
-    inverse = lax.rsqrt(variance + 1e-05)
-    unit = centred * inverse
+    inverse, grad = inverse_ref[...], grad_ref[...]
+    unit = (stream_ref[...] - average_ref[...]) * inverse
+    width, places = grad.shape
     scaled = grad * gain_ref[...]
     along = jnp.mean(scaled * unit, 0, keepdims=True)
     level = jnp.mean(scaled, 0, keepdims=True)
-    out_ref[...] = rest_ref[...] + (scaled - level - unit * along) * inverse
+    out = (scaled - level - unit * along) * inverse
+    for rest_ref in rest_refs:
+        out = out + rest_ref[...]
+    out_ref[...] = out
     weighted = grad * unit
     for at in range(0, places, 128):
         sums_ref[0] += weighted[:, at : at + 128]
         sums_ref[1] += grad[:, at : at + 128]
 
 
-def norm_backward(stream, gain, grad, rest):
+def norm_backward(kept, gain, grad, *rests):
+    stream, average, inverse = kept
     width, places = stream.shape
     columns = min(256, places)
     block = pl.BlockSpec((width, columns), lambda i: (0, i))
-    return pl.pallas_call(
+    row = pl.BlockSpec((1, columns), lambda i: (0, i))
+    out, sums = pl.pallas_call(
         norm_back_kernel,
         grid=(places // columns,),
-        in_specs=[block, pl.BlockSpec((width, 1), lambda i: (0, 0)), block, block],
+        in_specs=[block, row, row, pl.BlockSpec((width, 1), lambda i: (0, 0)), block]
+        + [block] * len(rests),
         out_specs=[block, pl.BlockSpec((2, width, 128), lambda i: (0, 0, 0))],
         out_shape=[
             jax.ShapeDtypeStruct((width, places), f32),
@@ -279,7 +285,8 @@
         ],
         compiler_params=pltpu.CompilerParams(vmem_limit_bytes=vmem_bytes),
         name="norm_backward",
-    )(stream, gain[:, None], grad, rest)
+    )(stream, average, inverse, gain[:, None], grad, *rests)
+    return out, jnp.sum(sums, 2)
 
 
 def chunk_plan(total):
@@ -385,8 +392,11 @@
     mine = plan[3]
     keep = pl.ds(pl.multiple_of(mine * owned, 8), owned)
     away = pl.ds(pl.multiple_of((1 - mine) * owned, 8), owned)
-    out_refs[0][0] = acc[keep, :]
-    out_refs[1][0] = acc[away, :].astype(low_type)
+    half = width // 2
+    out_refs[0][0] = acc[keep, :half]
+    out_refs[1][0] = acc[keep, half:]
+    out_refs[2][0] = acc[away, :half].astype(low_type)
+    out_refs[3][0] = acc[away, half:].astype(low_type)
 
 
 def word_block(words):
@@ -420,9 +430,9 @@
     places, width = rows.shape
     row = pl.BlockSpec((1, places), lambda i, *_: (0, 0))
     if owned:
-        out_specs = [pl.BlockSpec((1, owned, width), lambda i, *_: (i, 0, 0))] * 2
-        shape = (total // words, owned, width)
-        out_shape = [jax.ShapeDtypeStruct(shape, f32), jax.ShapeDtypeStruct(shape, low_type)]
+        out_specs = [pl.BlockSpec((1, owned, width // 2), lambda i, *_: (i, 0, 0))] * 4
+        shape = (total // words, owned, width // 2)
+        out_shape = [jax.ShapeDtypeStruct(shape, t) for t in (f32, f32, low_type, low_type)]
     else:
         out_specs = [pl.BlockSpec((words, width), lambda i, *_: (i, 0))]
         out_shape = [jax.ShapeDtypeStruct((total, width), f32)]
@@ -550,12 +560,31 @@
             self.square = jnp.where(lax.axis_index("seq") == 0, jnp.sum(part * part), 0.0)
 
 
-def table_to_owner(keep, arrived):
-    owners = lax.axis_size("dp")
-    groups = [list(range(core, owners, 2)) for core in range(2)]
-    return lax.psum_scatter(
-        keep + arrived.astype(f32), "dp", scatter_dimension=0, axis_index_groups=groups
-    )
+class TableChain(Chain):
+    def __init__(self, keep, away):
+        self.part, self.got = keep, None
+        self.rows, self.bit = keep.shape[1], 2
+        self.pending = swap(away, "dp", 1)
+
+    def launch(self):
+        if self.bit == lax.axis_size("dp"):
+            return
+        mine = (lax.axis_index("dp") // self.bit) & 1
+        shape = (-1, 2, self.rows, self.part.shape[2])
+        first, second = self.part.reshape(shape), self.got.reshape(shape)
+
+        def half(side):
+            return pick(first, 1, side) + pick(second, 1, side).astype(f32)
+
+        away = half(1 - mine).astype(low_type)
+        self.part = half(mine)
+        self.pending = swap(away, "dp", self.bit)
+        self.bit *= 2
+
+    def absorb(self, got):
+        self.pending, self.got = None, got
+        if self.bit == lax.axis_size("dp"):
+            self.value = (self.part + got.astype(f32)).reshape(self.rows, -1)
 
 
 def advance(main, chains):
@@ -563,6 +592,7 @@
     main, got = lax.optimization_barrier((main, [chain.pending for chain in live]))
     for chain, arrived in zip(live, got):
         chain.absorb(arrived)
+    for chain in live:
         chain.launch()
     return main
 
@@ -826,12 +856,14 @@
         mixed, lse = attend_forward(triple, keys, group == 1, *spans)
         return contract(weight_out, mixed, 0, 0), (triple, keys, mixed, lse)
 
-    def self_attention_back(inner, weight_in, weight_out, spans, kept, grad):
+    def self_attention_back(inner, weight_in, weight_out, spans, kept, grad, before, after):
         triple, keys, mixed, lse = kept
         grad_low = grad.astype(low_type)
         d_out = contract(mixed, grad_low, 1, 1)
         d_mixed = contract(weight_out, grad_low, 1, 0).astype(low_type)
+        d_mixed = advance(d_mixed, before)
         d_query, d_keys = attend_backward(triple, keys, group == 1, *spans, lse, d_mixed)
+        d_query, d_keys = advance((d_query, d_keys), after)
         d_triple = jnp.concatenate([d_query, keys_to_place(d_keys)], 0)
         return contract(weight_in, d_triple, 1, 0), contract(inner, d_triple, 1, 1), d_out
 
@@ -841,12 +873,14 @@
         mixed, lse = attend_forward(queries, keys, False, *spans)
         return contract(weight_out, mixed, 0, 0), (queries, keys, mixed, lse)
 
-    def cross_attention_back(inner, memory, weight_in, weight_out, spans, kept, grad):
+    def cross_attention_back(inner, memory, weight_in, weight_out, spans, kept, grad, before, after):
         queries, keys, mixed, lse = kept
         grad_low = grad.astype(low_type)
         d_out = contract(mixed, grad_low, 1, 1)
         d_mixed = contract(weight_out, grad_low, 1, 0).astype(low_type)
+        d_mixed = advance(d_mixed, before)
         d_query, d_keys = attend_backward(queries, keys, False, *spans, lse, d_mixed)
+        d_query, d_keys = advance((d_query, d_keys), after)
         d_keys = keys_to_place(d_keys)
         d_in = jnp.concatenate([contract(inner, d_query, 1, 1), contract(memory, d_keys, 1, 1)], 1)
         return (
@@ -869,28 +903,28 @@
         d_hidden = jax.vjp(jax.nn.gelu, hidden)[1](d_active)[0].astype(low_type)
         return contract(weight_one, d_hidden, 1, 0), contract(inner, d_hidden, 1, 1), d_two
 
-    inner0 = norm(stream0, 0).astype(low_type)
+    inner0, norm0 = norm(stream0, 0)
     branch0, keep0 = self_attention(inner0, w_in0, w_out0, enc_spans)
     stream1 = stream0 + branch0
     stream1, dec_rows = lax.optimization_barrier((stream1, dec_rows))
-    inner1 = norm(stream1, 1).astype(low_type)
+    inner1, norm1 = norm(stream1, 1)
     branch1, keep1 = ffn(inner1, f_in0, f_out0)
     stream2 = stream1 + branch1
-    memory = norm(stream2, 2).astype(low_type)
+    memory, norm2 = norm(stream2, 2)
     memory, dec_chosen = lax.optimization_barrier((memory, dec_maps[0]))
     dec_found = contract(dec_rows, dec_chosen, 0, 1)
     dec_found = later_rounds(dec_rounds, dec_found, lambda turn: fetch(round_of(dec_ask, turn)))
     target0 = dec_found * root + tgt_wave
-    inner3 = norm(target0, 3).astype(low_type)
+    inner3, norm3 = norm(target0, 3)
     branch3, keep3 = self_attention(inner3, w_in1, w_out1, self_spans)
     target1 = target0 + branch3
-    inner4 = norm(target1, 4).astype(low_type)
+    inner4, norm4 = norm(target1, 4)
     branch4, keep4 = cross_attention(inner4, memory, w_in2, w_out2, cross_spans)
     target2 = target1 + branch4
-    inner5 = norm(target2, 5).astype(low_type)
+    inner5, norm5 = norm(target2, 5)
     branch5, keep5 = ffn(inner5, f_in1, f_out1)
     target3 = target2 + branch5
-    final = norm(target3, 6).astype(low_type)
+    final, norm6 = norm(target3, 6)
 
     def pack(slots, rows):
         own_chosen, own_slots, far_slots = packing(slots, rows)
@@ -927,13 +961,12 @@
     token_local = jnp.sum(jnp.where(mine, log_total, 0.0))
     logs = jnp.where(valid, log_total + jnp.log(count), 1e30)
     weights = jnp.where(valid, 1.0 / count, 0.0)
-    split = halving_fits(own_words, width, False)
+    split = halving_fits(own_words, width // 2, False)
     *d_table, d_pieces, picks = head_back(
         plan, table_part, pieces, turned, targets, logs[None], weights[None], split and own_words
     )
     token_local = token_local - jnp.sum(picks)
-    if split:
-        arrived = swap(d_table[1], "dp", 1)
+    table_one = [TableChain(d_table[0], d_table[2])] if split else []
     if seqs == 2:
         d_final = lax.cond(
             more, lambda: unpack(2 * span, span), lambda: unpack(min(2 * cut, 2 * span), cut)
@@ -974,53 +1007,60 @@
         whole = owned(grad)
         return [whole[:, at : at + share] for at in range(0, whole.shape[1], share)]
 
-    none = jnp.zeros_like(stream0)
-    d_target3, scale6 = norm_backward(target3, gains[6], d_final, none)
+    d_target3, scale6 = norm_backward(norm6, gains[6], d_final)
     d_inner5, d_fin1, d_fout1 = ffn_back(inner5, f_in1, f_out1, keep5, d_target3)
-    if split:
-        d_inner5, d_target3, arrived = lax.optimization_barrier((d_inner5, d_target3, arrived))
-        table_grad = table_to_owner(d_table[0], arrived)
-    else:
-        table_grad = lax.psum_scatter(d_table[0], "dp", scatter_dimension=0, tiled=True)
+    d_inner5, d_target3, d_table = advance((d_inner5, d_target3, d_table), table_one)
+    table_two = [TableChain(d_table[1], d_table[3])] if split else []
     chain_a = LayerChain([owned(d_fin1)] + owned_columns(d_fout1))
-    d_target2, scale5 = norm_backward(target2, gains[5], d_inner5, d_target3)
+    d_target2, scale5 = norm_backward(norm5, gains[5], d_inner5, d_target3)
     d_inner4, d_cross, d_win2, d_wout2 = cross_attention_back(
-        inner4, memory, w_in2, w_out2, cross_spans, keep4, d_target2
-    )
-    chains = [chain_a]
-    d_inner4, d_target2, d_cross = advance((d_inner4, d_target2, d_cross), chains)
+        inner4, memory, w_in2, w_out2, cross_spans, keep4, d_target2, [], table_one + [chain_a]
+    )
     chain_b = LayerChain([owned(d_win2), owned(d_wout2)])
-    d_target1, scale4 = norm_backward(target1, gains[4], d_inner4, d_target2)
+    d_target1, scale4 = norm_backward(norm4, gains[4], d_inner4, d_target2)
     d_inner3, d_win1, d_wout1 = self_attention_back(
-        inner3, w_in1, w_out1, self_spans, keep3, d_target1
-    )
-    chains += [chain_b]
-    d_inner3, d_target1 = advance((d_inner3, d_target1), chains)
+        inner3,
+        w_in1,
+        w_out1,
+        self_spans,
+        keep3,
+        d_target1,
+        table_two,
+        table_one + [chain_a, chain_b],
+    )
     chain_c = LayerChain([owned(d_win1), owned(d_wout1)])
-    d_target0, scale3 = norm_backward(target0, gains[3], d_inner3, d_target1)
+    d_target0, scale3 = norm_backward(norm3, gains[3], d_inner3, d_target1)
+    d_stream2, scale2 = norm_backward(norm2, gains[2], d_memory + d_cross)
+    d_stream2, d_target0 = advance((d_stream2, d_target0), [chain_b])
     dec_grad = d_target0 * root
     dec_sums = give_rows(dec_maps[0], dec_grad)
-    d_stream2, scale2 = norm_backward(stream2, gains[2], d_memory + d_cross, none)
     d_inner1, d_fin0, d_fout0 = ffn_back(inner1, f_in0, f_out0, keep1, d_stream2)
-    chains += [chain_c]
+    chains = table_one + table_two + [chain_a, chain_c]
     d_inner1, d_stream2 = advance((d_inner1, d_stream2), chains)
     chain_d = LayerChain([owned(d_fin0)] + owned_columns(d_fout0))
-    d_stream1, scale1 = norm_backward(stream1, gains[1], d_inner1, d_stream2)
+    d_stream1, scale1 = norm_backward(norm1, gains[1], d_inner1, d_stream2)
     d_inner0, d_win0, d_wout0 = self_attention_back(
-        inner0, w_in0, w_out0, enc_spans, keep0, d_stream1
-    )
-    chains += [chain_d]
-    d_inner0, d_stream1, dec_sums = advance((d_inner0, d_stream1, dec_sums), chains)
-    d_stream0, scale0 = norm_backward(stream0, gains[0], d_inner0, d_stream1)
+        inner0,
+        w_in0,
+        w_out0,
+        enc_spans,
+        keep0,
+        d_stream1,
+        [chain_b, chain_c, chain_d],
+        table_two + [chain_a, chain_c, chain_d],
+    )
+    chain_e = LayerChain([owned(d_win0), owned(d_wout0), owned(d_w_len)])
+    d_stream0, scale0 = norm_backward(norm0, gains[0], d_inner0, d_stream1)
+    late = table_two + [chain_b, chain_c, chain_d, chain_e]
+    d_stream0, dec_sums = advance((d_stream0, dec_sums), late)
     src_grad = d_stream0 * root
     src_sums = give_rows(src_maps[0], src_grad)
-    chain_e = LayerChain([owned(d_win0), owned(d_wout0), owned(d_w_len)])
     norm_share = norms.shape[2]
-    scales = jnp.sum(jnp.stack([scale0, scale1, scale2, scale3, scale4, scale5, scale6], 1), 3)
+    scales = jnp.stack([scale0, scale1, scale2, scale3, scale4, scale5, scale6], 1)
     scales = scales.reshape(2 * norm_count, owners, norm_share).transpose(1, 0, 2)
     scales = jnp.broadcast_to(scales[None], (seqs,) + scales.shape)
     scales = to_each(scales.reshape((devices,) + scales.shape[2:]))
-    chains += [chain_e]
+    chains = table_one + table_two + [chain_a, chain_b, chain_c, chain_d, chain_e]
     advance((), chains)
     src_sums, scales = advance((src_sums, scales), chains)
     while any(chain.pending is not None for chain in chains):
@@ -1038,6 +1078,10 @@
         lambda turn: give(round_of(dec_ask, turn), dec_grad)
         + give(round_of(src_ask, turn), src_grad),
     )
+    if split:
+        table_grad = jnp.concatenate([chain.value for chain in table_one + table_two], 1)
+    else:
+        table_grad = lax.psum_scatter(d_table[0], "dp", scatter_dimension=0, tiled=True)
     table_grad = table_grad + given
     square = sum(chain.square for chain in layer_chains)
     square = square + jnp.sum(table_grad * table_grad) + norm_square

time: 1100 us -> 1040 us (0.945)
  waiting for transfers between devices: 316 us -> 209 us
  starting transfers between devices: 87.2 us -> 110 us
  other arithmetic: 151 us -> 168 us
  loops' own time: 2.45 us -> 14.9 us
  local copies, waits for them, and re-layouts: 105 us -> 93.5 us
    reduce_scatter x1 -> x0, waiting for transfers between devices: 49.7 us -> none  [table_to_owner(): lax.psum_scatter(keep + arrived.astype(f32), 'dp', scatter_dimension=0, a...]
    ppermute x20 -> x27, starting transfers between devices: 14.7 us -> 59.6 us  [swap(): return lax.ppermute(values, axis, [(i, i ^ bit) for i in range(size)])]
    all_to_all x5, waiting for transfers between devices: 64.8 us -> 22.5 us  [launch(): self.pending = lax.all_to_all(whole, 'dp', 0, 0, axis_index_groups=groups)]
    all_to_all x5, starting transfers between devices: 47.8 us -> 23.6 us  [launch(): self.pending = lax.all_to_all(whole, 'dp', 0, 0, axis_index_groups=groups)]
    ppermute x20 -> x27, waiting for transfers between devices: 62.7 us -> 45.4 us  [swap(): return lax.ppermute(values, axis, [(i, i ^ bit) for i in range(size)])]
    unnamed x437 -> x455, local copies, waits for them, and re-layouts: 64.1 us -> 55.8 us
  transfers between devices with their start and end apart: 35 -> 41, of which waited for: 21 -> 15; matrix products, arithmetic and copies ran while one was open for 31% -> 35% of each run, Pallas kernels for 11% -> 15%
where the time goes in v7:
time: 1040 us; the launch traced here: 1020 us
  Pallas kernels  212 us (20%)
  waiting for transfers between devices  209 us (20%)
  matrix products  182 us (18%)
  other arithmetic  168 us (16%)
  starting transfers between devices  110 us (11%)
  local copies, waits for them, and re-layouts  93.5 us (9%)
  between operations  35.6 us (3%)
  loops' own time  14.9 us (1%)
    dot_general x52, matrix products, contract(): lax.dot_general(left, right, (((left_dim,), (right_dim,)), ((), ())), pre...  179 us
    all_to_all x7, waiting for transfers between devices, to_each(): return lax.all_to_all(values, ('seq', 'dp'), 0, 0)  141 us
    pallas_call x3, Pallas kernels, attend_backward(): pl.pallas_call(functools.partial(attend_backward_kernel, head=width // HE...  70.6 us
    ppermute x27, starting transfers between devices, swap(): return lax.ppermute(values, axis, [(i, i ^ bit) for i in range(size)])  59.6 us
    unnamed x455, local copies, waits for them, and re-layouts  55.8 us
    ppermute x27, waiting for transfers between devices, swap(): return lax.ppermute(values, axis, [(i, i ^ bit) for i in range(size)])  45.4 us
    pallas_call x1, Pallas kernels, head_back(): pl.pallas_call(functools.partial(head_back_kernel, owned=owned), grid_spe...  44.1 us
    pallas_call x7, Pallas kernels, norm_backward(): pl.pallas_call(norm_back_kernel, grid=(places // columns,), in_specs=[blo...  40.2 us
  transfers between devices with their start and end apart: 41, of which 15 were waited for; matrix products, arithmetic and copies ran while one was open for 35% of the time, Pallas kernels for 15%

profile of v7, /device:TPU:0, one launch (start us, length us, event | category | flops | bytes accessed | tf_op | source)
XLA Modules:
  0.0 1024.7 jit_solution(3984616670255334565)
XLA Ops:
  55.3 7.1 all-to-all-done.8
  71.0 8.3 multiply_sine_fusion
  98.7 63.3 %all-to-all-done.9 = bf16[32,64,512]{2,1,0:T(8,128)(2,1)} async-done(((bf16[32,64,512]{2,1,0:T(8,128)(2,1)}), bf16[32,64,512]{2,1,0:T(8,128)(2,1)}, u32[]{:S(2)}, u32[]{:S(2)}) %all-to-all-start.9) | async-done | bytes 2097184 | tf_op jit(solution)/shard_map/all_to_all | solution.py:491
  188.1 13.4 %attend_forward.3 = (bf16[512,1024]{1,0:T(8,128)(2,1)}, f32[8,1024]{1,0:T(8,128)}) custom-call(s32[2,4]{1,0:T(2,128)} %pad_add_fusion.5.bounds, bf16[1536,1024]{1,0:T(8,128)(2,1)} %convolution_convert_fusion.2.q_ref.k_ref.v_ref, bf16[1536,1024]{1,0:T(8,128)(2,1)} %convolution_convert_fusion.2.q_ref.k_ref.v_ref, ...), custom_call_target="tpu_custom_call" | custom-call | tf_op jit(solution)/shard_map/attend_forward/pallas_call | solution.py:193
  203.7 37.0 %all-to-all-done.10 = bf16[32,48,512]{2,1,0:T(8,128)(2,1)} async-done(((bf16[32,48,512]{2,1,0:T(8,128)(2,1)}), bf16[32,48,512]{2,1,0:T(8,128)(2,1)}, u32[]{:S(2)}, u32[]{:S(2)}) %all-to-all-start.10) | async-done | bytes 1572896 | tf_op jit(solution)/shard_map/all_to_all | solution.py:491
  269.7 13.5 %attend_forward.4 = (bf16[512,1024]{1,0:T(8,128)(2,1)}, f32[8,1024]{1,0:T(8,128)}) custom-call(s32[2,4]{1,0:T(2,128)} %pad_add_fusion.6.bounds, bf16[1536,1024]{1,0:T(8,128)(2,1)} %convolution_convert_fusion.1.q_ref.k_ref.v_ref, bf16[1536,1024]{1,0:T(8,128)(2,1)} %convolution_convert_fusion.1.q_ref.k_ref.v_ref, ...), custom_call_target="tpu_custom_call" | custom-call | tf_op jit(solution)/shard_map/attend_forward/pallas_call | solution.py:193
  293.5 13.0 %attend_forward.5 = (bf16[512,1024]{1,0:T(8,128)(2,1)}, f32[8,1024]{1,0:T(8,128)}) custom-call(s32[2,4]{1,0:T(2,128)} %pad_add_fusion.7.bounds, bf16[512,1024]{1,0:T(8,128)(2,1)} %convolution_convert_fusion.8.q_ref, bf16[1024,1024]{1,0:T(8,128)(2,1)} %convolution_convert_fusion.4.k_ref.v_ref, bf16[1024,1024]{1,0:T(8,128)(2,1)} %convolution_convert_fusion.4.k_ref.v_ref, ...), custom_call_target="tpu_custom_call" | custom-call | tf_op jit(solution)/shard_map/attend_forward/pallas_call | solution.py:193
  319.5 16.4 %conditional.2 = (bf16[2048,512]{1,0:T(8,128)(2,1)S(1)}) conditional(s32[]{:T(128)} %convert_element_type.552, (s32[1024]{0:T(1024)S(1)}, bf16[512,1024]{1,0:T(8,128)(2,1)S(1)}, s32[]{:T(128)}, s32[2]{0:T(128)S(1)}, s32[2]{0:T(128)S(1)}, /*index=5*/s32[1024]{0:T(1024)S(1)}) %tuple.314, (s32[1024]{0:T(1024)S(1)}, bf16[512,1024]{1,0:T(8,128)(2,1)S(1)}, ...), branch_computations={%region_59.60_spmd, %region_60.61_spmd} | conditional | flops 5376576512 | bytes 18890878 | solution.py:948
  347.3 17.2 %head_stats.1 = f32[2,2048]{1,0:T(2,128)} custom-call(s32[4]{0:T(128)} %pad_add_fusion.8.plan, bf16[16000,512]{1,0:T(8,128)(2,1)} %all-gather.3.cloned.1.call-done.table_ref, bf16[512,2048]{1,0:T(8,128)(2,1)} %bitcast.711), custom_call_target="tpu_custom_call" | custom-call | tf_op jit(solution)/shard_map/head_stats/pallas_call | solution.py:409
  371.1 44.1 %head_back.1 = (f32[8,1000,256]{2,1,0:T(8,128)}, f32[8,1000,256]{2,1,0:T(8,128)}, bf16[8,1000,256]{2,1,0:T(8,128)(2,1)}, bf16[8,1000,256]{2,1,0:T(8,128)(2,1)}, f32[2048,512]{1,0:T(8,128)}, /*index=5*/f32[8,2048]{1,0:T(8,128)}) custom-call(s32[4]{0:T(128)} %pad_add_fusion.8.plan, bf16[16000,512]{1,0:T(8,128)(2,1)} %all-gather.3.cloned.1.call-done.table_ref, ...), custom_call_target="tpu_custom_call" | custom-call | tf_op jit(solution)/shard_map/head_back/pallas_call | solution.py:439
  415.3 23.0 %conditional.3 = (f32[512,1024]{1,0:T(8,128)}) conditional(s32[]{:T(128)} %convert_element_type.552, (s32[1024]{0:T(1024)S(1)}, f32[2048,512]{1,0:T(8,128)}, s32[]{:T(128)}, s32[2]{0:T(128)S(1)}, s32[2]{0:T(128)S(1)}, /*index=5*/s32[1024]{0:T(1024)S(1)}) %tuple.316, (s32[1024]{0:T(1024)S(1)}, f32[2048,512]{1,0:T(8,128)}, s32[]{:T(128)}, ...), branch_computations={%region_73.74_spmd, %region_74.75_spmd} | conditional | flops 7532448768 | bytes 50352280 | solution.py:971
  438.3 22.4 %collective-permute-start.6 = (bf16[8,1000,256]{2,1,0:T(8,128)(2,1)}, bf16[8,1000,256]{2,1,0:T(8,128)(2,1)S(1)}, u32[]{:S(2)}, u32[]{:S(2)}) collective-permute-start(bf16[8,1000,256]{2,1,0:T(8,128)(2,1)} %get-tuple-element.768), channel_id=1, source_target_pairs={{0,2},{2,0},{4,6},{6,4},{8,10},{10,8},{12,14},{14,12},{16,18},{18,... | collective-permute-start | bytes 12288008 | tf_op jit(solution)/shard_map/ppermute | solution.py:471
  465.9 9.6 fusion.95
  502.4 6.1 collective-permute-start.7
  515.2 6.3 norm_backward.8
  526.9 22.5 %attend_backward.3 = (bf16[512,1024]{1,0:T(8,128)(2,1)}, bf16[1024,1024]{1,0:T(8,128)(2,1)}) custom-call(s32[2,4]{1,0:T(2,128)} %pad_add_fusion.7.bounds, bf16[512,1024]{1,0:T(8,128)(2,1)} %convolution_convert_fusion.8.q_ref, bf16[1024,1024]{1,0:T(8,128)(2,1)} %convolution_convert_fusion.4.k_ref.v_ref, ...), custom_call_target="tpu_custom_call" | custom-call | tf_op jit(solution)/shard_map/attend_backward/pallas_call | solution.py:218
  571.8 5.9 norm_backward.10
  592.6 24.1 %attend_backward.4 = (bf16[512,1024]{1,0:T(8,128)(2,1)}, bf16[1024,1024]{1,0:T(8,128)(2,1)}) custom-call(s32[2,4]{1,0:T(2,128)} %pad_add_fusion.6.bounds, bf16[1536,1024]{1,0:T(8,128)(2,1)} %convolution_convert_fusion.1.q_ref.k_ref.v_ref, bf16[1536,1024]{1,0:T(8,128)(2,1)} %convolution_convert_fusion.1.q_ref.k_ref.v_ref, ...), custom_call_target="tpu_custom_call" | custom-call | tf_op jit(solution)/shard_map/attend_backward/pallas_call | solution.py:218
  625.2 6.0 bitcast_add_fusion.2
  645.9 6.1 norm_backward.11
  654.2 8.8 fusion.88
  663.0 7.0 fusion.197
  683.9 6.6 fusion.136.grad_ref
  697.4 13.0 %all-to-all-done.11 = bf16[8,16,4096]{2,1,0:T(8,128)(2,1)S(1)} async-done(((bf16[8,16,4096]{2,1,0:T(8,128)(2,1)}), bf16[8,16,4096]{2,1,0:T(8,128)(2,1)S(1)}, u32[]{:S(2)}, u32[]{:S(2)}) %all-to-all-start.11) | async-done | bytes 1048608 | tf_op jit(solution)/shard_map/all_to_all | solution.py:520
  768.3 24.0 %attend_backward.5 = (bf16[512,1024]{1,0:T(8,128)(2,1)}, bf16[1024,1024]{1,0:T(8,128)(2,1)}) custom-call(s32[2,4]{1,0:T(2,128)} %pad_add_fusion.5.bounds, bf16[1536,1024]{1,0:T(8,128)(2,1)} %convolution_convert_fusion.2.q_ref.k_ref.v_ref, bf16[1536,1024]{1,0:T(8,128)(2,1)} %convolution_convert_fusion.2.q_ref.k_ref.v_ref, ...), custom_call_target="tpu_custom_call" | custom-call | tf_op jit(solution)/shard_map/attend_backward/pallas_call | solution.py:218
  804.0 6.1 all-to-all-start.15
  829.5 28.1 %collective-permute-done.22 = bf16[1,1000,256]{2,1,0:T(8,128)(2,1)S(1)} collective-permute-done((bf16[1,1000,256]{2,1,0:T(8,128)(2,1)S(1)}, bf16[1,1000,256]{2,1,0:T(8,128)(2,1)S(1)}, u32[]{:S(2)}, u32[]{:S(2)}) %collective-permute-start.22) | collective-permute-done | bytes 512032 | tf_op jit(solution)/shard_map/ppermute | solution.py:471
  873.2 6.8 collective-permute-done.26
  902.7 9.5 all-to-all-done.18
  945.8 20.9 %all-to-all-done.16 = bf16[32,64,512]{2,1,0:T(8,128)(2,1)} async-done(((bf16[32,64,512]{2,1,0:T(8,128)(2,1)}), bf16[32,64,512]{2,1,0:T(8,128)(2,1)}, u32[]{:S(2)}, u32[]{:S(2)}) %all-to-all-start.16) | async-done | bytes 2097184 | tf_op jit(solution)/shard_map/all_to_all | solution.py:491
  991.1 7.0 all-to-all-done.19
  1001.5 7.5 multiply_subtract_fusion
  (852 shorter events, 504.8 us)
Async XLA Ops:
  7.2 172.5 %all-gather.5.cloned.1.call-start = ((), (), s32[]{:S(2)}) async-start(), calls=%async_computation.21 | async-start | bytes 15544320 | tf_op jit(solution)/shard_map/all_gather | solution.py:686
  24.0 323.3 %all-gather.3.cloned.1.call-start = ((), (), s32[]{:S(2)}) async-start(), calls=%async_computation.20 | async-start | bytes 17408000 | tf_op jit(solution)/shard_map/all_gather | solution.py:709
  67.3 94.8 %all-to-all-start.9 = ((bf16[32,64,512]{2,1,0:T(8,128)(2,1)}), bf16[32,64,512]{2,1,0:T(8,128)(2,1)}, u32[]{:S(2)}, u32[]{:S(2)}) async-start(bf16[32,64,512]{2,1,0:T(8,128)(2,1)} %bitcast.47), calls=%async_computation.9 | async-start | bytes 4194304 | tf_op jit(solution)/shard_map/all_to_all | solution.py:491
  168.8 71.9 %all-to-all-start.10 = ((bf16[32,48,512]{2,1,0:T(8,128)(2,1)}), bf16[32,48,512]{2,1,0:T(8,128)(2,1)}, u32[]{:S(2)}, u32[]{:S(2)}) async-start(bf16[32,48,512]{2,1,0:T(8,128)(2,1)} %bitcast.796), calls=%async_computation.10 | async-start | bytes 3145728 | tf_op jit(solution)/shard_map/all_to_all | solution.py:491
  438.3 57.5 %collective-permute-start.6 = (bf16[8,1000,256]{2,1,0:T(8,128)(2,1)}, bf16[8,1000,256]{2,1,0:T(8,128)(2,1)S(1)}, u32[]{:S(2)}, u32[]{:S(2)}) collective-permute-start(bf16[8,1000,256]{2,1,0:T(8,128)(2,1)} %get-tuple-element.768), channel_id=1, source_target_pairs={{0,2},{2,0},{4,6},{6,4},{8,10},{10,8},{12,14},{14,12},{16,18},{18,... | collective-permute-start | bytes 12288008 | tf_op jit(solution)/shard_map/ppermute | solution.py:471
  490.1 59.3 %collective-permute-start.8 = (bf16[8,32,4096]{2,1,0:T(8,128)(2,1)}, bf16[8,32,4096]{2,1,0:T(8,128)(2,1)}, u32[]{:S(2)}, u32[]{:S(2)}) collective-permute-start(bf16[8,32,4096]{2,1,0:T(8,128)(2,1)} %fusion.225), channel_id=1, source_target_pairs={{0,2},{2,0},{4,6},{6,4},{8,10},{10,8},{12,14},{14,12},{16,18},{18,... | collective-permute-start | bytes 6291464 | tf_op jit(solution)/shard_map/ppermute | solution.py:471
  502.4 51.2 %collective-permute-start.7 = (bf16[4,1000,256]{2,1,0:T(8,128)(2,1)}, bf16[4,1000,256]{2,1,0:T(8,128)(2,1)}, u32[]{:S(2)}, u32[]{:S(2)}) collective-permute-start(bf16[4,1000,256]{2,1,0:T(8,128)(2,1)} %get-tuple-element.1110), channel_id=1, source_target_pairs={{0,4},{2,6},{4,0},{6,2},{8,12},{10,14},{12,8},{14,10},{16,20},{18,... | collective-permute-start | bytes 6144008 | tf_op jit(solution)/shard_map/ppermute | solution.py:471
  515.2 77.3 %collective-permute-start.9 = (bf16[8,1000,256]{2,1,0:T(8,128)(2,1)}, bf16[8,1000,256]{2,1,0:T(8,128)(2,1)}, u32[]{:S(2)}, u32[]{:S(2)}) collective-permute-start(bf16[8,1000,256]{2,1,0:T(8,128)(2,1)} %get-tuple-element.781), channel_id=1, source_target_pairs={{0,2},{2,0},{4,6},{6,4},{8,10},{10,8},{12,14},{14,12},{16,18},{18,... | collective-permute-start | bytes 12288008 | tf_op jit(solution)/shard_map/ppermute | solution.py:471
  558.5 58.2 %collective-permute-start.12 = (bf16[8,32,2048]{2,1,0:T(8,128)(2,1)}, bf16[8,32,2048]{2,1,0:T(8,128)(2,1)}, u32[]{:S(2)}, u32[]{:S(2)}) collective-permute-start(bf16[8,32,2048]{2,1,0:T(8,128)(2,1)} %pad_maximum_fusion.7), channel_id=1, source_target_pairs={{0,2},{2,0},{4,6},{6,4},{8,10},{10,8},{12,14},{14,12},{16,18},{18,... | collective-permute-start | bytes 3145736 | tf_op jit(solution)/shard_map/ppermute | solution.py:471
  560.6 56.1 %collective-permute-start.11 = (bf16[8,16,4096]{2,1,0:T(8,128)(2,1)S(1)}, bf16[8,16,4096]{2,1,0:T(8,128)(2,1)}, u32[]{:S(2)}, u32[]{:S(2)}) collective-permute-start(bf16[8,16,4096]{2,1,0:T(8,128)(2,1)S(1)} %fusion.152), channel_id=1, source_target_pairs={{0,1},{1,0},{2,3},{3,2},{4,5},{5,4},{6,7},{7,6},{8,9},{9,8},{10,11... | collective-permute-start | bytes 3145736 | tf_op jit(solution)/shard_map/ppermute | solution.py:471
  564.4 52.3 %collective-permute-start.10 = (bf16[2,1000,256]{2,1,0:T(8,128)(2,1)}, bf16[2,1000,256]{2,1,0:T(8,128)(2,1)}, u32[]{:S(2)}, u32[]{:S(2)}) collective-permute-start(bf16[2,1000,256]{2,1,0:T(8,128)(2,1)} %get-tuple-element.1112), channel_id=1, source_target_pairs={{0,8},{2,10},{4,12},{6,14},{8,0},{10,2},{12,4},{14,6},{16,24},{18,... | collective-permute-start | bytes 3072008 | tf_op jit(solution)/shard_map/ppermute | solution.py:471
  624.2 92.3 %collective-permute-start.16 = (bf16[8,32,2048]{2,1,0:T(8,128)(2,1)}, bf16[8,32,2048]{2,1,0:T(8,128)(2,1)}, u32[]{:S(2)}, u32[]{:S(2)}) collective-permute-start(bf16[8,32,2048]{2,1,0:T(8,128)(2,1)} %pad_maximum_fusion.8), channel_id=1, source_target_pairs={{0,2},{2,0},{4,6},{6,4},{8,10},{10,8},{12,14},{14,12},{16,18},{18,... | collective-permute-start | bytes 3145736 | tf_op jit(solution)/shard_map/ppermute | solution.py:471
  631.1 85.4 %collective-permute-start.15 = (bf16[4,1000,256]{2,1,0:T(8,128)(2,1)}, bf16[4,1000,256]{2,1,0:T(8,128)(2,1)}, u32[]{:S(2)}, u32[]{:S(2)}) collective-permute-start(bf16[4,1000,256]{2,1,0:T(8,128)(2,1)} %get-tuple-element.1108), channel_id=1, source_target_pairs={{0,4},{2,6},{4,0},{6,2},{8,12},{10,14},{12,8},{14,10},{16,20},{18,... | collective-permute-start | bytes 6144008 | tf_op jit(solution)/shard_map/ppermute | solution.py:471
  634.9 81.6 %collective-permute-start.14 = (bf16[1,1000,256]{2,1,0:T(8,128)(2,1)}, bf16[1,1000,256]{2,1,0:T(8,128)(2,1)}, u32[]{:S(2)}, u32[]{:S(2)}) collective-permute-start(bf16[1,1000,256]{2,1,0:T(8,128)(2,1)} %fusion.181), channel_id=1, source_target_pairs={{0,16},{2,18},{4,20},{6,22},{8,24},{10,26},{12,28},{14,30},{16,0},... | collective-permute-start | bytes 1536008 | tf_op jit(solution)/shard_map/ppermute | solution.py:471
  636.8 16.4 %collective-permute-start.13 = (bf16[8,16,2048]{2,1,0:T(8,128)(2,1)S(1)}, bf16[8,16,2048]{2,1,0:T(8,128)(2,1)S(1)}, u32[]{:S(2)}, u32[]{:S(2)}) collective-permute-start(bf16[8,16,2048]{2,1,0:T(8,128)(2,1)S(1)} %fusion.192), channel_id=1, source_target_pairs={{0,1},{1,0},{2,3},{3,2},{4,5},{5,4},{6,7},{7,6},{8,9},{9,8},{10,11... | collective-permute-start | bytes 1572872 | tf_op jit(solution)/shard_map/ppermute | solution.py:471
  679.9 52.2 %collective-permute-start.18 = (bf16[8,32,4096]{2,1,0:T(8,128)(2,1)}, bf16[8,32,4096]{2,1,0:T(8,128)(2,1)}, u32[]{:S(2)}, u32[]{:S(2)}) collective-permute-start(bf16[8,32,4096]{2,1,0:T(8,128)(2,1)} %fusion.233), channel_id=1, source_target_pairs={{0,2},{2,0},{4,6},{6,4},{8,10},{10,8},{12,14},{14,12},{16,18},{18,... | collective-permute-start | bytes 6291464 | tf_op jit(solution)/shard_map/ppermute | solution.py:471
  679.9 30.5 %all-to-all-start.11 = ((bf16[8,16,4096]{2,1,0:T(8,128)(2,1)}), bf16[8,16,4096]{2,1,0:T(8,128)(2,1)S(1)}, u32[]{:S(2)}, u32[]{:S(2)}) async-start(bf16[8,16,4096]{2,1,0:T(8,128)(2,1)} %fusion.127), calls=%async_computation.11 | async-start | bytes 2097152 | tf_op jit(solution)/shard_map/all_to_all | solution.py:520
  710.3 20.8 %all-to-all-start.12 = ((bf16[8,16,2048]{2,1,0:T(8,128)(2,1)}), bf16[8,16,2048]{2,1,0:T(8,128)(2,1)}, u32[]{:S(2)}, u32[]{:S(2)}) async-start(bf16[8,16,2048]{2,1,0:T(8,128)(2,1)} %fusion.169), calls=%async_computation.12 | async-start | bytes 1048576 | tf_op jit(solution)/shard_map/all_to_all | solution.py:520
  734.3 19.5 %all-to-all-start.13 = ((bf16[8,16,2048]{2,1,0:T(8,128)(2,1)}), bf16[8,16,2048]{2,1,0:T(8,128)(2,1)S(1)}, u32[]{:S(2)}, u32[]{:S(2)}) async-start(bf16[8,16,2048]{2,1,0:T(8,128)(2,1)} %fusion.160), calls=%async_computation.13 | async-start | bytes 1048576 | tf_op jit(solution)/shard_map/all_to_all | solution.py:520
  747.6 44.7 %collective-permute-start.21 = (bf16[8,16,4096]{2,1,0:T(8,128)(2,1)}, bf16[8,16,4096]{2,1,0:T(8,128)(2,1)}, u32[]{:S(2)}, u32[]{:S(2)}) collective-permute-start(bf16[8,16,4096]{2,1,0:T(8,128)(2,1)} %fusion.155), channel_id=1, source_target_pairs={{0,1},{1,0},{2,3},{3,2},{4,5},{5,4},{6,7},{7,6},{8,9},{9,8},{10,11... | collective-permute-start | bytes 3145736 | tf_op jit(solution)/shard_map/ppermute | solution.py:471
  751.7 40.6 %collective-permute-start.19 = (bf16[2,1000,256]{2,1,0:T(8,128)(2,1)}, bf16[2,1000,256]{2,1,0:T(8,128)(2,1)}, u32[]{:S(2)}, u32[]{:S(2)}) collective-permute-start(bf16[2,1000,256]{2,1,0:T(8,128)(2,1)} %fusion.175), channel_id=1, source_target_pairs={{0,8},{2,10},{4,12},{6,14},{8,0},{10,2},{12,4},{14,6},{16,24},{18,... | collective-permute-start | bytes 3072008 | tf_op jit(solution)/shard_map/ppermute | solution.py:471
  754.6 49.4 %all-to-all-start.14 = ((bf16[32,48,512]{2,1,0:T(8,128)(2,1)}), bf16[32,48,512]{2,1,0:T(8,128)(2,1)}, u32[]{:S(2)}, u32[]{:S(2)}) async-start(bf16[32,48,512]{2,1,0:T(8,128)(2,1)} %bitcast.797), calls=%async_computation.14 | async-start | bytes 3145728 | tf_op jit(solution)/shard_map/all_to_all | solution.py:491
  759.0 33.3 %collective-permute-start.20 = (f32[16,4096]{1,0:T(8,128)S(1)}, f32[16,4096]{1,0:T(8,128)S(1)}, u32[]{:S(2)}, u32[]{:S(2)}) collective-permute-start(f32[16,4096]{1,0:T(8,128)S(1)} %convert_reduce_fusion.3), channel_id=1, source_target_pairs={{0,1},{1,0},{2,3},{3,2},{4,5},{5,4},{6,7},{7,6},{8,9},{9,8},{10,11... | collective-permute-start | bytes 786440 | tf_op jit(solution)/shard_map/ppermute | solution.py:471
  767.9 61.6 %collective-permute-start.23 = (f32[16,2048]{1,0:T(8,128)}, f32[16,2048]{1,0:T(8,128)}, u32[]{:S(2)}, u32[]{:S(2)}) collective-permute-start(f32[16,2048]{1,0:T(8,128)} %convert_reduce_fusion.6), channel_id=1, source_target_pairs={{0,1},{1,0},{2,3},{3,2},{4,5},{5,4},{6,7},{7,6},{8,9},{9,8},{10,11... | collective-permute-start | bytes 393224 | tf_op jit(solution)/shard_map/ppermute | solution.py:471
  804.0 54.4 %all-to-all-start.15 = ((bf16[8,16,4096]{2,1,0:T(8,128)(2,1)}), bf16[8,16,4096]{2,1,0:T(8,128)(2,1)S(1)}, u32[]{:S(2)}, u32[]{:S(2)}) async-start(bf16[8,16,4096]{2,1,0:T(8,128)(2,1)} %fusion.126), calls=%async_computation.15 | async-start | bytes 2097152 | tf_op jit(solution)/shard_map/all_to_all | solution.py:520
  811.5 46.9 %collective-permute-start.25 = (bf16[8,32,2304]{2,1,0:T(8,128)(2,1)S(1)}, bf16[8,32,2304]{2,1,0:T(8,128)(2,1)}, u32[]{:S(2)}, u32[]{:S(2)}) collective-permute-start(bf16[8,32,2304]{2,1,0:T(8,128)(2,1)S(1)} %pad_maximum_fusion.6), channel_id=1, source_target_pairs={{0,2},{2,0},{4,6},{6,4},{8,10},{10,8},{12,14},{14,12},{16,18},{18,... | collective-permute-start | bytes 3538952 | tf_op jit(solution)/shard_map/ppermute | solution.py:471
  812.8 44.8 %collective-permute-start.22 = (bf16[1,1000,256]{2,1,0:T(8,128)(2,1)S(1)}, bf16[1,1000,256]{2,1,0:T(8,128)(2,1)S(1)}, u32[]{:S(2)}, u32[]{:S(2)}) collective-permute-start(bf16[1,1000,256]{2,1,0:T(8,128)(2,1)S(1)} %fusion.180), channel_id=1, source_target_pairs={{0,16},{2,18},{4,20},{6,22},{8,24},{10,26},{12,28},{14,30},{16,0},... | collective-permute-start | bytes 1536008 | tf_op jit(solution)/shard_map/ppermute | solution.py:471
  815.8 13.6 %collective-permute-start.24 = (f32[16,2048]{1,0:T(8,128)S(1)}, f32[16,2048]{1,0:T(8,128)S(1)}, u32[]{:S(2)}, u32[]{:S(2)}) collective-permute-start(f32[16,2048]{1,0:T(8,128)S(1)} %convert_reduce_fusion.5), channel_id=1, source_target_pairs={{0,1},{1,0},{2,3},{3,2},{4,5},{5,4},{6,7},{7,6},{8,9},{9,8},{10,11... | collective-permute-start | bytes 393224 | tf_op jit(solution)/shard_map/ppermute | solution.py:471
  860.4 19.6 %collective-permute-start.27 = (bf16[8,16,2304]{2,1,0:T(8,128)(2,1)}, bf16[8,16,2304]{2,1,0:T(8,128)(2,1)}, u32[]{:S(2)}, u32[]{:S(2)}) collective-permute-start(bf16[8,16,2304]{2,1,0:T(8,128)(2,1)} %fusion.189), channel_id=1, source_target_pairs={{0,1},{1,0},{2,3},{3,2},{4,5},{5,4},{6,7},{7,6},{8,9},{9,8},{10,11... | collective-permute-start | bytes 1769480 | tf_op jit(solution)/shard_map/ppermute | solution.py:471
  862.5 17.4 %collective-permute-start.26 = (f32[16,4096]{1,0:T(8,128)}, f32[16,4096]{1,0:T(8,128)S(1)}, u32[]{:S(2)}, u32[]{:S(2)}) collective-permute-start(f32[16,4096]{1,0:T(8,128)} %convert_reduce_fusion.2), channel_id=1, source_target_pairs={{0,1},{1,0},{2,3},{3,2},{4,5},{5,4},{6,7},{7,6},{8,9},{9,8},{10,11... | collective-permute-start | bytes 786440 | tf_op jit(solution)/shard_map/ppermute | solution.py:471
  892.1 20.1 %all-to-all-start.18 = ((bf16[8,16,2304]{2,1,0:T(8,128)(2,1)}), bf16[8,16,2304]{2,1,0:T(8,128)(2,1)S(1)}, u32[]{:S(2)}, u32[]{:S(2)}) async-start(bf16[8,16,2304]{2,1,0:T(8,128)(2,1)} %fusion.149), calls=%async_computation.18 | async-start | bytes 1179648 | tf_op jit(solution)/shard_map/all_to_all | solution.py:520
  913.0 53.8 %all-to-all-start.16 = ((bf16[32,64,512]{2,1,0:T(8,128)(2,1)}), bf16[32,64,512]{2,1,0:T(8,128)(2,1)}, u32[]{:S(2)}, u32[]{:S(2)}) async-start(bf16[32,64,512]{2,1,0:T(8,128)(2,1)} %bitcast.769), calls=%async_computation.16 | async-start | bytes 4194304 | tf_op jit(solution)/shard_map/all_to_all | solution.py:491
  (217 other events, 2459.8 us)
Sparse Core Ops, SparseCore 0:
  24.1 145.7 all-gather.4
  172.1 149.1 all-gather.2

commit v8 on v7

--- a/solution.py
+++ b/solution.py
@@ -245,11 +245,11 @@
 
 
 def norm_back_kernel(stream_ref, average_ref, inverse_ref, gain_ref, grad_ref, *refs):
-    (*rest_refs, out_ref, sums_ref) = refs
+    (*rest_refs, out_ref, sums_ref, parts) = refs
 
     @pl.when(pl.program_id(0) == 0)
     def _():
-        sums_ref[...] = jnp.zeros_like(sums_ref)
+        parts[...] = jnp.zeros_like(parts)
 
     inverse, grad = inverse_ref[...], grad_ref[...]
     unit = (stream_ref[...] - average_ref[...]) * inverse
@@ -263,8 +263,12 @@
     out_ref[...] = out
     weighted = grad * unit
     for at in range(0, places, 128):
-        sums_ref[0] += weighted[:, at : at + 128]
-        sums_ref[1] += grad[:, at : at + 128]
+        parts[0] += weighted[:, at : at + 128]
+        parts[1] += grad[:, at : at + 128]
+
+    @pl.when(pl.program_id(0) == pl.num_programs(0) - 1)
+    def _():
+        sums_ref[...] = jnp.sum(parts[...], 2, keepdims=True)
 
 
 def norm_backward(kept, gain, grad, *rests):
@@ -278,15 +282,16 @@
         grid=(places // columns,),
         in_specs=[block, row, row, pl.BlockSpec((width, 1), lambda i: (0, 0)), block]
         + [block] * len(rests),
-        out_specs=[block, pl.BlockSpec((2, width, 128), lambda i: (0, 0, 0))],
+        out_specs=[block, pl.BlockSpec((2, width, 1), lambda i: (0, 0, 0))],
         out_shape=[
             jax.ShapeDtypeStruct((width, places), f32),
-            jax.ShapeDtypeStruct((2, width, 128), f32),
+            jax.ShapeDtypeStruct((2, width, 1), f32),
         ],
+        scratch_shapes=[pltpu.VMEM((2, width, 128), f32)],
         compiler_params=pltpu.CompilerParams(vmem_limit_bytes=vmem_bytes),
         name="norm_backward",
     )(stream, average, inverse, gain[:, None], grad, *rests)
-    return out, jnp.sum(sums, 2)
+    return out, sums[:, :, 0]
 
 
 def chunk_plan(total):
@@ -1051,8 +1056,7 @@
     )
     chain_e = LayerChain([owned(d_win0), owned(d_wout0), owned(d_w_len)])
     d_stream0, scale0 = norm_backward(norm0, gains[0], d_inner0, d_stream1)
-    late = table_two + [chain_b, chain_c, chain_d, chain_e]
-    d_stream0, dec_sums = advance((d_stream0, dec_sums), late)
+    d_stream0 = advance(d_stream0, [chain_b, chain_c, chain_d, chain_e])
     src_grad = d_stream0 * root
     src_sums = give_rows(src_maps[0], src_grad)
     norm_share = norms.shape[2]
@@ -1061,8 +1065,7 @@
     scales = jnp.broadcast_to(scales[None], (seqs,) + scales.shape)
     scales = to_each(scales.reshape((devices,) + scales.shape[2:]))
     chains = table_one + table_two + [chain_a, chain_b, chain_c, chain_d, chain_e]
-    advance((), chains)
-    src_sums, scales = advance((src_sums, scales), chains)
+    src_sums, dec_sums, scales = advance((src_sums, dec_sums, scales), chains)
     while any(chain.pending is not None for chain in chains):
         advance((), chains)
     layer_chains = [chain_a, chain_b, chain_c, chain_d, chain_e]

time: 1040 us -> 1030 us (level)
    unnamed x455 -> x503, local copies, waits for them, and re-layouts: 55.8 us -> 47 us
where the time goes in v8:
time: 1030 us; the launch traced here: 1020 us
  waiting for transfers between devices  217 us (21%)
  Pallas kernels  215 us (21%)
  matrix products  184 us (18%)
  other arithmetic  165 us (16%)
  starting transfers between devices  101 us (10%)
  local copies, waits for them, and re-layouts  89.4 us (9%)
  between operations  35.8 us (3%)
  loops' own time  10.4 us (1%)
    dot_general x52, matrix products, contract(): lax.dot_general(left, right, (((left_dim,), (right_dim,)), ((), ())), pre...  182 us
    all_to_all x7, waiting for transfers between devices, to_each(): return lax.all_to_all(values, ('seq', 'dp'), 0, 0)  135 us
    pallas_call x3, Pallas kernels, attend_backward(): pl.pallas_call(functools.partial(attend_backward_kernel, head=width // HE...  70.4 us
    ppermute x27, waiting for transfers between devices, swap(): return lax.ppermute(values, axis, [(i, i ^ bit) for i in range(size)])  55.3 us
    ppermute x27, starting transfers between devices, swap(): return lax.ppermute(values, axis, [(i, i ^ bit) for i in range(size)])  52.2 us
    unnamed x503, local copies, waits for them, and re-layouts  47 us
    pallas_call x1, Pallas kernels, head_back(): pl.pallas_call(functools.partial(head_back_kernel, owned=owned), grid_spe...  44.2 us
    pallas_call x7, Pallas kernels, norm_backward(): pl.pallas_call(norm_back_kernel, grid=(places // columns,), in_specs=[blo...  43.5 us
  transfers between devices with their start and end apart: 41, of which 15 were waited for; matrix products, arithmetic and copies ran while one was open for 35% of the time, Pallas kernels for 15%

profile of v8, /device:TPU:0, one launch (start us, length us, event | category | flops | bytes accessed | tf_op | source)
XLA Modules:
  0.0 1018.0 jit_solution(6688063588785914489)
XLA Ops:
  55.4 7.1 all-to-all-done.8
  71.0 8.3 multiply_sine_fusion
  98.7 63.8 %all-to-all-done.9 = bf16[32,64,512]{2,1,0:T(8,128)(2,1)} async-done(((bf16[32,64,512]{2,1,0:T(8,128)(2,1)}), bf16[32,64,512]{2,1,0:T(8,128)(2,1)}, u32[]{:S(2)}, u32[]{:S(2)}) %all-to-all-start.9) | async-done | bytes 2097184 | tf_op jit(solution)/shard_map/all_to_all | solution.py:496
  188.7 13.4 %attend_forward.3 = (bf16[512,1024]{1,0:T(8,128)(2,1)}, f32[8,1024]{1,0:T(8,128)}) custom-call(s32[2,4]{1,0:T(2,128)} %pad_add_fusion.5.bounds, bf16[1536,1024]{1,0:T(8,128)(2,1)} %convolution_convert_fusion.2.q_ref.k_ref.v_ref, bf16[1536,1024]{1,0:T(8,128)(2,1)} %convolution_convert_fusion.2.q_ref.k_ref.v_ref, ...), custom_call_target="tpu_custom_call" | custom-call | tf_op jit(solution)/shard_map/attend_forward/pallas_call | solution.py:193
  204.3 37.5 %all-to-all-done.10 = bf16[32,48,512]{2,1,0:T(8,128)(2,1)} async-done(((bf16[32,48,512]{2,1,0:T(8,128)(2,1)}), bf16[32,48,512]{2,1,0:T(8,128)(2,1)}, u32[]{:S(2)}, u32[]{:S(2)}) %all-to-all-start.10) | async-done | bytes 1572896 | tf_op jit(solution)/shard_map/all_to_all | solution.py:496
  271.5 13.6 %attend_forward.4 = (bf16[512,1024]{1,0:T(8,128)(2,1)}, f32[8,1024]{1,0:T(8,128)}) custom-call(s32[2,4]{1,0:T(2,128)} %pad_add_fusion.6.bounds, bf16[1536,1024]{1,0:T(8,128)(2,1)} %convolution_convert_fusion.1.q_ref.k_ref.v_ref, bf16[1536,1024]{1,0:T(8,128)(2,1)} %convolution_convert_fusion.1.q_ref.k_ref.v_ref, ...), custom_call_target="tpu_custom_call" | custom-call | tf_op jit(solution)/shard_map/attend_forward/pallas_call | solution.py:193
  295.3 12.6 %attend_forward.5 = (bf16[512,1024]{1,0:T(8,128)(2,1)}, f32[8,1024]{1,0:T(8,128)}) custom-call(s32[2,4]{1,0:T(2,128)} %pad_add_fusion.7.bounds, bf16[512,1024]{1,0:T(8,128)(2,1)} %convolution_convert_fusion.8.q_ref, bf16[1024,1024]{1,0:T(8,128)(2,1)} %convolution_convert_fusion.4.k_ref.v_ref, bf16[1024,1024]{1,0:T(8,128)(2,1)} %convolution_convert_fusion.4.k_ref.v_ref, ...), custom_call_target="tpu_custom_call" | custom-call | tf_op jit(solution)/shard_map/attend_forward/pallas_call | solution.py:193
  321.0 13.1 %conditional.2 = (bf16[2048,512]{1,0:T(8,128)(2,1)S(1)}) conditional(s32[]{:T(128)} %convert_element_type.552, (s32[1024]{0:T(1024)S(1)}, bf16[512,1024]{1,0:T(8,128)(2,1)S(1)}, s32[]{:T(128)}, s32[2]{0:T(128)S(1)}, s32[2]{0:T(128)S(1)}, /*index=5*/s32[1024]{0:T(1024)S(1)}) %tuple.312, (s32[1024]{0:T(1024)S(1)}, bf16[512,1024]{1,0:T(8,128)(2,1)S(1)}, ...), branch_computations={%region_59.60_spmd, %region_60.61_spmd} | conditional | flops 5376576512 | bytes 18890878 | solution.py:953
  343.2 17.2 %head_stats.1 = f32[2,2048]{1,0:T(2,128)} custom-call(s32[4]{0:T(128)} %pad_add_fusion.8.plan, bf16[16000,512]{1,0:T(8,128)(2,1)} %all-gather.3.cloned.1.call-done.table_ref, bf16[512,2048]{1,0:T(8,128)(2,1)} %bitcast.725), custom_call_target="tpu_custom_call" | custom-call | tf_op jit(solution)/shard_map/head_stats/pallas_call | solution.py:414
  367.2 44.2 %head_back.1 = (f32[8,1000,256]{2,1,0:T(8,128)}, f32[8,1000,256]{2,1,0:T(8,128)}, bf16[8,1000,256]{2,1,0:T(8,128)(2,1)}, bf16[8,1000,256]{2,1,0:T(8,128)(2,1)}, f32[2048,512]{1,0:T(8,128)}, /*index=5*/f32[8,2048]{1,0:T(8,128)}) custom-call(s32[4]{0:T(128)} %pad_add_fusion.8.plan, bf16[16000,512]{1,0:T(8,128)(2,1)} %all-gather.3.cloned.1.call-done.table_ref, ...), custom_call_target="tpu_custom_call" | custom-call | tf_op jit(solution)/shard_map/head_back/pallas_call | solution.py:444
  411.4 23.9 %conditional.3 = (f32[512,1024]{1,0:T(8,128)}) conditional(s32[]{:T(128)} %convert_element_type.552, (s32[1024]{0:T(1024)S(1)}, f32[2048,512]{1,0:T(8,128)}, s32[]{:T(128)}, s32[2]{0:T(128)S(1)}, s32[2]{0:T(128)S(1)}, /*index=5*/s32[1024]{0:T(1024)S(1)}) %tuple.314, (s32[1024]{0:T(1024)S(1)}, f32[2048,512]{1,0:T(8,128)}, s32[]{:T(128)}, ...), branch_computations={%region_73.74_spmd, %region_74.75_spmd} | conditional | flops 7532448768 | bytes 50352280 | solution.py:976
  440.9 9.6 fusion.95
  474.0 21.6 %collective-permute-start.7 = (bf16[4,1000,256]{2,1,0:T(8,128)(2,1)}, bf16[4,1000,256]{2,1,0:T(8,128)(2,1)}, u32[]{:S(2)}, u32[]{:S(2)}) collective-permute-start(bf16[4,1000,256]{2,1,0:T(8,128)(2,1)} %get-tuple-element.1108), channel_id=1, source_target_pairs={{0,4},{2,6},{4,0},{6,2},{8,12},{10,14},{12,8},{14,10},{16,20},{18,... | collective-permute-start | bytes 6144008 | tf_op jit(solution)/shard_map/ppermute | solution.py:476
  498.0 7.8 norm_backward.8
  513.0 22.3 %attend_backward.3 = (bf16[512,1024]{1,0:T(8,128)(2,1)}, bf16[1024,1024]{1,0:T(8,128)(2,1)}) custom-call(s32[2,4]{1,0:T(2,128)} %pad_add_fusion.7.bounds, bf16[512,1024]{1,0:T(8,128)(2,1)} %convolution_convert_fusion.8.q_ref, bf16[1024,1024]{1,0:T(8,128)(2,1)} %convolution_convert_fusion.4.k_ref.v_ref, ...), custom_call_target="tpu_custom_call" | custom-call | tf_op jit(solution)/shard_map/attend_backward/pallas_call | solution.py:218
  560.9 6.3 norm_backward.10
  581.5 24.1 %attend_backward.4 = (bf16[512,1024]{1,0:T(8,128)(2,1)}, bf16[1024,1024]{1,0:T(8,128)(2,1)}) custom-call(s32[2,4]{1,0:T(2,128)} %pad_add_fusion.6.bounds, bf16[1536,1024]{1,0:T(8,128)(2,1)} %convolution_convert_fusion.1.q_ref.k_ref.v_ref, bf16[1536,1024]{1,0:T(8,128)(2,1)} %convolution_convert_fusion.1.q_ref.k_ref.v_ref, ...), custom_call_target="tpu_custom_call" | custom-call | tf_op jit(solution)/shard_map/attend_backward/pallas_call | solution.py:218
  614.5 6.1 bitcast_add_fusion.2
  635.5 6.3 norm_backward.11
  643.8 8.8 fusion.88
  652.7 7.0 fusion.197
  691.9 9.4 all-to-all-done.11
  715.2 6.1 norm_backward.12
  751.6 23.9 %attend_backward.5 = (bf16[512,1024]{1,0:T(8,128)(2,1)}, bf16[1024,1024]{1,0:T(8,128)(2,1)}) custom-call(s32[2,4]{1,0:T(2,128)} %pad_add_fusion.5.bounds, bf16[1536,1024]{1,0:T(8,128)(2,1)} %convolution_convert_fusion.2.q_ref.k_ref.v_ref, bf16[1536,1024]{1,0:T(8,128)(2,1)} %convolution_convert_fusion.2.q_ref.k_ref.v_ref, ...), custom_call_target="tpu_custom_call" | custom-call | tf_op jit(solution)/shard_map/attend_backward/pallas_call | solution.py:218
  779.3 6.0 all-to-all-start.14
  802.3 7.0 all-to-all-done.14
  822.5 6.1 norm_backward.13
  834.3 17.4 %all-to-all-done.16 = bf16[32,48,512]{2,1,0:T(8,128)(2,1)S(1)} async-done(((bf16[32,48,512]{2,1,0:T(8,128)(2,1)}), bf16[32,48,512]{2,1,0:T(8,128)(2,1)S(1)}, u32[]{:S(2)}, u32[]{:S(2)}) %all-to-all-start.16) | async-done | bytes 1572896 | tf_op jit(solution)/shard_map/all_to_all | solution.py:496
  900.6 36.9 %collective-permute-done.25 = bf16[1,1000,256]{2,1,0:T(8,128)(2,1)} collective-permute-done((bf16[1,1000,256]{2,1,0:T(8,128)(2,1)}, bf16[1,1000,256]{2,1,0:T(8,128)(2,1)}, u32[]{:S(2)}, u32[]{:S(2)}) %collective-permute-start.25) | collective-permute-done | bytes 512032 | tf_op jit(solution)/shard_map/ppermute | solution.py:476
  961.1 10.7 %all-to-all-done.18 = bf16[8,16,2304]{2,1,0:T(8,128)(2,1)S(1)} async-done(((bf16[8,16,2304]{2,1,0:T(8,128)(2,1)}), bf16[8,16,2304]{2,1,0:T(8,128)(2,1)S(1)}, u32[]{:S(2)}, u32[]{:S(2)}) %all-to-all-start.18) | async-done | bytes 589856 | tf_op jit(solution)/shard_map/all_to_all | solution.py:525
  984.6 7.0 all-to-all-done.19
  995.0 7.5 multiply_subtract_fusion
  (894 shorter events, 498.1 us)
Async XLA Ops:
  7.2 173.1 %all-gather.5.cloned.1.call-start = ((), (), s32[]{:S(2)}) async-start(), calls=%async_computation.21 | async-start | bytes 15544320 | tf_op jit(solution)/shard_map/all_gather | solution.py:691
  24.0 319.3 %all-gather.3.cloned.1.call-start = ((), (), s32[]{:S(2)}) async-start(), calls=%async_computation.20 | async-start | bytes 17408000 | tf_op jit(solution)/shard_map/all_gather | solution.py:714
  67.4 95.1 %all-to-all-start.9 = ((bf16[32,64,512]{2,1,0:T(8,128)(2,1)}), bf16[32,64,512]{2,1,0:T(8,128)(2,1)}, u32[]{:S(2)}, u32[]{:S(2)}) async-start(bf16[32,64,512]{2,1,0:T(8,128)(2,1)} %bitcast.47), calls=%async_computation.9 | async-start | bytes 4194304 | tf_op jit(solution)/shard_map/all_to_all | solution.py:496
  169.4 72.5 %all-to-all-start.10 = ((bf16[32,48,512]{2,1,0:T(8,128)(2,1)}), bf16[32,48,512]{2,1,0:T(8,128)(2,1)}, u32[]{:S(2)}, u32[]{:S(2)}) async-start(bf16[32,48,512]{2,1,0:T(8,128)(2,1)} %bitcast.810), calls=%async_computation.10 | async-start | bytes 3145728 | tf_op jit(solution)/shard_map/all_to_all | solution.py:496
  435.3 36.1 %collective-permute-start.6 = (bf16[8,1000,256]{2,1,0:T(8,128)(2,1)}, bf16[8,1000,256]{2,1,0:T(8,128)(2,1)S(1)}, u32[]{:S(2)}, u32[]{:S(2)}) collective-permute-start(bf16[8,1000,256]{2,1,0:T(8,128)(2,1)} %get-tuple-element.767), channel_id=1, source_target_pairs={{0,2},{2,0},{4,6},{6,4},{8,10},{10,8},{12,14},{14,12},{16,18},{18,... | collective-permute-start | bytes 12288008 | tf_op jit(solution)/shard_map/ppermute | solution.py:476
  465.3 70.0 %collective-permute-start.8 = (bf16[8,32,4096]{2,1,0:T(8,128)(2,1)}, bf16[8,32,4096]{2,1,0:T(8,128)(2,1)}, u32[]{:S(2)}, u32[]{:S(2)}) collective-permute-start(bf16[8,32,4096]{2,1,0:T(8,128)(2,1)} %fusion.225), channel_id=1, source_target_pairs={{0,2},{2,0},{4,6},{6,4},{8,10},{10,8},{12,14},{14,12},{16,18},{18,... | collective-permute-start | bytes 6291464 | tf_op jit(solution)/shard_map/ppermute | solution.py:476
  474.0 67.1 %collective-permute-start.7 = (bf16[4,1000,256]{2,1,0:T(8,128)(2,1)}, bf16[4,1000,256]{2,1,0:T(8,128)(2,1)}, u32[]{:S(2)}, u32[]{:S(2)}) collective-permute-start(bf16[4,1000,256]{2,1,0:T(8,128)(2,1)} %get-tuple-element.1108), channel_id=1, source_target_pairs={{0,4},{2,6},{4,0},{6,2},{8,12},{10,14},{12,8},{14,10},{16,20},{18,... | collective-permute-start | bytes 6144008 | tf_op jit(solution)/shard_map/ppermute | solution.py:476
  497.8 83.7 %collective-permute-start.9 = (bf16[8,1000,256]{2,1,0:T(8,128)(2,1)}, bf16[8,1000,256]{2,1,0:T(8,128)(2,1)}, u32[]{:S(2)}, u32[]{:S(2)}) collective-permute-start(bf16[8,1000,256]{2,1,0:T(8,128)(2,1)} %get-tuple-element.780), channel_id=1, source_target_pairs={{0,2},{2,0},{4,6},{6,4},{8,10},{10,8},{12,14},{14,12},{16,18},{18,... | collective-permute-start | bytes 12288008 | tf_op jit(solution)/shard_map/ppermute | solution.py:476
  547.0 58.6 %collective-permute-start.12 = (bf16[8,32,2048]{2,1,0:T(8,128)(2,1)}, bf16[8,32,2048]{2,1,0:T(8,128)(2,1)}, u32[]{:S(2)}, u32[]{:S(2)}) collective-permute-start(bf16[8,32,2048]{2,1,0:T(8,128)(2,1)} %pad_maximum_fusion.7), channel_id=1, source_target_pairs={{0,2},{2,0},{4,6},{6,4},{8,10},{10,8},{12,14},{14,12},{16,18},{18,... | collective-permute-start | bytes 3145736 | tf_op jit(solution)/shard_map/ppermute | solution.py:476
  549.5 56.2 %collective-permute-start.11 = (bf16[8,16,4096]{2,1,0:T(8,128)(2,1)}, bf16[8,16,4096]{2,1,0:T(8,128)(2,1)S(1)}, u32[]{:S(2)}, u32[]{:S(2)}) collective-permute-start(bf16[8,16,4096]{2,1,0:T(8,128)(2,1)} %fusion.152), channel_id=1, source_target_pairs={{0,1},{1,0},{2,3},{3,2},{4,5},{5,4},{6,7},{7,6},{8,9},{9,8},{10,11... | collective-permute-start | bytes 3145736 | tf_op jit(solution)/shard_map/ppermute | solution.py:476
  555.1 50.5 %collective-permute-start.10 = (bf16[2,1000,256]{2,1,0:T(8,128)(2,1)}, bf16[2,1000,256]{2,1,0:T(8,128)(2,1)S(1)}, u32[]{:S(2)}, u32[]{:S(2)}) collective-permute-start(bf16[2,1000,256]{2,1,0:T(8,128)(2,1)} %get-tuple-element.1110), channel_id=1, source_target_pairs={{0,8},{2,10},{4,12},{6,14},{8,0},{10,2},{12,4},{14,6},{16,24},{18,... | collective-permute-start | bytes 3072008 | tf_op jit(solution)/shard_map/ppermute | solution.py:476
  612.7 94.2 %collective-permute-start.16 = (bf16[8,32,2048]{2,1,0:T(8,128)(2,1)}, bf16[8,32,2048]{2,1,0:T(8,128)(2,1)}, u32[]{:S(2)}, u32[]{:S(2)}) collective-permute-start(bf16[8,32,2048]{2,1,0:T(8,128)(2,1)} %pad_maximum_fusion.8), channel_id=1, source_target_pairs={{0,2},{2,0},{4,6},{6,4},{8,10},{10,8},{12,14},{14,12},{16,18},{18,... | collective-permute-start | bytes 3145736 | tf_op jit(solution)/shard_map/ppermute | solution.py:476
  620.6 86.3 %collective-permute-start.15 = (bf16[4,1000,256]{2,1,0:T(8,128)(2,1)}, bf16[4,1000,256]{2,1,0:T(8,128)(2,1)}, u32[]{:S(2)}, u32[]{:S(2)}) collective-permute-start(bf16[4,1000,256]{2,1,0:T(8,128)(2,1)} %get-tuple-element.1106), channel_id=1, source_target_pairs={{0,4},{2,6},{4,0},{6,2},{8,12},{10,14},{12,8},{14,10},{16,20},{18,... | collective-permute-start | bytes 6144008 | tf_op jit(solution)/shard_map/ppermute | solution.py:476
  622.4 84.4 %collective-permute-start.14 = (bf16[1,1000,256]{2,1,0:T(8,128)(2,1)}, bf16[1,1000,256]{2,1,0:T(8,128)(2,1)}, u32[]{:S(2)}, u32[]{:S(2)}) collective-permute-start(bf16[1,1000,256]{2,1,0:T(8,128)(2,1)} %fusion.181), channel_id=1, source_target_pairs={{0,16},{2,18},{4,20},{6,22},{8,24},{10,26},{12,28},{14,30},{16,0},... | collective-permute-start | bytes 1536008 | tf_op jit(solution)/shard_map/ppermute | solution.py:476
  626.8 16.8 %collective-permute-start.13 = (bf16[8,16,2048]{2,1,0:T(8,128)(2,1)S(1)}, bf16[8,16,2048]{2,1,0:T(8,128)(2,1)S(1)}, u32[]{:S(2)}, u32[]{:S(2)}) collective-permute-start(bf16[8,16,2048]{2,1,0:T(8,128)(2,1)S(1)} %fusion.192), channel_id=1, source_target_pairs={{0,1},{1,0},{2,3},{3,2},{4,5},{5,4},{6,7},{7,6},{8,9},{9,8},{10,11... | collective-permute-start | bytes 1572872 | tf_op jit(solution)/shard_map/ppermute | solution.py:476
  671.4 29.9 %all-to-all-start.11 = ((bf16[8,16,4096]{2,1,0:T(8,128)(2,1)}), bf16[8,16,4096]{2,1,0:T(8,128)(2,1)}, u32[]{:S(2)}, u32[]{:S(2)}) async-start(bf16[8,16,4096]{2,1,0:T(8,128)(2,1)} %fusion.127), calls=%async_computation.11 | async-start | bytes 2097152 | tf_op jit(solution)/shard_map/all_to_all | solution.py:525
  677.5 47.3 %collective-permute-start.18 = (bf16[8,32,4096]{2,1,0:T(8,128)(2,1)}, bf16[8,32,4096]{2,1,0:T(8,128)(2,1)}, u32[]{:S(2)}, u32[]{:S(2)}) collective-permute-start(bf16[8,32,4096]{2,1,0:T(8,128)(2,1)} %fusion.233), channel_id=1, source_target_pairs={{0,2},{2,0},{4,6},{6,4},{8,10},{10,8},{12,14},{14,12},{16,18},{18,... | collective-permute-start | bytes 6291464 | tf_op jit(solution)/shard_map/ppermute | solution.py:476
  701.3 23.4 %all-to-all-start.12 = ((bf16[8,16,2048]{2,1,0:T(8,128)(2,1)}), bf16[8,16,2048]{2,1,0:T(8,128)(2,1)S(1)}, u32[]{:S(2)}, u32[]{:S(2)}) async-start(bf16[8,16,2048]{2,1,0:T(8,128)(2,1)} %fusion.169), calls=%async_computation.12 | async-start | bytes 1048576 | tf_op jit(solution)/shard_map/all_to_all | solution.py:525
  709.0 15.8 %collective-permute-start.17 = (bf16[8,16,2048]{2,1,0:T(8,128)(2,1)}, bf16[8,16,2048]{2,1,0:T(8,128)(2,1)}, u32[]{:S(2)}, u32[]{:S(2)}) collective-permute-start(bf16[8,16,2048]{2,1,0:T(8,128)(2,1)} %fusion.193), channel_id=1, source_target_pairs={{0,1},{1,0},{2,3},{3,2},{4,5},{5,4},{6,7},{7,6},{8,9},{9,8},{10,11... | collective-permute-start | bytes 1572872 | tf_op jit(solution)/shard_map/ppermute | solution.py:476
  713.1 62.4 %collective-permute-start.19 = (bf16[2,1000,256]{2,1,0:T(8,128)(2,1)}, bf16[2,1000,256]{2,1,0:T(8,128)(2,1)}, u32[]{:S(2)}, u32[]{:S(2)}) collective-permute-start(bf16[2,1000,256]{2,1,0:T(8,128)(2,1)} %fusion.175), channel_id=1, source_target_pairs={{0,8},{2,10},{4,12},{6,14},{8,0},{10,2},{12,4},{14,6},{16,24},{18,... | collective-permute-start | bytes 3072008 | tf_op jit(solution)/shard_map/ppermute | solution.py:476
  728.1 47.5 %collective-permute-start.21 = (bf16[8,16,4096]{2,1,0:T(8,128)(2,1)}, bf16[8,16,4096]{2,1,0:T(8,128)(2,1)}, u32[]{:S(2)}, u32[]{:S(2)}) collective-permute-start(bf16[8,16,4096]{2,1,0:T(8,128)(2,1)} %fusion.155), channel_id=1, source_target_pairs={{0,1},{1,0},{2,3},{3,2},{4,5},{5,4},{6,7},{7,6},{8,9},{9,8},{10,11... | collective-permute-start | bytes 3145736 | tf_op jit(solution)/shard_map/ppermute | solution.py:476
  731.6 43.9 %all-to-all-start.13 = ((bf16[8,16,2048]{2,1,0:T(8,128)(2,1)}), bf16[8,16,2048]{2,1,0:T(8,128)(2,1)S(1)}, u32[]{:S(2)}, u32[]{:S(2)}) async-start(bf16[8,16,2048]{2,1,0:T(8,128)(2,1)} %fusion.160), calls=%async_computation.13 | async-start | bytes 1048576 | tf_op jit(solution)/shard_map/all_to_all | solution.py:525
  749.5 26.0 %collective-permute-start.20 = (f32[16,4096]{1,0:T(8,128)S(1)}, f32[16,4096]{1,0:T(8,128)S(1)}, u32[]{:S(2)}, u32[]{:S(2)}) collective-permute-start(f32[16,4096]{1,0:T(8,128)S(1)} %convert_reduce_fusion.3), channel_id=1, source_target_pairs={{0,1},{1,0},{2,3},{3,2},{4,5},{5,4},{6,7},{7,6},{8,9},{9,8},{10,11... | collective-permute-start | bytes 786440 | tf_op jit(solution)/shard_map/ppermute | solution.py:476
  779.3 29.9 %all-to-all-start.14 = ((bf16[8,16,4096]{2,1,0:T(8,128)(2,1)}), bf16[8,16,4096]{2,1,0:T(8,128)(2,1)S(1)}, u32[]{:S(2)}, u32[]{:S(2)}) async-start(bf16[8,16,4096]{2,1,0:T(8,128)(2,1)} %fusion.126), calls=%async_computation.14 | async-start | bytes 2097152 | tf_op jit(solution)/shard_map/all_to_all | solution.py:525
  794.1 36.9 %collective-permute-start.22 = (f32[16,2048]{1,0:T(8,128)S(1)}, f32[16,2048]{1,0:T(8,128)}, u32[]{:S(2)}, u32[]{:S(2)}) collective-permute-start(f32[16,2048]{1,0:T(8,128)S(1)} %convert_reduce_fusion.6), channel_id=1, source_target_pairs={{0,1},{1,0},{2,3},{3,2},{4,5},{5,4},{6,7},{7,6},{8,9},{9,8},{10,11... | collective-permute-start | bytes 393224 | tf_op jit(solution)/shard_map/ppermute | solution.py:476
  809.2 42.4 %all-to-all-start.16 = ((bf16[32,48,512]{2,1,0:T(8,128)(2,1)}), bf16[32,48,512]{2,1,0:T(8,128)(2,1)S(1)}, u32[]{:S(2)}, u32[]{:S(2)}) async-start(bf16[32,48,512]{2,1,0:T(8,128)(2,1)} %bitcast.811), calls=%async_computation.16 | async-start | bytes 3145728 | tf_op jit(solution)/shard_map/all_to_all | solution.py:496
  815.8 15.3 %collective-permute-start.24 = (bf16[8,32,2304]{2,1,0:T(8,128)(2,1)}, bf16[8,32,2304]{2,1,0:T(8,128)(2,1)S(1)}, u32[]{:S(2)}, u32[]{:S(2)}) collective-permute-start(bf16[8,32,2304]{2,1,0:T(8,128)(2,1)} %pad_maximum_fusion.6), channel_id=1, source_target_pairs={{0,2},{2,0},{4,6},{6,4},{8,10},{10,8},{12,14},{14,12},{16,18},{18,... | collective-permute-start | bytes 3538952 | tf_op jit(solution)/shard_map/ppermute | solution.py:476
  862.3 75.2 %all-to-all-start.15 = ((bf16[32,64,512]{2,1,0:T(8,128)(2,1)}), bf16[32,64,512]{2,1,0:T(8,128)(2,1)}, u32[]{:S(2)}, u32[]{:S(2)}) async-start(bf16[32,64,512]{2,1,0:T(8,128)(2,1)} %bitcast.211), calls=%async_computation.15 | async-start | bytes 4194304 | tf_op jit(solution)/shard_map/all_to_all | solution.py:496
  878.1 59.4 %collective-permute-start.25 = (bf16[1,1000,256]{2,1,0:T(8,128)(2,1)}, bf16[1,1000,256]{2,1,0:T(8,128)(2,1)}, u32[]{:S(2)}, u32[]{:S(2)}) collective-permute-start(bf16[1,1000,256]{2,1,0:T(8,128)(2,1)} %fusion.180), channel_id=1, source_target_pairs={{0,16},{2,18},{4,20},{6,22},{8,24},{10,26},{12,28},{14,30},{16,0},... | collective-permute-start | bytes 1536008 | tf_op jit(solution)/shard_map/ppermute | solution.py:476
  890.0 47.4 %collective-permute-start.27 = (bf16[8,16,2304]{2,1,0:T(8,128)(2,1)}, bf16[8,16,2304]{2,1,0:T(8,128)(2,1)}, u32[]{:S(2)}, u32[]{:S(2)}) collective-permute-start(bf16[8,16,2304]{2,1,0:T(8,128)(2,1)} %fusion.189), channel_id=1, source_target_pairs={{0,1},{1,0},{2,3},{3,2},{4,5},{5,4},{6,7},{7,6},{8,9},{9,8},{10,11... | collective-permute-start | bytes 1769480 | tf_op jit(solution)/shard_map/ppermute | solution.py:476
  892.3 45.1 %collective-permute-start.26 = (f32[16,4096]{1,0:T(8,128)}, f32[16,4096]{1,0:T(8,128)}, u32[]{:S(2)}, u32[]{:S(2)}) collective-permute-start(f32[16,4096]{1,0:T(8,128)} %convert_reduce_fusion.2), channel_id=1, source_target_pairs={{0,1},{1,0},{2,3},{3,2},{4,5},{5,4},{6,7},{7,6},{8,9},{9,8},{10,11... | collective-permute-start | bytes 786440 | tf_op jit(solution)/shard_map/ppermute | solution.py:476
  952.3 19.4 %all-to-all-start.18 = ((bf16[8,16,2304]{2,1,0:T(8,128)(2,1)}), bf16[8,16,2304]{2,1,0:T(8,128)(2,1)S(1)}, u32[]{:S(2)}, u32[]{:S(2)}) async-start(bf16[8,16,2304]{2,1,0:T(8,128)(2,1)} %fusion.149), calls=%async_computation.18 | async-start | bytes 1179648 | tf_op jit(solution)/shard_map/all_to_all | solution.py:525
  (238 other events, 2613.9 us)
Sparse Core Ops, SparseCore 0:
  24.1 145.5 all-gather.4
  171.9 149.9 all-gather.2

commit v9 on v8

--- a/solution.py
+++ b/solution.py
@@ -1051,12 +1051,12 @@
         enc_spans,
         keep0,
         d_stream1,
-        [chain_b, chain_c, chain_d],
+        table_two + [chain_b, chain_c, chain_d],
         table_two + [chain_a, chain_c, chain_d],
     )
     chain_e = LayerChain([owned(d_win0), owned(d_wout0), owned(d_w_len)])
     d_stream0, scale0 = norm_backward(norm0, gains[0], d_inner0, d_stream1)
-    d_stream0 = advance(d_stream0, [chain_b, chain_c, chain_d, chain_e])
+    d_stream0 = advance(d_stream0, [chain_b, chain_c, chain_e])
     src_grad = d_stream0 * root
     src_sums = give_rows(src_maps[0], src_grad)
     norm_share = norms.shape[2]
@@ -1065,7 +1065,8 @@
     scales = jnp.broadcast_to(scales[None], (seqs,) + scales.shape)
     scales = to_each(scales.reshape((devices,) + scales.shape[2:]))
     chains = table_one + table_two + [chain_a, chain_b, chain_c, chain_d, chain_e]
-    src_sums, dec_sums, scales = advance((src_sums, dec_sums, scales), chains)
+    src_sums, dec_sums = advance((src_sums, dec_sums), chains)
+    scales = advance(scales, chains)
     while any(chain.pending is not None for chain in chains):
         advance((), chains)
     layer_chains = [chain_a, chain_b, chain_c, chain_d, chain_e]

time: 1030 us -> 1040 us (level)
    ppermute x27, waiting for transfers between devices: 55.3 us -> 34.5 us  [swap(): return lax.ppermute(values, axis, [(i, i ^ bit) for i in range(size)])]
    all_to_all x5, waiting for transfers between devices: 27.1 us -> 41 us  [launch(): self.pending = lax.all_to_all(whole, 'dp', 0, 0, axis_index_groups=groups)]
    all_to_all x7, waiting for transfers between devices: 135 us -> 148 us  [to_each(): return lax.all_to_all(values, ('seq', 'dp'), 0, 0)]
    unnamed x503 -> x467, local copies, waits for them, and re-layouts: 47 us -> 51.4 us
  transfers between devices with their start and end apart: 41 -> 41, of which waited for: 15 -> 20; matrix products, arithmetic and copies ran while one was open for 35% -> 34% of each run, Pallas kernels for 15% -> 15%
where the time goes in v9:
time: 1040 us; the launch traced here: 1030 us
  waiting for transfers between devices  223 us (21%)
  Pallas kernels  216 us (21%)
  matrix products  183 us (18%)
  other arithmetic  170 us (16%)
  starting transfers between devices  97 us (9%)
  local copies, waits for them, and re-layouts  90.6 us (9%)
  between operations  35.6 us (3%)
  loops' own time  15.2 us (1%)
    dot_general x52, matrix products, contract(): lax.dot_general(left, right, (((left_dim,), (right_dim,)), ((), ())), pre...  181 us
    all_to_all x7, waiting for transfers between devices, to_each(): return lax.all_to_all(values, ('seq', 'dp'), 0, 0)  148 us
    pallas_call x3, Pallas kernels, attend_backward(): pl.pallas_call(functools.partial(attend_backward_kernel, head=width // HE...  72 us
    unnamed x467, local copies, waits for them, and re-layouts  51.4 us
    ppermute x27, starting transfers between devices, swap(): return lax.ppermute(values, axis, [(i, i ^ bit) for i in range(size)])  51 us
    pallas_call x1, Pallas kernels, head_back(): pl.pallas_call(functools.partial(head_back_kernel, owned=owned), grid_spe...  44.1 us
    pallas_call x7, Pallas kernels, norm_backward(): pl.pallas_call(norm_back_kernel, grid=(places // columns,), in_specs=[blo...  42 us
    all_to_all x5, waiting for transfers between devices, launch(): self.pending = lax.all_to_all(whole, 'dp', 0, 0, axis_index_groups=groups)  41 us
  transfers between devices with their start and end apart: 41, of which 20 were waited for; matrix products, arithmetic and copies ran while one was open for 34% of the time, Pallas kernels for 15%

profile of v9, /device:TPU:0, one launch (start us, length us, event | category | flops | bytes accessed | tf_op | source)
XLA Modules:
  0.0 1031.1 jit_solution(3727798470400113692)
XLA Ops:
  55.1 7.1 all-to-all-done.8
  70.8 8.3 multiply_sine_fusion
  98.6 63.4 %all-to-all-done.9 = bf16[32,64,512]{2,1,0:T(8,128)(2,1)} async-done(((bf16[32,64,512]{2,1,0:T(8,128)(2,1)}), bf16[32,64,512]{2,1,0:T(8,128)(2,1)}, u32[]{:S(2)}, u32[]{:S(2)}) %all-to-all-start.9) | async-done | bytes 2097184 | tf_op jit(solution)/shard_map/all_to_all | solution.py:496
  187.8 13.4 %attend_forward.3 = (bf16[512,1024]{1,0:T(8,128)(2,1)}, f32[8,1024]{1,0:T(8,128)}) custom-call(s32[2,4]{1,0:T(2,128)} %pad_add_fusion.5.bounds, bf16[1536,1024]{1,0:T(8,128)(2,1)} %convolution_convert_fusion.2.q_ref.k_ref.v_ref, bf16[1536,1024]{1,0:T(8,128)(2,1)} %convolution_convert_fusion.2.q_ref.k_ref.v_ref, ...), custom_call_target="tpu_custom_call" | custom-call | tf_op jit(solution)/shard_map/attend_forward/pallas_call | solution.py:193
  203.3 37.2 %all-to-all-done.10 = bf16[32,48,512]{2,1,0:T(8,128)(2,1)} async-done(((bf16[32,48,512]{2,1,0:T(8,128)(2,1)}), bf16[32,48,512]{2,1,0:T(8,128)(2,1)}, u32[]{:S(2)}, u32[]{:S(2)}) %all-to-all-start.10) | async-done | bytes 1572896 | tf_op jit(solution)/shard_map/all_to_all | solution.py:496
  269.6 13.5 %attend_forward.4 = (bf16[512,1024]{1,0:T(8,128)(2,1)}, f32[8,1024]{1,0:T(8,128)}) custom-call(s32[2,4]{1,0:T(2,128)} %pad_add_fusion.6.bounds, bf16[1536,1024]{1,0:T(8,128)(2,1)} %convolution_convert_fusion.1.q_ref.k_ref.v_ref, bf16[1536,1024]{1,0:T(8,128)(2,1)} %convolution_convert_fusion.1.q_ref.k_ref.v_ref, ...), custom_call_target="tpu_custom_call" | custom-call | tf_op jit(solution)/shard_map/attend_forward/pallas_call | solution.py:193
  293.5 13.6 %attend_forward.5 = (bf16[512,1024]{1,0:T(8,128)(2,1)}, f32[8,1024]{1,0:T(8,128)}) custom-call(s32[2,4]{1,0:T(2,128)} %pad_add_fusion.7.bounds, bf16[512,1024]{1,0:T(8,128)(2,1)} %convolution_convert_fusion.8.q_ref, bf16[1024,1024]{1,0:T(8,128)(2,1)} %convolution_convert_fusion.4.k_ref.v_ref, bf16[1024,1024]{1,0:T(8,128)(2,1)} %convolution_convert_fusion.4.k_ref.v_ref, ...), custom_call_target="tpu_custom_call" | custom-call | tf_op jit(solution)/shard_map/attend_forward/pallas_call | solution.py:193
  320.2 16.4 %conditional.2 = (bf16[2048,512]{1,0:T(8,128)(2,1)S(1)}) conditional(s32[]{:T(128)} %convert_element_type.552, (s32[1024]{0:T(1024)S(1)}, bf16[512,1024]{1,0:T(8,128)(2,1)S(1)}, s32[]{:T(128)}, s32[2]{0:T(128)S(1)}, s32[2]{0:T(128)S(1)}, /*index=5*/s32[1024]{0:T(1024)S(1)}) %tuple.314, (s32[1024]{0:T(1024)S(1)}, bf16[512,1024]{1,0:T(8,128)(2,1)S(1)}, ...), branch_computations={%region_59.60_spmd, %region_60.61_spmd} | conditional | flops 5376576512 | bytes 18890878 | solution.py:953
  347.1 17.3 %head_stats.1 = f32[2,2048]{1,0:T(2,128)} custom-call(s32[4]{0:T(128)} %pad_add_fusion.8.plan, bf16[16000,512]{1,0:T(8,128)(2,1)} %all-gather.3.cloned.1.call-done.table_ref, bf16[512,2048]{1,0:T(8,128)(2,1)} %bitcast.721), custom_call_target="tpu_custom_call" | custom-call | tf_op jit(solution)/shard_map/head_stats/pallas_call | solution.py:414
  371.0 44.1 %head_back.1 = (f32[8,1000,256]{2,1,0:T(8,128)}, f32[8,1000,256]{2,1,0:T(8,128)}, bf16[8,1000,256]{2,1,0:T(8,128)(2,1)}, bf16[8,1000,256]{2,1,0:T(8,128)(2,1)}, f32[2048,512]{1,0:T(8,128)}, /*index=5*/f32[8,2048]{1,0:T(8,128)}) custom-call(s32[4]{0:T(128)} %pad_add_fusion.8.plan, bf16[16000,512]{1,0:T(8,128)(2,1)} %all-gather.3.cloned.1.call-done.table_ref, ...), custom_call_target="tpu_custom_call" | custom-call | tf_op jit(solution)/shard_map/head_back/pallas_call | solution.py:444
  415.1 24.9 %conditional.3 = (f32[512,1024]{1,0:T(8,128)}) conditional(s32[]{:T(128)} %convert_element_type.552, (s32[1024]{0:T(1024)S(1)}, f32[2048,512]{1,0:T(8,128)}, s32[]{:T(128)}, s32[2]{0:T(128)S(1)}, s32[2]{0:T(128)S(1)}, /*index=5*/s32[1024]{0:T(1024)S(1)}) %tuple.316, (s32[1024]{0:T(1024)S(1)}, f32[2048,512]{1,0:T(8,128)}, s32[]{:T(128)}, ...), branch_computations={%region_73.74_spmd, %region_74.75_spmd} | conditional | flops 7532448768 | bytes 50352280 | solution.py:976
  445.6 9.6 fusion.95
  474.9 6.6 fusion.132.grad_ref
  481.5 6.2 bitcast_add_fusion.4
  487.7 25.4 %collective-permute-start.7 = (bf16[4,1000,256]{2,1,0:T(8,128)(2,1)}, bf16[4,1000,256]{2,1,0:T(8,128)(2,1)}, u32[]{:S(2)}, u32[]{:S(2)}) collective-permute-start(bf16[4,1000,256]{2,1,0:T(8,128)(2,1)} %get-tuple-element.1110), channel_id=1, source_target_pairs={{0,4},{2,6},{4,0},{6,2},{8,12},{10,14},{12,8},{14,10},{16,20},{18,... | collective-permute-start | bytes 6144008 | tf_op jit(solution)/shard_map/ppermute | solution.py:476
  518.4 6.6 norm_backward.8
  530.8 24.0 %attend_backward.3 = (bf16[512,1024]{1,0:T(8,128)(2,1)}, bf16[1024,1024]{1,0:T(8,128)(2,1)}) custom-call(s32[2,4]{1,0:T(2,128)} %pad_add_fusion.7.bounds, bf16[512,1024]{1,0:T(8,128)(2,1)} %convolution_convert_fusion.8.q_ref, bf16[1024,1024]{1,0:T(8,128)(2,1)} %convolution_convert_fusion.4.k_ref.v_ref, ...), custom_call_target="tpu_custom_call" | custom-call | tf_op jit(solution)/shard_map/attend_backward/pallas_call | solution.py:218
  586.6 6.2 norm_backward.10
  601.2 24.1 %attend_backward.4 = (bf16[512,1024]{1,0:T(8,128)(2,1)}, bf16[1024,1024]{1,0:T(8,128)(2,1)}) custom-call(s32[2,4]{1,0:T(2,128)} %pad_add_fusion.6.bounds, bf16[1536,1024]{1,0:T(8,128)(2,1)} %convolution_convert_fusion.1.q_ref.k_ref.v_ref, bf16[1536,1024]{1,0:T(8,128)(2,1)} %convolution_convert_fusion.1.q_ref.k_ref.v_ref, ...), custom_call_target="tpu_custom_call" | custom-call | tf_op jit(solution)/shard_map/attend_backward/pallas_call | solution.py:218
  632.7 6.1 bitcast_add_fusion.3
  664.9 9.9 fusion.88
  674.9 7.1 fusion.196
  698.5 6.6 fusion.136.grad_ref
  711.0 11.6 %all-to-all-done.11 = bf16[8,16,4096]{2,1,0:T(8,128)(2,1)} async-done(((bf16[8,16,4096]{2,1,0:T(8,128)(2,1)}), bf16[8,16,4096]{2,1,0:T(8,128)(2,1)}, u32[]{:S(2)}, u32[]{:S(2)}) %all-to-all-start.11) | async-done | bytes 1048608 | tf_op jit(solution)/shard_map/all_to_all | solution.py:525
  745.3 13.5 %all-to-all-done.12 = bf16[8,16,2048]{2,1,0:T(8,128)(2,1)S(1)} async-done(((bf16[8,16,2048]{2,1,0:T(8,128)(2,1)}), bf16[8,16,2048]{2,1,0:T(8,128)(2,1)S(1)}, u32[]{:S(2)}, u32[]{:S(2)}) %all-to-all-start.12) | async-done | bytes 524320 | tf_op jit(solution)/shard_map/all_to_all | solution.py:525
  783.4 24.0 %attend_backward.5 = (bf16[512,1024]{1,0:T(8,128)(2,1)}, bf16[1024,1024]{1,0:T(8,128)(2,1)}) custom-call(s32[2,4]{1,0:T(2,128)} %pad_add_fusion.5.bounds, bf16[1536,1024]{1,0:T(8,128)(2,1)} %convolution_convert_fusion.2.q_ref.k_ref.v_ref, bf16[1536,1024]{1,0:T(8,128)(2,1)} %convolution_convert_fusion.2.q_ref.k_ref.v_ref, ...), custom_call_target="tpu_custom_call" | custom-call | tf_op jit(solution)/shard_map/attend_backward/pallas_call | solution.py:218
  835.7 18.3 %all-to-all-done.15 = bf16[32,48,512]{2,1,0:T(8,128)(2,1)} async-done(((bf16[32,48,512]{2,1,0:T(8,128)(2,1)}), bf16[32,48,512]{2,1,0:T(8,128)(2,1)}, u32[]{:S(2)}, u32[]{:S(2)}) %all-to-all-start.15) | async-done | bytes 1572896 | tf_op jit(solution)/shard_map/all_to_all | solution.py:496
  882.2 11.8 %all-to-all-done.16 = bf16[8,16,4096]{2,1,0:T(8,128)(2,1)S(1)} async-done(((bf16[8,16,4096]{2,1,0:T(8,128)(2,1)}), bf16[8,16,4096]{2,1,0:T(8,128)(2,1)S(1)}, u32[]{:S(2)}, u32[]{:S(2)}) %all-to-all-start.16) | async-done | bytes 1048608 | tf_op jit(solution)/shard_map/all_to_all | solution.py:525
  924.7 13.0 %collective-permute-done.26 = bf16[8,16,2304]{2,1,0:T(8,128)(2,1)} collective-permute-done((bf16[8,16,2304]{2,1,0:T(8,128)(2,1)}, bf16[8,16,2304]{2,1,0:T(8,128)(2,1)}, u32[]{:S(2)}, u32[]{:S(2)}) %collective-permute-start.26) | collective-permute-done | bytes 589856 | tf_op jit(solution)/shard_map/ppermute | solution.py:476
  937.8 11.0 %all-to-all-done.14 = bf16[32,64,512]{2,1,0:T(8,128)(2,1)} async-done(((bf16[32,64,512]{2,1,0:T(8,128)(2,1)}), bf16[32,64,512]{2,1,0:T(8,128)(2,1)}, u32[]{:S(2)}, u32[]{:S(2)}) %all-to-all-start.14) | async-done | bytes 2097184 | tf_op jit(solution)/shard_map/all_to_all | solution.py:496
  997.6 7.0 all-to-all-done.19
  1008.0 7.5 multiply_subtract_fusion
  (858 shorter events, 508.3 us)
Async XLA Ops:
  7.2 172.2 %all-gather.5.cloned.1.call-start = ((), (), s32[]{:S(2)}) async-start(), calls=%async_computation.21 | async-start | bytes 15544320 | tf_op jit(solution)/shard_map/all_gather | solution.py:691
  24.0 323.2 %all-gather.3.cloned.1.call-start = ((), (), s32[]{:S(2)}) async-start(), calls=%async_computation.20 | async-start | bytes 17408000 | tf_op jit(solution)/shard_map/all_gather | solution.py:714
  50.2 12.0 %all-to-all-start.8 = ((s32[32,1,128]{2,1,0:T(1,128)}), s32[32,1,128]{2,1,0:T(1,128)S(1)}, u32[]{:S(2)}, u32[]{:S(2)}) async-start(s32[32,1,128]{2,1,0:T(1,128)} %bitcast.44), calls=%async_computation.8 | async-start | bytes 32768 | tf_op jit(solution)/shard_map/all_to_all | solution.py:496
  67.1 94.8 %all-to-all-start.9 = ((bf16[32,64,512]{2,1,0:T(8,128)(2,1)}), bf16[32,64,512]{2,1,0:T(8,128)(2,1)}, u32[]{:S(2)}, u32[]{:S(2)}) async-start(bf16[32,64,512]{2,1,0:T(8,128)(2,1)} %bitcast.47), calls=%async_computation.9 | async-start | bytes 4194304 | tf_op jit(solution)/shard_map/all_to_all | solution.py:496
  168.7 71.9 %all-to-all-start.10 = ((bf16[32,48,512]{2,1,0:T(8,128)(2,1)}), bf16[32,48,512]{2,1,0:T(8,128)(2,1)}, u32[]{:S(2)}, u32[]{:S(2)}) async-start(bf16[32,48,512]{2,1,0:T(8,128)(2,1)} %bitcast.805), calls=%async_computation.10 | async-start | bytes 3145728 | tf_op jit(solution)/shard_map/all_to_all | solution.py:496
  440.0 41.5 %collective-permute-start.6 = (bf16[8,1000,256]{2,1,0:T(8,128)(2,1)}, bf16[8,1000,256]{2,1,0:T(8,128)(2,1)}, u32[]{:S(2)}, u32[]{:S(2)}) collective-permute-start(bf16[8,1000,256]{2,1,0:T(8,128)(2,1)} %get-tuple-element.768), channel_id=1, source_target_pairs={{0,2},{2,0},{4,6},{6,4},{8,10},{10,8},{12,14},{14,12},{16,18},{18,... | collective-permute-start | bytes 12288008 | tf_op jit(solution)/shard_map/ppermute | solution.py:476
  470.3 84.6 %collective-permute-start.8 = (bf16[8,32,4096]{2,1,0:T(8,128)(2,1)}, bf16[8,32,4096]{2,1,0:T(8,128)(2,1)}, u32[]{:S(2)}, u32[]{:S(2)}) collective-permute-start(bf16[8,32,4096]{2,1,0:T(8,128)(2,1)} %fusion.224), channel_id=1, source_target_pairs={{0,2},{2,0},{4,6},{6,4},{8,10},{10,8},{12,14},{14,12},{16,18},{18,... | collective-permute-start | bytes 6291464 | tf_op jit(solution)/shard_map/ppermute | solution.py:476
  487.7 70.5 %collective-permute-start.7 = (bf16[4,1000,256]{2,1,0:T(8,128)(2,1)}, bf16[4,1000,256]{2,1,0:T(8,128)(2,1)}, u32[]{:S(2)}, u32[]{:S(2)}) collective-permute-start(bf16[4,1000,256]{2,1,0:T(8,128)(2,1)} %get-tuple-element.1110), channel_id=1, source_target_pairs={{0,4},{2,6},{4,0},{6,2},{8,12},{10,14},{12,8},{14,10},{16,20},{18,... | collective-permute-start | bytes 6144008 | tf_op jit(solution)/shard_map/ppermute | solution.py:476
  518.4 82.7 %collective-permute-start.9 = (bf16[8,1000,256]{2,1,0:T(8,128)(2,1)}, bf16[8,1000,256]{2,1,0:T(8,128)(2,1)}, u32[]{:S(2)}, u32[]{:S(2)}) collective-permute-start(bf16[8,1000,256]{2,1,0:T(8,128)(2,1)} %get-tuple-element.781), channel_id=1, source_target_pairs={{0,2},{2,0},{4,6},{6,4},{8,10},{10,8},{12,14},{14,12},{16,18},{18,... | collective-permute-start | bytes 12288008 | tf_op jit(solution)/shard_map/ppermute | solution.py:476
  563.1 62.1 %collective-permute-start.12 = (bf16[8,32,2048]{2,1,0:T(8,128)(2,1)}, bf16[8,32,2048]{2,1,0:T(8,128)(2,1)}, u32[]{:S(2)}, u32[]{:S(2)}) collective-permute-start(bf16[8,32,2048]{2,1,0:T(8,128)(2,1)} %pad_maximum_fusion.7), channel_id=1, source_target_pairs={{0,2},{2,0},{4,6},{6,4},{8,10},{10,8},{12,14},{14,12},{16,18},{18,... | collective-permute-start | bytes 3145736 | tf_op jit(solution)/shard_map/ppermute | solution.py:476
  565.4 59.9 %collective-permute-start.11 = (bf16[8,16,4096]{2,1,0:T(8,128)(2,1)S(1)}, bf16[8,16,4096]{2,1,0:T(8,128)(2,1)}, u32[]{:S(2)}, u32[]{:S(2)}) collective-permute-start(bf16[8,16,4096]{2,1,0:T(8,128)(2,1)S(1)} %fusion.151), channel_id=1, source_target_pairs={{0,1},{1,0},{2,3},{3,2},{4,5},{5,4},{6,7},{7,6},{8,9},{9,8},{10,11... | collective-permute-start | bytes 3145736 | tf_op jit(solution)/shard_map/ppermute | solution.py:476
  570.2 55.1 %collective-permute-start.10 = (bf16[2,1000,256]{2,1,0:T(8,128)(2,1)}, bf16[2,1000,256]{2,1,0:T(8,128)(2,1)}, u32[]{:S(2)}, u32[]{:S(2)}) collective-permute-start(bf16[2,1000,256]{2,1,0:T(8,128)(2,1)} %get-tuple-element.1112), channel_id=1, source_target_pairs={{0,8},{2,10},{4,12},{6,14},{8,0},{10,2},{12,4},{14,6},{16,24},{18,... | collective-permute-start | bytes 3072008 | tf_op jit(solution)/shard_map/ppermute | solution.py:476
  632.1 78.9 %collective-permute-start.16 = (bf16[8,32,2048]{2,1,0:T(8,128)(2,1)}, bf16[8,32,2048]{2,1,0:T(8,128)(2,1)}, u32[]{:S(2)}, u32[]{:S(2)}) collective-permute-start(bf16[8,32,2048]{2,1,0:T(8,128)(2,1)} %pad_maximum_fusion.8), channel_id=1, source_target_pairs={{0,2},{2,0},{4,6},{6,4},{8,10},{10,8},{12,14},{14,12},{16,18},{18,... | collective-permute-start | bytes 3145736 | tf_op jit(solution)/shard_map/ppermute | solution.py:476
  638.8 83.8 %collective-permute-start.15 = (bf16[4,1000,256]{2,1,0:T(8,128)(2,1)}, bf16[4,1000,256]{2,1,0:T(8,128)(2,1)}, u32[]{:S(2)}, u32[]{:S(2)}) collective-permute-start(bf16[4,1000,256]{2,1,0:T(8,128)(2,1)} %get-tuple-element.1108), channel_id=1, source_target_pairs={{0,4},{2,6},{4,0},{6,2},{8,12},{10,14},{12,8},{14,10},{16,20},{18,... | collective-permute-start | bytes 6144008 | tf_op jit(solution)/shard_map/ppermute | solution.py:476
  642.5 68.4 %collective-permute-start.14 = (bf16[1,1000,256]{2,1,0:T(8,128)(2,1)}, bf16[1,1000,256]{2,1,0:T(8,128)(2,1)}, u32[]{:S(2)}, u32[]{:S(2)}) collective-permute-start(bf16[1,1000,256]{2,1,0:T(8,128)(2,1)} %fusion.180), channel_id=1, source_target_pairs={{0,16},{2,18},{4,20},{6,22},{8,24},{10,26},{12,28},{14,30},{16,0},... | collective-permute-start | bytes 1536008 | tf_op jit(solution)/shard_map/ppermute | solution.py:476
  645.1 19.4 %collective-permute-start.13 = (bf16[8,16,2048]{2,1,0:T(8,128)(2,1)}, bf16[8,16,2048]{2,1,0:T(8,128)(2,1)}, u32[]{:S(2)}, u32[]{:S(2)}) collective-permute-start(bf16[8,16,2048]{2,1,0:T(8,128)(2,1)} %fusion.191), channel_id=1, source_target_pairs={{0,1},{1,0},{2,3},{3,2},{4,5},{5,4},{6,7},{7,6},{8,9},{9,8},{10,11... | collective-permute-start | bytes 1572872 | tf_op jit(solution)/shard_map/ppermute | solution.py:476
  692.4 30.2 %all-to-all-start.11 = ((bf16[8,16,4096]{2,1,0:T(8,128)(2,1)}), bf16[8,16,4096]{2,1,0:T(8,128)(2,1)}, u32[]{:S(2)}, u32[]{:S(2)}) async-start(bf16[8,16,4096]{2,1,0:T(8,128)(2,1)} %fusion.127), calls=%async_computation.11 | async-start | bytes 2097152 | tf_op jit(solution)/shard_map/all_to_all | solution.py:525
  705.9 52.9 %collective-permute-start.19 = (bf16[8,32,4096]{2,1,0:T(8,128)(2,1)}, bf16[8,32,4096]{2,1,0:T(8,128)(2,1)}, u32[]{:S(2)}, u32[]{:S(2)}) collective-permute-start(bf16[8,32,4096]{2,1,0:T(8,128)(2,1)} %fusion.232), channel_id=1, source_target_pairs={{0,2},{2,0},{4,6},{6,4},{8,10},{10,8},{12,14},{14,12},{16,18},{18,... | collective-permute-start | bytes 6291464 | tf_op jit(solution)/shard_map/ppermute | solution.py:476
  725.7 33.1 %collective-permute-start.17 = (bf16[2,1000,256]{2,1,0:T(8,128)(2,1)}, bf16[2,1000,256]{2,1,0:T(8,128)(2,1)}, u32[]{:S(2)}, u32[]{:S(2)}) collective-permute-start(bf16[2,1000,256]{2,1,0:T(8,128)(2,1)} %fusion.174), channel_id=1, source_target_pairs={{0,8},{2,10},{4,12},{6,14},{8,0},{10,2},{12,4},{14,6},{16,24},{18,... | collective-permute-start | bytes 3072008 | tf_op jit(solution)/shard_map/ppermute | solution.py:476
  726.6 32.2 %all-to-all-start.12 = ((bf16[8,16,2048]{2,1,0:T(8,128)(2,1)}), bf16[8,16,2048]{2,1,0:T(8,128)(2,1)S(1)}, u32[]{:S(2)}, u32[]{:S(2)}) async-start(bf16[8,16,2048]{2,1,0:T(8,128)(2,1)} %fusion.168), calls=%async_computation.12 | async-start | bytes 1048576 | tf_op jit(solution)/shard_map/all_to_all | solution.py:525
  733.7 25.1 %collective-permute-start.18 = (bf16[8,16,2048]{2,1,0:T(8,128)(2,1)}, bf16[8,16,2048]{2,1,0:T(8,128)(2,1)}, u32[]{:S(2)}, u32[]{:S(2)}) collective-permute-start(bf16[8,16,2048]{2,1,0:T(8,128)(2,1)} %fusion.192), channel_id=1, source_target_pairs={{0,1},{1,0},{2,3},{3,2},{4,5},{5,4},{6,7},{7,6},{8,9},{9,8},{10,11... | collective-permute-start | bytes 1572872 | tf_op jit(solution)/shard_map/ppermute | solution.py:476
  762.1 45.4 %collective-permute-start.22 = (bf16[8,16,4096]{2,1,0:T(8,128)(2,1)}, bf16[8,16,4096]{2,1,0:T(8,128)(2,1)}, u32[]{:S(2)}, u32[]{:S(2)}) collective-permute-start(bf16[8,16,4096]{2,1,0:T(8,128)(2,1)} %fusion.154), channel_id=1, source_target_pairs={{0,1},{1,0},{2,3},{3,2},{4,5},{5,4},{6,7},{7,6},{8,9},{9,8},{10,11... | collective-permute-start | bytes 3145736 | tf_op jit(solution)/shard_map/ppermute | solution.py:476
  764.7 42.7 %all-to-all-start.13 = ((bf16[8,16,2048]{2,1,0:T(8,128)(2,1)}), bf16[8,16,2048]{2,1,0:T(8,128)(2,1)S(1)}, u32[]{:S(2)}, u32[]{:S(2)}) async-start(bf16[8,16,2048]{2,1,0:T(8,128)(2,1)} %fusion.159), calls=%async_computation.13 | async-start | bytes 1048576 | tf_op jit(solution)/shard_map/all_to_all | solution.py:525
  776.2 31.2 %collective-permute-start.20 = (bf16[1,1000,256]{2,1,0:T(8,128)(2,1)}, bf16[1,1000,256]{2,1,0:T(8,128)(2,1)S(1)}, u32[]{:S(2)}, u32[]{:S(2)}) collective-permute-start(bf16[1,1000,256]{2,1,0:T(8,128)(2,1)} %fusion.179), channel_id=1, source_target_pairs={{0,16},{2,18},{4,20},{6,22},{8,24},{10,26},{12,28},{14,30},{16,0},... | collective-permute-start | bytes 1536008 | tf_op jit(solution)/shard_map/ppermute | solution.py:476
  780.6 26.8 %collective-permute-start.21 = (f32[16,4096]{1,0:T(8,128)S(1)}, f32[16,4096]{1,0:T(8,128)S(1)}, u32[]{:S(2)}, u32[]{:S(2)}) collective-permute-start(f32[16,4096]{1,0:T(8,128)S(1)} %convert_reduce_fusion.3), channel_id=1, source_target_pairs={{0,1},{1,0},{2,3},{3,2},{4,5},{5,4},{6,7},{7,6},{8,9},{9,8},{10,11... | collective-permute-start | bytes 786440 | tf_op jit(solution)/shard_map/ppermute | solution.py:476
  811.7 42.2 %all-to-all-start.15 = ((bf16[32,48,512]{2,1,0:T(8,128)(2,1)}), bf16[32,48,512]{2,1,0:T(8,128)(2,1)}, u32[]{:S(2)}, u32[]{:S(2)}) async-start(bf16[32,48,512]{2,1,0:T(8,128)(2,1)} %bitcast.806), calls=%async_computation.15 | async-start | bytes 3145728 | tf_op jit(solution)/shard_map/all_to_all | solution.py:496
  820.5 55.7 %collective-permute-start.25 = (bf16[8,32,2304]{2,1,0:T(8,128)(2,1)}, bf16[8,32,2304]{2,1,0:T(8,128)(2,1)}, u32[]{:S(2)}, u32[]{:S(2)}) collective-permute-start(bf16[8,32,2304]{2,1,0:T(8,128)(2,1)} %pad_maximum_fusion.6), channel_id=1, source_target_pairs={{0,2},{2,0},{4,6},{6,4},{8,10},{10,8},{12,14},{14,12},{16,18},{18,... | collective-permute-start | bytes 3538952 | tf_op jit(solution)/shard_map/ppermute | solution.py:476
  864.0 30.0 %all-to-all-start.16 = ((bf16[8,16,4096]{2,1,0:T(8,128)(2,1)}), bf16[8,16,4096]{2,1,0:T(8,128)(2,1)S(1)}, u32[]{:S(2)}, u32[]{:S(2)}) async-start(bf16[8,16,4096]{2,1,0:T(8,128)(2,1)} %fusion.126), calls=%async_computation.16 | async-start | bytes 2097152 | tf_op jit(solution)/shard_map/all_to_all | solution.py:525
  895.0 53.8 %all-to-all-start.14 = ((bf16[32,64,512]{2,1,0:T(8,128)(2,1)}), bf16[32,64,512]{2,1,0:T(8,128)(2,1)}, u32[]{:S(2)}, u32[]{:S(2)}) async-start(bf16[32,64,512]{2,1,0:T(8,128)(2,1)} %bitcast.778), calls=%async_computation.14 | async-start | bytes 4194304 | tf_op jit(solution)/shard_map/all_to_all | solution.py:496
  917.3 20.4 %collective-permute-start.26 = (bf16[8,16,2304]{2,1,0:T(8,128)(2,1)}, bf16[8,16,2304]{2,1,0:T(8,128)(2,1)}, u32[]{:S(2)}, u32[]{:S(2)}) collective-permute-start(bf16[8,16,2304]{2,1,0:T(8,128)(2,1)} %fusion.188), channel_id=1, source_target_pairs={{0,1},{1,0},{2,3},{3,2},{4,5},{5,4},{6,7},{7,6},{8,9},{9,8},{10,11... | collective-permute-start | bytes 1769480 | tf_op jit(solution)/shard_map/ppermute | solution.py:476
  960.8 20.3 %all-to-all-start.18 = ((bf16[8,16,2304]{2,1,0:T(8,128)(2,1)}), bf16[8,16,2304]{2,1,0:T(8,128)(2,1)}, u32[]{:S(2)}, u32[]{:S(2)}) async-start(bf16[8,16,2304]{2,1,0:T(8,128)(2,1)} %fusion.148), calls=%async_computation.18 | async-start | bytes 1179648 | tf_op jit(solution)/shard_map/all_to_all | solution.py:525
  994.1 10.6 %all-to-all-start.19 = ((f32[32,1,8]{2,1,0:T(1,128)}), f32[32,1,8]{2,1,0:T(1,128)S(1)}, u32[]{:S(2)}, u32[]{:S(2)}) async-start(f32[32,1,8]{2,1,0:T(1,128)} %broadcast_in_dim.411), calls=%async_computation.19 | async-start | bytes 32768 | tf_op jit(solution)/shard_map/all_to_all | solution.py:496
  (220 other events, 2395.5 us)
Sparse Core Ops, SparseCore 0:
  24.1 145.5 all-gather.4
  172.0 149.1 all-gather.2
